TPU v7x, 32 devices: a whole 2x2x4 slice. The times are simulated.
32 devices in a mesh: expert: 4 (over z), shard: 8 (over y, x, core).
Axes of the slice: x: 2, y: 2, z: 4, core: 2. Of those that a mesh axis runs over, the one named last changes fastest.
Arguments:
- hidden_in: bfloat16 [26624, 768], P(('expert', 'shard')), may hold values from -6 to 6
- prior_logits: float32 [26624, 8], P(('expert', 'shard')), may hold values from -3 to 3
- project_weight: bfloat16 [2, 3, 768, 768], P(None, None, 'shard'), may hold values from -0.21875 to 0.21875
- output_weight: bfloat16 [2, 768, 768], P(None, 'shard'), may hold values from -1.75 to 1.75
- norm_gain: bfloat16 [2, 2, 768], P(None, None, 'shard'), may hold values from 0.5 to 1.5
- router_weight: bfloat16 [2, 768, 8], P(None, 'shard'), may hold values from -0.15625 to 0.15625
- mixing_weight: float32 [2, 8, 8], replicated, may hold values from -1.5 to 1.5
- const_vector: bfloat16 [2, 2, 768], P(None, None, 'shard'), may hold values from -6 to 6
- const_weight: bfloat16 [2, 2, 768, 2], P(None, None, 'shard'), may hold values from -0.21875 to 0.21875
- gate_weight: bfloat16 [2, 4, 768, 2048], P(None, 'expert', 'shard'), may hold values from -0.21875 to 0.21875
- up_weight: bfloat16 [2, 4, 768, 2048], P(None, 'expert', 'shard'), may hold values from -0.21875 to 0.21875
- down_weight: bfloat16 [2, 4, 2048, 768], P(None, 'expert', 'shard'), may hold values from -0.75 to 0.75
- routes: int32 [2, 26624, 2], P(None, ('expert', 'shard')), may hold values from 0 to 7, all different within a row
- priority: int32 [32, 832], P(('expert', 'shard')), may hold values from 0 to 831, each once within a row
- leaf_parent: int32 [32, 8], P(('expert', 'shard')), may hold values from 0 to 3
- cotangent: bfloat16 [26624, 768], P(('expert', 'shard')), may hold values from -6 to 6
Outputs:
- hidden_out: bfloat16 [26624, 768], P(('expert', 'shard'))
- hidden_grad: float32 [26624, 768], P(('expert', 'shard'))
- prior_grad: float32 [26624, 8], P(('expert', 'shard'))
- project_grad: float32 [2, 3, 768, 768], P(None, None, 'shard')
- output_grad: float32 [2, 768, 768], P(None, 'shard')
- gain_grad: float32 [2, 2, 768], P(None, None, 'shard')
- router_grad: float32 [2, 768, 8], P(None, 'shard')
- mixing_grad: float32 [2, 8, 8], replicated
- vector_grad: float32 [2, 2, 768], P(None, None, 'shard')
- const_grad: float32 [2, 2, 768, 2], P(None, None, 'shard')
- gate_grad: float32 [2, 4, 768, 2048], P(None, 'expert', 'shard')
- up_grad: float32 [2, 4, 768, 2048], P(None, 'expert', 'shard')
- down_grad: float32 [2, 4, 2048, 768], P(None, 'expert', 'shard')
Inputs may be any that keep to these rules, and one draw needn't show every extreme that they name: A token's 2 routes in a block name different experts. `priority`: each device's row is a permutation.
All inputs are finite; a program needn't handle non-finite values.
Results may differ from a plain program's by a relative error of at most 0.023.
Values may be sent and summed in bfloat16 or wider, within the bound.
A program may use at most 256 MiB of HBM per device.

v0:
```python
import jax
import jax.numpy as jnp
from jax import lax
from jax.sharding import PartitionSpec as P

D = 768
H = 12
HD = 64
TOP = 2
LAYERS = 2
EXP_DEV = 1
TRUNK = 320
BRANCH = 64
LEAF = 32
TREES_DEV = 1
TREE = 832


epsilon = 1e-06
highest = lax.Precision.HIGHEST
masked_fill = -1e30


def rmsnorm(values, gain):
    return values * lax.rsqrt(jnp.mean(values * values, axis=-1, keepdims=True) + epsilon) * gain


def softmax_rows(logits):
    peak_value = jnp.max(logits, axis=-1, keepdims=True)
    exponent = jnp.exp(logits - peak_value)
    return exponent / jnp.sum(exponent, axis=-1, keepdims=True)


def tree_visible(parents):
    position = jnp.arange(TREE, dtype=jnp.int32)
    offset = position - TRUNK
    segment = jnp.where(
        position < TRUNK,
        0,
        jnp.where(offset < 4 * BRANCH, 1 + offset // BRANCH, 5 + (offset - 4 * BRANCH) // LEAF),
    )
    leaf_hits = (segment[:, None] - 5 == jnp.arange(8, dtype=jnp.int32)[None, :]).astype(jnp.int32)
    upper = jnp.where(segment >= 5, 1 + jnp.sum(leaf_hits * parents[None, :], axis=1), 0)
    key_segment = segment[None, :]
    causal = position[None, :] <= position[:, None]
    return causal & (
        (key_segment == segment[:, None]) | (key_segment == 0) | (key_segment == upper[:, None])
    )


def side_experts(normed, gate_values, chosen, vectors, constants, experts_ffn):
    copy_share = jnp.sum(gate_values * (chosen == experts_ffn + 1).astype(jnp.float32), axis=1)
    result = copy_share[:, None] * normed
    for const_index in range(2):
        share_const = jnp.sum(
            gate_values * (chosen == experts_ffn + 2 + const_index).astype(jnp.float32), axis=1
        )
        mixture = softmax_rows(jnp.dot(normed, constants[const_index], precision=highest))
        result = result + share_const[:, None] * (
            mixture[:, 0:1] * normed + mixture[:, 1:2] * vectors[const_index][None, :]
        )
    return result


def combine_local(
    normed,
    prior,
    router_full,
    mixing,
    vectors,
    constants,
    expert_rows,
    chosen,
    route_kept,
    experts_ffn,
):
    logits = jnp.dot(normed, router_full, precision=highest) + jnp.dot(
        prior, mixing, precision=highest
    )
    chances = softmax_rows(logits)
    labels = jnp.arange(experts_ffn + 4, dtype=jnp.int32)
    choose = (chosen[:, :, None] == labels[None, None, :]).astype(jnp.float32)
    gate_values = jnp.sum(choose * chances[:, None, :], axis=2)
    routed = jnp.sum((gate_values * route_kept)[:, :, None] * expert_rows, axis=1)
    return (
        routed + side_experts(normed, gate_values, chosen, vectors, constants, experts_ffn),
        logits,
    )


def dispatch_plan(chosen, ranking, experts_ffn, capacity):
    tokens_here = chosen.shape[0]
    labels = jnp.arange(experts_ffn, dtype=jnp.int32)
    route_hits = (chosen[:, :, None] == labels[None, None, :]).astype(jnp.int32)
    loaded = jnp.sum(route_hits, axis=1)
    earlier = (ranking[None, :] < ranking[:, None]).astype(jnp.int32)
    ranked = jnp.dot(earlier, loaded)
    kept_mask = loaded * (ranked < capacity).astype(jnp.int32)
    route_rank = jnp.sum(route_hits * ranked[:, None, :], axis=2)
    route_kept = jnp.sum(route_hits * kept_mask[:, None, :], axis=2)
    position = jnp.where(route_kept > 0, chosen * capacity + route_rank, 0)
    slot_ids = jnp.arange(capacity, dtype=jnp.int32)
    filled = (
        (ranked.T[:, None, :] == slot_ids[None, :, None]) & (kept_mask.T[:, None, :] > 0)
    ).astype(jnp.int32)
    token_ids = jnp.arange(tokens_here, dtype=jnp.int32)
    source_token = jnp.sum(filled * token_ids[None, None, :], axis=2)
    route_number = jnp.sum(route_hits * jnp.arange(TOP, dtype=jnp.int32)[None, :, None], axis=1).T
    source_route = source_token * TOP + jnp.sum(filled * route_number[:, None, :], axis=2)
    occupied = jnp.sum(filled, axis=2)
    return (route_kept, position, source_route, occupied)


def attention_forward(queries, keys, values, visible):
    score_scale = HD ** (-0.5)

    def one_tree(packed):
        tree_query, tree_keys, tree_values, tree_seen = packed

        def one_head(head_index):
            head_query = lax.dynamic_slice_in_dim(tree_query, head_index * HD, HD, 1)
            head_keys = lax.dynamic_slice_in_dim(tree_keys, head_index * HD, HD, 1)
            head_values = lax.dynamic_slice_in_dim(tree_values, head_index * HD, HD, 1)
            scores = (
                jnp.dot(head_query, head_keys.T, preferred_element_type=jnp.float32) * score_scale
            )
            scores = jnp.where(tree_seen, scores, masked_fill)
            peak_score = jnp.max(scores, axis=1, keepdims=True)
            exponent = jnp.exp(scores - peak_score)
            summed = jnp.sum(exponent, axis=1, keepdims=True)
            mixed = jnp.dot(
                (exponent / summed).astype(jnp.bfloat16),
                head_values,
                preferred_element_type=jnp.float32,
            )
            return (mixed, (peak_score + jnp.log(summed))[:, 0])

        return lax.map(one_head, jnp.arange(H))

    return lax.map(one_tree, (queries, keys, values, visible))


def attention_backward(queries, keys, values, grad_mixed, log_totals, visible):
    score_scale = HD ** (-0.5)

    def one_tree(packed):
        tree_query, tree_keys, tree_values, tree_grad, tree_logsum, tree_seen = packed

        def one_head(head_index):
            head_query = lax.dynamic_slice_in_dim(tree_query, head_index * HD, HD, 1)
            head_keys = lax.dynamic_slice_in_dim(tree_keys, head_index * HD, HD, 1)
            head_values = lax.dynamic_slice_in_dim(tree_values, head_index * HD, HD, 1)
            head_grad = lax.dynamic_slice_in_dim(tree_grad, head_index * HD, HD, 1)
            scores = (
                jnp.dot(head_query, head_keys.T, preferred_element_type=jnp.float32) * score_scale
            )
            attention = jnp.where(
                tree_seen, jnp.exp(scores - tree_logsum[head_index][:, None]), 0.0
            )
            grad_attention = jnp.dot(head_grad, head_values.T, preferred_element_type=jnp.float32)
            grad_value = jnp.dot(
                attention.astype(jnp.bfloat16).T, head_grad, preferred_element_type=jnp.float32
            )
            dot_inner = jnp.sum(grad_attention * attention, axis=1, keepdims=True)
            grad_scores = (attention * (grad_attention - dot_inner)).astype(jnp.bfloat16)
            grad_query = (
                jnp.dot(grad_scores, head_keys, preferred_element_type=jnp.float32) * score_scale
            )
            grad_key = (
                jnp.dot(grad_scores.T, head_query, preferred_element_type=jnp.float32) * score_scale
            )
            return (grad_query, grad_key, grad_value)

        return lax.map(one_head, jnp.arange(H))

    return lax.map(one_tree, (queries, keys, values, grad_mixed, log_totals, visible))


def fetch_dense(
    project_weight, output_weight, norm_gain, router_weight, const_vector, const_weight, layer_index
):
    return (
        lax.all_gather(project_weight[layer_index], "shard", axis=1, tiled=True),
        lax.all_gather(output_weight[layer_index], "shard", axis=0, tiled=True),
        lax.all_gather(norm_gain[layer_index], "shard", axis=1, tiled=True),
        lax.all_gather(router_weight[layer_index], "shard", axis=0, tiled=True),
        lax.all_gather(const_vector[layer_index], "shard", axis=1, tiled=True),
        lax.all_gather(const_weight[layer_index], "shard", axis=1, tiled=True),
    )


def fetch_experts(gate_weight, up_weight, down_weight, layer_index):
    return (
        lax.all_gather(gate_weight[layer_index], "shard", axis=1, tiled=True),
        lax.all_gather(up_weight[layer_index], "shard", axis=1, tiled=True),
        lax.all_gather(down_weight[layer_index], "shard", axis=1, tiled=True),
    )


def heads_to_rows(per_head, tokens_here):
    return per_head.transpose(0, 2, 1, 3).reshape(tokens_here, D)


def on_device(
    hidden_in,
    prior_logits,
    project_weight,
    output_weight,
    norm_gain,
    router_weight,
    mixing_weight,
    const_vector,
    const_weight,
    gate_weight,
    up_weight,
    down_weight,
    routes,
    priority,
    leaf_parent,
    cotangent,
):
    owners = lax.axis_size("expert")
    experts_ffn = EXP_DEV * owners
    tokens_here = hidden_in.shape[0]
    capacity = 9 * tokens_here * TOP // (8 * (experts_ffn + 4))
    ranking = priority[0]
    visible = jax.vmap(tree_visible)(leaf_parent)
    hidden = hidden_in.astype(jnp.float32)
    logits = prior_logits
    kept_states = []
    kept_dense = []
    kept_experts = []
    for layer_index in range(LAYERS):
        dense = fetch_dense(
            project_weight,
            output_weight,
            norm_gain,
            router_weight,
            const_vector,
            const_weight,
            layer_index,
        )
        experts = fetch_experts(gate_weight, up_weight, down_weight, layer_index)
        project_full, output_full, gains_full, router_full, vectors_full, constants_full = dense
        gate_full, up_full, down_full = experts
        normed = rmsnorm(hidden, gains_full[0].astype(jnp.float32)).astype(jnp.bfloat16)
        projected = jnp.einsum(
            "td,cde->cte", normed, project_full, preferred_element_type=jnp.float32
        ).astype(jnp.bfloat16)
        trees = projected.reshape(3, TREES_DEV, TREE, D)
        mixed, log_totals = attention_forward(trees[0], trees[1], trees[2], visible)
        attended = heads_to_rows(mixed, tokens_here).astype(jnp.bfloat16)
        middle = hidden + jnp.dot(attended, output_full, preferred_element_type=jnp.float32)
        normed_mid = rmsnorm(middle, gains_full[1].astype(jnp.float32)).astype(jnp.bfloat16)
        route_kept, position, source_route, occupied = dispatch_plan(
            routes[layer_index], ranking, experts_ffn, capacity
        )
        outgoing = jnp.where(occupied[:, :, None] > 0, normed_mid[source_route // TOP], 0)
        received = lax.all_to_all(outgoing, "expert", split_axis=0, concat_axis=1, tiled=True)
        gate_value = jnp.einsum(
            "erd,edf->erf", received, gate_full, preferred_element_type=jnp.float32
        )
        up_value = jnp.einsum("erd,edf->erf", received, up_full, preferred_element_type=jnp.float32)
        hidden_act = (jax.nn.silu(gate_value) * up_value).astype(jnp.bfloat16)
        produced = jnp.einsum(
            "erf,efd->erd", hidden_act, down_full, preferred_element_type=jnp.float32
        ).astype(jnp.bfloat16)
        returned = lax.all_to_all(produced, "expert", split_axis=1, concat_axis=0, tiled=True)
        expert_rows = (
            returned.reshape(experts_ffn * capacity, D)[position.reshape(-1)]
            .reshape(tokens_here, TOP, D)
            .astype(jnp.float32)
        )
        moe, next_logits = combine_local(
            normed_mid.astype(jnp.float32),
            logits,
            router_full.astype(jnp.float32),
            mixing_weight[layer_index],
            vectors_full.astype(jnp.float32),
            constants_full.astype(jnp.float32),
            expert_rows,
            routes[layer_index],
            route_kept.astype(jnp.float32),
            experts_ffn,
        )
        kept_states.append(
            (
                hidden,
                middle,
                normed,
                projected,
                attended,
                log_totals,
                normed_mid,
                route_kept,
                position,
                source_route,
                occupied,
                received,
                gate_value,
                up_value,
                hidden_act,
                expert_rows,
                logits,
            )
        )
        kept_dense.append(dense)
        kept_experts.append(experts)
        hidden = middle + moe
        logits = next_logits
    hidden_out = hidden.astype(jnp.bfloat16)
    grad_hidden = cotangent.astype(jnp.float32)
    grad_logits = jnp.zeros_like(logits)
    grads_project = [None] * LAYERS
    grads_output = [None] * LAYERS
    grads_gain = [None] * LAYERS
    grads_router = [None] * LAYERS
    grads_mixing = [None] * LAYERS
    grads_vector = [None] * LAYERS
    grads_const = [None] * LAYERS
    grads_gate = [None] * LAYERS
    grads_up = [None] * LAYERS
    grads_down = [None] * LAYERS
    for layer_index in range(LAYERS - 1, -1, -1):
        (
            hidden,
            middle,
            normed,
            projected,
            attended,
            log_totals,
            normed_mid,
            route_kept,
            position,
            source_route,
            occupied,
            received,
            gate_value,
            up_value,
            hidden_act,
            expert_rows,
            logits,
        ) = kept_states[layer_index]
        dense = fetch_dense(
            project_weight,
            output_weight,
            norm_gain,
            router_weight,
            const_vector,
            const_weight,
            layer_index,
        )
        experts = fetch_experts(gate_weight, up_weight, down_weight, layer_index)
        project_full, output_full, gains_full, router_full, vectors_full, constants_full = dense
        gate_full, up_full, down_full = experts
        chosen = routes[layer_index]
        kept_float = route_kept.astype(jnp.float32)

        def combine_fixed(
            normed_float, prior, router_float, mixing, vectors, constants, rows_float
        ):
            return combine_local(
                normed_float,
                prior,
                router_float,
                mixing,
                vectors,
                constants,
                rows_float,
                chosen,
                kept_float,
                experts_ffn,
            )

        outputs_pair, pullback = jax.vjp(
            combine_fixed,
            normed_mid.astype(jnp.float32),
            logits,
            router_full.astype(jnp.float32),
            mixing_weight[layer_index],
            vectors_full.astype(jnp.float32),
            constants_full.astype(jnp.float32),
            expert_rows,
        )
        (
            grad_normed,
            grad_prior,
            grad_router,
            grad_mixing,
            grad_vectors,
            grad_constants,
            grad_rows,
        ) = pullback((grad_hidden, grad_logits))
        rows_half = grad_rows.astype(jnp.bfloat16).reshape(tokens_here * TOP, D)
        outgoing_grad = jnp.where(occupied[:, :, None] > 0, rows_half[source_route], 0)
        grad_received = lax.all_to_all(
            outgoing_grad, "expert", split_axis=0, concat_axis=1, tiled=True
        )
        grad_act = jnp.einsum(
            "erd,efd->erf", grad_received, down_full, preferred_element_type=jnp.float32
        )
        grads_down[layer_index] = jnp.einsum(
            "erf,erd->efd", hidden_act, grad_received, preferred_element_type=jnp.float32
        )
        sigmoid_gate = jax.nn.sigmoid(gate_value)
        grad_gate_val = (
            grad_act * up_value * sigmoid_gate * (1.0 + gate_value * (1.0 - sigmoid_gate))
        ).astype(jnp.bfloat16)
        grad_up_val = (grad_act * gate_value * sigmoid_gate).astype(jnp.bfloat16)
        grad_inputs = (
            jnp.einsum("erf,edf->erd", grad_gate_val, gate_full, preferred_element_type=jnp.float32)
            + jnp.einsum("erf,edf->erd", grad_up_val, up_full, preferred_element_type=jnp.float32)
        ).astype(jnp.bfloat16)
        grads_gate[layer_index] = jnp.einsum(
            "erd,erf->edf", received, grad_gate_val, preferred_element_type=jnp.float32
        )
        grads_up[layer_index] = jnp.einsum(
            "erd,erf->edf", received, grad_up_val, preferred_element_type=jnp.float32
        )
        returned_grad = lax.all_to_all(
            grad_inputs, "expert", split_axis=1, concat_axis=0, tiled=True
        )
        back_rows = (
            returned_grad.reshape(experts_ffn * capacity, D)[position.reshape(-1)]
            .reshape(tokens_here, TOP, D)
            .astype(jnp.float32)
        )
        grad_normed = grad_normed + jnp.sum(kept_float[:, :, None] * back_rows, axis=1)
        norm_value, norm_pull = jax.vjp(rmsnorm, middle, gains_full[1].astype(jnp.float32))
        grad_mid_norm, grad_gain_mid = norm_pull(grad_normed)
        grad_middle = grad_hidden + grad_mid_norm
        grad_attn = grad_middle.astype(jnp.bfloat16)
        grads_output[layer_index] = jnp.dot(
            attended.T, grad_attn, preferred_element_type=jnp.float32
        )
        grad_attended = jnp.dot(
            grad_attn, output_full.T, preferred_element_type=jnp.float32
        ).astype(jnp.bfloat16)
        trees = projected.reshape(3, TREES_DEV, TREE, D)
        grad_query, grad_key, grad_value = attention_backward(
            trees[0],
            trees[1],
            trees[2],
            grad_attended.reshape(TREES_DEV, TREE, D),
            log_totals,
            visible,
        )
        grad_projected = jnp.stack(
            [
                heads_to_rows(grad_query, tokens_here),
                heads_to_rows(grad_key, tokens_here),
                heads_to_rows(grad_value, tokens_here),
            ]
        ).astype(jnp.bfloat16)
        grads_project[layer_index] = jnp.einsum(
            "td,cte->cde", normed, grad_projected, preferred_element_type=jnp.float32
        )
        grad_normed_in = jnp.einsum(
            "cte,cde->td", grad_projected, project_full, preferred_element_type=jnp.float32
        )
        input_value, input_pull = jax.vjp(rmsnorm, hidden, gains_full[0].astype(jnp.float32))
        grad_in_norm, grad_gain_in = input_pull(grad_normed_in)
        grad_hidden = grad_middle + grad_in_norm
        grad_logits = grad_prior
        grads_gain[layer_index] = jnp.stack([grad_gain_in, grad_gain_mid])
        grads_router[layer_index] = grad_router
        grads_mixing[layer_index] = grad_mixing
        grads_vector[layer_index] = grad_vectors
        grads_const[layer_index] = grad_constants
    dense_parts = (
        lax.psum_scatter(
            jnp.stack(grads_project).astype(jnp.bfloat16), "shard", scatter_dimension=2, tiled=True
        ).astype(jnp.float32),
        lax.psum_scatter(
            jnp.stack(grads_output).astype(jnp.bfloat16), "shard", scatter_dimension=1, tiled=True
        ).astype(jnp.float32),
        lax.psum_scatter(
            jnp.stack(grads_gain).astype(jnp.bfloat16), "shard", scatter_dimension=2, tiled=True
        ).astype(jnp.float32),
        lax.psum_scatter(
            jnp.stack(grads_router).astype(jnp.bfloat16), "shard", scatter_dimension=1, tiled=True
        ).astype(jnp.float32),
        lax.psum_scatter(
            jnp.stack(grads_vector).astype(jnp.bfloat16), "shard", scatter_dimension=2, tiled=True
        ).astype(jnp.float32),
        lax.psum_scatter(
            jnp.stack(grads_const).astype(jnp.bfloat16), "shard", scatter_dimension=2, tiled=True
        ).astype(jnp.float32),
    )
    dense_parts = (
        lax.psum(dense_parts[0].astype(jnp.bfloat16), "expert").astype(jnp.float32),
        lax.psum(dense_parts[1].astype(jnp.bfloat16), "expert").astype(jnp.float32),
        lax.psum(dense_parts[2].astype(jnp.bfloat16), "expert").astype(jnp.float32),
        lax.psum(dense_parts[3].astype(jnp.bfloat16), "expert").astype(jnp.float32),
        lax.psum(dense_parts[4].astype(jnp.bfloat16), "expert").astype(jnp.float32),
        lax.psum(dense_parts[5].astype(jnp.bfloat16), "expert").astype(jnp.float32),
    )
    expert_parts = (
        lax.psum_scatter(
            jnp.stack(grads_gate).astype(jnp.bfloat16), "shard", scatter_dimension=2, tiled=True
        ).astype(jnp.float32),
        lax.psum_scatter(
            jnp.stack(grads_up).astype(jnp.bfloat16), "shard", scatter_dimension=2, tiled=True
        ).astype(jnp.float32),
        lax.psum_scatter(
            jnp.stack(grads_down).astype(jnp.bfloat16), "shard", scatter_dimension=2, tiled=True
        ).astype(jnp.float32),
    )
    mixing_total = lax.psum(jnp.stack(grads_mixing), ("expert", "shard"))
    return (
        hidden_out,
        grad_hidden,
        grad_logits,
        dense_parts[0],
        dense_parts[1],
        dense_parts[2],
        dense_parts[3],
        mixing_total,
        dense_parts[4],
        dense_parts[5],
        expert_parts[0],
        expert_parts[1],
        expert_parts[2],
    )


def solution(mesh):
    in_specs = (
        P(("expert", "shard"), None),
        P(("expert", "shard"), None),
        P(None, None, "shard", None),
        P(None, "shard", None),
        P(None, None, "shard"),
        P(None, "shard", None),
        P(),
        P(None, None, "shard"),
        P(None, None, "shard", None),
        P(None, "expert", "shard", None),
        P(None, "expert", "shard", None),
        P(None, "expert", "shard", None),
        P(None, ("expert", "shard"), None),
        P(("expert", "shard"), None),
        P(("expert", "shard"), None),
        P(("expert", "shard"), None),
    )
    out_specs = (
        P(("expert", "shard"), None),
        P(("expert", "shard"), None),
        P(("expert", "shard"), None),
        P(None, None, "shard", None),
        P(None, "shard", None),
        P(None, None, "shard"),
        P(None, "shard", None),
        P(),
        P(None, None, "shard"),
        P(None, None, "shard", None),
        P(None, "expert", "shard", None),
        P(None, "expert", "shard", None),
        P(None, "expert", "shard", None),
    )
    return jax.shard_map(
        on_device, mesh=mesh, in_specs=in_specs, out_specs=out_specs, check_vma=False
    )
```

profile of v0, /device:TPU:0, one launch (start us, length us, event | category | flops | bytes accessed | tf_op | source)
XLA Modules:
  0.0 1980.6 jit_solution(13416180009815129708)
XLA Ops:
  18.0 12.6 all-gather
  41.4 12.3 convert_reduce_fusion.1
  56.0 9.7 all-gather.7
  75.6 73.0 %while.96 = (s32[]{:T(128)}, bf16[12,832,64]{1,2,0:T(8,128)(2,1)}, f32[12,832]{1,0:T(8,128)S(1)}, s32[12]{0:T(128)S(1)}, bf16[832,768]{1,0:T(8,128)(2,1)}, /*ind...) while((s32[]{:T(128)}, bf16[12,832,64]{1,2,0:T(8,128)(2,1)}, ...), condition=%wide.region_5.6_spmd.clone, body=%wide.region_2.5_spmd.clone.sunk | while | flops 186899648 | bytes 9229523 | solution.py:138
  173.6 8.7 all-gather.3
  182.7 9.4 all-gather.8
  198.8 7.6 broadcast_in_dim.345
  206.5 9.8 all-gather.12
  216.7 12.6 convert_reduce_fusion
  229.8 10.7 all-gather.9
  254.0 8.5 fusion.122
  262.5 13.0 multiply_convert_fusion.7
  286.1 11.8 reduce.50
  309.6 30.5 %all-to-all-done.1 = bf16[4,2,89856]{2,1,0:T(2,128)(2,1)} async-done(((bf16[4,2,89856]{2,1,0:T(2,128)(2,1)}), bf16[4,2,89856]{2,1,0:T(2,128)(2,1)}, u32[]{:S(2)}, u32[]{:S(2)}) %all-to-all-start.1) | async-done | bytes 1437728 | tf_op jit(solution)/shard_map/all_to_all | solution.py:268
  360.5 26.0 %multiply_reduce_fusion.7 = f32[832,768]{1,0:T(8,128)S(1)} fusion(f32[832,2,768]{2,1,0:T(2,128)} %reshape.1382, f32[832,2]{1,0:T(8,128)S(1)} %copy.272), kind=kLoop, calls=%fused_computation.131 | loop fusion | flops 1916928 | bytes 7674368 | tf_op jit(solution)/shard_map/reduce_sum | solution.py:84
  399.1 72.9 %while.97 = (s32[]{:T(128)}, bf16[12,832,64]{1,2,0:T(8,128)(2,1)}, f32[12,832]{1,0:T(8,128)S(1)}, s32[12]{0:T(128)S(1)}, bf16[832,768]{1,0:T(8,128)(2,1)}, /*ind...) while((s32[]{:T(128)}, bf16[12,832,64]{1,2,0:T(8,128)(2,1)}, ...), condition=%wide.region_29.30_spmd.clone, body=%wide.region_26.29_spmd.clone.sunk | while | flops 186899648 | bytes 9229523 | solution.py:138
  483.0 7.6 gather_fusion.4
  510.0 34.0 %all-to-all-done.4 = bf16[4,234,768]{2,1,0:T(8,128)(2,1)} async-done(((bf16[4,234,768]{2,1,0:T(8,128)(2,1)}), bf16[4,234,768]{2,1,0:T(8,128)(2,1)}, u32[]{:S(2)}, u32[]{:S(2)}) %all-to-all-start.4) | async-done | bytes 1437728 | tf_op jit(solution)/shard_map/all_to_all | solution.py:396
  553.0 8.6 all-gather.17
  562.2 9.5 all-gather.16
  589.8 8.6 fusion.100
  598.3 8.6 fusion.106
  606.9 13.4 multiply_convert_fusion.5
  631.6 11.6 reduce.51
  660.6 11.2 reduce.52
  674.8 10.9 all-to-all-done.5
  744.3 14.5 multiply_reduce_fusion.5
  760.2 25.8 %multiply_reduce_fusion.4 = f32[832,768]{1,0:T(8,128)S(1)} fusion(f32[832,2,768]{2,1,0:T(2,128)} %reshape.1386, f32[832,2]{1,0:T(8,128)} %copy.298), kind=kLoop, calls=%fused_computation.127 | loop fusion | flops 1916928 | bytes 7674368 | tf_op jit(solution)/shard_map/reduce_sum | solution.py:428
  799.0 173.9 %while.98 = (s32[]{:T(128)}, bf16[12,832,64]{1,2,0:T(8,128)(2,1)S(1)}, bf16[12,832,64]{1,2,0:T(8,128)(2,1)S(1)}, bf16[12,832,64]{1,2,0:T(8,128)(2,1)}, s32[12]{0...) while((s32[]{:T(128)}, ...), condition=%wide.region_71.72_spmd.clone, body=%wide.region_69.71_spmd.clone.sunk | while | flops 453512384 | bytes 23191844 | solution.py:174
  998.7 7.5 broadcast_in_dim.362
  1030.5 28.4 %all-to-all-done.6 = bf16[4,234,768]{2,1,0:T(8,128)(2,1)} async-done(((bf16[4,234,768]{2,1,0:T(8,128)(2,1)}), bf16[4,234,768]{2,1,0:T(8,128)(2,1)}, u32[]{:S(2)}, u32[]{:S(2)}) %all-to-all-start.6) | async-done | bytes 1437728 | tf_op jit(solution)/shard_map/all_to_all | solution.py:396
  1060.6 9.9 multiply_convert_fusion.3
  1080.3 11.0 reduce.53
  1109.9 21.5 %all-to-all-done.7 = bf16[4,2,89856]{2,1,0:T(2,128)(2,1)S(1)} async-done(((bf16[4,2,89856]{2,1,0:T(2,128)(2,1)}), bf16[4,2,89856]{2,1,0:T(2,128)(2,1)S(1)}, u32[]{:S(2)}, u32[]{:S(2)}) %all-to-all-start.7) | async-done | bytes 1437728 | tf_op jit(solution)/shard_map/all_to_all | solution.py:420
  1150.5 25.7 %multiply_reduce_fusion.2 = f32[832,768]{1,0:T(8,128)S(1)} fusion(f32[832,2,768]{2,1,0:T(2,128)} %reshape.1387, f32[832,2]{1,0:T(8,128)S(1)} %copy-done.38), kind=kLoop, calls=%fused_computation.124 | loop fusion | flops 1916928 | bytes 7674368 | tf_op jit(solution)/shard_map/reduce_sum | solution.py:428
  1187.2 188.9 %while.99 = (s32[]{:T(128)}, bf16[12,832,64]{1,2,0:T(8,128)(2,1)}, bf16[12,832,64]{1,2,0:T(8,128)(2,1)}, bf16[12,832,64]{1,2,0:T(8,128)(2,1)}, s32[12]{0:T(128)S...) while((s32[]{:T(128)}, bf16[12,832,64]{1,2,0:T(8,128)(2,1)}, ...), condition=%wide.region_95.96_spmd.clone, body=%wide.region_93.95_spmd.clone.sunk | while | flops 453512384 | bytes 22978852 | solution.py:174
  1394.2 18.3 copy.313
  1429.8 8.2 fusion.133
  1439.4 84.3 %all-reduce.22.cloned.1.call-done = bf16[2,3,768,768]{3,0,1,2:T(2,128)(2,1)} async-done(((bf16[2,3,768,768]{3,0,1,2:T(2,128)(2,1)}), bf16[2,3,768,768]{3,0,1,2:T(2,128)(2,1)}) %all-reduce.22.cloned.1.call-update) | async-done | bytes 7077904
  1526.3 43.1 %reduce-scatter.17.cloned.1.call-done = bf16[2,96,768]{2,1,0:T(8,128)(2,1)} async-done(((bf16[2,768,768]{2,1,0:T(8,128)(2,1)}), bf16[2,96,768]{2,1,0:T(8,128)(2,1)}) %reduce-scatter.17.cloned.1.call-update) | async-done | bytes 294928 | tf_op jit(solution)/shard_map/reduce_scatter | solution.py:474
  1611.1 39.4 %psum.53 = f32[2,8,8]{2,1,0:T(8,128)} all-reduce(f32[2,8,8]{2,1,0:T(8,128)S(1)} %pad_maximum_fusion.13), channel_id=1, replica_groups=mesh['expert'=4,'shard'=8] {'expert','shard'}, use_global_device_ids=true, to_apply=%region_109.110 | all-reduce | flops 128 | bytes 1024 | tf_op jit(solution)/shard_map/psum | solution.py:509
  1653.2 26.2 %reduce-scatter.27.cloned.1.call-done = bf16[96,16]{1,0:T(8,128)(2,1)} async-done(((bf16[768,16]{1,0:T(8,128)(2,1)}), bf16[96,16]{1,0:T(8,128)(2,1)}) %reduce-scatter.27.cloned.1.call-update) | async-done | bytes 3088
  1684.6 31.8 %reduce-scatter.25.cloned.1.call-done = bf16[96,4]{1,0:T(8,128)(2,1)} async-done(((bf16[768,4]{1,0:T(8,128)(2,1)}), bf16[96,4]{1,0:T(8,128)(2,1)}) %reduce-scatter.25.cloned.1.call-update) | async-done | bytes 784
  1717.3 11.9 all-reduce.17
  1731.6 44.1 %all-reduce.24.cloned.1.call-done = (bf16[2,3,96,768]{3,0,1,2:T(2,128)(2,1)}, bf16[2,96,768]{2,1,0:T(8,128)(2,1)}) async-done(((bf16[2,3,96,768]{3,0,1,2:T(2,128)(2,1)}, bf16[2,96,768]{2,1,0:T(8,128)(2,1)}), (bf16[2,3,96,768]{3,0,1,2:T(2,128)(2,1)}, bf16[2,96,768]{2,1,0:T(8,128)(2,1)})) %all-reduce.24.cloned.1.call-update) | async-done | bytes 1179664 | tf_op jit(solution)/shard_map/psum | solution.py:491
  1779.1 61.5 %reduce-scatter.19.cloned.1.call-done = bf16[2,1,96,2048]{3,2,1,0:T(8,128)(2,1)} async-done(((bf16[2,1,768,2048]{3,2,1,0:T(8,128)(2,1)}), bf16[2,1,96,2048]{3,2,1,0:T(8,128)(2,1)}) %reduce-scatter.19.cloned.1.call-update) | async-done | bytes 786448 | tf_op jit(solution)/shard_map/reduce_scatter | solution.py:499
  1843.1 62.7 %reduce-scatter.21.cloned.1.call-done = bf16[2,1,96,2048]{3,2,1,0:T(8,128)(2,1)} async-done(((bf16[2,1,768,2048]{3,2,1,0:T(8,128)(2,1)}), bf16[2,1,96,2048]{3,2,1,0:T(8,128)(2,1)}) %reduce-scatter.21.cloned.1.call-update) | async-done | bytes 786448 | tf_op jit(solution)/shard_map/reduce_scatter | solution.py:502
  1908.2 62.9 %reduce-scatter.23.cloned.1.call-done = bf16[2,1,256,768]{3,2,1,0:T(8,128)(2,1)} async-done(((bf16[2,1,2048,768]{3,2,1,0:T(8,128)(2,1)}), bf16[2,1,256,768]{3,2,1,0:T(8,128)(2,1)}) %reduce-scatter.23.cloned.1.call-update) | async-done | bytes 786448 | tf_op jit(solution)/shard_map/reduce_scatter | solution.py:505
  (1142 shorter events, 936.6 us)
Async XLA Ops:
  7.2 298.3 %copy-start = (f32[832,8]{0,1:T(8,128)S(1)}, f32[832,8]{0,1:T(8,128)}, u32[]{:S(2)}) copy-start(f32[832,8]{0,1:T(8,128)} %param.25) | copy-start | bytes 79876
  7.2 59.8 %all-gather.29.cloned.1.call-start = ((), (), s32[]{:S(2)}) async-start(), calls=%async_computation.20 | async-start | bytes 3981312 | tf_op jit(solution)/shard_map/all_gather | solution.py:183
  9.5 139.1 %all-gather.31.cloned.1.call-start = ((), (), s32[]{:S(2)}) async-start(), calls=%async_computation.21 | async-start | bytes 1327104 | tf_op jit(solution)/shard_map/all_gather | solution.py:184
  11.4 242.7 %all-gather.33.cloned.1.call-start = ((), (), s32[]{:S(2)}) async-start(), calls=%async_computation.22 | async-start | bytes 3538944 | tf_op jit(solution)/shard_map/all_gather | solution.py:194
  12.4 250.2 %all-gather.35.cloned.1.call-start = ((), (), s32[]{:S(2)}) async-start(), calls=%async_computation.23 | async-start | bytes 3538944 | tf_op jit(solution)/shard_map/all_gather | solution.py:195
  13.4 262.1 %all-gather.37.cloned.1.call-start = ((), (), s32[]{:S(2)}) async-start(), calls=%async_computation.24 | async-start | bytes 3538944 | tf_op jit(solution)/shard_map/all_gather | solution.py:196
  14.5 375.5 %all-gather.39.cloned.1.call-start = ((), (), s32[]{:S(2)}) async-start(), calls=%async_computation.25 | async-start | bytes 3981312 | tf_op jit(solution)/shard_map/all_gather | solution.py:183
  15.0 456.9 %all-gather.41.cloned.1.call-start = ((), (), s32[]{:S(2)}) async-start(), calls=%async_computation.26 | async-start | bytes 1327104 | tf_op jit(solution)/shard_map/all_gather | solution.py:184
  15.8 574.0 %all-gather.47.cloned.1.call-start = ((), (), s32[]{:S(2)}) async-start(), calls=%async_computation.29 | async-start | bytes 3538944 | tf_op jit(solution)/shard_map/all_gather | solution.py:196
  16.5 581.8 %all-gather.45.cloned.1.call-start = ((), (), s32[]{:S(2)}) async-start(), calls=%async_computation.28 | async-start | bytes 3538944 | tf_op jit(solution)/shard_map/all_gather | solution.py:195
  35.3 351.2 %copy-start.67 = (f32[768]{0:T(1024)}, f32[768]{0:T(1024)S(1)}, u32[]{:S(2)}) copy-start(f32[768]{0:T(1024)S(1)} %get-tuple-element.566) | copy-start | bytes 9220
  36.4 269.4 %copy-start.63 = (s32[832,2]{0,1:T(2,128)}, s32[832,2]{0,1:T(2,128)S(1)}, u32[]{:S(2)}) copy-start(s32[832,2]{0,1:T(2,128)S(1)} %get-tuple-element.761) | copy-start | bytes 19972
  41.4 509.0 %copy-start.60 = (s32[832,2]{0,1:T(2,128)}, s32[832,2]{0,1:T(2,128)S(1)}, u32[]{:S(2)}) copy-start(s32[832,2]{0,1:T(2,128)S(1)} %get-tuple-element.806) | copy-start | bytes 19972
  54.7 107.3 %copy-start.155 = (pred[4,234]{1,0:T(4,128)(4,1)}, pred[4,234]{1,0:T(4,128)(4,1)S(1)}, u32[]{:S(2)}) copy-start(pred[4,234]{1,0:T(4,128)(4,1)S(1)} %broadcast_compare_fusion.15) | copy-start | bytes 2812
  152.3 234.2 %copy-start.69 = (f32[832]{0:T(1024)}, f32[832]{0:T(1024)S(1)}, u32[]{:S(2)}) copy-start(f32[832]{0:T(1024)S(1)} %fusion.281) | copy-start | bytes 9988
  154.0 152.6 %copy-start.1 = (bf16[832,768]{1,0:T(8,128)(2,1)}, bf16[832,768]{1,0:T(8,128)(2,1)S(1)}, u32[]{:S(2)}) copy-start(bf16[832,768]{1,0:T(8,128)(2,1)S(1)} %multiply_convert_fusion.12) | copy-start | bytes 3833860
  164.7 86.3 %all-to-all-start = ((bf16[4,234,768]{2,1,0:T(8,128)(2,1)}), bf16[4,234,768]{2,1,0:T(8,128)(2,1)}, u32[]{:S(2)}, u32[]{:S(2)}) async-start(bf16[4,234,768]{2,1,0:T(8,128)(2,1)} %broadcast_select_fusion.3), calls=%async_computation | async-start | bytes 2949120 | tf_op jit(solution)/shard_map/all_to_all | solution.py:259
  241.3 106.0 %copy-start.82 = (s32[2048]{0:T(1024)}, s32[2048]{0:T(1024)S(1)}, u32[]{:S(2)}) copy-start(s32[2048]{0:T(1024)S(1)} %pad_clamp_fusion.1) | copy-start | bytes 24580
  245.9 140.6 %copy-start.102 = (f32[768]{0:T(1024)}, f32[768]{0:T(1024)S(1)}, u32[]{:S(2)}) copy-start(f32[768]{0:T(1024)S(1)} %get-tuple-element.564) | copy-start | bytes 9220
  245.9 140.6 %copy-start.104 = (f32[768]{0:T(1024)}, f32[768]{0:T(1024)S(1)}, u32[]{:S(2)}) copy-start(f32[768]{0:T(1024)S(1)} %get-tuple-element.565) | copy-start | bytes 9220
  250.6 139.4 %copy-start.138 = (f32[768]{0:T(1024)}, f32[768]{0:T(1024)S(1)}, u32[]{:S(2)}) copy-start(f32[768]{0:T(1024)S(1)} %get-tuple-element.563) | copy-start | bytes 9220
  300.7 39.4 %all-to-all-start.1 = ((bf16[4,2,89856]{2,1,0:T(2,128)(2,1)}), bf16[4,2,89856]{2,1,0:T(2,128)(2,1)}, u32[]{:S(2)}, u32[]{:S(2)}) async-start(bf16[4,2,89856]{2,1,0:T(2,128)(2,1)} %reshape.1544), calls=%async_computation.1 | async-start | bytes 2875392 | tf_op jit(solution)/shard_map/all_to_all | solution.py:268
  305.7 171.4 %copy-start.44 = (f32[832,8]{0,1:T(8,128)}, f32[832,8]{0,1:T(8,128)S(1)}, u32[]{:S(2)}) copy-start(f32[832,8]{0,1:T(8,128)S(1)} %get-tuple-element.785) | copy-start | bytes 79876
  305.7 277.1 %copy-start.88 = (f32[832]{0:T(1024)}, f32[832]{0:T(1024)S(1)}, u32[]{:S(2)}) copy-start(f32[832]{0:T(1024)S(1)} %fusion.231) | copy-start | bytes 9988
  307.1 276.3 %copy-start.86 = (f32[832]{0:T(1024)}, f32[832]{0:T(1024)S(1)}, u32[]{:S(2)}) copy-start(f32[832]{0:T(1024)S(1)} %get-tuple-element.804) | copy-start | bytes 9988
  476.7 174.9 %copy-start.3 = (bf16[832,768]{1,0:T(8,128)(2,1)}, bf16[832,768]{1,0:T(8,128)(2,1)S(1)}, u32[]{:S(2)}) copy-start(bf16[832,768]{1,0:T(8,128)(2,1)S(1)} %multiply_convert_fusion.10) | copy-start | bytes 3833860
  505.1 38.9 %all-to-all-start.4 = ((bf16[4,234,768]{2,1,0:T(8,128)(2,1)}), bf16[4,234,768]{2,1,0:T(8,128)(2,1)}, u32[]{:S(2)}, u32[]{:S(2)}) async-start(bf16[4,234,768]{2,1,0:T(8,128)(2,1)} %get-tuple-element.772), calls=%async_computation.4 | async-start | bytes 2949120 | tf_op jit(solution)/shard_map/all_to_all | solution.py:396
  509.4 97.6 %all-gather.43.cloned.1.call-start = ((), (), s32[]{:S(2)}) async-start(), calls=%async_computation.27 | async-start | bytes 3538944 | tf_op jit(solution)/shard_map/all_gather | solution.py:194
  544.0 42.9 %all-to-all-start.2 = ((bf16[4,234,768]{2,1,0:T(8,128)(2,1)}), bf16[4,234,768]{2,1,0:T(8,128)(2,1)}, u32[]{:S(2)}, u32[]{:S(2)}) async-start(bf16[4,234,768]{2,1,0:T(8,128)(2,1)} %get-tuple-element.773), calls=%async_computation.2 | async-start | bytes 2949120 | tf_op jit(solution)/shard_map/all_to_all | solution.py:259
  646.0 39.7 %all-to-all-start.5 = ((bf16[4,2,89856]{2,1,0:T(2,128)(2,1)}), bf16[4,2,89856]{2,1,0:T(2,128)(2,1)}, u32[]{:S(2)}, u32[]{:S(2)}) async-start(bf16[4,2,89856]{2,1,0:T(2,128)(2,1)} %reshape.1546), calls=%async_computation.5 | async-start | bytes 2875392 | tf_op jit(solution)/shard_map/all_to_all | solution.py:420
  652.1 135.2 %copy-start.123 = (pred[832,2]{0,1:T(4,128)(4,1)}, pred[832,2]{0,1:T(4,128)(4,1)S(1)}, u32[]{:S(2)}) copy-start(pred[832,2]{0,1:T(4,128)(4,1)S(1)} %get-tuple-element.706) | copy-start | bytes 4996
  685.7 38.1 %all-to-all-start.3 = ((bf16[4,2,89856]{2,1,0:T(2,128)(2,1)}), bf16[4,2,89856]{2,1,0:T(2,128)(2,1)}, u32[]{:S(2)}, u32[]{:S(2)}) async-start(bf16[4,2,89856]{2,1,0:T(2,128)(2,1)} %reshape.1548), calls=%async_computation.3 | async-start | bytes 2875392 | tf_op jit(solution)/shard_map/all_to_all | solution.py:268
  695.6 91.7 %copy-start.98 = (f32[832,2]{0,1:T(2,128)}, f32[832,2]{0,1:T(2,128)S(1)}, u32[]{:S(2)}) copy-start(f32[832,2]{0,1:T(2,128)S(1)} %get-tuple-element.704) | copy-start | bytes 19972
  695.6 91.7 %copy-start.118 = (f32[832]{0:T(1024)}, f32[832]{0:T(1024)S(1)}, u32[]{:S(2)}) copy-start(f32[832]{0:T(1024)S(1)} %negate_divide_fusion.4) | copy-start | bytes 9988
  1019.9 38.9 %all-to-all-start.6 = ((bf16[4,234,768]{2,1,0:T(8,128)(2,1)}), bf16[4,234,768]{2,1,0:T(8,128)(2,1)}, u32[]{:S(2)}, u32[]{:S(2)}) async-start(bf16[4,234,768]{2,1,0:T(8,128)(2,1)} %broadcast_select_fusion.2), calls=%async_computation.6 | async-start | bytes 2949120 | tf_op jit(solution)/shard_map/all_to_all | solution.py:396
  1094.2 37.2 %all-to-all-start.7 = ((bf16[4,2,89856]{2,1,0:T(2,128)(2,1)}), bf16[4,2,89856]{2,1,0:T(2,128)(2,1)S(1)}, u32[]{:S(2)}, u32[]{:S(2)}) async-start(bf16[4,2,89856]{2,1,0:T(2,128)(2,1)} %reshape.1550), calls=%async_computation.7 | async-start | bytes 2875392 | tf_op jit(solution)/shard_map/all_to_all | solution.py:420
  1097.9 425.8 %all-reduce.22.cloned.1.call-start = ((), (), s32[]{:S(2)}) async-start(), calls=%async_computation.34 | async-start | bytes 14155776
  1181.1 235.1 %copy-start.17 = (f32[832,768]{1,0:T(8,128)}, f32[832,768]{1,0:T(8,128)S(1)}, u32[]{:S(2)}) copy-start(f32[832,768]{1,0:T(8,128)S(1)} %fusion.135) | copy-start | bytes 7667716
  1412.5 157.0 %reduce-scatter.17.cloned.1.call-start = ((), (), s32[]{:S(2)}) async-start(), calls=%async_computation.16 | async-start | bytes 2654208 | tf_op jit(solution)/shard_map/reduce_scatter | solution.py:474
  1419.3 232.0 %reduce-scatter.29.cloned.1.call-start = ((), (), s32[]{:S(2)}) async-start(), calls=%async_computation.32 | async-start | bytes 221184
  1426.0 226.3 %reduce-scatter.31.cloned.1.call-start = ((), (), s32[]{:S(2)}) async-start(), calls=%async_computation.33 | async-start | bytes 221184
  1427.9 251.5 %reduce-scatter.27.cloned.1.call-start = ((), (), s32[]{:S(2)}) async-start(), calls=%async_computation.31 | async-start | bytes 221184
  1429.3 287.1 %reduce-scatter.25.cloned.1.call-start = ((), (), s32[]{:S(2)}) async-start(), calls=%async_computation.30 | async-start | bytes 221184
  1437.9 131.6 %copy-start.41 = (bf16[936,768]{1,0:T(8,128)(2,1)S(1)}, bf16[936,768]{1,0:T(8,128)(2,1)}, u32[]{:S(2)}) copy-start(bf16[936,768]{1,0:T(8,128)(2,1)} %reshape.1355) | copy-start | bytes 4313092
  1439.3 336.4 %all-reduce.24.cloned.1.call-start = ((), (), s32[]{:S(2)}) async-start(), calls=%async_computation.35 | async-start | bytes 2359296 | tf_op jit(solution)/shard_map/psum | solution.py:491
  1569.5 271.1 %reduce-scatter.19.cloned.1.call-start = ((), (), s32[]{:S(2)}) async-start(), calls=%async_computation.17 | async-start | bytes 7077888 | tf_op jit(solution)/shard_map/reduce_scatter | solution.py:499
  1582.6 323.1 %reduce-scatter.21.cloned.1.call-start = ((), (), s32[]{:S(2)}) async-start(), calls=%async_computation.18 | async-start | bytes 7077888 | tf_op jit(solution)/shard_map/reduce_scatter | solution.py:502
  1595.7 375.4 %reduce-scatter.23.cloned.1.call-start = ((), (), s32[]{:S(2)}) async-start(), calls=%async_computation.19 | async-start | bytes 7077888 | tf_op jit(solution)/shard_map/reduce_scatter | solution.py:505
  (172 other events, 2402.3 us)
Sparse Core Ops, SparseCore 0:
  10.5 38.2 all-gather.28
  51.3 24.7 all-gather.30
  78.5 32.3 all-gather.32
  112.6 32.3 all-gather.34
  146.7 32.3 all-gather.36
  181.4 35.4 all-gather.38
  218.8 24.2 all-gather.40
  245.0 32.3 all-gather.46
  279.2 32.3 all-gather.44
  511.8 32.7 all-gather.42
  1412.6 110.9 all-reduce.21
  1526.8 42.5 reduce-scatter.16
  1572.8 33.4 reduce-scatter.28
  1609.2 33.4 reduce-scatter.30
  1645.9 33.5 reduce-scatter.26
  1682.9 33.4 reduce-scatter.24
  1719.4 56.2 all-reduce.23
  1779.3 61.2 reduce-scatter.18
  1844.0 61.7 reduce-scatter.20
  1909.4 61.7 reduce-scatter.22
where the time goes:
time: 2000 us; the launch traced here: 1980 us
  matrix products  563 us (28%)
  waiting for transfers between devices  551 us (28%)
  local copies, waits for them, and re-layouts  328 us (16%)
  other arithmetic  273 us (14%)
  blocking collectives  130 us (6%)
  loops' own time  79.4 us (4%)
  starting transfers between devices  37.4 us (2%)
    unnamed x25, waiting for transfers between devices  146 us
    dot_general x48, matrix products, one_head(): jnp.dot(head_query, head_keys.T, preferred_element_type=jnp.float32)  124 us
    another operation x4, loops' own time, one_tree(): return lax.map(one_head, jnp.arange(H))  79.4 us
    reduce_scatter x1, waiting for transfers between devices, on_device(): lax.psum_scatter(jnp.stack(grads_down).astype(jnp.bfloat16), 'shard', sca...  62.9 us
    unnamed x424, local copies, waits for them, and re-layouts  62.9 us
    reduce_scatter x1, waiting for transfers between devices, on_device(): lax.psum_scatter(jnp.stack(grads_up).astype(jnp.bfloat16), 'shard', scatt...  62.7 us
    all_to_all x2, waiting for transfers between devices, on_device(): lax.all_to_all(outgoing_grad, 'expert', split_axis=0, concat_axis=1, tile...  62.4 us
    reduce_scatter x1, waiting for transfers between devices, on_device(): lax.psum_scatter(jnp.stack(grads_gate).astype(jnp.bfloat16), 'shard', sca...  61.5 us
  transfers between devices with their start and end apart: 28, of which 14 were waited for; matrix products, arithmetic and copies ran while one was open for 29% of the time, Pallas kernels for 0%

commit v1 on v0

v1 whole, which is shorter than its diff:
```python
import functools

import jax
import jax.numpy as jnp
from jax import lax
from jax.experimental import pallas as pl
from jax.experimental.pallas import tpu as pltpu
from jax.sharding import PartitionSpec as P

D = 768
H = 12
HD = 64
TOP = 2
LAYERS = 2
TRUNK = 320
BRANCH = 64
LEAF = 32
TREE = 832

W_OUT = 3 * D
W_SMALL = 4 * D
W_ALL = 4 * D + 128
S_CONST = 16
S_GAIN = 24
S_VEC = 26

epsilon = 1e-06
masked_fill = -1e30
f32 = jnp.float32
bf16 = jnp.bfloat16
BLOCKS = 4
VMEM = 56 << 20


def dot(a, b):
    return jnp.dot(a, b, preferred_element_type=f32)


def dot_nt(a, b):
    return lax.dot_general(a, b, (((1,), (1,)), ((), ())), preferred_element_type=f32)


def dot_tn(a, b):
    return lax.dot_general(a, b, (((0,), (0,)), ((), ())), preferred_element_type=f32)


def split_bf16(v):
    high = v.astype(bf16)
    return high, (v - high.astype(f32)).astype(bf16)


def inv_rms(v):
    return lax.rsqrt(jnp.mean(v * v, axis=1, keepdims=True) + epsilon)


def tree_visible(parents):
    position = jnp.arange(TREE, dtype=jnp.int32)
    offset = position - TRUNK
    segment = jnp.where(
        position < TRUNK,
        0,
        jnp.where(offset < 4 * BRANCH, 1 + offset // BRANCH, 5 + (offset - 4 * BRANCH) // LEAF),
    )
    leaf_hits = (segment[:, None] - 5 == jnp.arange(8, dtype=jnp.int32)[None, :]).astype(jnp.int32)
    upper = jnp.where(segment >= 5, 1 + jnp.sum(leaf_hits * parents[None, :], axis=1), 0)
    key_segment = segment[None, :]
    causal = position[None, :] <= position[:, None]
    return causal & (
        (key_segment == segment[:, None]) | (key_segment == 0) | (key_segment == upper[:, None])
    )


def one_hot(slot_row, e, slots):
    row = lax.broadcasted_iota(jnp.int32, (slots, slot_row.shape[1]), 0).astype(f32)
    return jnp.where(row == slot_row[e : e + 1, :], 1.0, 0.0).astype(bf16)


def one_hot_col(slot_col, e, slots, scale=None):
    lane = lax.broadcasted_iota(jnp.int32, (slot_col.shape[0], slots), 1).astype(f32)
    value = 1.0 if scale is None else scale
    return jnp.where(lane == slot_col[:, e : e + 1], value, 0.0).astype(bf16)


def combine_rows(rows, middle_ref, n2_ref, y_ref, gcol_ref, slotc_ref, vectors, experts, slots):
    gcol = gcol_ref[rows, :]
    slot = slotc_ref[rows, :]
    total = middle_ref[rows, :] + gcol[:, 16:17] * n2_ref[rows, :].astype(f32)
    for c in range(2):
        total = total + gcol[:, 17 + c : 18 + c] * vectors[c : c + 1, :]
    for e in range(experts):
        weight = one_hot_col(slot, e, slots, gcol[:, e : e + 1])
        total = total + dot(weight, y_ref[e * slots : (e + 1) * slots, :])
    return total


def send_grads(slot_row, gx, gpack, gxs_ref, gy_ref, experts, slots):
    for e in range(experts):
        hot = one_hot(slot_row, e, slots)
        rows = slice(e * slots, (e + 1) * slots)
        got = dot(hot, gx)
        gates = dot(hot, gpack)
        gxs_ref[rows, :] = got.astype(bf16)
        gy_ref[rows, :] = (got * (gates[:, e : e + 1] + gates[:, 64 + e : 65 + e])).astype(bf16)


def row_blocks(tokens):
    size = tokens // BLOCKS
    return size, lambda i: pl.ds(pl.multiple_of(i * size, 16), size)


def causal_spans(tokens):
    edges = [0, 384, 640, tokens]
    return list(zip(edges[:-1], edges[1:]))


def forward_kernel(first, last, experts, slots, *refs):
    refs = list(refs)
    if first:
        x_in = refs.pop(0)
    else:
        mid_prev, n2_prev, y_ref, gcol_prev, slotc_prev, w_prev = [refs.pop(0) for _ in range(6)]
    w_ref, bias_ref, z_ref, mixt_ref, chosen_ref, slotr_ref = [refs.pop(0) for _ in range(6)]
    if last:
        cot_ref = refs.pop(0)
    if not first:
        x_out = refs.pop(0)
    n1_ref, qkv_ref, att_ref, lse_ref, mid_ref, n2_ref, info_ref, gcol_ref, gpack_ref, send_ref = [
        refs.pop(0) for _ in range(10)
    ]
    if last:
        gxs_ref, gy_ref = refs.pop(0), refs.pop(0)
    lse_cols, turn = refs
    tokens = n1_ref.shape[0]
    size, block = row_blocks(tokens)
    small = w_ref[:, W_SMALL:].astype(f32).T
    gain0 = small[S_GAIN : S_GAIN + 1, :]
    gain1 = small[S_GAIN + 1 : S_GAIN + 2, :]
    if not first:
        vectors_prev = w_prev[...].astype(f32).T[S_VEC : S_VEC + 2, :]

    def project(i, carry):
        rows = block(i)
        if first:
            x = x_in[rows, :].astype(f32)
        else:
            x = combine_rows(
                rows, mid_prev, n2_prev, y_ref, gcol_prev, slotc_prev, vectors_prev, experts, slots
            )
            x_out[rows, :] = x
        n1 = (x * inv_rms(x) * gain0).astype(bf16)
        n1_ref[rows, :] = n1
        for c in range(3):
            qkv_ref[rows, c * D : (c + 1) * D] = dot(n1, w_ref[:, c * D : (c + 1) * D]).astype(bf16)
        return carry

    lax.fori_loop(0, BLOCKS, project, 0)
    lane = lax.broadcasted_iota(jnp.int32, (1, 128), 1)
    low_f = jnp.where(lane < HD, 1.0, 0.0)
    low = low_f.astype(bf16)
    high = (1.0 - low_f).astype(bf16)
    lse_cols[...] = jnp.zeros_like(lse_cols)

    def pair(p, carry):
        k = qkv_ref[:, pl.ds(pl.multiple_of(D + p * 128, 128), 128)]
        v = qkv_ref[:, pl.ds(pl.multiple_of(2 * D + p * 128, 128), 128)]
        va = v * low + high
        vb = v * high + low
        here = pl.ds(pl.multiple_of(p * 128, 128), 128)
        for start, stop in causal_spans(tokens):
            q = qkv_ref[start:stop, here] * bf16(HD**-0.5)
            outs = []
            for mask, value in ((low, va), (high, vb)):
                s = dot_nt(q * mask, k[:stop]) + bias_ref[start:stop, :stop]
                peak = jnp.max(s, axis=1, keepdims=True)
                expo = jnp.exp(s - peak).astype(bf16)
                outs.append((dot(expo, value[:stop]), peak))
            (oa, ma), (ob, mb) = outs
            numer = jnp.where(lane < HD, oa, ob)
            denom = pltpu.roll(jnp.where(lane < HD, ob, oa), HD, 1)
            att_ref[start:stop, here] = (numer / denom).astype(bf16)
            la = ma + jnp.log(oa[:, HD : HD + 1])
            lb = mb + jnp.log(ob[:, 0:1])
            old = lse_cols[start:stop, :]
            lse_cols[start:stop, :] = jnp.where(
                lane == 2 * p, la, jnp.where(lane == 2 * p + 1, lb, old)
            )
        return carry

    lax.fori_loop(0, H // 2, pair, 0)
    lse_ref[...] = lse_cols[...].T[0:16, :]

    def finish(i, carry):
        rows = block(i)
        if first:
            x = x_in[rows, :].astype(f32)
        else:
            x = x_out[rows, :]
        middle = x + dot(att_ref[rows, :], w_ref[:, W_OUT:W_SMALL])
        mid_ref[rows, :] = middle
        n2_ref[rows, :] = (middle * inv_rms(middle) * gain1).astype(bf16)
        return carry

    lax.fori_loop(0, BLOCKS, finish, 0)
    n2 = n2_ref[...]
    scores = dot_nt(small[0:32, :].astype(bf16), n2)
    logits = scores[0:16, :]
    z = z_ref[...]
    mixt = mixt_ref[...]
    for i in range(experts + 4):
        logits = logits + mixt[:, i : i + 1] * z[i : i + 1, :]
    row = lax.broadcasted_iota(jnp.int32, (16, tokens), 0)
    valid = row < experts + 4
    peak = jnp.max(jnp.where(valid, logits, masked_fill), axis=0, keepdims=True)
    expo = jnp.where(valid, jnp.exp(jnp.minimum(logits - peak, 0.0)), 0.0)
    prob = expo / jnp.sum(expo, axis=0, keepdims=True)
    gates = prob * chosen_ref[...]
    info_ref[0:16, :] = logits
    info_ref[16:32, :] = prob
    turn[...] = jnp.zeros_like(turn)
    turn[0:16, 0:tokens] = gates
    own = gates[experts + 1 : experts + 2, :]
    alphas = []
    for c in range(2):
        l0 = scores[S_CONST + 2 * c : S_CONST + 2 * c + 1, :]
        l1 = scores[S_CONST + 2 * c + 1 : S_CONST + 2 * c + 2, :]
        a0 = jax.nn.sigmoid(l0 - l1)
        a1 = jax.nn.sigmoid(l1 - l0)
        alphas += [a0, a1]
        share = gates[experts + 2 + c : experts + 3 + c, :]
        own = own + share * a0
        turn[17 + c : 18 + c, 0:tokens] = share * a1
    turn[16:17, 0:tokens] = own
    zero_row = jnp.zeros((4, tokens), f32)
    info_ref[32:40, :] = jnp.concatenate(alphas + [zero_row], axis=0)
    gcol = turn[...].T[0:tokens, :]
    gcol_ref[...] = gcol
    upper, lower = split_bf16(jnp.where(lane < 16, gcol, 0.0))
    gpack = upper + pltpu.roll(lower.astype(f32), 64, 1).astype(bf16)
    gpack_ref[...] = gpack
    slot_row = slotr_ref[...]
    for e in range(experts):
        hot = one_hot(slot_row, e, slots)
        rows = slice(e * slots, (e + 1) * slots)
        send_ref[rows, :] = dot(hot, n2).astype(bf16)
    if last:
        send_grads(slot_row, cot_ref[...], gpack, gxs_ref, gy_ref, experts, slots)


def shape(dims, dtype=f32):
    return jax.ShapeDtypeStruct(tuple(dims), dtype)


def whole_call(body, name, outs, scratch, args, flops):
    moved = sum(a.size * a.dtype.itemsize for a in args) + sum(
        o.size * o.dtype.itemsize for o in outs
    )
    return pl.pallas_call(
        body,
        out_shape=outs,
        in_specs=[pl.BlockSpec(memory_space=pltpu.VMEM)] * len(args),
        out_specs=[pl.BlockSpec(memory_space=pltpu.VMEM)] * len(outs),
        scratch_shapes=scratch,
        compiler_params=pltpu.CompilerParams(vmem_limit_bytes=VMEM),
        cost_estimate=pl.CostEstimate(flops=flops, bytes_accessed=moved, transcendentals=0),
        name=name,
    )(*args)


def forward_call(first, last, experts, slots, args):
    tokens = TREE
    sent = experts * slots
    outs = [] if first else [shape((tokens, D))]
    outs += [
        shape((tokens, D), bf16),
        shape((tokens, 3 * D), bf16),
        shape((tokens, D), bf16),
        shape((16, tokens)),
        shape((tokens, D)),
        shape((tokens, D), bf16),
        shape((40, tokens)),
        shape((tokens, 128)),
        shape((tokens, 128), bf16),
        shape((sent, D), bf16),
    ]
    if last:
        outs += [shape((sent, D), bf16), shape((sent, D), bf16)]
    padded = -(-tokens // 128) * 128
    scratch = [pltpu.VMEM((tokens, 128), f32), pltpu.VMEM((128, padded), f32)]
    body = functools.partial(forward_kernel, first, last, experts, slots)
    return whole_call(body, "block_forward", outs, scratch, args, 20 * 10**9)


def gating_kernel(last, experts, slots, *refs):
    refs = list(refs)
    gx_ref, n2_ref, y_ref, gxs_ref, slotr_ref, info_ref, chosen_ref, gcol_ref, small_ref = [
        refs.pop(0) for _ in range(9)
    ]
    z_ref, mix_ref = refs.pop(0), refs.pop(0)
    if last:
        mid_ref, slotc_ref = refs.pop(0), refs.pop(0)
    else:
        gz_ref = refs.pop(0)
    gn2_ref, gsm_ref, gmix_ref, gprev_ref = [refs.pop(0) for _ in range(4)]
    if last:
        out_ref = refs.pop(0)
    tokens = n2_ref.shape[0]
    size, block = row_blocks(tokens)
    small = small_ref[...].astype(f32).T
    small_half = small[0:32, :].astype(bf16)
    vectors = small[S_VEC : S_VEC + 2, :]
    slot_row = slotr_ref[...]
    ones = jnp.ones((16, D), bf16)
    row = lax.broadcasted_iota(jnp.int32, (16, slots), 0)
    scattered = jnp.zeros((16, tokens), f32)
    for e in range(experts):
        rows = slice(e * slots, (e + 1) * slots)
        inner = y_ref[rows, :].astype(f32) * gxs_ref[rows, :].astype(f32)
        upper, lower = split_bf16(inner)
        sums = dot_nt(ones, upper) + dot_nt(ones, lower)
        upper, lower = split_bf16(sums)
        lhs = jnp.where(row == e, upper.astype(f32), 0.0) + jnp.where(
            row == 8 + e, lower.astype(f32), 0.0
        )
        scattered = scattered + dot(lhs.astype(bf16), one_hot(slot_row, e, slots))
    gx = gx_ref[...].astype(f32)
    gx_half = gx.astype(bf16)
    n2 = n2_ref[...]
    upper, lower = split_bf16(gx * n2.astype(f32))
    gx_n2 = (dot_nt(ones, upper) + dot_nt(ones, lower))[0:1, :]
    gx_small = dot_nt(small_half, gx_half)
    prob = info_ref[16:32, :]
    chosen = chosen_ref[...]
    gates = prob * chosen
    trow = lax.broadcasted_iota(jnp.int32, (16, tokens), 0)
    gp = jnp.concatenate([scattered[0:8, :] + scattered[8:16, :], jnp.zeros((8, tokens), f32)], 0)
    gp = jnp.where(trow == experts + 1, gx_n2, jnp.where(trow < experts, gp, 0.0))
    crow = lax.broadcasted_iota(jnp.int32, (8, tokens), 0)
    glog = jnp.zeros((8, tokens), f32)
    coefs = jnp.zeros((8, tokens), f32)
    for c in range(2):
        a0 = info_ref[32 + 2 * c : 33 + 2 * c, :]
        a1 = info_ref[33 + 2 * c : 34 + 2 * c, :]
        gx_v = gx_small[S_VEC + c : S_VEC + c + 1, :]
        share = gates[experts + 2 + c : experts + 3 + c, :]
        gp = jnp.where(trow == experts + 2 + c, a0 * gx_n2 + a1 * gx_v, gp)
        gl = share * (gx_n2 - gx_v) * a0 * a1
        glog = jnp.where(crow == 2 * c, gl, jnp.where(crow == 2 * c + 1, -gl, glog))
        coefs = jnp.where(crow == c, share * a1, coefs)
    gp = gp * chosen
    gz = prob * (gp - jnp.sum(prob * gp, axis=0, keepdims=True))
    if not last:
        gz = gz + gz_ref[...]
    z = z_ref[...]
    gmix_ref[...] = lax.dot_general(
        z, gz, (((1,), (1,)), ((), ())), precision=lax.Precision.HIGHEST, preferred_element_type=f32
    )
    mix = mix_ref[...]
    gprev = jnp.zeros((16, tokens), f32)
    for o in range(experts + 4):
        gprev = gprev + mix[:, o : o + 1] * gz[o : o + 1, :]
    gprev_ref[...] = gprev
    allg = jnp.concatenate([gz, glog, jnp.zeros((8, tokens), f32)], axis=0)
    upper, lower = split_bf16(allg)
    gsm = dot(upper, n2) + dot(lower, n2)
    cu, cl = split_bf16(jnp.concatenate([coefs, jnp.zeros((8, tokens), f32)], axis=0))
    gvec = dot(cu, gx_half) + dot(cl, gx_half)
    gsm_ref[0:24, :] = gsm[0:24, :]
    gsm_ref[24:32, :] = jnp.concatenate(
        [jnp.zeros((2, D), f32), gvec[0:2, :], jnp.zeros((4, D), f32)], axis=0
    )
    both = jnp.concatenate([upper, lower], axis=0)
    twice = jnp.concatenate([small_half, small_half], axis=0)
    gn2_ref[...] = dot_tn(both, twice)

    def add(i, carry):
        rows = block(i)
        gn2_ref[rows, :] = gn2_ref[rows, :] + gcol_ref[rows, 16:17] * gx_ref[rows, :].astype(f32)
        if last:
            out_ref[rows, :] = combine_rows(
                rows, mid_ref, n2_ref, y_ref, gcol_ref, slotc_ref, vectors, experts, slots
            ).astype(bf16)
        return carry

    lax.fori_loop(0, BLOCKS, add, 0)


def gating_call(last, experts, slots, args):
    tokens = TREE
    outs = [shape((tokens, D)), shape((32, D)), shape((16, 16)), shape((16, tokens))]
    if last:
        outs += [shape((tokens, D), bf16)]
    body = functools.partial(gating_kernel, last, experts, slots)
    return whole_call(body, "gating_backward", outs, [], args, 5 * 10**9)


def backward_kernel(first, experts, slots, *refs):
    refs = list(refs)
    gx_ref, gn2p_ref, gn2e_ref, slotc_ref, mid_ref, att_ref, w_ref, qkv_ref, n1_ref, x_ref = [
        refs.pop(0) for _ in range(10)
    ]
    biast_ref, lse_ref, gsm_ref = [refs.pop(0) for _ in range(3)]
    if not first:
        slotr_ref, gpack_ref = refs.pop(0), refs.pop(0)
    gout_ref, dw_ref = refs.pop(0), refs.pop(0)
    if not first:
        gxs_ref, gy_ref = refs.pop(0), refs.pop(0)
    gatt, go, gqkv, turn = refs
    tokens = n1_ref.shape[0]
    size, block = row_blocks(tokens)
    small = w_ref[:, W_SMALL:].astype(f32).T
    gain0 = small[S_GAIN : S_GAIN + 1, :]
    gain1 = small[S_GAIN + 1 : S_GAIN + 2, :]

    def enter(i, total):
        rows = block(i)
        gn2 = gn2p_ref[rows, :]
        slot = slotc_ref[rows, :]
        for e in range(experts):
            gn2 = gn2 + dot(one_hot_col(slot, e, slots), gn2e_ref[e * slots : (e + 1) * slots, :])
        middle = mid_ref[rows, :]
        r = inv_rms(middle)
        scaled = gain1 * gn2
        inner = jnp.mean(middle * scaled, axis=1, keepdims=True)
        gmid = gx_ref[rows, :].astype(f32) + r * scaled - middle * (r * r * r * inner)
        gout_ref[rows, :] = gmid
        half = gmid.astype(bf16)
        gatt[rows, :] = half
        go[rows, :] = dot_nt(half, w_ref[:, W_OUT:W_SMALL]).astype(bf16)
        return total + jnp.sum(gn2 * middle * r, axis=0, keepdims=True)

    ggain1 = lax.fori_loop(0, BLOCKS, enter, jnp.zeros((1, D), f32))
    lane = lax.broadcasted_iota(jnp.int32, (1, 128), 1)
    low_f = jnp.where(lane < HD, 1.0, 0.0)
    low = low_f.astype(bf16)
    high = (1.0 - low_f).astype(bf16)
    scale = HD**-0.5

    def out_grad(p, carry):
        here = pl.ds(pl.multiple_of(p * 128, 128), 128)
        dw_ref[here, W_OUT:W_SMALL] = dot_tn(att_ref[:, here], gatt[...]).astype(bf16)
        return carry

    lax.fori_loop(0, D // 128, out_grad, 0)
    spans = causal_spans(tokens)

    def pair(p, carry):
        here = pl.ds(pl.multiple_of(p * 128, 128), 128)
        lanes_k = pl.ds(pl.multiple_of(D + p * 128, 128), 128)
        lanes_v = pl.ds(pl.multiple_of(2 * D + p * 128, 128), 128)
        q = qkv_ref[:, here] * bf16(scale)
        k = qkv_ref[:, lanes_k]
        v = qkv_ref[:, lanes_v]
        g = go[:, here]
        turn[0:tokens, :] = g.astype(f32) * att_ref[:, here].astype(f32)
        inner = turn[...].T[:, 0:tokens]
        turn[0:tokens, :] = k.astype(f32)
        kt = turn[...].T[:, 0:tokens].astype(bf16)
        gq_t = []
        gk = [0.0] * len(spans)
        gv = [0.0] * len(spans)
        for h, mask in ((0, low), (1, high)):
            qh = q * mask
            gh = g * mask
            dsum = jnp.sum(inner[h * HD : (h + 1) * HD, :], axis=0, keepdims=True)
            lse = lse_ref[pl.ds(2 * p + h, 1), :]
            gq_h = []
            for n, (start, stop) in enumerate(spans):
                st = dot_nt(k[start:stop], qh[start:]) + biast_ref[start:stop, start:]
                pt = jnp.exp(st - lse[:, start:])
                gpt = dot_nt(v[start:stop], gh[start:])
                gst = (pt * (gpt - dsum[:, start:])).astype(bf16)
                gv[n] = gv[n] + dot(pt.astype(bf16), gh[start:])
                gk[n] = gk[n] + dot(gst, qh[start:])
                part = dot(kt[h * HD : (h + 1) * HD, start:stop], gst)
                gq_h.append(part)
            cols = []
            for n, (start, stop) in enumerate(spans):
                piece = 0.0
                for m in range(n + 1):
                    origin = spans[m][0]
                    piece = piece + gq_h[m][:, start - origin : stop - origin]
                cols.append(piece)
            gq_t.append(jnp.concatenate(cols, axis=1))
        turn_t = jnp.concatenate(gq_t, axis=0) * scale
        pad = turn.shape[0] - tokens
        turn_t = jnp.concatenate([turn_t, jnp.zeros((128, pad), f32)], axis=1)
        gqkv[:, here] = turn_t.T[0:tokens, :].astype(bf16)
        for n, (start, stop) in enumerate(spans):
            gqkv[start:stop, lanes_k] = gk[n].astype(bf16)
            gqkv[start:stop, lanes_v] = gv[n].astype(bf16)
        return carry

    turn[...] = jnp.zeros_like(turn)
    lax.fori_loop(0, H // 2, pair, 0)

    def in_grad(p, carry):
        here = pl.ds(pl.multiple_of(p * 128, 128), 128)
        dw_ref[here, 0:W_OUT] = dot_tn(n1_ref[:, here], gqkv[...]).astype(bf16)
        return carry

    lax.fori_loop(0, D // 128, in_grad, 0)

    def leave(i, total):
        rows = block(i)
        gn1 = dot_nt(gqkv[rows, :], w_ref[:, 0:W_OUT])
        x = x_ref[rows, :].astype(f32)
        r = inv_rms(x)
        scaled = gain0 * gn1
        inner = jnp.mean(x * scaled, axis=1, keepdims=True)
        gx = gout_ref[rows, :] + r * scaled - x * (r * r * r * inner)
        gout_ref[rows, :] = gx
        gatt[rows, :] = gx.astype(bf16)
        return total + jnp.sum(gn1 * x * r, axis=0, keepdims=True)

    ggain0 = lax.fori_loop(0, BLOCKS, leave, jnp.zeros((1, D), f32))
    rows = jnp.concatenate(
        [gsm_ref[0:24, :], ggain0, ggain1, gsm_ref[26:32, :], jnp.zeros((96, D), f32)], axis=0
    )
    dw_ref[:, W_SMALL:] = rows.T.astype(bf16)
    if not first:
        send_grads(slotr_ref[...], gatt[...], gpack_ref[...], gxs_ref, gy_ref, experts, slots)


def backward_call(first, experts, slots, args):
    tokens = TREE
    sent = experts * slots
    outs = [shape((tokens, D)), shape((D, W_ALL), bf16)]
    if not first:
        outs += [shape((sent, D), bf16), shape((sent, D), bf16)]
    padded = -(-tokens // 128) * 128
    scratch = [
        pltpu.VMEM((tokens, D), bf16),
        pltpu.VMEM((tokens, D), bf16),
        pltpu.VMEM((tokens, 3 * D), bf16),
        pltpu.VMEM((padded, 128), f32),
    ]
    body = functools.partial(backward_kernel, first, experts, slots)
    return whole_call(body, "block_backward", outs, scratch, args, 40 * 10**9)


class Packing:
    def __init__(self, shards, part, ff):
        self.shards, self.part, self.ff = shards, part, ff
        self.padded = -(-part // 16) * 16
        self.chunks = ff // 256
        self.own = ff // shards
        self.down = 2 * self.chunks * self.padded
        self.rows = self.down + (D // 256) * self.own
        self.group = 2 * 256 // self.own

    def pack(self, gate, up, down):
        pieces = []
        for wide in (gate, up):
            cut = wide.reshape(self.part, self.chunks, 256).transpose(1, 0, 2)
            cut = jnp.pad(cut, [(0, 0), (0, self.padded - self.part), (0, 0)])
            pieces.append(cut.reshape(self.chunks * self.padded, 256))
        pieces.append(
            down.reshape(self.own, D // 256, 256).transpose(1, 0, 2).reshape(-1, 256)
        )
        return jnp.concatenate(pieces, axis=0)

    def unpack(self, packed):
        wide = []
        for n in range(2):
            cut = packed[n * self.chunks * self.padded : (n + 1) * self.chunks * self.padded]
            cut = cut.reshape(self.chunks, self.padded, 256)[:, : self.part]
            wide.append(cut.transpose(1, 0, 2).reshape(self.part, self.ff))
        down = packed[self.down :].reshape(D // 256, self.own, 256)
        return wide[0], wide[1], down.transpose(1, 0, 2).reshape(self.own, D)

    def specs(self):
        two = self.shards, 2 * self.padded, 256
        steps = self.chunks // 2
        wide = [pl.BlockSpec(two, lambda j, n=n: (0, n * steps + j, 0)) for n in range(2)]
        base = self.down // self.own
        tall = [
            pl.BlockSpec((self.group, self.own, 256), lambda j, c=c: (j, base + c, 0))
            for c in range(D // 256)
        ]
        return wide + tall

    def wide_part(self, ref, i):
        at = i * self.padded
        return ref[:, at : at + self.part, :].reshape(D, 256)

    def tall_part(self, refs):
        return jnp.concatenate([ref[...].reshape(512, 256) for ref in refs], axis=1)


def accumulate(total, part, out_ref):
    j = pl.program_id(0)

    @pl.when(j == 0)
    def _():
        total[...] = part

    @pl.when(j > 0)
    def _():
        total[...] = total[...] + part

    @pl.when(j == pl.num_programs(0) - 1)
    def _():
        out_ref[...] = total[...].astype(bf16)


def ffn_forward_kernel(pack, r_ref, g_w, u_w, d0, d1, d2, y_ref, gu_ref, uv_ref, total):
    r = r_ref[...]
    hids = []
    for i in range(2):
        lanes = slice(i * 256, (i + 1) * 256)
        gate = dot(r, pack.wide_part(g_w, i))
        up = dot(r, pack.wide_part(u_w, i))
        gu_ref[:, lanes] = gate.astype(bf16)
        uv_ref[:, lanes] = up.astype(bf16)
        hids.append((gate * jax.nn.sigmoid(gate) * up).astype(bf16))
    hid = jnp.concatenate(hids, axis=1)
    accumulate(total, dot(hid, pack.tall_part((d0, d1, d2))), y_ref)


def ffn_call(body, name, pack, count, flat, wide, with_weights, outs, out_specs, scratch, args):
    ff = pack.ff
    in_specs = [pl.BlockSpec((count, D), lambda j: (0, 0))] * flat
    in_specs += [pl.BlockSpec((count, 512), lambda j: (0, j))] * wide
    if with_weights:
        in_specs += pack.specs()
        args = list(args) + [args[-1]] * 4
    return pl.pallas_call(
        functools.partial(body, pack),
        grid=(ff // 512,),
        out_shape=outs,
        in_specs=in_specs,
        out_specs=out_specs,
        scratch_shapes=scratch,
        compiler_params=pltpu.CompilerParams(vmem_limit_bytes=VMEM),
        cost_estimate=pl.CostEstimate(
            flops=6 * count * D * ff, bytes_accessed=6 * D * ff + 8 * count * ff, transcendentals=0
        ),
        name=name,
    )(*args)


def ffn_forward(pack, rows, weights):
    count, ff = rows.shape[0], pack.ff
    flat = pl.BlockSpec((count, D), lambda j: (0, 0))
    wide = pl.BlockSpec((count, 512), lambda j: (0, j))
    outs = [shape((count, D), bf16), shape((count, ff), bf16), shape((count, ff), bf16)]
    scratch = [pltpu.VMEM((count, D), f32)]
    return ffn_call(
        ffn_forward_kernel, "ffn_forward", pack, count, 1, 0, True, outs, [flat, wide, wide],
        scratch, [rows, weights],
    )


def ffn_input_kernel(
    pack, gy_ref, gu_ref, uv_ref, g_w, u_w, d0, d1, d2, gin_ref, hid_ref, ggu_ref, guv_ref, total
):
    ghid_all = dot_nt(gy_ref[...], pack.tall_part((d0, d1, d2)))
    part = 0.0
    for i in range(2):
        lanes = slice(i * 256, (i + 1) * 256)
        ghid = ghid_all[:, lanes]
        gate = gu_ref[:, lanes].astype(f32)
        up = uv_ref[:, lanes].astype(f32)
        s = jax.nn.sigmoid(gate)
        act = gate * s
        hid_ref[:, lanes] = (act * up).astype(bf16)
        guv = (ghid * act).astype(bf16)
        ggu = (ghid * up * (s * (1.0 + gate * (1.0 - s)))).astype(bf16)
        ggu_ref[:, lanes] = ggu
        guv_ref[:, lanes] = guv
        part = part + dot_nt(ggu, pack.wide_part(g_w, i)) + dot_nt(guv, pack.wide_part(u_w, i))
    accumulate(total, part, gin_ref)


def ffn_input_grad(pack, gy, gate, up, weights):
    count, ff = gy.shape[0], pack.ff
    flat = pl.BlockSpec((count, D), lambda j: (0, 0))
    wide = pl.BlockSpec((count, 512), lambda j: (0, j))
    outs = [shape((count, D), bf16)] + [shape((count, ff), bf16)] * 3
    scratch = [pltpu.VMEM((count, D), f32)]
    return ffn_call(
        ffn_input_kernel, "ffn_input_grad", pack, count, 1, 2, True, outs,
        [flat, wide, wide, wide], scratch, [gy, gate, up, weights],
    )


def ffn_weight_kernel(pack, r_ref, gy_ref, hid_ref, ggu_ref, guv_ref, out_ref, rt):
    j = pl.program_id(0)

    @pl.when(j == 0)
    def _():
        rt[...] = r_ref[...].T
        if pack.padded != pack.part:
            out_ref[...] = jnp.zeros_like(out_ref)

    for n, ref in enumerate((ggu_ref, guv_ref)):
        for i in range(2):
            grad = dot(rt[...], ref[:, i * 256 : (i + 1) * 256]).astype(bf16)
            at = (n * pack.chunks + i) * pack.padded + j * (2 * pack.padded)
            at = pl.multiple_of(at, 16)
            out_ref[:, pl.ds(at, pack.part), :] = grad.reshape(pack.shards, pack.part, 256)
    grad = dot_tn(hid_ref[...], gy_ref[...]).astype(bf16)
    for c in range(D // 256):
        at = pack.down + c * pack.own
        out_ref[pl.ds(j * pack.group, pack.group), at : at + pack.own, :] = grad[
            :, c * 256 : (c + 1) * 256
        ].reshape(pack.group, pack.own, 256)


def ffn_weight_grad(pack, rows, gy, hid, ggu, guv):
    count = rows.shape[0]
    outs = shape((pack.shards, pack.rows, 256), bf16)
    spec = pl.BlockSpec(outs.shape, lambda j: (0, 0, 0))
    return ffn_call(
        ffn_weight_kernel, "ffn_weight_grad", pack, count, 2, 3, False, outs, spec,
        [pltpu.VMEM((D, count), bf16)], [rows, gy, hid, ggu, guv],
    )


def to_owner(rows, owners):
    slots = rows.shape[0] // owners
    return lax.all_to_all(
        rows.reshape(owners, slots, D), "expert", split_axis=0, concat_axis=0, tiled=True
    ).reshape(owners * slots, D)


def on_device(
    hidden_in,
    prior_logits,
    project_weight,
    output_weight,
    norm_gain,
    router_weight,
    mixing_weight,
    const_vector,
    const_weight,
    gate_weight,
    up_weight,
    down_weight,
    routes,
    priority,
    leaf_parent,
    cotangent,
):
    experts = lax.axis_size("expert")
    total_experts = experts + 4
    tokens = hidden_in.shape[0]
    capacity = 9 * tokens * TOP // (8 * total_experts)
    slots = -(-capacity // 16) * 16
    part = project_weight.shape[2]

    def pad_cols(a, width):
        return jnp.pad(a, [(0, 0)] * (a.ndim - 1) + [(0, width - a.shape[-1])])

    dense = []
    experts_w = []
    pack = Packing(lax.axis_size("shard"), part, gate_weight.shape[3])
    for l in range(LAYERS):
        small = jnp.concatenate(
            [
                pad_cols(router_weight[l], S_CONST),
                const_weight[l, 0],
                const_weight[l, 1],
                jnp.zeros((part, S_GAIN - S_CONST - 4), bf16),
                norm_gain[l].T,
                const_vector[l].T,
            ],
            axis=1,
        )
        packed = jnp.concatenate(
            [project_weight[l, c] for c in range(3)] + [output_weight[l], pad_cols(small, 128)],
            axis=1,
        )
        dense.append(lax.all_gather(packed, "shard", axis=0, tiled=True))
        mine = pack.pack(gate_weight[l, 0], up_weight[l, 0], down_weight[l, 0])
        experts_w.append(lax.all_gather(mine, "shard", axis=0, tiled=False))

    ranking = priority[0]
    earlier = (ranking[None, :] < ranking[:, None]).astype(bf16)
    labels = jnp.arange(total_experts, dtype=jnp.int32)
    hits = jnp.sum((routes[:, :, :, None] == labels).astype(f32), axis=2)
    chosen_rows = [jnp.pad(hits[l].T, [(0, 16 - total_experts), (0, 0)]) for l in range(LAYERS)]
    loaded = jnp.concatenate([hits[l, :, :experts] for l in range(LAYERS)], axis=1)
    loaded_half = loaded.astype(bf16)
    rank_col = dot(earlier, loaded_half)
    rank_row = lax.dot_general(
        loaded_half, earlier, (((0,), (1,)), ((), ())), preferred_element_type=f32
    )
    slot_col_all = jnp.where((loaded > 0) & (rank_col < capacity), rank_col, -1.0)
    slot_row_all = jnp.where((loaded.T > 0) & (rank_row < capacity), rank_row, -1.0)
    slot_col = [slot_col_all[:, l * experts : (l + 1) * experts] for l in range(LAYERS)]
    slot_row = [
        jnp.pad(
            slot_row_all[l * experts : (l + 1) * experts],
            [(0, 8 - experts), (0, 0)],
            constant_values=-1.0,
        )
        for l in range(LAYERS)
    ]
    visible = tree_visible(leaf_parent[0])
    bias = jnp.where(visible, 0.0, masked_fill)
    bias_t = jnp.where(visible.T, 0.0, masked_fill)
    mixes = [
        jnp.pad(mixing_weight[l], [(0, 16 - total_experts), (0, 16 - total_experts)])
        for l in range(LAYERS)
    ]
    z_rows = jnp.pad(prior_logits.T, [(0, 16 - total_experts), (0, 0)])

    saved = []
    front = [hidden_in]
    x_now = hidden_in
    for l in range(LAYERS):
        last = l == LAYERS - 1
        args = front + [dense[l], bias, z_rows, mixes[l].T, chosen_rows[l], slot_row[l]]
        if last:
            args.append(cotangent)
        outs = list(forward_call(l == 0, last, experts, slots, args))
        if l > 0:
            x_now = outs.pop(0)
        n1, qkv, att, lse, middle, n2, info, gcol, gpack, send = outs[:10]
        received = to_owner(send, experts)
        keep = dict(
            x=x_now, n1=n1, qkv=qkv, att=att, lse=lse, middle=middle, n2=n2, info=info,
            gcol=gcol, gpack=gpack, received=received, z=z_rows,
        )
        if last:
            keep["gxs"] = outs[10]
            keep["gy"] = to_owner(outs[11], experts)
        produced, keep["gate"], keep["up"] = ffn_forward(pack, received, experts_w[l])
        keep["y"] = to_owner(produced, experts)
        front = [middle, n2, keep["y"], gcol, slot_col[l], dense[l][:, W_SMALL:]]
        z_rows = info[0:16]
        saved.append(keep)

    gx = cotangent
    gz = None
    dense_grads = [None] * LAYERS
    expert_grads = [None] * LAYERS
    mix_grads = [None] * LAYERS
    hidden_out = None
    for l in range(LAYERS - 1, -1, -1):
        last = l == LAYERS - 1
        keep = saved[l]
        gin, hid, ggu, guv = ffn_input_grad(
            pack, keep["gy"], keep["gate"], keep["up"], experts_w[l]
        )
        gin_back = to_owner(gin, experts)
        d_experts = ffn_weight_grad(pack, keep["received"], keep["gy"], hid, ggu, guv)
        d_experts, keep["n2"] = lax.optimization_barrier((d_experts, keep["n2"]))
        expert_grads[l] = lax.psum_scatter(d_experts, "shard", scatter_dimension=0, tiled=False)
        args = [
            gx, keep["n2"], keep["y"], keep["gxs"], slot_row[l], keep["info"], chosen_rows[l],
            keep["gcol"], dense[l][:, W_SMALL:], keep["z"], mixes[l],
        ]
        args += [keep["middle"], slot_col[l]] if last else [gz]
        outs = gating_call(last, experts, slots, args)
        gn2, gsm, mix_grads[l], gz = outs[:4]
        if last:
            hidden_out = outs[4]
        args = [
            gx, gn2, gin_back, slot_col[l], keep["middle"], keep["att"], dense[l], keep["qkv"],
            keep["n1"], keep["x"], bias_t, keep["lse"], gsm,
        ]
        if l > 0:
            args += [slot_row[l - 1], saved[l - 1]["gpack"]]
        outs = backward_call(l == 0, experts, slots, args)
        gx, d_dense = outs[:2]
        if l > 0:
            saved[l - 1]["gxs"] = outs[2]
            saved[l - 1]["gy"] = to_owner(outs[3], experts)
        if not last:
            d_dense, dense_grads[l + 1] = lax.optimization_barrier((d_dense, dense_grads[l + 1]))
        mine = lax.psum_scatter(d_dense, "shard", scatter_dimension=0, tiled=True)
        dense_grads[l] = lax.psum(mine, "expert").astype(f32)

    mixing_total = lax.psum(jnp.stack(mix_grads), ("expert", "shard"))
    grads = jnp.stack(dense_grads)
    small = grads[:, :, W_SMALL:]
    project_grad = jnp.stack([grads[:, :, c * D : (c + 1) * D] for c in range(3)], axis=1)
    const_grad = jnp.stack(
        [small[:, :, S_CONST + 2 * c : S_CONST + 2 * c + 2] for c in range(2)], axis=1
    )
    unpacked = [pack.unpack(expert_grads[l].astype(f32)) for l in range(LAYERS)]
    return (
        hidden_out,
        gx,
        gz[0:total_experts].T,
        project_grad,
        grads[:, :, W_OUT:W_SMALL],
        small[:, :, S_GAIN : S_GAIN + 2].transpose(0, 2, 1),
        small[:, :, 0:total_experts],
        mixing_total[:, 0:total_experts, 0:total_experts],
        small[:, :, S_VEC : S_VEC + 2].transpose(0, 2, 1),
        const_grad,
        *[jnp.stack([unpacked[l][n] for l in range(LAYERS)])[:, None] for n in range(3)],
    )


def solution(mesh):
    both = ("expert", "shard")
    in_specs = (
        P(both, None),
        P(both, None),
        P(None, None, "shard", None),
        P(None, "shard", None),
        P(None, None, "shard"),
        P(None, "shard", None),
        P(),
        P(None, None, "shard"),
        P(None, None, "shard", None),
        P(None, "expert", "shard", None),
        P(None, "expert", "shard", None),
        P(None, "expert", "shard", None),
        P(None, both, None),
        P(both, None),
        P(both, None),
        P(both, None),
    )
    out_specs = (
        P(both, None),
        P(both, None),
        P(both, None),
        P(None, None, "shard", None),
        P(None, "shard", None),
        P(None, None, "shard"),
        P(None, "shard", None),
        P(),
        P(None, None, "shard"),
        P(None, None, "shard", None),
        P(None, "expert", "shard", None),
        P(None, "expert", "shard", None),
        P(None, "expert", "shard", None),
    )
    return jax.shard_map(
        on_device, mesh=mesh, in_specs=in_specs, out_specs=out_specs, check_vma=False
    )
```

time: 2000 us -> 859 us (0.43)
  matrix products: 563 us -> 1.26 us
  Pallas kernels: 0 us -> 299 us
  local copies, waits for them, and re-layouts: 328 us -> 49 us
  other arithmetic: 273 us -> 14.8 us
  waiting for transfers between devices: 551 us -> 296 us
  loops' own time: 79.4 us -> 0 us
  blocking collectives: 130 us -> 156 us
    dot_general x224 -> x2, matrix products: 563 us -> 1.26 us  [the longest x1 0.63 us: on_device(): lax.dot_general(loaded_half, earlier, (((0,), (1,)), ((), ())), preferred...]
    pallas_call x0 -> x12, Pallas kernels: none -> 299 us  [the longest x6 196 us: whole_call(): pl.pallas_call(body, out_shape=outs, in_specs=[pl.BlockSpec(memory_space=...]
    reduce_sum x66 -> x1, other arithmetic: 151 us -> 0.01 us  [on_device(): hits = jnp.sum((routes[:, :, :, None] == labels).astype(f32), axis=2)]
    unnamed x25 -> x10, waiting for transfers between devices: 146 us -> 1.36 us
    all_to_all x0 -> x3, blocking collectives: none -> 117 us  [to_owner(): lax.all_to_all(rows.reshape(owners, slots, D), 'expert', split_axis=0, co...]
    another operation x4 -> x0, loops' own time: 79.4 us -> none  [one_tree(): return lax.map(one_head, jnp.arange(H))]
    all_gather x8 -> x0, blocking collectives: 79.1 us -> none  [the longest x2 23.3 us: fetch_dense(): lax.all_gather(norm_gain[layer_index], 'shard', axis=1, tiled=True)]
    all_to_all x8 -> x5, waiting for transfers between devices: 131 us -> 63.5 us  [to_owner(): lax.all_to_all(rows.reshape(owners, slots, D), 'expert', split_axis=0, co...]
  transfers between devices with their start and end apart: 28 -> 15, of which waited for: 14 -> 11; matrix products, arithmetic and copies ran while one was open for 29% -> 5% of each run, Pallas kernels for 0% -> 29%
where the time goes in v1:
time: 859 us; the launch traced here: 850 us
  Pallas kernels  299 us (35%)
  waiting for transfers between devices  296 us (34%)
  blocking collectives  156 us (18%)
  local copies, waits for them, and re-layouts  49 us (6%)
  starting transfers between devices  18.6 us (2%)
  between operations  14.9 us (2%)
  other arithmetic  14.8 us (2%)
    pallas_call x6, Pallas kernels, whole_call(): pl.pallas_call(body, out_shape=outs, in_specs=[pl.BlockSpec(memory_space=...  196 us
    all_to_all x3, blocking collectives, to_owner(): lax.all_to_all(rows.reshape(owners, slots, D), 'expert', split_axis=0, co...  117 us
    reduce_scatter x2, waiting for transfers between devices, on_device(): lax.psum_scatter(d_experts, 'shard', scatter_dimension=0, tiled=False)  112 us
    pallas_call x6, Pallas kernels, ffn_call(): pl.pallas_call(functools.partial(body, pack), grid=(ff // 512,), out_shap...  104 us
    all_to_all x5, waiting for transfers between devices, to_owner(): lax.all_to_all(rows.reshape(owners, slots, D), 'expert', split_axis=0, co...  63.5 us
    reduce_scatter x2, waiting for transfers between devices, on_device(): mine = lax.psum_scatter(d_dense, 'shard', scatter_dimension=0, tiled=True)  52.4 us
    psum x1, blocking collectives, on_device(): mixing_total = lax.psum(jnp.stack(mix_grads), ('expert', 'shard'))  39.6 us
    all_gather x2, waiting for transfers between devices, on_device(): dense.append(lax.all_gather(packed, 'shard', axis=0, tiled=True))  34.3 us
  transfers between devices with their start and end apart: 15, of which 11 were waited for; matrix products, arithmetic and copies ran while one was open for 5% of the time, Pallas kernels for 29%

profile of v1, /device:TPU:0, one launch (start us, length us, event | category | flops | bytes accessed | tf_op | source)
XLA Modules:
  0.0 850.3 jit_solution(3668948589747811861)
XLA Ops:
  19.3 1.2 pad_maximum_fusion.2
  25.0 4.1 fusion.7
  29.1 28.1 %all-gather.7.cloned.1.call-done.refs_1_.refs_6_ = bf16[768,3200]{1,0:T(8,128)(2,1)} async-done(((bf16[96,3200]{1,0:T(8,128)(2,1)}), bf16[768,3200]{1,0:T(8,128)(2,1)}) %all-gather.7.cloned.1.call-update) | async-done | bytes 4915216 | tf_op jit(solution)/shard_map/all_gather | solution.py:774
  57.2 29.6 %block_forward.2 = (bf16[832,768]{1,0:T(8,128)(2,1)}, bf16[832,2304]{1,0:T(8,128)(2,1)}, bf16[832,768]{1,0:T(8,128)(2,1)}, f32[16,832]{1,0:T(8,128)}, f32[832,76...) custom-call(bf16[832,768]{1,0:T(8,128)(2,1)} %refs_9_.1, ...), custom_call_target="tpu_custom_call" | custom-call | flops 20000000000 | bytes 21619712 | tf_op jit(solution)/shard_map/block_forward/pallas_call | solution.py:257
  86.8 40.5 %all_to_all.40 = bf16[4,240,768]{2,1,0:T(8,128)(2,1)} all-to-all(bf16[4,240,768]{2,1,0:T(8,128)(2,1)} %bitcast.236), channel_id=1, replica_groups=mesh['expert'=4,'shard'=8] {'expert'}, dimensions={0} | all-to-all | bytes 2949120 | tf_op jit(solution)/shard_map/all_to_all | solution.py:722
  127.4 16.0 %ffn_forward.2 = (bf16[960,768]{1,0:T(8,128)(2,1)}, bf16[960,2048]{1,0:T(8,128)(2,1)}, bf16[960,2048]{1,0:T(8,128)(2,1)}) custom-call(bf16[960,768]{1,0:T(8,128)(2,1)} %bitcast.197, bf16[8,2304,256]{2,1,0:T(8,128)(2,1)} %bitcast.170, bf16[8,2304,256]{2,1,0:T(8,128)(2,1)} %bitcast.171, bf16[8,2304,256]{2,1,0:T(8,128)(2,1)} %bitcast.172, ...), custom_call_target="tpu_custom_call" | custom-call | flops 9059696640 | bytes 25165824 | tf_op jit(solution)/shard_map/ffn_forward/pallas_call | solution.py:627
  143.4 3.6 all-to-all-start.1
  151.5 1.4 slice.201.refs_8_.refs_9_
  152.9 1.6 slice.231.refs_5_.refs_8_
  154.6 6.2 all-gather.9.cloned.1.call-done.refs_6_
  160.8 20.7 %all-to-all-done.1 = bf16[4,240,768]{2,1,0:T(8,128)(2,1)S(1)} async-done(((bf16[4,240,768]{2,1,0:T(8,128)(2,1)}), bf16[4,240,768]{2,1,0:T(8,128)(2,1)S(1)}, u32[]{:S(2)}, u32[]{:S(2)}) %all-to-all-start.1) | async-done | bytes 1474592 | tf_op jit(solution)/shard_map/all_to_all | solution.py:722
  182.6 38.2 %block_forward.3 = (f32[832,768]{1,0:T(8,128)}, bf16[832,768]{1,0:T(8,128)(2,1)}, bf16[832,2304]{1,0:T(8,128)(2,1)}, bf16[832,768]{1,0:T(8,128)(2,1)}, f32[16,83...) custom-call(f32[832,768]{1,0:T(8,128)} %get-tuple-element.70.refs_0_, ...), custom_call_target="tpu_custom_call" | custom-call | flops 20000000000 | bytes 33069056 | tf_op jit(solution)/shard_map/block_forward/pallas_call | solution.py:257
  220.8 38.7 %all_to_all.41 = bf16[4,240,768]{2,1,0:T(8,128)(2,1)} all-to-all(bf16[4,240,768]{2,1,0:T(8,128)(2,1)} %bitcast.235), channel_id=1, replica_groups=mesh['expert'=4,'shard'=8] {'expert'}, dimensions={0} | all-to-all | bytes 2949120 | tf_op jit(solution)/shard_map/all_to_all | solution.py:722
  259.5 3.7 all-to-all-start.3
  263.3 15.7 %ffn_forward.3 = (bf16[960,768]{1,0:T(8,128)(2,1)}, bf16[960,2048]{1,0:T(8,128)(2,1)}, bf16[960,2048]{1,0:T(8,128)(2,1)}) custom-call(bf16[960,768]{1,0:T(8,128)(2,1)} %bitcast.199, bf16[8,2304,256]{2,1,0:T(8,128)(2,1)} %bitcast.180, bf16[8,2304,256]{2,1,0:T(8,128)(2,1)} %bitcast.181, bf16[8,2304,256]{2,1,0:T(8,128)(2,1)} %bitcast.182, ...), custom_call_target="tpu_custom_call" | custom-call | flops 9059696640 | bytes 25165824 | tf_op jit(solution)/shard_map/ffn_forward/pallas_call | solution.py:627
  279.0 18.0 %all-to-all-done.3 = bf16[4,240,768]{2,1,0:T(8,128)(2,1)S(1)} async-done(((bf16[4,240,768]{2,1,0:T(8,128)(2,1)}), bf16[4,240,768]{2,1,0:T(8,128)(2,1)S(1)}, u32[]{:S(2)}, u32[]{:S(2)}) %all-to-all-start.3) | async-done | bytes 1474592 | tf_op jit(solution)/shard_map/all_to_all | solution.py:722
  297.0 3.6 all-to-all-start.4
  300.6 18.2 %ffn_input_grad.2 = (bf16[960,768]{1,0:T(8,128)(2,1)}, bf16[960,2048]{1,0:T(8,128)(2,1)}, bf16[960,2048]{1,0:T(8,128)(2,1)}, bf16[960,2048]{1,0:T(8,128)(2,1)}) custom-call(bf16[960,768]{1,0:T(8,128)(2,1)} %bitcast.193, bf16[960,2048]{1,0:T(8,128)(2,1)} %get-tuple-element.78.gu_ref, bf16[960,2048]{1,0:T(8,128)(2,1)} %get-tuple-element.79.uv_ref, ...), custom_call_target="tpu_custom_call" | custom-call | flops 9059696640 | bytes 25165824 | tf_op jit(solution)/shard_map/ffn_input_grad/pallas_call | solution.py:627
  318.8 16.1 %all-to-all-done.4 = bf16[4,240,768]{2,1,0:T(8,128)(2,1)S(1)} async-done(((bf16[4,240,768]{2,1,0:T(8,128)(2,1)}), bf16[4,240,768]{2,1,0:T(8,128)(2,1)S(1)}, u32[]{:S(2)}, u32[]{:S(2)}) %all-to-all-start.4) | async-done | bytes 1474592 | tf_op jit(solution)/shard_map/all_to_all | solution.py:722
  334.9 3.6 all-to-all-start.5
  338.7 1.6 slice.234.refs_8_
  340.4 17.8 %ffn_weight_grad.2 = bf16[8,2304,256]{2,1,0:T(8,128)(2,1)} custom-call(bf16[960,768]{1,0:T(8,128)(2,1)} %bitcast.200, bf16[960,768]{1,0:T(8,128)(2,1)} %bitcast.194, bf16[960,2048]{1,0:T(8,128)(2,1)} %get-tuple-element.80.hid_ref, bf16[960,2048]{1,0:T(8,128)(2,1)} %get-tuple-element.81.ggu_ref, bf16[960,2048]{1,0:T(8,128)(2,1)} %get-tuple-element.82.guv_ref), custom_call_target="tpu_custom_call" | custom-call | flops 9059696640 | bytes 25165824 | tf_op jit(solution)/shard_map/ffn_weight_grad/pallas_call | solution.py:627
  358.1 12.2 %gating_backward.2 = (f32[832,768]{1,0:T(8,128)}, f32[32,768]{1,0:T(8,128)}, f32[16,16]{1,0:T(8,128)}, f32[16,832]{1,0:T(8,128)}, bf16[832,768]{1,0:T(8,128)(2,1)}) custom-call(bf16[832,768]{1,0:T(8,128)(2,1)} %refs_0_.5, bf16[832,768]{1,0:T(8,128)(2,1)} %get-tuple-element.84.refs_1_, bf16[960,768]{1,0:T(8,128)(2,1)} %bitcast.229, ...), custom_call_target="tpu_custom_call" | custom-call | flops 5000000000 | bytes 12950528 | tf_op jit(solution)/shard_map/gating_backward/pallas_call | solution.py:257
  370.3 2.5 all-to-all-done.5
  373.9 54.3 %block_backward.2 = (f32[832,768]{1,0:T(8,128)}, bf16[768,3200]{1,0:T(8,128)(2,1)}, bf16[960,768]{1,0:T(8,128)(2,1)}, bf16[960,768]{1,0:T(8,128)(2,1)}) custom-call(bf16[832,768]{1,0:T(8,128)(2,1)} %refs_0_.5, f32[832,768]{1,0:T(8,128)} %get-tuple-element.91.refs_1_, bf16[960,768]{1,0:T(8,128)(2,1)} %bitcast.228, ...), custom_call_target="tpu_custom_call" | custom-call | flops 40000000000 | bytes 35318784 | tf_op jit(solution)/shard_map/block_backward/pallas_call | solution.py:257
  428.2 1.3 copy-done.9
  429.6 37.5 %all_to_all.42 = bf16[4,240,768]{2,1,0:T(8,128)(2,1)} all-to-all(bf16[4,240,768]{2,1,0:T(8,128)(2,1)S(1)} %bitcast.233), channel_id=1, replica_groups=mesh['expert'=4,'shard'=8] {'expert'}, dimensions={0} | all-to-all | bytes 2949120 | tf_op jit(solution)/shard_map/all_to_all | solution.py:722
  467.1 18.1 %ffn_input_grad.3 = (bf16[960,768]{1,0:T(8,128)(2,1)}, bf16[960,2048]{1,0:T(8,128)(2,1)}, bf16[960,2048]{1,0:T(8,128)(2,1)}, bf16[960,2048]{1,0:T(8,128)(2,1)}) custom-call(bf16[960,768]{1,0:T(8,128)(2,1)} %bitcast.195, bf16[960,2048]{1,0:T(8,128)(2,1)} %get-tuple-element.102.gu_ref, bf16[960,2048]{1,0:T(8,128)(2,1)} %get-tuple-element.103.uv_ref, ...), custom_call_target="tpu_custom_call" | custom-call | flops 9059696640 | bytes 25165824 | tf_op jit(solution)/shard_map/ffn_input_grad/pallas_call | solution.py:627
  485.3 3.6 all-to-all-start.7
  488.9 17.9 %ffn_weight_grad.3 = bf16[8,2304,256]{2,1,0:T(8,128)(2,1)} custom-call(bf16[960,768]{1,0:T(8,128)(2,1)} %bitcast.198, bf16[960,768]{1,0:T(8,128)(2,1)} %bitcast.196, bf16[960,2048]{1,0:T(8,128)(2,1)} %get-tuple-element.104.hid_ref, bf16[960,2048]{1,0:T(8,128)(2,1)} %get-tuple-element.105.ggu_ref, bf16[960,2048]{1,0:T(8,128)(2,1)} %get-tuple-element.106.guv_ref), custom_call_target="tpu_custom_call" | custom-call | flops 9059696640 | bytes 25165824 | tf_op jit(solution)/shard_map/ffn_weight_grad/pallas_call | solution.py:627
  506.7 9.5 %gating_backward.3 = (f32[832,768]{1,0:T(8,128)}, f32[32,768]{1,0:T(8,128)}, f32[16,16]{1,0:T(8,128)}, f32[16,832]{1,0:T(8,128)}) custom-call(f32[832,768]{1,0:T(8,128)} %get-tuple-element.100.refs_0_, bf16[832,768]{1,0:T(8,128)(2,1)} %get-tuple-element.107.refs_1_, bf16[960,768]{1,0:T(8,128)(2,1)} %bitcast.226, ...), custom_call_target="tpu_custom_call" | custom-call | flops 5000000000 | bytes 10434560 | tf_op jit(solution)/shard_map/gating_backward/pallas_call | solution.py:257
  516.4 6.2 all-to-all-done.7
  523.7 51.6 %block_backward.3 = (f32[832,768]{1,0:T(8,128)}, bf16[768,3200]{1,0:T(8,128)(2,1)}) custom-call(f32[832,768]{1,0:T(8,128)} %get-tuple-element.100.refs_0_, f32[832,768]{1,0:T(8,128)} %get-tuple-element.110.refs_1_, bf16[960,768]{1,0:T(8,128)(2,1)} %bitcast.227, f32[832,4]{1,0:T(8,128)} %get-tuple-element.219.refs_4_.refs_3_, ...), custom_call_target="tpu_custom_call" | custom-call | flops 40000000000 | bytes 32130048 | tf_op jit(solution)/shard_map/block_backward/pallas_call | solution.py:257
  577.3 52.3 %reduce-scatter.7.cloned.1.call-done = bf16[96,3200]{1,0:T(8,128)(2,1)} async-done(((bf16[768,3200]{1,0:T(8,128)(2,1)}), bf16[96,3200]{1,0:T(8,128)(2,1)}) %reduce-scatter.7.cloned.1.call-update) | async-done | bytes 614416 | tf_op jit(solution)/shard_map/reduce_scatter | solution.py:873
  630.4 39.6 %psum.23 = f32[2,16,16]{2,1,0:T(8,128)S(1)} all-reduce(f32[2,16,16]{2,1,0:T(8,128)S(1)} %pad_maximum_fusion.5), channel_id=1, replica_groups=mesh['expert'=4,'shard'=8] {'expert','shard'}, use_global_device_ids=true, to_apply=%region_6.7 | all-reduce | flops 512 | bytes 4096 | tf_op jit(solution)/shard_map/psum | solution.py:876
  671.3 39.0 %reduce-scatter.11.cloned.1.call-done = bf16[1,2304,256]{2,1,0:T(8,128)(2,1)} async-done(((bf16[8,2304,256]{2,1,0:T(8,128)(2,1)}), bf16[1,2304,256]{2,1,0:T(8,128)(2,1)}) %reduce-scatter.11.cloned.1.call-update) | async-done | bytes 1179664 | tf_op jit(solution)/shard_map/reduce_scatter | solution.py:850
  710.3 2.3 fusion.58
  712.6 2.3 copy.227
  714.9 1.3 copy.225
  716.2 2.1 stack_reshape.21
  719.8 32.5 %all-reduce.15.cloned.1.call-done = bf16[1,96,3200]{2,1,0:T(8,128)(2,1)} async-done(((bf16[1,96,3200]{2,1,0:T(8,128)(2,1)}), bf16[1,96,3200]{2,1,0:T(8,128)(2,1)}) %all-reduce.15.cloned.1.call-update) | async-done | bytes 614416 | tf_op jit(solution)/shard_map/psum | solution.py:874
  757.0 1.3 copy.228
  758.9 73.0 %reduce-scatter.9.cloned.1.call-done = bf16[1,2304,256]{2,1,0:T(8,128)(2,1)} async-done(((bf16[8,2304,256]{2,1,0:T(8,128)(2,1)}), bf16[1,2304,256]{2,1,0:T(8,128)(2,1)}) %reduce-scatter.9.cloned.1.call-update) | async-done | bytes 1179664 | tf_op jit(solution)/shard_map/reduce_scatter | solution.py:850
  831.9 1.4 fusion.57
  834.5 1.5 maximum_bitcast_fusion.2
  835.9 1.6 copy.232
  840.5 1.2 maximum_bitcast_fusion.1
  842.0 1.2 maximum_bitcast_fusion
  (151 shorter events, 39.4 us)
Async XLA Ops:
  7.2 7.5 copy-start.12
  7.2 50.0 %all-gather.7.cloned.1.call-start = ((), (), s32[]{:S(2)}) async-start(), calls=%async_computation.12 | async-start | bytes 5529600 | tf_op jit(solution)/shard_map/all_gather | solution.py:774
  11.6 3.3 copy-start.13
  13.8 0.8 copy-start.11
  14.6 112.8 %all-gather.11.cloned.1.call-start = ((), (), s32[]{:S(2)}) async-start(), calls=%async_computation.20 | async-start | bytes 10616832 | tf_op jit(solution)/shard_map/all_gather | solution.py:776
  14.7 1.1 copy-start.14
  17.4 143.4 %all-gather.9.cloned.1.call-start = ((), (), s32[]{:S(2)}) async-start(), calls=%async_computation.13 | async-start | bytes 5529600 | tf_op jit(solution)/shard_map/all_gather | solution.py:774
  17.7 0.8 copy-start.10
  18.5 244.8 %all-gather.13.cloned.1.call-start = ((), (), s32[]{:S(2)}) async-start(), calls=%async_computation.21 | async-start | bytes 10616832 | tf_op jit(solution)/shard_map/all_gather | solution.py:776
  19.1 1.4 copy-start.17
  19.1 1.7 copy-start.21
  19.3 1.6 copy-start.23
  20.5 1.8 copy-start.18
  20.5 3.7 copy-start.15
  20.5 4.4 copy-start.22
  143.4 38.1 %all-to-all-start.1 = ((bf16[4,240,768]{2,1,0:T(8,128)(2,1)}), bf16[4,240,768]{2,1,0:T(8,128)(2,1)S(1)}, u32[]{:S(2)}, u32[]{:S(2)}) async-start(bf16[4,240,768]{2,1,0:T(8,128)(2,1)} %bitcast.232), calls=%async_computation.1 | async-start | bytes 2949120 | tf_op jit(solution)/shard_map/all_to_all | solution.py:722
  181.5 1.1 copy-start.5
  259.5 37.5 %all-to-all-start.3 = ((bf16[4,240,768]{2,1,0:T(8,128)(2,1)}), bf16[4,240,768]{2,1,0:T(8,128)(2,1)S(1)}, u32[]{:S(2)}, u32[]{:S(2)}) async-start(bf16[4,240,768]{2,1,0:T(8,128)(2,1)} %bitcast.49), calls=%async_computation.3 | async-start | bytes 2949120 | tf_op jit(solution)/shard_map/all_to_all | solution.py:722
  297.0 3.6 copy-start
  297.0 37.9 %all-to-all-start.4 = ((bf16[4,240,768]{2,1,0:T(8,128)(2,1)}), bf16[4,240,768]{2,1,0:T(8,128)(2,1)S(1)}, u32[]{:S(2)}, u32[]{:S(2)}) async-start(bf16[4,240,768]{2,1,0:T(8,128)(2,1)} %bitcast.234), calls=%async_computation.4 | async-start | bytes 2949120 | tf_op jit(solution)/shard_map/all_to_all | solution.py:722
  334.9 23.2 %copy-start.8 = (bf16[4,240,768]{2,1,0:T(8,128)(2,1)}, bf16[4,240,768]{2,1,0:T(8,128)(2,1)S(1)}, u32[]{:S(2)}) copy-start(bf16[4,240,768]{2,1,0:T(8,128)(2,1)S(1)} %all-to-all-done.4) | copy-start | bytes 4423684
  334.9 37.9 %all-to-all-start.5 = ((bf16[4,240,768]{2,1,0:T(8,128)(2,1)}), bf16[4,240,768]{2,1,0:T(8,128)(2,1)S(1)}, u32[]{:S(2)}, u32[]{:S(2)}) async-start(bf16[4,240,768]{2,1,0:T(8,128)(2,1)} %bitcast.231), calls=%async_computation.5 | async-start | bytes 2949120 | tf_op jit(solution)/shard_map/all_to_all | solution.py:722
  338.5 177.8 %reduce-scatter.5.cloned.1.call-start = ((), (), s32[]{:S(2)}) async-start(), calls=%async_computation.14 | async-start | bytes 5529600 | tf_op jit(solution)/shard_map/reduce_scatter | solution.py:873
  372.8 1.1 copy-start.7
  428.2 1.4 copy-start.9
  485.3 37.3 %all-to-all-start.7 = ((bf16[4,240,768]{2,1,0:T(8,128)(2,1)}), bf16[4,240,768]{2,1,0:T(8,128)(2,1)S(1)}, u32[]{:S(2)}, u32[]{:S(2)}) async-start(bf16[4,240,768]{2,1,0:T(8,128)(2,1)} %bitcast.230), calls=%async_computation.7 | async-start | bytes 2949120 | tf_op jit(solution)/shard_map/all_to_all | solution.py:722
  488.8 86.5 %all-reduce.13.cloned.1.call-start = ((), (), s32[]{:S(2)}) async-start(), calls=%async_computation.15 | async-start | bytes 1228800 | tf_op jit(solution)/shard_map/psum | solution.py:874
  516.3 113.4 %reduce-scatter.7.cloned.1.call-start = ((), (), s32[]{:S(2)}) async-start(), calls=%async_computation.16 | async-start | bytes 5529600 | tf_op jit(solution)/shard_map/reduce_scatter | solution.py:873
  522.6 1.1 copy-start.6
  576.5 133.8 %reduce-scatter.11.cloned.1.call-start = ((), (), s32[]{:S(2)}) async-start(), calls=%async_computation.19 | async-start | bytes 10616832 | tf_op jit(solution)/shard_map/reduce_scatter | solution.py:850
  577.3 175.1 %all-reduce.15.cloned.1.call-start = ((), (), s32[]{:S(2)}) async-start(), calls=%async_computation.17 | async-start | bytes 1228800 | tf_op jit(solution)/shard_map/psum | solution.py:874
  629.7 0.7 copy-start.19
  629.7 0.7 copy-start.20
  629.7 40.9 %copy-start.16 = (f32[16,832]{1,0:T(8,128)S(1)}, f32[16,832]{1,0:T(8,128)}, u32[]{:S(2)}) copy-start(f32[16,832]{1,0:T(8,128)} %get-tuple-element.118) | copy-start | bytes 159748
  629.7 202.2 %reduce-scatter.9.cloned.1.call-start = ((), (), s32[]{:S(2)}) async-start(), calls=%async_computation.18 | async-start | bytes 10616832 | tf_op jit(solution)/shard_map/reduce_scatter | solution.py:850
  838.0 2.5 copy-start.1
  839.0 1.5 copy-start.3
  839.5 2.3 copy-start.2
  840.5 1.5 copy-start.4
Sparse Core Ops, SparseCore 0:
  14.7 42.4 all-gather.6
  59.7 58.8 all-gather.10
  121.0 39.7 all-gather.8
  162.5 58.8 all-gather.12
  428.4 52.9 reduce-scatter.4
  516.4 39.9 all-reduce.12
  576.6 52.9 reduce-scatter.6
  633.2 77.1 reduce-scatter.10
  712.7 39.6 all-reduce.14
  755.7 76.1 reduce-scatter.8

commit v2 on v1

--- a/solution.py
+++ b/solution.py
@@ -559,15 +559,6 @@
         )
         return jnp.concatenate(pieces, axis=0)
 
-    def unpack(self, packed):
-        wide = []
-        for n in range(2):
-            cut = packed[n * self.chunks * self.padded : (n + 1) * self.chunks * self.padded]
-            cut = cut.reshape(self.chunks, self.padded, 256)[:, : self.part]
-            wide.append(cut.transpose(1, 0, 2).reshape(self.part, self.ff))
-        down = packed[self.down :].reshape(D // 256, self.own, 256)
-        return wide[0], wide[1], down.transpose(1, 0, 2).reshape(self.own, D)
-
     def specs(self):
         two = self.shards, 2 * self.padded, 256
         steps = self.chunks // 2
@@ -715,6 +706,55 @@
         ffn_weight_kernel, "ffn_weight_grad", pack, count, 2, 3, False, outs, spec,
         [pltpu.VMEM((D, count), bf16)], [rows, gy, hid, ggu, guv],
     )
+
+
+def expert_outputs_kernel(pack, first_ref, second_ref, gate_ref, up_ref, down_ref):
+    for l, ref in enumerate((first_ref, second_ref)):
+        for n, out in enumerate((gate_ref, up_ref)):
+            for j in range(pack.chunks):
+                at = (n * pack.chunks + j) * pack.padded
+                out[l, :, j * 256 : (j + 1) * 256] = ref[at : at + pack.part, :].astype(f32)
+        for c in range(D // 256):
+            at = pack.down + c * pack.own
+            down_ref[l, :, c * 256 : (c + 1) * 256] = ref[at : at + pack.own, :].astype(f32)
+
+
+def expert_outputs(pack, grads):
+    wide = shape((LAYERS, pack.part, pack.ff))
+    outs = [wide, wide, shape((LAYERS, pack.own, D))]
+    body = functools.partial(expert_outputs_kernel, pack)
+    return whole_call(body, "expert_outputs", outs, [], grads, 10**6)
+
+
+def dense_outputs_kernel(
+    part, labels, first_ref, second_ref, proj_ref, out_ref, gain_ref, router_ref, vec_ref, const_ref,
+    turn,
+):
+    for l, ref in enumerate((first_ref, second_ref)):
+        for c in range(3):
+            proj_ref[l, c] = ref[:, c * D : (c + 1) * D].astype(f32)
+        out_ref[l] = ref[:, W_OUT:W_SMALL].astype(f32)
+        small = ref[:, W_SMALL:].astype(f32)
+        router_ref[l] = small[:, 0:labels]
+        for c in range(2):
+            const_ref[l, c] = small[:, S_CONST + 2 * c : S_CONST + 2 * c + 2]
+        turn[0:part, :] = small
+        rows = turn[...].T
+        gain_ref[l] = rows[S_GAIN : S_GAIN + 2, 0:part]
+        vec_ref[l] = rows[S_VEC : S_VEC + 2, 0:part]
+
+
+def dense_outputs(part, labels, grads):
+    outs = [
+        shape((LAYERS, 3, part, D)),
+        shape((LAYERS, part, D)),
+        shape((LAYERS, 2, part)),
+        shape((LAYERS, part, labels)),
+        shape((LAYERS, 2, part)),
+        shape((LAYERS, 2, part, 2)),
+    ]
+    body = functools.partial(dense_outputs_kernel, part, labels)
+    return whole_call(body, "dense_outputs", outs, [pltpu.VMEM((128, 128), f32)], grads, 10**6)
 
 
 def to_owner(rows, owners):
@@ -835,12 +875,15 @@
     gx = cotangent
     gz = None
     dense_grads = [None] * LAYERS
+    mix_grads = [None] * LAYERS
     expert_grads = [None] * LAYERS
-    mix_grads = [None] * LAYERS
     hidden_out = None
     for l in range(LAYERS - 1, -1, -1):
         last = l == LAYERS - 1
         keep = saved[l]
+        if not last:
+            keep["info"], mine = lax.optimization_barrier((keep["info"], mine))
+            dense_grads[l + 1] = lax.psum(mine, "expert")
         gin, hid, ggu, guv = ffn_input_grad(
             pack, keep["gy"], keep["gate"], keep["up"], experts_w[l]
         )
@@ -865,34 +908,37 @@
             args += [slot_row[l - 1], saved[l - 1]["gpack"]]
         outs = backward_call(l == 0, experts, slots, args)
         gx, d_dense = outs[:2]
+        d_dense, expert_grads[l] = lax.optimization_barrier((d_dense, expert_grads[l]))
         if l > 0:
             saved[l - 1]["gxs"] = outs[2]
-            saved[l - 1]["gy"] = to_owner(outs[3], experts)
+            gy, d_dense = lax.optimization_barrier((outs[3], d_dense))
+            saved[l - 1]["gy"] = to_owner(gy, experts)
         if not last:
             d_dense, dense_grads[l + 1] = lax.optimization_barrier((d_dense, dense_grads[l + 1]))
+        if l == 0:
+            mix_grads[0], d_dense = lax.optimization_barrier((mix_grads[0], d_dense))
         mine = lax.psum_scatter(d_dense, "shard", scatter_dimension=0, tiled=True)
-        dense_grads[l] = lax.psum(mine, "expert").astype(f32)
-
+
+    dense_grads[0] = lax.psum(mine, "expert")
     mixing_total = lax.psum(jnp.stack(mix_grads), ("expert", "shard"))
-    grads = jnp.stack(dense_grads)
-    small = grads[:, :, W_SMALL:]
-    project_grad = jnp.stack([grads[:, :, c * D : (c + 1) * D] for c in range(3)], axis=1)
-    const_grad = jnp.stack(
-        [small[:, :, S_CONST + 2 * c : S_CONST + 2 * c + 2] for c in range(2)], axis=1
-    )
-    unpacked = [pack.unpack(expert_grads[l].astype(f32)) for l in range(LAYERS)]
+    gate_grad, up_grad, down_grad = expert_outputs(pack, expert_grads)
+    project_grad, output_grad, gain_grad, router_grad, vector_grad, const_grad = dense_outputs(
+        part, total_experts, dense_grads
+    )
     return (
         hidden_out,
         gx,
         gz[0:total_experts].T,
         project_grad,
-        grads[:, :, W_OUT:W_SMALL],
-        small[:, :, S_GAIN : S_GAIN + 2].transpose(0, 2, 1),
-        small[:, :, 0:total_experts],
+        output_grad,
+        gain_grad,
+        router_grad,
         mixing_total[:, 0:total_experts, 0:total_experts],
-        small[:, :, S_VEC : S_VEC + 2].transpose(0, 2, 1),
+        vector_grad,
         const_grad,
-        *[jnp.stack([unpacked[l][n] for l in range(LAYERS)])[:, None] for n in range(3)],
+        gate_grad[:, None],
+        up_grad[:, None],
+        down_grad[:, None],
     )
 
 

time: 859 us -> 782 us (0.910)
  waiting for transfers between devices: 296 us -> 200 us
  blocking collectives: 156 us -> 194 us
  local copies, waits for them, and re-layouts: 49 us -> 34.1 us
  Pallas kernels: 299 us -> 308 us
    reduce_scatter x2, waiting for transfers between devices: 112 us -> 0.01 us  [on_device(): lax.psum_scatter(d_experts, 'shard', scatter_dimension=0, tiled=False)]
    all_to_all x3 -> x4, blocking collectives: 117 us -> 154 us  [to_owner(): lax.all_to_all(rows.reshape(owners, slots, D), 'expert', split_axis=0, co...]
    all_to_all x5 -> x4, waiting for transfers between devices: 63.5 us -> 79.5 us  [to_owner(): lax.all_to_all(rows.reshape(owners, slots, D), 'expert', split_axis=0, co...]
    pallas_call x6 -> x8, Pallas kernels: 196 us -> 204 us  [whole_call(): pl.pallas_call(body, out_shape=outs, in_specs=[pl.BlockSpec(memory_space=...]
    all_to_all x5 -> x4, starting transfers between devices: 17.9 us -> 14.2 us  [to_owner(): lax.all_to_all(rows.reshape(owners, slots, D), 'expert', split_axis=0, co...]
    unnamed x64 -> x53, local copies, waits for them, and re-layouts: 17.3 us -> 17.7 us
  transfers between devices with their start and end apart: 15 -> 14, of which waited for: 11 -> 8; matrix products, arithmetic and copies ran while one was open for 5% -> 3% of each run, Pallas kernels for 29% -> 35%
where the time goes in v2:
time: 782 us; the launch traced here: 774 us
  Pallas kernels  308 us (39%)
  waiting for transfers between devices  200 us (26%)
  blocking collectives  194 us (25%)
  local copies, waits for them, and re-layouts  34.1 us (4%)
  starting transfers between devices  15.1 us (2%)
  between operations  15 us (2%)
    pallas_call x8, Pallas kernels, whole_call(): pl.pallas_call(body, out_shape=outs, in_specs=[pl.BlockSpec(memory_space=...  204 us
    all_to_all x4, blocking collectives, to_owner(): lax.all_to_all(rows.reshape(owners, slots, D), 'expert', split_axis=0, co...  154 us
    pallas_call x6, Pallas kernels, ffn_call(): pl.pallas_call(functools.partial(body, pack), grid=(ff // 512,), out_shap...  104 us
    all_to_all x4, waiting for transfers between devices, to_owner(): lax.all_to_all(rows.reshape(owners, slots, D), 'expert', split_axis=0, co...  79.5 us
    reduce_scatter x2, waiting for transfers between devices, on_device(): mine = lax.psum_scatter(d_dense, 'shard', scatter_dimension=0, tiled=True)  58.4 us
    psum x1, blocking collectives, on_device(): mixing_total = lax.psum(jnp.stack(mix_grads), ('expert', 'shard'))  40.2 us
    all_gather x2, waiting for transfers between devices, on_device(): dense.append(lax.all_gather(packed, 'shard', axis=0, tiled=True))  34.7 us
    psum x1, waiting for transfers between devices, on_device(): dense_grads[l + 1] = lax.psum(mine, 'expert')  26.5 us
  transfers between devices with their start and end apart: 14, of which 8 were waited for; matrix products, arithmetic and copies ran while one was open for 3% of the time, Pallas kernels for 35%

profile of v2, /device:TPU:0, one launch (start us, length us, event | category | flops | bytes accessed | tf_op | source)
XLA Modules:
  0.0 774.0 jit_solution(7744689041008233433)
XLA Ops:
  7.2 1.1 bitcast_dynamic-update-slice_fusion.3
  11.7 1.1 bitcast_dynamic-update-slice_fusion.1
  12.7 1.0 bitcast_dynamic-update-slice_fusion
  16.3 1.1 pad_maximum_fusion
  19.3 1.2 pad_maximum_fusion.1
  25.0 4.1 fusion.7
  29.1 28.2 %all-gather.7.cloned.1.call-done.refs_1_.refs_6_ = bf16[768,3200]{1,0:T(8,128)(2,1)} async-done(((bf16[96,3200]{1,0:T(8,128)(2,1)}), bf16[768,3200]{1,0:T(8,128)(2,1)}) %all-gather.7.cloned.1.call-update) | async-done | bytes 4915216 | tf_op jit(solution)/shard_map/all_gather | solution.py:814
  57.2 29.6 %block_forward.2 = (bf16[832,768]{1,0:T(8,128)(2,1)}, bf16[832,2304]{1,0:T(8,128)(2,1)}, bf16[832,768]{1,0:T(8,128)(2,1)}, f32[16,832]{1,0:T(8,128)}, f32[832,76...) custom-call(bf16[832,768]{1,0:T(8,128)(2,1)} %refs_9_.1, ...), custom_call_target="tpu_custom_call" | custom-call | flops 20000000000 | bytes 21619712 | tf_op jit(solution)/shard_map/block_forward/pallas_call | solution.py:257
  86.9 40.3 %all_to_all.40 = bf16[4,240,768]{2,1,0:T(8,128)(2,1)} all-to-all(bf16[4,240,768]{2,1,0:T(8,128)(2,1)} %bitcast.192), channel_id=1, replica_groups=mesh['expert'=4,'shard'=8] {'expert'}, dimensions={0} | all-to-all | bytes 2949120 | tf_op jit(solution)/shard_map/all_to_all | solution.py:762
  127.1 16.0 %ffn_forward.2 = (bf16[960,768]{1,0:T(8,128)(2,1)}, bf16[960,2048]{1,0:T(8,128)(2,1)}, bf16[960,2048]{1,0:T(8,128)(2,1)}) custom-call(bf16[960,768]{1,0:T(8,128)(2,1)} %bitcast.163, bf16[8,2304,256]{2,1,0:T(8,128)(2,1)} %bitcast.139, bf16[8,2304,256]{2,1,0:T(8,128)(2,1)} %bitcast.140, bf16[8,2304,256]{2,1,0:T(8,128)(2,1)} %bitcast.141, ...), custom_call_target="tpu_custom_call" | custom-call | flops 9059696640 | bytes 25165824 | tf_op jit(solution)/shard_map/ffn_forward/pallas_call | solution.py:618
  143.1 3.6 all-to-all-start.1
  151.2 1.4 slice.144.refs_8_.refs_9_
  152.7 1.6 slice.159.refs_5_.refs_8_
  154.3 6.5 all-gather.9.cloned.1.call-done.refs_6_
  160.8 20.3 %all-to-all-done.1 = bf16[4,240,768]{2,1,0:T(8,128)(2,1)S(1)} async-done(((bf16[4,240,768]{2,1,0:T(8,128)(2,1)}), bf16[4,240,768]{2,1,0:T(8,128)(2,1)S(1)}, u32[]{:S(2)}, u32[]{:S(2)}) %all-to-all-start.1) | async-done | bytes 1474592 | tf_op jit(solution)/shard_map/all_to_all | solution.py:762
  181.1 1.1 copy-done.1
  182.2 38.2 %block_forward.3 = (f32[832,768]{1,0:T(8,128)}, bf16[832,768]{1,0:T(8,128)(2,1)}, bf16[832,2304]{1,0:T(8,128)(2,1)}, bf16[832,768]{1,0:T(8,128)(2,1)}, f32[16,83...) custom-call(f32[832,768]{1,0:T(8,128)} %get-tuple-element.89.refs_0_, ...), custom_call_target="tpu_custom_call" | custom-call | flops 20000000000 | bytes 33069056 | tf_op jit(solution)/shard_map/block_forward/pallas_call | solution.py:257
  220.4 38.7 %all_to_all.41 = bf16[4,240,768]{2,1,0:T(8,128)(2,1)} all-to-all(bf16[4,240,768]{2,1,0:T(8,128)(2,1)} %bitcast.191), channel_id=1, replica_groups=mesh['expert'=4,'shard'=8] {'expert'}, dimensions={0} | all-to-all | bytes 2949120 | tf_op jit(solution)/shard_map/all_to_all | solution.py:762
  259.2 3.6 all-to-all-start.3
  263.2 15.7 %ffn_forward.3 = (bf16[960,768]{1,0:T(8,128)(2,1)}, bf16[960,2048]{1,0:T(8,128)(2,1)}, bf16[960,2048]{1,0:T(8,128)(2,1)}) custom-call(bf16[960,768]{1,0:T(8,128)(2,1)} %bitcast.165, bf16[8,2304,256]{2,1,0:T(8,128)(2,1)} %bitcast.149, bf16[8,2304,256]{2,1,0:T(8,128)(2,1)} %bitcast.150, bf16[8,2304,256]{2,1,0:T(8,128)(2,1)} %bitcast.151, ...), custom_call_target="tpu_custom_call" | custom-call | flops 9059696640 | bytes 25165824 | tf_op jit(solution)/shard_map/ffn_forward/pallas_call | solution.py:618
  278.9 17.6 %all-to-all-done.3 = bf16[4,240,768]{2,1,0:T(8,128)(2,1)S(1)} async-done(((bf16[4,240,768]{2,1,0:T(8,128)(2,1)}), bf16[4,240,768]{2,1,0:T(8,128)(2,1)S(1)}, u32[]{:S(2)}, u32[]{:S(2)}) %all-to-all-start.3) | async-done | bytes 1474592 | tf_op jit(solution)/shard_map/all_to_all | solution.py:762
  296.5 1.1 copy-done
  297.6 18.1 %ffn_input_grad.2 = (bf16[960,768]{1,0:T(8,128)(2,1)}, bf16[960,2048]{1,0:T(8,128)(2,1)}, bf16[960,2048]{1,0:T(8,128)(2,1)}, bf16[960,2048]{1,0:T(8,128)(2,1)}) custom-call(bf16[960,768]{1,0:T(8,128)(2,1)} %bitcast.159, bf16[960,2048]{1,0:T(8,128)(2,1)} %get-tuple-element.97.gu_ref, bf16[960,2048]{1,0:T(8,128)(2,1)} %get-tuple-element.98.uv_ref, ...), custom_call_target="tpu_custom_call" | custom-call | flops 9059696640 | bytes 25165824 | tf_op jit(solution)/shard_map/ffn_input_grad/pallas_call | solution.py:618
  315.8 17.8 %ffn_weight_grad.2 = bf16[8,2304,256]{2,1,0:T(8,128)(2,1)} custom-call(bf16[960,768]{1,0:T(8,128)(2,1)} %bitcast.166, bf16[960,768]{1,0:T(8,128)(2,1)} %bitcast.160, bf16[960,2048]{1,0:T(8,128)(2,1)} %get-tuple-element.99.hid_ref, bf16[960,2048]{1,0:T(8,128)(2,1)} %get-tuple-element.100.ggu_ref, bf16[960,2048]{1,0:T(8,128)(2,1)} %get-tuple-element.101.guv_ref), custom_call_target="tpu_custom_call" | custom-call | flops 9059696640 | bytes 25165824 | tf_op jit(solution)/shard_map/ffn_weight_grad/pallas_call | solution.py:618
  333.6 1.3 copy-done.5
  335.0 37.5 %all_to_all.42 = bf16[4,240,768]{2,1,0:T(8,128)(2,1)} all-to-all(bf16[4,240,768]{2,1,0:T(8,128)(2,1)S(1)} %bitcast.189), channel_id=1, replica_groups=mesh['expert'=4,'shard'=8] {'expert'}, dimensions={0} | all-to-all | bytes 2949120 | tf_op jit(solution)/shard_map/all_to_all | solution.py:762
  372.5 3.6 all-to-all-start.5
  376.1 1.6 slice.162.refs_8_
  377.7 12.4 %gating_backward.2 = (f32[832,768]{1,0:T(8,128)}, f32[32,768]{1,0:T(8,128)}, f32[16,16]{1,0:T(8,128)}, f32[16,832]{1,0:T(8,128)}, bf16[832,768]{1,0:T(8,128)(2,1)}) custom-call(bf16[832,768]{1,0:T(8,128)(2,1)} %refs_0_.5, bf16[832,768]{1,0:T(8,128)(2,1)} %get-tuple-element.103.refs_1_, bf16[960,768]{1,0:T(8,128)(2,1)} %bitcast.190, ...), custom_call_target="tpu_custom_call" | custom-call | flops 5000000000 | bytes 12950528 | tf_op jit(solution)/shard_map/gating_backward/pallas_call | solution.py:257
  390.2 19.6 %all-to-all-done.5 = bf16[4,240,768]{2,1,0:T(8,128)(2,1)S(1)} async-done(((bf16[4,240,768]{2,1,0:T(8,128)(2,1)}), bf16[4,240,768]{2,1,0:T(8,128)(2,1)S(1)}, u32[]{:S(2)}, u32[]{:S(2)}) %all-to-all-start.5) | async-done | bytes 1474592 | tf_op jit(solution)/shard_map/all_to_all | solution.py:762
  409.8 1.1 copy-done.3
  410.9 53.9 %block_backward.2 = (f32[832,768]{1,0:T(8,128)}, bf16[768,3200]{1,0:T(8,128)(2,1)}, bf16[960,768]{1,0:T(8,128)(2,1)}, bf16[960,768]{1,0:T(8,128)(2,1)}) custom-call(bf16[832,768]{1,0:T(8,128)(2,1)} %refs_0_.5, f32[832,768]{1,0:T(8,128)} %get-tuple-element.110.refs_1_, bf16[960,768]{1,0:T(8,128)(2,1)} %bitcast.186, ...), custom_call_target="tpu_custom_call" | custom-call | flops 40000000000 | bytes 35318784 | tf_op jit(solution)/shard_map/block_backward/pallas_call | solution.py:257
  464.9 1.3 copy-done.4
  466.2 37.7 %all_to_all.43 = bf16[4,240,768]{2,1,0:T(8,128)(2,1)} all-to-all(bf16[4,240,768]{2,1,0:T(8,128)(2,1)S(1)} %bitcast.188), channel_id=1, replica_groups=mesh['expert'=4,'shard'=8] {'expert'}, dimensions={0} | all-to-all | bytes 2949120 | tf_op jit(solution)/shard_map/all_to_all | solution.py:762
  503.9 18.2 %ffn_input_grad.3 = (bf16[960,768]{1,0:T(8,128)(2,1)}, bf16[960,2048]{1,0:T(8,128)(2,1)}, bf16[960,2048]{1,0:T(8,128)(2,1)}, bf16[960,2048]{1,0:T(8,128)(2,1)}) custom-call(bf16[960,768]{1,0:T(8,128)(2,1)} %bitcast.161, bf16[960,2048]{1,0:T(8,128)(2,1)} %get-tuple-element.125.gu_ref, bf16[960,2048]{1,0:T(8,128)(2,1)} %get-tuple-element.126.uv_ref, ...), custom_call_target="tpu_custom_call" | custom-call | flops 9059696640 | bytes 25165824 | tf_op jit(solution)/shard_map/ffn_input_grad/pallas_call | solution.py:618
  522.1 17.9 %ffn_weight_grad.3 = bf16[8,2304,256]{2,1,0:T(8,128)(2,1)} custom-call(bf16[960,768]{1,0:T(8,128)(2,1)} %bitcast.164, bf16[960,768]{1,0:T(8,128)(2,1)} %bitcast.162, bf16[960,2048]{1,0:T(8,128)(2,1)} %get-tuple-element.127.hid_ref, bf16[960,2048]{1,0:T(8,128)(2,1)} %get-tuple-element.128.ggu_ref, bf16[960,2048]{1,0:T(8,128)(2,1)} %get-tuple-element.129.guv_ref), custom_call_target="tpu_custom_call" | custom-call | flops 9059696640 | bytes 25165824 | tf_op jit(solution)/shard_map/ffn_weight_grad/pallas_call | solution.py:618
  539.9 3.6 all-to-all-start.7
  544.3 10.9 %gating_backward.3 = (f32[832,768]{1,0:T(8,128)}, f32[32,768]{1,0:T(8,128)}, f32[16,16]{1,0:T(8,128)}, f32[16,832]{1,0:T(8,128)}) custom-call(f32[832,768]{1,0:T(8,128)} %get-tuple-element.119.refs_0_, bf16[832,768]{1,0:T(8,128)(2,1)} %get-tuple-element.130.refs_1_, bf16[960,768]{1,0:T(8,128)(2,1)} %bitcast.184, ...), custom_call_target="tpu_custom_call" | custom-call | flops 5000000000 | bytes 10434560 | tf_op jit(solution)/shard_map/gating_backward/pallas_call | solution.py:257
  555.3 22.1 %all-to-all-done.7 = bf16[4,240,768]{2,1,0:T(8,128)(2,1)S(1)} async-done(((bf16[4,240,768]{2,1,0:T(8,128)(2,1)}), bf16[4,240,768]{2,1,0:T(8,128)(2,1)S(1)}, u32[]{:S(2)}, u32[]{:S(2)}) %all-to-all-start.7) | async-done | bytes 1474592 | tf_op jit(solution)/shard_map/all_to_all | solution.py:762
  577.3 1.1 copy-done.2
  578.4 51.9 %block_backward.3 = (f32[832,768]{1,0:T(8,128)}, bf16[768,3200]{1,0:T(8,128)(2,1)}) custom-call(f32[832,768]{1,0:T(8,128)} %get-tuple-element.119.refs_0_, f32[832,768]{1,0:T(8,128)} %get-tuple-element.135.refs_1_, bf16[960,768]{1,0:T(8,128)(2,1)} %bitcast.185, f32[832,4]{1,0:T(8,128)} %get-tuple-element.243.refs_4_.refs_3_, ...), custom_call_target="tpu_custom_call" | custom-call | flops 40000000000 | bytes 32130048 | tf_op jit(solution)/shard_map/block_backward/pallas_call | solution.py:257
  630.3 26.5 %all-reduce.13.cloned.1.call-done.second_ref = bf16[96,3200]{1,0:T(8,128)(2,1)} async-done(((bf16[96,3200]{1,0:T(8,128)(2,1)}), bf16[96,3200]{1,0:T(8,128)(2,1)}) %all-reduce.13.cloned.1.call-update) | async-done | bytes 614416 | tf_op jit(solution)/shard_map/psum | solution.py:886
  657.0 58.4 %reduce-scatter.11.cloned.1.call-done = bf16[96,3200]{1,0:T(8,128)(2,1)} async-done(((bf16[768,3200]{1,0:T(8,128)(2,1)}), bf16[96,3200]{1,0:T(8,128)(2,1)}) %reduce-scatter.11.cloned.1.call-update) | async-done | bytes 614416 | tf_op jit(solution)/shard_map/reduce_scatter | solution.py:920
  716.1 40.2 %psum.23 = f32[2,16,16]{2,1,0:T(8,128)S(1)} all-reduce(f32[2,16,16]{2,1,0:T(8,128)S(1)} %pad_maximum_fusion.3), channel_id=1, replica_groups=mesh['expert'=4,'shard'=8] {'expert','shard'}, use_global_device_ids=true, to_apply=%region_8.9 | all-reduce | flops 512 | bytes 4096 | tf_op jit(solution)/shard_map/psum | solution.py:923
  756.8 3.9 expert_outputs.1
  760.7 2.8 dense_outputs.1
  763.6 1.6 copy.192
  765.1 1.6 copy.193
  (117 shorter events, 19.2 us)
Async XLA Ops:
  7.2 7.5 copy-start.8
  7.2 50.1 %all-gather.7.cloned.1.call-start = ((), (), s32[]{:S(2)}) async-start(), calls=%async_computation.12 | async-start | bytes 5529600 | tf_op jit(solution)/shard_map/all_gather | solution.py:814
  11.6 3.3 copy-start.9
  13.8 0.8 copy-start.7
  14.6 112.5 %all-gather.11.cloned.1.call-start = ((), (), s32[]{:S(2)}) async-start(), calls=%async_computation.20 | async-start | bytes 10616832 | tf_op jit(solution)/shard_map/all_gather | solution.py:816
  14.8 1.1 copy-start.10
  17.4 143.4 %all-gather.9.cloned.1.call-start = ((), (), s32[]{:S(2)}) async-start(), calls=%async_computation.13 | async-start | bytes 5529600 | tf_op jit(solution)/shard_map/all_gather | solution.py:814
  17.7 0.8 copy-start.6
  18.5 244.7 %all-gather.13.cloned.1.call-start = ((), (), s32[]{:S(2)}) async-start(), calls=%async_computation.21 | async-start | bytes 10616832 | tf_op jit(solution)/shard_map/all_gather | solution.py:816
  19.1 1.4 copy-start.13
  19.1 1.7 copy-start.17
  19.3 1.6 copy-start.19
  20.5 1.8 copy-start.14
  20.5 3.7 copy-start.11
  20.5 4.4 copy-start.18
  143.1 38.0 %all-to-all-start.1 = ((bf16[4,240,768]{2,1,0:T(8,128)(2,1)}), bf16[4,240,768]{2,1,0:T(8,128)(2,1)S(1)}, u32[]{:S(2)}, u32[]{:S(2)}) async-start(bf16[4,240,768]{2,1,0:T(8,128)(2,1)} %bitcast.187), calls=%async_computation.1 | async-start | bytes 2949120 | tf_op jit(solution)/shard_map/all_to_all | solution.py:762
  181.1 1.1 copy-start.1
  259.2 37.3 %all-to-all-start.3 = ((bf16[4,240,768]{2,1,0:T(8,128)(2,1)}), bf16[4,240,768]{2,1,0:T(8,128)(2,1)S(1)}, u32[]{:S(2)}, u32[]{:S(2)}) async-start(bf16[4,240,768]{2,1,0:T(8,128)(2,1)} %bitcast.49), calls=%async_computation.3 | async-start | bytes 2949120 | tf_op jit(solution)/shard_map/all_to_all | solution.py:762
  262.7 202.0 %reduce-scatter.5.cloned.1.call-start = ((), (), s32[]{:S(2)}) async-start(), calls=%async_computation.14 | async-start | bytes 10616832 | tf_op jit(solution)/shard_map/reduce_scatter | solution.py:893
  296.5 1.1 copy-start
  333.6 1.4 copy-start.5
  372.5 37.3 %all-to-all-start.5 = ((bf16[4,240,768]{2,1,0:T(8,128)(2,1)}), bf16[4,240,768]{2,1,0:T(8,128)(2,1)S(1)}, u32[]{:S(2)}, u32[]{:S(2)}) async-start(bf16[4,240,768]{2,1,0:T(8,128)(2,1)} %bitcast.61), calls=%async_computation.5 | async-start | bytes 2949120 | tf_op jit(solution)/shard_map/all_to_all | solution.py:762
  376.1 167.5 %reduce-scatter.7.cloned.1.call-start = ((), (), s32[]{:S(2)}) async-start(), calls=%async_computation.15 | async-start | bytes 5529600 | tf_op jit(solution)/shard_map/reduce_scatter | solution.py:920
  409.8 1.1 copy-start.3
  464.8 1.4 copy-start.4
  464.8 165.5 %reduce-scatter.9.cloned.1.call-start = ((), (), s32[]{:S(2)}) async-start(), calls=%async_computation.16 | async-start | bytes 10616832 | tf_op jit(solution)/shard_map/reduce_scatter | solution.py:893
  539.9 37.4 %all-to-all-start.7 = ((bf16[4,240,768]{2,1,0:T(8,128)(2,1)}), bf16[4,240,768]{2,1,0:T(8,128)(2,1)S(1)}, u32[]{:S(2)}, u32[]{:S(2)}) async-start(bf16[4,240,768]{2,1,0:T(8,128)(2,1)} %bitcast.66), calls=%async_computation.9 | async-start | bytes 2949120 | tf_op jit(solution)/shard_map/all_to_all | solution.py:762
  543.5 113.4 %all-reduce.13.cloned.1.call-start = ((), (), s32[]{:S(2)}) async-start(), calls=%async_computation.17 | async-start | bytes 1228800 | tf_op jit(solution)/shard_map/psum | solution.py:886
  544.3 171.1 %reduce-scatter.11.cloned.1.call-start = ((), (), s32[]{:S(2)}) async-start(), calls=%async_computation.18 | async-start | bytes 5529600 | tf_op jit(solution)/shard_map/reduce_scatter | solution.py:920
  577.3 1.1 copy-start.2
  656.9 58.5 %copy-start.12 = (f32[16,832]{1,0:T(8,128)S(1)}, f32[16,832]{1,0:T(8,128)}, u32[]{:S(2)}) copy-start(f32[16,832]{1,0:T(8,128)} %get-tuple-element.143) | copy-start | bytes 159748
  656.9 59.2 %copy-start.15 = (f32[16,16]{1,0:T(8,128)S(1)}, f32[16,16]{1,0:T(8,128)}, u32[]{:S(2)}) copy-start(f32[16,16]{1,0:T(8,128)} %get-tuple-element.157) | copy-start | bytes 3076
  656.9 59.2 %copy-start.16 = (f32[16,16]{1,0:T(8,128)S(1)}, f32[16,16]{1,0:T(8,128)}, u32[]{:S(2)}) copy-start(f32[16,16]{1,0:T(8,128)} %get-tuple-element.156) | copy-start | bytes 3076
  656.9 103.8 %all-reduce.15.cloned.1.call-start = ((), (), s32[]{:S(2)}) async-start(), calls=%async_computation.19 | async-start | bytes 1228800 | tf_op jit(solution)/shard_map/psum | solution.py:922
Sparse Core Ops, SparseCore 0:
  14.7 42.4 all-gather.6
  59.7 58.8 all-gather.10
  121.0 39.7 all-gather.8
  162.5 58.8 all-gather.12
  333.8 74.6 reduce-scatter.4
  464.9 53.0 reduce-scatter.6
  540.1 74.6 reduce-scatter.8
  617.3 39.5 all-reduce.12
  660.8 54.5 reduce-scatter.10
  717.6 39.9 all-reduce.14

commit v3 on v2

--- a/solution.py
+++ b/solution.py
@@ -127,6 +127,8 @@
     n1_ref, qkv_ref, att_ref, lse_ref, mid_ref, n2_ref, info_ref, gcol_ref, gpack_ref, send_ref = [
         refs.pop(0) for _ in range(10)
     ]
+    small_out = refs.pop(0)
+    small_out[...] = w_ref[:, W_SMALL:]
     if last:
         gxs_ref, gy_ref = refs.pop(0), refs.pop(0)
     lse_cols, turn = refs
@@ -281,6 +283,7 @@
         shape((tokens, 128)),
         shape((tokens, 128), bf16),
         shape((sent, D), bf16),
+        shape((D, 128), bf16),
     ]
     if last:
         outs += [shape((sent, D), bf16), shape((sent, D), bf16)]
@@ -546,7 +549,6 @@
         self.own = ff // shards
         self.down = 2 * self.chunks * self.padded
         self.rows = self.down + (D // 256) * self.own
-        self.group = 2 * 256 // self.own
 
     def pack(self, gate, up, down):
         pieces = []
@@ -559,153 +561,280 @@
         )
         return jnp.concatenate(pieces, axis=0)
 
-    def specs(self):
-        two = self.shards, 2 * self.padded, 256
-        steps = self.chunks // 2
-        wide = [pl.BlockSpec(two, lambda j, n=n: (0, n * steps + j, 0)) for n in range(2)]
-        base = self.down // self.own
-        tall = [
-            pl.BlockSpec((self.group, self.own, 256), lambda j, c=c: (j, base + c, 0))
-            for c in range(D // 256)
-        ]
-        return wide + tall
-
-    def wide_part(self, ref, i):
-        at = i * self.padded
-        return ref[:, at : at + self.part, :].reshape(D, 256)
-
-    def tall_part(self, refs):
-        return jnp.concatenate([ref[...].reshape(512, 256) for ref in refs], axis=1)
-
-
-def accumulate(total, part, out_ref):
-    j = pl.program_id(0)
-
-    @pl.when(j == 0)
-    def _():
-        total[...] = part
-
-    @pl.when(j > 0)
-    def _():
-        total[...] = total[...] + part
-
-    @pl.when(j == pl.num_programs(0) - 1)
-    def _():
-        out_ref[...] = total[...].astype(bf16)
-
-
-def ffn_forward_kernel(pack, r_ref, g_w, u_w, d0, d1, d2, y_ref, gu_ref, uv_ref, total):
-    r = r_ref[...]
-    hids = []
-    for i in range(2):
-        lanes = slice(i * 256, (i + 1) * 256)
-        gate = dot(r, pack.wide_part(g_w, i))
-        up = dot(r, pack.wide_part(u_w, i))
-        gu_ref[:, lanes] = gate.astype(bf16)
-        uv_ref[:, lanes] = up.astype(bf16)
-        hids.append((gate * jax.nn.sigmoid(gate) * up).astype(bf16))
-    hid = jnp.concatenate(hids, axis=1)
-    accumulate(total, dot(hid, pack.tall_part((d0, d1, d2))), y_ref)
-
-
-def ffn_call(body, name, pack, count, flat, wide, with_weights, outs, out_specs, scratch, args):
-    ff = pack.ff
-    in_specs = [pl.BlockSpec((count, D), lambda j: (0, 0))] * flat
-    in_specs += [pl.BlockSpec((count, 512), lambda j: (0, j))] * wide
-    if with_weights:
-        in_specs += pack.specs()
-        args = list(args) + [args[-1]] * 4
+    def wide_part(self, ref, n, j):
+        at = pl.multiple_of((n * self.chunks + j) * self.padded, 16)
+        return ref[:, pl.ds(at, self.padded), :][:, : self.part, :].reshape(D, 256)
+
+    def tall_part(self, ref, j):
+        group = 256 // self.own
+        here = pl.ds(j * group, group)
+        pieces = []
+        for c in range(D // 256):
+            at = self.down + c * self.own
+            pieces.append(ref[here, at : at + self.own, :].reshape(256, 256))
+        return jnp.concatenate(pieces, axis=1)
+
+    def put_wide(self, ref, n, j, grad):
+        at = pl.multiple_of((n * self.chunks + j) * self.padded, 16)
+        ref[:, pl.ds(at, self.part), :] = grad.reshape(self.shards, self.part, 256)
+
+    def put_tall(self, ref, j, grad):
+        group = 256 // self.own
+        for c in range(D // 256):
+            at = self.down + c * self.own
+            ref[pl.ds(j * group, group), at : at + self.own, :] = grad[
+                :, c * 256 : (c + 1) * 256
+            ].reshape(group, self.own, 256)
+
+
+class Exchange:
+    def __init__(self, experts, slots):
+        self.experts, self.slots = experts, slots
+        first = -(-slots // 32) * 16
+        self.waves = ((0, first), (first, slots - first))
+        self.ranges = [(0, slots)]
+        for _, size in self.waves:
+            start = self.ranges[-1][0] + self.ranges[-1][1]
+            self.ranges.append((start, (experts - 1) * size))
+        self.total = experts * slots
+
+    def held(self, wave, d):
+        size = self.waves[wave][1]
+        return pl.ds(self.ranges[1 + wave][0] + (d - 1) * size, size)
+
+    def slot(self, device, wave):
+        offset, size = self.waves[wave]
+        return pl.ds(pl.multiple_of(device * self.slots + offset, 16), size)
+
+
+def exchange_kernel(mode, pack, ex, *refs):
+    refs = list(refs)
+    forward, backward = mode in ("forward", "both"), mode in ("backward", "both")
+    if forward:
+        send_n = refs.pop(0)
+    if backward:
+        send_g = refs.pop(0)
+    w_hbm = refs.pop(0)
+    if mode == "backward":
+        gate_hbm, up_hbm, rows_hbm = refs.pop(0), refs.pop(0), refs.pop(0)
+    if mode == "forward":
+        recv_n, back_y, gates, ups = [refs.pop(0) for _ in range(4)]
+    elif mode == "both":
+        back_y, back_g, dw = [refs.pop(0) for _ in range(3)]
+        recv_n = refs.pop(0)
+    else:
+        back_g, dw = refs.pop(0), refs.pop(0)
+        recv_n = refs.pop(0)
+    if forward:
+        out_y = refs.pop(0)
+    if backward:
+        recv_g, out_g, hids, gates, ups, rows_t, acc_g = [refs.pop(0) for _ in range(7)]
+    if forward:
+        acc_y = refs.pop(0)
+    w, sends, recvs, backs, gots, local = refs
+
+    experts, slots = ex.experts, ex.slots
+    me = lax.axis_index("expert")
+    peers = range(1, experts)
+
+    def ahead(d):
+        return lax.rem(me + d, experts)
+
+    def behind(d):
+        return lax.rem(me + experts - d, experts)
+
+    loads = [pltpu.make_async_copy(w_hbm, w, local.at[0])]
+    if mode == "backward":
+        loads.append(pltpu.make_async_copy(gate_hbm, gates, local.at[1]))
+        loads.append(pltpu.make_async_copy(up_hbm, ups, local.at[2]))
+        loads.append(pltpu.make_async_copy(rows_hbm, recv_n, local.at[3]))
+    for copy in loads:
+        copy.start()
+    barrier = pltpu.get_barrier_semaphore()
+    for d in peers:
+        pl.semaphore_signal(
+            barrier, inc=1, device_id={"expert": ahead(d)}, device_id_type=pl.DeviceIdType.MESH
+        )
+    pl.semaphore_wait(barrier, experts - 1)
+
+    kinds = []
+    if forward:
+        kinds.append((send_n, recv_n))
+    if backward:
+        kinds.append((send_g, recv_g))
+    returns = []
+    if forward:
+        returns.append((out_y, back_y))
+    if backward:
+        returns.append((out_g, back_g))
+
+    def out_copies(wave):
+        copies = []
+        for d in peers:
+            for n, (src, dst) in enumerate(kinds):
+                copies.append(
+                    pltpu.make_async_remote_copy(
+                        src_ref=src.at[ex.slot(ahead(d), wave)],
+                        dst_ref=dst.at[ex.held(wave, d)],
+                        send_sem=sends.at[n, wave, d - 1],
+                        recv_sem=recvs.at[n, wave, d - 1],
+                        device_id={"expert": ahead(d)},
+                        device_id_type=pl.DeviceIdType.MESH,
+                    )
+                )
+        return copies
+
+    def back_copies(wave):
+        copies = []
+        for n, (src, dst) in enumerate(returns):
+            for d in peers:
+                copies.append(
+                    pltpu.make_async_remote_copy(
+                        src_ref=src.at[ex.held(wave, d)],
+                        dst_ref=dst.at[ex.slot(me, wave)],
+                        send_sem=backs.at[n, wave, d - 1],
+                        recv_sem=gots.at[n, wave, d - 1],
+                        device_id={"expert": behind(d)},
+                        device_id_type=pl.DeviceIdType.MESH,
+                    )
+                )
+        return copies
+
+    def work(start, size):
+        rows = slice(start, start + size)
+        part = slice(0, size)
+        if forward:
+            acc_y[part, :] = jnp.zeros((size, D), f32)
+        if backward:
+            acc_g[part, :] = jnp.zeros((size, D), f32)
+
+        def chunk(j, carry):
+            lanes = pl.ds(pl.multiple_of(j * 256, 256), 256)
+            gate_w, up_w = pack.wide_part(w, 0, j), pack.wide_part(w, 1, j)
+            down_w = pack.tall_part(w, j)
+            if forward:
+                r = recv_n[rows, :]
+                gate, up = dot(r, gate_w), dot(r, up_w)
+                if mode == "forward":
+                    gates[rows, lanes] = gate.astype(bf16)
+                    ups[rows, lanes] = up.astype(bf16)
+            else:
+                gate, up = gates[rows, lanes].astype(f32), ups[rows, lanes].astype(f32)
+            s = jax.nn.sigmoid(gate)
+            act = gate * s
+            hid = (act * up).astype(bf16)
+            if forward:
+                acc_y[part, :] = acc_y[part, :] + dot(hid, down_w)
+            if backward:
+                hids[rows, lanes] = hid
+                ghid = dot_nt(recv_g[rows, :], down_w)
+                guv = (ghid * act).astype(bf16)
+                ggu = (ghid * up * (s * (1.0 + gate * (1.0 - s)))).astype(bf16)
+                gates[rows, lanes] = ggu
+                ups[rows, lanes] = guv
+                acc_g[part, :] = acc_g[part, :] + dot_nt(ggu, gate_w) + dot_nt(guv, up_w)
+            return carry
+
+        lax.fori_loop(0, pack.chunks, chunk, 0)
+        if forward:
+            out_y[rows, :] = acc_y[part, :].astype(bf16)
+        if backward:
+            out_g[rows, :] = acc_g[part, :].astype(bf16)
+
+    waves = [out_copies(0), out_copies(1)]
+    for copy in waves[0]:
+        copy.start()
+    mine = pl.ds(pl.multiple_of(me * slots, 16), slots)
+    for copy in loads:
+        copy.wait()
+    for src, dst in kinds:
+        dst[0:slots, :] = src[mine, :]
+    work(*ex.ranges[0])
+    for src, dst in returns:
+        dst[mine, :] = src[0:slots, :]
+    for copy in waves[0]:
+        copy.wait_send()
+    for copy in waves[1]:
+        copy.start()
+    for copy in waves[0]:
+        copy.wait_recv()
+    work(*ex.ranges[1])
+    first = back_copies(0)
+    for copy in first:
+        copy.start()
+    for copy in waves[1]:
+        copy.wait()
+    work(*ex.ranges[2])
+    second = back_copies(1)
+    for copy in second:
+        copy.start()
+    if backward:
+        rows_t[...] = recv_n[...].T
+        if pack.padded != pack.part:
+            dw[...] = jnp.zeros_like(dw)
+
+        def weights(j, carry):
+            lanes = pl.ds(pl.multiple_of(j * 256, 256), 256)
+            pack.put_wide(dw, 0, j, dot(rows_t[...], gates[:, lanes]).astype(bf16))
+            pack.put_wide(dw, 1, j, dot(rows_t[...], ups[:, lanes]).astype(bf16))
+            pack.put_tall(dw, j, dot_tn(hids[:, lanes], recv_g[...]).astype(bf16))
+            return carry
+
+        lax.fori_loop(0, pack.chunks, weights, 0)
+    for copy in first + second:
+        copy.wait()
+
+
+EXCHANGE_IDS = {"forward": 0, "both": 1, "backward": 2}
+
+
+def exchange_call(mode, pack, experts, slots, args):
+    ex = Exchange(experts, slots)
+    rows, ff = ex.total, pack.ff
+    forward, backward = mode in ("forward", "both"), mode in ("backward", "both")
+    flat, wide = shape((rows, D), bf16), shape((rows, ff), bf16)
+    packed = (pack.shards, pack.rows, 256)
+    most = max(size for _, size in ex.ranges)
+    vmem = pl.BlockSpec(memory_space=pltpu.VMEM)
+    far = pl.BlockSpec(memory_space=pl.ANY)
+    in_specs = [vmem] * (2 if mode == "both" else 1) + [far]
+    scratch = []
+    if mode == "forward":
+        outs = [flat, flat, wide, wide]
+    elif mode == "both":
+        outs = [flat, flat, shape(packed, bf16)]
+        scratch.append(pltpu.VMEM((rows, D), bf16))
+    else:
+        in_specs += [far] * 3
+        outs = [flat, shape(packed, bf16)]
+        scratch.append(pltpu.VMEM((rows, D), bf16))
+    if forward:
+        scratch.append(pltpu.VMEM((rows, D), bf16))
+    if backward:
+        scratch += [pltpu.VMEM((rows, D), bf16)] * 2
+        scratch += [pltpu.VMEM((rows, ff), bf16)] * 3
+        scratch += [pltpu.VMEM((D, rows), bf16), pltpu.VMEM((most, D), f32)]
+    if forward:
+        scratch.append(pltpu.VMEM((most, D), f32))
+    kinds = 2 if mode == "both" else 1
+    scratch.append(pltpu.VMEM(packed, bf16))
+    scratch += [pltpu.SemaphoreType.DMA((kinds, 2, experts - 1))] * 4
+    scratch.append(pltpu.SemaphoreType.DMA((4,)))
+    work = 6 * rows * D * ff * (1 if mode == "forward" else 2 if mode == "backward" else 3)
     return pl.pallas_call(
-        functools.partial(body, pack),
-        grid=(ff // 512,),
+        functools.partial(exchange_kernel, mode, pack, ex),
         out_shape=outs,
         in_specs=in_specs,
-        out_specs=out_specs,
+        out_specs=[vmem] * len(outs),
         scratch_shapes=scratch,
-        compiler_params=pltpu.CompilerParams(vmem_limit_bytes=VMEM),
+        compiler_params=pltpu.CompilerParams(
+            vmem_limit_bytes=60 << 20, collective_id=EXCHANGE_IDS[mode], has_side_effects=True
+        ),
         cost_estimate=pl.CostEstimate(
-            flops=6 * count * D * ff, bytes_accessed=6 * D * ff + 8 * count * ff, transcendentals=0
+            flops=work + 40 * 10**9, bytes_accessed=6 * D * ff, transcendentals=0
         ),
-        name=name,
+        name="experts_" + mode,
     )(*args)
-
-
-def ffn_forward(pack, rows, weights):
-    count, ff = rows.shape[0], pack.ff
-    flat = pl.BlockSpec((count, D), lambda j: (0, 0))
-    wide = pl.BlockSpec((count, 512), lambda j: (0, j))
-    outs = [shape((count, D), bf16), shape((count, ff), bf16), shape((count, ff), bf16)]
-    scratch = [pltpu.VMEM((count, D), f32)]
-    return ffn_call(
-        ffn_forward_kernel, "ffn_forward", pack, count, 1, 0, True, outs, [flat, wide, wide],
-        scratch, [rows, weights],
-    )
-
-
-def ffn_input_kernel(
-    pack, gy_ref, gu_ref, uv_ref, g_w, u_w, d0, d1, d2, gin_ref, hid_ref, ggu_ref, guv_ref, total
-):
-    ghid_all = dot_nt(gy_ref[...], pack.tall_part((d0, d1, d2)))
-    part = 0.0
-    for i in range(2):
-        lanes = slice(i * 256, (i + 1) * 256)
-        ghid = ghid_all[:, lanes]
-        gate = gu_ref[:, lanes].astype(f32)
-        up = uv_ref[:, lanes].astype(f32)
-        s = jax.nn.sigmoid(gate)
-        act = gate * s
-        hid_ref[:, lanes] = (act * up).astype(bf16)
-        guv = (ghid * act).astype(bf16)
-        ggu = (ghid * up * (s * (1.0 + gate * (1.0 - s)))).astype(bf16)
-        ggu_ref[:, lanes] = ggu
-        guv_ref[:, lanes] = guv
-        part = part + dot_nt(ggu, pack.wide_part(g_w, i)) + dot_nt(guv, pack.wide_part(u_w, i))
-    accumulate(total, part, gin_ref)
-
-
-def ffn_input_grad(pack, gy, gate, up, weights):
-    count, ff = gy.shape[0], pack.ff
-    flat = pl.BlockSpec((count, D), lambda j: (0, 0))
-    wide = pl.BlockSpec((count, 512), lambda j: (0, j))
-    outs = [shape((count, D), bf16)] + [shape((count, ff), bf16)] * 3
-    scratch = [pltpu.VMEM((count, D), f32)]
-    return ffn_call(
-        ffn_input_kernel, "ffn_input_grad", pack, count, 1, 2, True, outs,
-        [flat, wide, wide, wide], scratch, [gy, gate, up, weights],
-    )
-
-
-def ffn_weight_kernel(pack, r_ref, gy_ref, hid_ref, ggu_ref, guv_ref, out_ref, rt):
-    j = pl.program_id(0)
-
-    @pl.when(j == 0)
-    def _():
-        rt[...] = r_ref[...].T
-        if pack.padded != pack.part:
-            out_ref[...] = jnp.zeros_like(out_ref)
-
-    for n, ref in enumerate((ggu_ref, guv_ref)):
-        for i in range(2):
-            grad = dot(rt[...], ref[:, i * 256 : (i + 1) * 256]).astype(bf16)
-            at = (n * pack.chunks + i) * pack.padded + j * (2 * pack.padded)
-            at = pl.multiple_of(at, 16)
-            out_ref[:, pl.ds(at, pack.part), :] = grad.reshape(pack.shards, pack.part, 256)
-    grad = dot_tn(hid_ref[...], gy_ref[...]).astype(bf16)
-    for c in range(D // 256):
-        at = pack.down + c * pack.own
-        out_ref[pl.ds(j * pack.group, pack.group), at : at + pack.own, :] = grad[
-            :, c * 256 : (c + 1) * 256
-        ].reshape(pack.group, pack.own, 256)
-
-
-def ffn_weight_grad(pack, rows, gy, hid, ggu, guv):
-    count = rows.shape[0]
-    outs = shape((pack.shards, pack.rows, 256), bf16)
-    spec = pl.BlockSpec(outs.shape, lambda j: (0, 0, 0))
-    return ffn_call(
-        ffn_weight_kernel, "ffn_weight_grad", pack, count, 2, 3, False, outs, spec,
-        [pltpu.VMEM((D, count), bf16)], [rows, gy, hid, ggu, guv],
-    )
 
 
 def expert_outputs_kernel(pack, first_ref, second_ref, gate_ref, up_ref, down_ref):
@@ -755,13 +884,6 @@
     ]
     body = functools.partial(dense_outputs_kernel, part, labels)
     return whole_call(body, "dense_outputs", outs, [pltpu.VMEM((128, 128), f32)], grads, 10**6)
-
-
-def to_owner(rows, owners):
-    slots = rows.shape[0] // owners
-    return lax.all_to_all(
-        rows.reshape(owners, slots, D), "expert", split_axis=0, concat_axis=0, tiled=True
-    ).reshape(owners * slots, D)
 
 
 def on_device(
@@ -857,18 +979,21 @@
         outs = list(forward_call(l == 0, last, experts, slots, args))
         if l > 0:
             x_now = outs.pop(0)
-        n1, qkv, att, lse, middle, n2, info, gcol, gpack, send = outs[:10]
-        received = to_owner(send, experts)
+        n1, qkv, att, lse, middle, n2, info, gcol, gpack, send, small = outs[:11]
         keep = dict(
             x=x_now, n1=n1, qkv=qkv, att=att, lse=lse, middle=middle, n2=n2, info=info,
-            gcol=gcol, gpack=gpack, received=received, z=z_rows,
+            gcol=gcol, gpack=gpack, z=z_rows, small=small,
         )
         if last:
-            keep["gxs"] = outs[10]
-            keep["gy"] = to_owner(outs[11], experts)
-        produced, keep["gate"], keep["up"] = ffn_forward(pack, received, experts_w[l])
-        keep["y"] = to_owner(produced, experts)
-        front = [middle, n2, keep["y"], gcol, slot_col[l], dense[l][:, W_SMALL:]]
+            keep["gxs"] = outs[11]
+            keep["y"], keep["gin"], keep["dw"] = exchange_call(
+                "both", pack, experts, slots, [send, outs[12], experts_w[l]]
+            )
+        else:
+            keep["received"], keep["y"], keep["gate"], keep["up"] = exchange_call(
+                "forward", pack, experts, slots, [send, experts_w[l]]
+            )
+        front = [middle, n2, keep["y"], gcol, slot_col[l], small]
         z_rows = info[0:16]
         saved.append(keep)
 
@@ -884,16 +1009,16 @@
         if not last:
             keep["info"], mine = lax.optimization_barrier((keep["info"], mine))
             dense_grads[l + 1] = lax.psum(mine, "expert")
-        gin, hid, ggu, guv = ffn_input_grad(
-            pack, keep["gy"], keep["gate"], keep["up"], experts_w[l]
-        )
-        gin_back = to_owner(gin, experts)
-        d_experts = ffn_weight_grad(pack, keep["received"], keep["gy"], hid, ggu, guv)
-        d_experts, keep["n2"] = lax.optimization_barrier((d_experts, keep["n2"]))
+        if not last:
+            keep["gin"], keep["dw"] = exchange_call(
+                "backward", pack, experts, slots,
+                [keep["gy"], experts_w[l], keep["gate"], keep["up"], keep["received"]],
+            )
+        d_experts, keep["n2"] = lax.optimization_barrier((keep["dw"], keep["n2"]))
         expert_grads[l] = lax.psum_scatter(d_experts, "shard", scatter_dimension=0, tiled=False)
         args = [
             gx, keep["n2"], keep["y"], keep["gxs"], slot_row[l], keep["info"], chosen_rows[l],
-            keep["gcol"], dense[l][:, W_SMALL:], keep["z"], mixes[l],
+            keep["gcol"], keep["small"], keep["z"], mixes[l],
         ]
         args += [keep["middle"], slot_col[l]] if last else [gz]
         outs = gating_call(last, experts, slots, args)
@@ -901,7 +1026,7 @@
         if last:
             hidden_out = outs[4]
         args = [
-            gx, gn2, gin_back, slot_col[l], keep["middle"], keep["att"], dense[l], keep["qkv"],
+            gx, gn2, keep["gin"], slot_col[l], keep["middle"], keep["att"], dense[l], keep["qkv"],
             keep["n1"], keep["x"], bias_t, keep["lse"], gsm,
         ]
         if l > 0:
@@ -912,7 +1037,7 @@
         if l > 0:
             saved[l - 1]["gxs"] = outs[2]
             gy, d_dense = lax.optimization_barrier((outs[3], d_dense))
-            saved[l - 1]["gy"] = to_owner(gy, experts)
+            saved[l - 1]["gy"] = gy
         if not last:
             d_dense, dense_grads[l + 1] = lax.optimization_barrier((d_dense, dense_grads[l + 1]))
         if l == 0:

time: 782 us -> 756 us (0.967)
  Pallas kernels: 308 us -> 491 us
  blocking collectives: 194 us -> 40.2 us
  waiting for transfers between devices: 200 us -> 173 us
  starting transfers between devices: 15.1 us -> 0.4 us
  local copies, waits for them, and re-layouts: 34.1 us -> 23.8 us
    pallas_call x6 -> x3, Pallas kernels: 104 us -> 288 us  [exchange_call(): pl.pallas_call(functools.partial(exchange_kernel, mode, pack, ex), out_sh...]
    all_to_all x4 -> x0, blocking collectives: 154 us -> none  [to_owner(): lax.all_to_all(rows.reshape(owners, slots, D), 'expert', split_axis=0, co...]
    all_to_all x4 -> x0, waiting for transfers between devices: 79.5 us -> none  [to_owner(): lax.all_to_all(rows.reshape(owners, slots, D), 'expert', split_axis=0, co...]
    all_gather x2, waiting for transfers between devices: 0.02 us -> 30.2 us  [on_device(): experts_w.append(lax.all_gather(mine, 'shard', axis=0, tiled=False))]
    reduce_scatter x2, waiting for transfers between devices: 0.01 us -> 18.1 us  [on_device(): lax.psum_scatter(d_experts, 'shard', scatter_dimension=0, tiled=False)]
    psum x1, waiting for transfers between devices: 26.5 us -> 42.1 us  [on_device(): dense_grads[l + 1] = lax.psum(mine, 'expert')]
    all_to_all x4 -> x0, starting transfers between devices: 14.2 us -> none  [to_owner(): lax.all_to_all(rows.reshape(owners, slots, D), 'expert', split_axis=0, co...]
    all_gather x2, waiting for transfers between devices: 34.7 us -> 23.1 us  [on_device(): dense.append(lax.all_gather(packed, 'shard', axis=0, tiled=True))]
  transfers between devices with their start and end apart: 14 -> 10, of which waited for: 8 -> 6; matrix products, arithmetic and copies ran while one was open for 3% -> 3% of each run, Pallas kernels for 35% -> 47%
where the time goes in v3:
time: 756 us; the launch traced here: 752 us
  Pallas kernels  491 us (65%)
  waiting for transfers between devices  173 us (23%)
  blocking collectives  40.2 us (5%)
  local copies, waits for them, and re-layouts  23.8 us (3%)
  between operations  14.8 us (2%)
    pallas_call x3, Pallas kernels, exchange_call(): pl.pallas_call(functools.partial(exchange_kernel, mode, pack, ex), out_sh...  288 us
    pallas_call x8, Pallas kernels, whole_call(): pl.pallas_call(body, out_shape=outs, in_specs=[pl.BlockSpec(memory_space=...  204 us
    reduce_scatter x2, waiting for transfers between devices, on_device(): mine = lax.psum_scatter(d_dense, 'shard', scatter_dimension=0, tiled=True)  58.4 us
    psum x1, waiting for transfers between devices, on_device(): dense_grads[l + 1] = lax.psum(mine, 'expert')  42.1 us
    psum x1, blocking collectives, on_device(): mixing_total = lax.psum(jnp.stack(mix_grads), ('expert', 'shard'))  40.2 us
    all_gather x2, waiting for transfers between devices, on_device(): experts_w.append(lax.all_gather(mine, 'shard', axis=0, tiled=False))  30.2 us
    all_gather x2, waiting for transfers between devices, on_device(): dense.append(lax.all_gather(packed, 'shard', axis=0, tiled=True))  23.1 us
    reduce_scatter x2, waiting for transfers between devices, on_device(): lax.psum_scatter(d_experts, 'shard', scatter_dimension=0, tiled=False)  18.1 us
  transfers between devices with their start and end apart: 10, of which 6 were waited for; matrix products, arithmetic and copies ran while one was open for 3% of the time, Pallas kernels for 47%

profile of v3, /device:TPU:0, one launch (start us, length us, event | category | flops | bytes accessed | tf_op | source)
XLA Modules:
  0.0 751.6 jit_solution(384863166314497315)
XLA Ops:
  7.2 0.8 slice_bitcast_fusion.11
  8.0 0.7 slice_bitcast_fusion.7
  8.7 0.7 slice_bitcast_fusion.9
  9.6 1.0 bitcast_dynamic-update-slice_fusion.3
  10.6 1.0 bitcast_dynamic-update-slice_fusion.2
  11.7 1.1 bitcast_dynamic-update-slice_fusion.1
  12.7 1.0 bitcast_dynamic-update-slice_fusion
  13.8 0.8 copy-done.1
  15.2 0.7 copy-done.4
  16.3 1.1 pad_maximum_fusion
  17.7 0.8 copy-done
  19.3 1.1 pad_maximum_fusion.1
  21.1 0.7 copy.183.refs_9_
  21.8 0.6 fusion.46
  22.4 0.7 copy.174.refs_4_
  23.0 0.6 pad.40.refs_3_.refs_9_
  23.7 0.6 pad.47.refs_10_.refs_6_
  24.3 0.6 pad.42.refs_5_.refs_6_
  25.3 0.6 broadcast_select_fusion
  25.9 0.8 copy.175.refs_6_.refs_13_.refs_4_
  27.0 0.6 pad.48.clone.refs_11_.refs_4_
  27.8 0.6 and_select_fusion
  28.4 1.0 fusion.45
  29.4 4.7 fusion.7
  34.1 23.1 %all-gather.7.cloned.1.call-done.refs_1_.refs_6_ = bf16[768,3200]{1,0:T(8,128)(2,1)} async-done(((bf16[96,3200]{1,0:T(8,128)(2,1)}), bf16[768,3200]{1,0:T(8,128)(2,1)}) %all-gather.7.cloned.1.call-update) | async-done | bytes 4915216 | tf_op jit(solution)/shard_map/all_gather | solution.py:936
  57.2 29.7 %block_forward.2 = (bf16[832,768]{1,0:T(8,128)(2,1)}, bf16[832,2304]{1,0:T(8,128)(2,1)}, bf16[832,768]{1,0:T(8,128)(2,1)}, f32[16,832]{1,0:T(8,128)}, f32[832,76...) custom-call(bf16[832,768]{1,0:T(8,128)(2,1)} %refs_9_.1, ...), custom_call_target="tpu_custom_call" | custom-call | flops 20000000000 | bytes 21816320 | tf_op jit(solution)/shard_map/block_forward/pallas_call | solution.py:259
  86.9 1.4 slice.136.refs_8_.refs_9_
  88.3 30.2 %all-gather.11.cloned.1.call-done = bf16[18432,256]{1,0:T(8,128)(2,1)} async-done(((bf16[2304,256]{1,0:T(8,128)(2,1)}), bf16[18432,256]{1,0:T(8,128)(2,1)}) %all-gather.11.cloned.1.call-update) | async-done | bytes 9437200 | tf_op jit(solution)/shard_map/all_gather | solution.py:938
  118.5 77.9 %experts_forward.1 = (bf16[960,768]{1,0:T(8,128)(2,1)}, bf16[960,768]{1,0:T(8,128)(2,1)}, bf16[960,2048]{1,0:T(8,128)(2,1)}, bf16[960,2048]{1,0:T(8,128)(2,1)}) custom-call(bf16[960,768]{1,0:T(8,128)(2,1)} %get-tuple-element.88.refs_0_, bf16[8,2304,256]{2,1,0:T(8,128)(2,1)} %bitcast.145), custom_call_target="tpu_custom_call" | custom-call | flops 49059696640 | bytes 9437184 | tf_op jit(solution)/shard_map/experts_forward/pallas_call | solution.py:824
  196.4 36.8 %block_forward.3 = (f32[832,768]{1,0:T(8,128)}, bf16[832,768]{1,0:T(8,128)(2,1)}, bf16[832,2304]{1,0:T(8,128)(2,1)}, bf16[832,768]{1,0:T(8,128)(2,1)}, f32[16,83...) custom-call(f32[832,768]{1,0:T(8,128)} %get-tuple-element.86.refs_0_, ...), custom_call_target="tpu_custom_call" | custom-call | flops 20000000000 | bytes 33265664 | tf_op jit(solution)/shard_map/block_forward/pallas_call | solution.py:259
  233.2 135.3 %experts_both.1 = (bf16[960,768]{1,0:T(8,128)(2,1)}, bf16[960,768]{1,0:T(8,128)(2,1)}, bf16[8,2304,256]{2,1,0:T(8,128)(2,1)}) custom-call(bf16[960,768]{1,0:T(8,128)(2,1)} %get-tuple-element.93.refs_0_, bf16[960,768]{1,0:T(8,128)(2,1)} %get-tuple-element.94.refs_1_, bf16[8,2304,256]{2,1,0:T(8,128)(2,1)} %bitcast.147), custom_call_target="tpu_custom_call" | custom-call | flops 67179089920 | bytes 9437184 | tf_op jit(solution)/shard_map/experts_both/pallas_call | solution.py:824
  368.6 13.0 %gating_backward.2 = (f32[832,768]{1,0:T(8,128)}, f32[32,768]{1,0:T(8,128)}, f32[16,16]{1,0:T(8,128)}, f32[16,832]{1,0:T(8,128)}, bf16[832,768]{1,0:T(8,128)(2,1)}) custom-call(bf16[832,768]{1,0:T(8,128)(2,1)} %refs_0_.5, bf16[832,768]{1,0:T(8,128)(2,1)} %get-tuple-element.97.refs_1_, bf16[960,768]{1,0:T(8,128)(2,1)} %get-tuple-element.98.refs_2_, ...), custom_call_target="tpu_custom_call" | custom-call | flops 5000000000 | bytes 12950528 | tf_op jit(solution)/shard_map/gating_backward/pallas_call | solution.py:259
  381.7 54.2 %block_backward.2 = (f32[832,768]{1,0:T(8,128)}, bf16[768,3200]{1,0:T(8,128)(2,1)}, bf16[960,768]{1,0:T(8,128)(2,1)}, bf16[960,768]{1,0:T(8,128)(2,1)}) custom-call(bf16[832,768]{1,0:T(8,128)(2,1)} %refs_0_.5, f32[832,768]{1,0:T(8,128)} %get-tuple-element.105.refs_1_, bf16[960,768]{1,0:T(8,128)(2,1)} %get-tuple-element.106.refs_2_, ...), custom_call_target="tpu_custom_call" | custom-call | flops 40000000000 | bytes 35318784 | tf_op jit(solution)/shard_map/block_backward/pallas_call | solution.py:259
  435.9 6.4 reduce-scatter.5.cloned.1.call-done
  442.3 74.5 %experts_backward.1 = (bf16[960,768]{1,0:T(8,128)(2,1)}, bf16[8,2304,256]{2,1,0:T(8,128)(2,1)}) custom-call(bf16[960,768]{1,0:T(8,128)(2,1)} %get-tuple-element.119.refs_0_, bf16[8,2304,256]{2,1,0:T(8,128)(2,1)} %bitcast.146, bf16[960,2048]{1,0:T(8,128)(2,1)} %get-tuple-element.120.refs_2_, bf16[960,2048]{1,0:T(8,128)(2,1)} %get-tuple-element.121.refs_3_, ...), custom_call_target="tpu_custom_call" | custom-call | flops 58119393280 | bytes 9437184 | tf_op jit(solution)/shard_map/experts_backward/pallas_call | solution.py:824
  517.0 0.7 all-reduce.13.cloned.1.call-update
  517.7 9.6 %gating_backward.3 = (f32[832,768]{1,0:T(8,128)}, f32[32,768]{1,0:T(8,128)}, f32[16,16]{1,0:T(8,128)}, f32[16,832]{1,0:T(8,128)}) custom-call(f32[832,768]{1,0:T(8,128)} %get-tuple-element.114.refs_0_, bf16[832,768]{1,0:T(8,128)(2,1)} %get-tuple-element.124.refs_1_, bf16[960,768]{1,0:T(8,128)(2,1)} %get-tuple-element.89.refs_2_, ...), custom_call_target="tpu_custom_call" | custom-call | flops 5000000000 | bytes 10434560 | tf_op jit(solution)/shard_map/gating_backward/pallas_call | solution.py:259
  527.3 53.6 %block_backward.3 = (f32[832,768]{1,0:T(8,128)}, bf16[768,3200]{1,0:T(8,128)(2,1)}) custom-call(f32[832,768]{1,0:T(8,128)} %get-tuple-element.114.refs_0_, f32[832,768]{1,0:T(8,128)} %get-tuple-element.129.refs_1_, bf16[960,768]{1,0:T(8,128)(2,1)} %get-tuple-element.130.refs_2_, f32[832,4]{1,0:T(8,128)} %get-tuple-element.237.refs_4_.refs_3_, ...), custom_call_target="tpu_custom_call" | custom-call | flops 40000000000 | bytes 32130048 | tf_op jit(solution)/shard_map/block_backward/pallas_call | solution.py:259
  580.9 11.7 %reduce-scatter.9.cloned.1.call-done = bf16[1,2304,256]{2,1,0:T(8,128)(2,1)} async-done(((bf16[8,2304,256]{2,1,0:T(8,128)(2,1)}), bf16[1,2304,256]{2,1,0:T(8,128)(2,1)}) %reduce-scatter.9.cloned.1.call-update) | async-done | bytes 1179664 | tf_op jit(solution)/shard_map/reduce_scatter | solution.py:1018
  592.7 42.1 %all-reduce.13.cloned.1.call-done.second_ref = bf16[96,3200]{1,0:T(8,128)(2,1)} async-done(((bf16[96,3200]{1,0:T(8,128)(2,1)}), bf16[96,3200]{1,0:T(8,128)(2,1)}) %all-reduce.13.cloned.1.call-update) | async-done | bytes 614416 | tf_op jit(solution)/shard_map/psum | solution.py:1011
  634.8 58.4 %reduce-scatter.11.cloned.1.call-done = bf16[96,3200]{1,0:T(8,128)(2,1)} async-done(((bf16[768,3200]{1,0:T(8,128)(2,1)}), bf16[96,3200]{1,0:T(8,128)(2,1)}) %reduce-scatter.11.cloned.1.call-update) | async-done | bytes 614416 | tf_op jit(solution)/shard_map/reduce_scatter | solution.py:1045
  693.3 0.6 slice_bitcast_fusion.2
  693.9 40.2 %psum.23 = f32[2,16,16]{2,1,0:T(8,128)S(1)} all-reduce(f32[2,16,16]{2,1,0:T(8,128)S(1)} %pad_maximum_fusion.3), channel_id=1, replica_groups=mesh['expert'=4,'shard'=8] {'expert','shard'}, use_global_device_ids=true, to_apply=%region_8.9 | all-reduce | flops 512 | bytes 4096 | tf_op jit(solution)/shard_map/psum | solution.py:1048
  734.1 0.6 slice.153
  734.7 3.9 expert_outputs.1
  738.6 2.8 dense_outputs.1
  741.4 1.6 copy.193
  743.0 1.6 copy.192
  (88 shorter events, 3.9 us)
Async XLA Ops:
  7.2 7.5 copy-start.2
  7.2 50.0 %all-gather.7.cloned.1.call-start = ((), (), s32[]{:S(2)}) async-start(), calls=%async_computation.4 | async-start | bytes 5529600 | tf_op jit(solution)/shard_map/all_gather | solution.py:936
  11.6 3.3 copy-start.3
  13.8 0.8 copy-start.1
  14.6 103.9 %all-gather.11.cloned.1.call-start = ((), (), s32[]{:S(2)}) async-start(), calls=%async_computation.12 | async-start | bytes 10616832 | tf_op jit(solution)/shard_map/all_gather | solution.py:938
  14.7 1.1 copy-start.4
  17.4 179.0 %all-gather.9.cloned.1.call-start = ((), (), s32[]{:S(2)}) async-start(), calls=%async_computation.5 | async-start | bytes 5529600 | tf_op jit(solution)/shard_map/all_gather | solution.py:936
  17.7 0.8 copy-start
  18.5 214.7 %all-gather.13.cloned.1.call-start = ((), (), s32[]{:S(2)}) async-start(), calls=%async_computation.13 | async-start | bytes 10616832 | tf_op jit(solution)/shard_map/all_gather | solution.py:938
  19.1 1.4 copy-start.8
  19.1 3.9 copy-start.5
  19.1 4.6 copy-start.7
  19.3 5.9 copy-start.11
  19.3 5.9 copy-start.13
  20.4 421.8 %reduce-scatter.5.cloned.1.call-start = ((), (), s32[]{:S(2)}) async-start(), calls=%async_computation.6 | async-start | bytes 10616832 | tf_op jit(solution)/shard_map/reduce_scatter | solution.py:1018
  25.0 2.7 copy-start.12
  368.6 148.4 %reduce-scatter.7.cloned.1.call-start = ((), (), s32[]{:S(2)}) async-start(), calls=%async_computation.7 | async-start | bytes 5529600 | tf_op jit(solution)/shard_map/reduce_scatter | solution.py:1045
  442.3 150.4 %reduce-scatter.9.cloned.1.call-start = ((), (), s32[]{:S(2)}) async-start(), calls=%async_computation.8 | async-start | bytes 10616832 | tf_op jit(solution)/shard_map/reduce_scatter | solution.py:1018
  516.9 117.8 %all-reduce.13.cloned.1.call-start = ((), (), s32[]{:S(2)}) async-start(), calls=%async_computation.9 | async-start | bytes 1228800 | tf_op jit(solution)/shard_map/psum | solution.py:1011
  517.7 175.6 %reduce-scatter.11.cloned.1.call-start = ((), (), s32[]{:S(2)}) async-start(), calls=%async_computation.10 | async-start | bytes 5529600 | tf_op jit(solution)/shard_map/reduce_scatter | solution.py:1045
  634.7 58.5 %copy-start.6 = (f32[16,832]{1,0:T(8,128)S(1)}, f32[16,832]{1,0:T(8,128)}, u32[]{:S(2)}) copy-start(f32[16,832]{1,0:T(8,128)} %get-tuple-element.137) | copy-start | bytes 159748
  634.7 59.2 %copy-start.9 = (f32[16,16]{1,0:T(8,128)S(1)}, f32[16,16]{1,0:T(8,128)}, u32[]{:S(2)}) copy-start(f32[16,16]{1,0:T(8,128)} %get-tuple-element.151) | copy-start | bytes 3076
  634.7 59.2 %copy-start.10 = (f32[16,16]{1,0:T(8,128)S(1)}, f32[16,16]{1,0:T(8,128)}, u32[]{:S(2)}) copy-start(f32[16,16]{1,0:T(8,128)} %get-tuple-element.150) | copy-start | bytes 3076
  634.8 103.8 %all-reduce.15.cloned.1.call-start = ((), (), s32[]{:S(2)}) async-start(), calls=%async_computation.11 | async-start | bytes 1228800 | tf_op jit(solution)/shard_map/psum | solution.py:1047
Sparse Core Ops, SparseCore 0:
  14.7 42.4 all-gather.6
  59.7 58.8 all-gather.10
  121.0 39.7 all-gather.8
  162.5 58.8 all-gather.12
  368.7 73.5 reduce-scatter.4
  445.6 54.8 reduce-scatter.6
  517.0 75.5 reduce-scatter.8
  595.1 39.5 all-reduce.12
  638.7 54.5 reduce-scatter.10
  695.5 39.8 all-reduce.14

commit v4 on v3

--- a/solution.py
+++ b/solution.py
@@ -387,13 +387,12 @@
     lax.fori_loop(0, BLOCKS, add, 0)
 
 
-def gating_call(last, experts, slots, args):
+def gating_outputs(last):
     tokens = TREE
     outs = [shape((tokens, D)), shape((32, D)), shape((16, 16)), shape((16, tokens))]
     if last:
         outs += [shape((tokens, D), bf16)]
-    body = functools.partial(gating_kernel, last, experts, slots)
-    return whole_call(body, "gating_backward", outs, [], args, 5 * 10**9)
+    return outs
 
 
 def backward_kernel(first, experts, slots, *refs):
@@ -607,98 +606,120 @@
         return pl.ds(pl.multiple_of(device * self.slots + offset, 16), size)
 
 
+MESH = pl.DeviceIdType.MESH
+
+
+def greet(experts):
+    me = lax.axis_index("expert")
+    barrier = pltpu.get_barrier_semaphore()
+    for d in range(1, experts):
+        pl.semaphore_signal(
+            barrier, inc=1, device_id={"expert": lax.rem(me + d, experts)}, device_id_type=MESH
+        )
+    pl.semaphore_wait(barrier, experts - 1)
+
+
+def out_copies(ex, wave, src, dst, sends, recvs):
+    me = lax.axis_index("expert")
+    copies = []
+    for d in range(1, ex.experts):
+        to = lax.rem(me + d, ex.experts)
+        copies.append(
+            pltpu.make_async_remote_copy(
+                src_ref=src.at[ex.slot(to, wave)],
+                dst_ref=dst.at[ex.held(wave, d)],
+                send_sem=sends.at[wave, d - 1],
+                recv_sem=recvs.at[wave, d - 1],
+                device_id={"expert": to},
+                device_id_type=MESH,
+            )
+        )
+    return copies
+
+
+def back_copies(ex, wave, n, src, dst, sends, recvs):
+    me = lax.axis_index("expert")
+    copies = []
+    for d in range(1, ex.experts):
+        copies.append(
+            pltpu.make_async_remote_copy(
+                src_ref=src.at[ex.held(wave, d)],
+                dst_ref=dst.at[ex.slot(me, wave)],
+                send_sem=sends.at[n, wave, d - 1],
+                recv_sem=recvs.at[n, wave, d - 1],
+                device_id={"expert": lax.rem(me + ex.experts - d, ex.experts)},
+                device_id_type=MESH,
+            )
+        )
+    return copies
+
+
+def own_slots(ex):
+    me = lax.axis_index("expert")
+    return pl.ds(pl.multiple_of(me * ex.slots, 16), ex.slots)
+
+
+def dispatch_kernel(ex, send, recv, sends, recvs):
+    greet(ex.experts)
+    copies = out_copies(ex, 0, send, recv, sends, recvs)
+    copies += out_copies(ex, 1, send, recv, sends, recvs)
+    for copy in copies:
+        copy.start()
+    recv[0 : ex.slots, :] = send[own_slots(ex), :]
+    for copy in copies:
+        copy.wait()
+
+
+def dispatch_call(ex, rows):
+    vmem = pl.BlockSpec(memory_space=pltpu.VMEM)
+    return pl.pallas_call(
+        functools.partial(dispatch_kernel, ex),
+        out_shape=shape((ex.total, D), bf16),
+        in_specs=[vmem],
+        out_specs=vmem,
+        scratch_shapes=[pltpu.SemaphoreType.DMA((2, ex.experts - 1))] * 2,
+        compiler_params=pltpu.CompilerParams(
+            vmem_limit_bytes=8 << 20, collective_id=3, has_side_effects=True
+        ),
+        cost_estimate=pl.CostEstimate(flops=35 * 10**9, bytes_accessed=10**6, transcendentals=0),
+        name="dispatch",
+    )(rows)
+
+
 def exchange_kernel(mode, pack, ex, *refs):
     refs = list(refs)
     forward, backward = mode in ("forward", "both"), mode in ("backward", "both")
-    if forward:
-        send_n = refs.pop(0)
+    recv_n = refs.pop(0)
+    w_hbm = refs.pop(0)
+    gating = []
     if backward:
         send_g = refs.pop(0)
-    w_hbm = refs.pop(0)
-    if mode == "backward":
-        gate_hbm, up_hbm, rows_hbm = refs.pop(0), refs.pop(0), refs.pop(0)
+        if mode == "backward":
+            gate_hbm, up_hbm = refs.pop(0), refs.pop(0)
+        gating = [refs.pop(0) for _ in range(12)]
+    if forward:
+        back_y = refs.pop(0)
     if mode == "forward":
-        recv_n, back_y, gates, ups = [refs.pop(0) for _ in range(4)]
-    elif mode == "both":
-        back_y, back_g, dw = [refs.pop(0) for _ in range(3)]
-        recv_n = refs.pop(0)
+        gates, ups = refs.pop(0), refs.pop(0)
     else:
         back_g, dw = refs.pop(0), refs.pop(0)
-        recv_n = refs.pop(0)
+        gating_outs = [refs.pop(0) for _ in range(5 if mode == "both" else 4)]
     if forward:
-        out_y = refs.pop(0)
+        out_y, acc_y = refs.pop(0), refs.pop(0)
     if backward:
         recv_g, out_g, hids, gates, ups, rows_t, acc_g = [refs.pop(0) for _ in range(7)]
-    if forward:
-        acc_y = refs.pop(0)
-    w, sends, recvs, backs, gots, local = refs
-
-    experts, slots = ex.experts, ex.slots
-    me = lax.axis_index("expert")
-    peers = range(1, experts)
-
-    def ahead(d):
-        return lax.rem(me + d, experts)
-
-    def behind(d):
-        return lax.rem(me + experts - d, experts)
+        w = dw
+    else:
+        w = refs.pop(0)
+    sends, recvs, backs, gots, local = refs
 
     loads = [pltpu.make_async_copy(w_hbm, w, local.at[0])]
     if mode == "backward":
         loads.append(pltpu.make_async_copy(gate_hbm, gates, local.at[1]))
         loads.append(pltpu.make_async_copy(up_hbm, ups, local.at[2]))
-        loads.append(pltpu.make_async_copy(rows_hbm, recv_n, local.at[3]))
     for copy in loads:
         copy.start()
-    barrier = pltpu.get_barrier_semaphore()
-    for d in peers:
-        pl.semaphore_signal(
-            barrier, inc=1, device_id={"expert": ahead(d)}, device_id_type=pl.DeviceIdType.MESH
-        )
-    pl.semaphore_wait(barrier, experts - 1)
-
-    kinds = []
-    if forward:
-        kinds.append((send_n, recv_n))
-    if backward:
-        kinds.append((send_g, recv_g))
-    returns = []
-    if forward:
-        returns.append((out_y, back_y))
-    if backward:
-        returns.append((out_g, back_g))
-
-    def out_copies(wave):
-        copies = []
-        for d in peers:
-            for n, (src, dst) in enumerate(kinds):
-                copies.append(
-                    pltpu.make_async_remote_copy(
-                        src_ref=src.at[ex.slot(ahead(d), wave)],
-                        dst_ref=dst.at[ex.held(wave, d)],
-                        send_sem=sends.at[n, wave, d - 1],
-                        recv_sem=recvs.at[n, wave, d - 1],
-                        device_id={"expert": ahead(d)},
-                        device_id_type=pl.DeviceIdType.MESH,
-                    )
-                )
-        return copies
-
-    def back_copies(wave):
-        copies = []
-        for n, (src, dst) in enumerate(returns):
-            for d in peers:
-                copies.append(
-                    pltpu.make_async_remote_copy(
-                        src_ref=src.at[ex.held(wave, d)],
-                        dst_ref=dst.at[ex.slot(me, wave)],
-                        send_sem=backs.at[n, wave, d - 1],
-                        recv_sem=gots.at[n, wave, d - 1],
-                        device_id={"expert": behind(d)},
-                        device_id_type=pl.DeviceIdType.MESH,
-                    )
-                )
-        return copies
+    greet(ex.experts)
 
     def work(start, size):
         rows = slice(start, start + size)
@@ -741,34 +762,44 @@
         if backward:
             out_g[rows, :] = acc_g[part, :].astype(bf16)
 
-    waves = [out_copies(0), out_copies(1)]
-    for copy in waves[0]:
-        copy.start()
-    mine = pl.ds(pl.multiple_of(me * slots, 16), slots)
+    def send_back(wave):
+        ys = back_copies(ex, wave, 0, out_y, back_y, backs, gots) if forward else []
+        gs = back_copies(ex, wave, 1, out_g, back_g, backs, gots) if backward else []
+        for copy in ys + gs:
+            copy.start()
+        return ys, gs
+
+    if backward:
+        waves = [out_copies(ex, n, send_g, recv_g, sends, recvs) for n in range(2)]
+        for copy in waves[0]:
+            copy.start()
+        recv_g[0 : ex.slots, :] = send_g[own_slots(ex), :]
+        if mode == "backward":
+            gating_kernel(False, ex.experts, ex.slots, *gating, *gating_outs)
     for copy in loads:
         copy.wait()
-    for src, dst in kinds:
-        dst[0:slots, :] = src[mine, :]
-    work(*ex.ranges[0])
-    for src, dst in returns:
-        dst[mine, :] = src[0:slots, :]
-    for copy in waves[0]:
-        copy.wait_send()
-    for copy in waves[1]:
-        copy.start()
-    for copy in waves[0]:
-        copy.wait_recv()
+    if backward:
+        work(*ex.ranges[0])
+        for copy in waves[0]:
+            copy.wait_send()
+        for copy in waves[1]:
+            copy.start()
+        for copy in waves[0]:
+            copy.wait_recv()
     work(*ex.ranges[1])
-    first = back_copies(0)
-    for copy in first:
-        copy.start()
-    for copy in waves[1]:
-        copy.wait()
+    ys, gs = send_back(0)
+    if backward:
+        for copy in waves[1]:
+            copy.wait()
     work(*ex.ranges[2])
-    second = back_copies(1)
-    for copy in second:
-        copy.start()
+    more = send_back(1)
+    ys, gs = ys + more[0], gs + more[1]
+    if mode == "forward":
+        work(*ex.ranges[0])
+    if forward:
+        back_y[own_slots(ex), :] = out_y[0 : ex.slots, :]
     if backward:
+        back_g[own_slots(ex), :] = out_g[0 : ex.slots, :]
         rows_t[...] = recv_n[...].T
         if pack.padded != pack.part:
             dw[...] = jnp.zeros_like(dw)
@@ -781,15 +812,18 @@
             return carry
 
         lax.fori_loop(0, pack.chunks, weights, 0)
-    for copy in first + second:
+    for copy in ys:
         copy.wait()
+    if mode == "both":
+        gating_kernel(True, ex.experts, ex.slots, *gating[:2], back_y, *gating[2:], *gating_outs)
+    for copy in gs:
+        copy.wait()
 
 
 EXCHANGE_IDS = {"forward": 0, "both": 1, "backward": 2}
 
 
-def exchange_call(mode, pack, experts, slots, args):
-    ex = Exchange(experts, slots)
+def exchange_call(mode, pack, ex, args):
     rows, ff = ex.total, pack.ff
     forward, backward = mode in ("forward", "both"), mode in ("backward", "both")
     flat, wide = shape((rows, D), bf16), shape((rows, ff), bf16)
@@ -797,29 +831,27 @@
     most = max(size for _, size in ex.ranges)
     vmem = pl.BlockSpec(memory_space=pltpu.VMEM)
     far = pl.BlockSpec(memory_space=pl.ANY)
-    in_specs = [vmem] * (2 if mode == "both" else 1) + [far]
+    in_specs = [vmem] * len(args)
+    in_specs[1] = far
     scratch = []
     if mode == "forward":
-        outs = [flat, flat, wide, wide]
+        outs = [flat, wide, wide]
     elif mode == "both":
-        outs = [flat, flat, shape(packed, bf16)]
-        scratch.append(pltpu.VMEM((rows, D), bf16))
+        outs = [flat, flat, shape(packed, bf16)] + gating_outputs(True)
     else:
-        in_specs += [far] * 3
-        outs = [flat, shape(packed, bf16)]
-        scratch.append(pltpu.VMEM((rows, D), bf16))
+        in_specs[3] = in_specs[4] = far
+        outs = [flat, shape(packed, bf16)] + gating_outputs(False)
     if forward:
-        scratch.append(pltpu.VMEM((rows, D), bf16))
+        scratch += [pltpu.VMEM((rows, D), bf16), pltpu.VMEM((most, D), f32)]
     if backward:
         scratch += [pltpu.VMEM((rows, D), bf16)] * 2
         scratch += [pltpu.VMEM((rows, ff), bf16)] * 3
         scratch += [pltpu.VMEM((D, rows), bf16), pltpu.VMEM((most, D), f32)]
-    if forward:
-        scratch.append(pltpu.VMEM((most, D), f32))
-    kinds = 2 if mode == "both" else 1
-    scratch.append(pltpu.VMEM(packed, bf16))
-    scratch += [pltpu.SemaphoreType.DMA((kinds, 2, experts - 1))] * 4
-    scratch.append(pltpu.SemaphoreType.DMA((4,)))
+    else:
+        scratch.append(pltpu.VMEM(packed, bf16))
+    scratch += [pltpu.SemaphoreType.DMA((2, ex.experts - 1))] * 2
+    scratch += [pltpu.SemaphoreType.DMA((2, 2, ex.experts - 1))] * 2
+    scratch.append(pltpu.SemaphoreType.DMA((3,)))
     work = 6 * rows * D * ff * (1 if mode == "forward" else 2 if mode == "backward" else 3)
     return pl.pallas_call(
         functools.partial(exchange_kernel, mode, pack, ex),
@@ -828,7 +860,7 @@
         out_specs=[vmem] * len(outs),
         scratch_shapes=scratch,
         compiler_params=pltpu.CompilerParams(
-            vmem_limit_bytes=60 << 20, collective_id=EXCHANGE_IDS[mode], has_side_effects=True
+            vmem_limit_bytes=62 << 20, collective_id=EXCHANGE_IDS[mode], has_side_effects=True
         ),
         cost_estimate=pl.CostEstimate(
             flops=work + 40 * 10**9, bytes_accessed=6 * D * ff, transcendentals=0
@@ -968,6 +1000,7 @@
     ]
     z_rows = jnp.pad(prior_logits.T, [(0, 16 - total_experts), (0, 0)])
 
+    ex = Exchange(experts, slots)
     saved = []
     front = [hidden_in]
     x_now = hidden_in
@@ -984,14 +1017,20 @@
             x=x_now, n1=n1, qkv=qkv, att=att, lse=lse, middle=middle, n2=n2, info=info,
             gcol=gcol, gpack=gpack, z=z_rows, small=small,
         )
+        keep["received"] = dispatch_call(ex, send)
         if last:
-            keep["gxs"] = outs[11]
-            keep["y"], keep["gin"], keep["dw"] = exchange_call(
-                "both", pack, experts, slots, [send, outs[12], experts_w[l]]
+            gating = [
+                cotangent, n2, outs[11], slot_row[l], info, chosen_rows[l], gcol, small, z_rows,
+                mixes[l], middle, slot_col[l],
+            ]
+            done = exchange_call(
+                "both", pack, ex, [keep["received"], experts_w[l], outs[12]] + gating
             )
+            keep["y"], keep["gin"], keep["dw"] = done[:3]
+            keep["gating"] = done[3:]
         else:
-            keep["received"], keep["y"], keep["gate"], keep["up"] = exchange_call(
-                "forward", pack, experts, slots, [send, experts_w[l]]
+            keep["y"], keep["gate"], keep["up"] = exchange_call(
+                "forward", pack, ex, [keep["received"], experts_w[l]]
             )
         front = [middle, n2, keep["y"], gcol, slot_col[l], small]
         z_rows = info[0:16]
@@ -1007,24 +1046,23 @@
         last = l == LAYERS - 1
         keep = saved[l]
         if not last:
-            keep["info"], mine = lax.optimization_barrier((keep["info"], mine))
-            dense_grads[l + 1] = lax.psum(mine, "expert")
+            gating = [
+                gx, keep["n2"], keep["y"], keep["gxs"], slot_row[l], keep["info"], chosen_rows[l],
+                keep["gcol"], keep["small"], keep["z"], mixes[l], gz,
+            ]
+            done = exchange_call(
+                "backward", pack, ex,
+                [keep["received"], experts_w[l], keep["gy"], keep["gate"], keep["up"]] + gating,
+            )
+            keep["gin"], keep["dw"] = done[:2]
+            keep["gating"] = done[2:]
+        gn2, gsm, mix_grads[l], gz = keep["gating"][:4]
+        if last:
+            hidden_out = keep["gating"][4]
+        d_experts, gn2 = lax.optimization_barrier((keep["dw"], gn2))
         if not last:
-            keep["gin"], keep["dw"] = exchange_call(
-                "backward", pack, experts, slots,
-                [keep["gy"], experts_w[l], keep["gate"], keep["up"], keep["received"]],
-            )
-        d_experts, keep["n2"] = lax.optimization_barrier((keep["dw"], keep["n2"]))
+            gn2, dense_grads[l + 1] = lax.optimization_barrier((gn2, dense_grads[l + 1]))
         expert_grads[l] = lax.psum_scatter(d_experts, "shard", scatter_dimension=0, tiled=False)
-        args = [
-            gx, keep["n2"], keep["y"], keep["gxs"], slot_row[l], keep["info"], chosen_rows[l],
-            keep["gcol"], keep["small"], keep["z"], mixes[l],
-        ]
-        args += [keep["middle"], slot_col[l]] if last else [gz]
-        outs = gating_call(last, experts, slots, args)
-        gn2, gsm, mix_grads[l], gz = outs[:4]
-        if last:
-            hidden_out = outs[4]
         args = [
             gx, gn2, keep["gin"], slot_col[l], keep["middle"], keep["att"], dense[l], keep["qkv"],
             keep["n1"], keep["x"], bias_t, keep["lse"], gsm,
@@ -1038,13 +1076,12 @@
             saved[l - 1]["gxs"] = outs[2]
             gy, d_dense = lax.optimization_barrier((outs[3], d_dense))
             saved[l - 1]["gy"] = gy
-        if not last:
-            d_dense, dense_grads[l + 1] = lax.optimization_barrier((d_dense, dense_grads[l + 1]))
         if l == 0:
             mix_grads[0], d_dense = lax.optimization_barrier((mix_grads[0], d_dense))
-        mine = lax.psum_scatter(d_dense, "shard", scatter_dimension=0, tiled=True)
-
-    dense_grads[0] = lax.psum(mine, "expert")
+        dense_grads[l] = lax.psum_scatter(d_dense, "shard", scatter_dimension=0, tiled=True)
+
+    both_dense = lax.psum(jnp.stack(dense_grads), "expert")
+    dense_grads = [both_dense[l] for l in range(LAYERS)]
     mixing_total = lax.psum(jnp.stack(mix_grads), ("expert", "shard"))
     gate_grad, up_grad, down_grad = expert_outputs(pack, expert_grads)
     project_grad, output_grad, gain_grad, router_grad, vector_grad, const_grad = dense_outputs(

time: 756 us -> 729 us (0.964)
  waiting for transfers between devices: 173 us -> 134 us
  local copies, waits for them, and re-layouts: 23.8 us -> 32.6 us
    pallas_call x0 -> x2, Pallas kernels: none -> 64.7 us  [dispatch_call(): pl.pallas_call(functools.partial(dispatch_kernel, ex), out_shape=shape((e...]
    pallas_call x3, Pallas kernels: 288 us -> 243 us  [exchange_call(): pl.pallas_call(functools.partial(exchange_kernel, mode, pack, ex), out_sh...]
    all_gather x2, waiting for transfers between devices: 30.2 us -> 0.01 us  [on_device(): experts_w.append(lax.all_gather(mine, 'shard', axis=0, tiled=False))]
    psum x2 -> x1, waiting for transfers between devices: 42.1 us -> 13.1 us  [on_device(): both_dense = lax.psum(jnp.stack(dense_grads), 'expert')]
    reduce_scatter x2, waiting for transfers between devices: 18.1 us -> 38.5 us  [on_device(): lax.psum_scatter(d_experts, 'shard', scatter_dimension=0, tiled=False)]
    pallas_call x8 -> x6, Pallas kernels: 204 us -> 185 us  [whole_call(): pl.pallas_call(body, out_shape=outs, in_specs=[pl.BlockSpec(memory_space=...]
    unnamed x41 -> x54, local copies, waits for them, and re-layouts: 10.5 us -> 16.9 us
  transfers between devices with their start and end apart: 10 -> 9, of which waited for: 6 -> 5; matrix products, arithmetic and copies ran while one was open for 3% -> 3% of each run, Pallas kernels for 47% -> 52%
where the time goes in v4:
time: 729 us; the launch traced here: 725 us
  Pallas kernels  492 us (67%)
  waiting for transfers between devices  134 us (18%)
  blocking collectives  41.2 us (6%)
  local copies, waits for them, and re-layouts  32.6 us (4%)
  between operations  14.6 us (2%)
  other arithmetic  8.98 us (1%)
    pallas_call x3, Pallas kernels, exchange_call(): pl.pallas_call(functools.partial(exchange_kernel, mode, pack, ex), out_sh...  243 us
    pallas_call x6, Pallas kernels, whole_call(): pl.pallas_call(body, out_shape=outs, in_specs=[pl.BlockSpec(memory_space=...  185 us
    pallas_call x2, Pallas kernels, dispatch_call(): pl.pallas_call(functools.partial(dispatch_kernel, ex), out_shape=shape((e...  64.7 us
    reduce_scatter x2, waiting for transfers between devices, on_device(): lax.psum_scatter(d_dense, 'shard', scatter_dimension=0, tiled=True)  58.7 us
    psum x1, blocking collectives, on_device(): mixing_total = lax.psum(jnp.stack(mix_grads), ('expert', 'shard'))  41.2 us
    reduce_scatter x2, waiting for transfers between devices, on_device(): lax.psum_scatter(d_experts, 'shard', scatter_dimension=0, tiled=False)  38.5 us
    all_gather x2, waiting for transfers between devices, on_device(): dense.append(lax.all_gather(packed, 'shard', axis=0, tiled=True))  23.4 us
    unnamed x54, local copies, waits for them, and re-layouts  16.9 us
  transfers between devices with their start and end apart: 9, of which 5 were waited for; matrix products, arithmetic and copies ran while one was open for 3% of the time, Pallas kernels for 52%

profile of v4, /device:TPU:0, one launch (start us, length us, event | category | flops | bytes accessed | tf_op | source)
XLA Modules:
  0.0 725.2 jit_solution(2499785547770740992)
XLA Ops:
  7.2 0.8 slice_bitcast_fusion.13
  8.0 0.7 slice_bitcast_fusion.9
  8.7 0.7 slice_bitcast_fusion.11
  9.6 1.0 bitcast_dynamic-update-slice_fusion.3
  10.6 1.0 bitcast_dynamic-update-slice_fusion.2
  11.7 1.1 bitcast_dynamic-update-slice_fusion.1
  12.7 1.0 bitcast_dynamic-update-slice_fusion
  13.8 0.8 copy-done.6
  15.2 0.7 copy-done.9
  16.3 1.1 pad_maximum_fusion.1
  17.7 0.8 copy-done.5
  19.3 1.1 pad_maximum_fusion.2
  21.2 0.7 copy.183.refs_9_
  22.4 0.7 copy.174.refs_4_
  23.1 0.6 pad.40.refs_3_.refs_14_
  25.3 0.6 broadcast_select_fusion
  25.9 0.8 copy.175.refs_6_.refs_13_.refs_9_
  27.0 0.7 pad.48.clone.refs_11_.refs_6_
  27.8 0.6 and_select_fusion
  28.5 1.0 fusion.45
  29.5 4.3 fusion.7
  33.9 23.4 %all-gather.7.cloned.1.call-done.refs_1_.refs_6_ = bf16[768,3200]{1,0:T(8,128)(2,1)} async-done(((bf16[96,3200]{1,0:T(8,128)(2,1)}), bf16[768,3200]{1,0:T(8,128)(2,1)}) %all-gather.7.cloned.1.call-update) | async-done | bytes 4915216 | tf_op jit(solution)/shard_map/all_gather | solution.py:968
  57.2 29.7 %block_forward.2 = (bf16[832,768]{1,0:T(8,128)(2,1)}, bf16[832,2304]{1,0:T(8,128)(2,1)}, bf16[832,768]{1,0:T(8,128)(2,1)}, f32[16,832]{1,0:T(8,128)}, f32[832,76...) custom-call(bf16[832,768]{1,0:T(8,128)(2,1)} %refs_9_.1, ...), custom_call_target="tpu_custom_call" | custom-call | flops 20000000000 | bytes 21816320 | tf_op jit(solution)/shard_map/block_forward/pallas_call | solution.py:259
  86.9 1.4 slice.142.refs_8_.refs_11_
  88.3 1.8 copy-done.1
  90.2 32.9 %dispatch.2.refs_0_ = bf16[960,768]{1,0:T(8,128)(2,1)S(1)} custom-call(bf16[960,768]{1,0:T(8,128)(2,1)S(1)} %copy-done.1), custom_call_target="tpu_custom_call" | custom-call | flops 35000000512 | bytes 1000000 | tf_op jit(solution)/shard_map/dispatch/pallas_call | solution.py:675
  123.0 1.1 copy-done.2
  124.1 51.2 %experts_forward.1 = (bf16[960,768]{1,0:T(8,128)(2,1)}, bf16[960,2048]{1,0:T(8,128)(2,1)}, bf16[960,2048]{1,0:T(8,128)(2,1)}) custom-call(bf16[960,768]{1,0:T(8,128)(2,1)} %copy-done.2, bf16[8,2304,256]{2,1,0:T(8,128)(2,1)} %bitcast.153), custom_call_target="tpu_custom_call" | custom-call | flops 49059696640 | bytes 9437184 | tf_op jit(solution)/shard_map/experts_forward/pallas_call | solution.py:856
  175.4 36.9 %block_forward.3 = (f32[832,768]{1,0:T(8,128)}, bf16[832,768]{1,0:T(8,128)(2,1)}, bf16[832,2304]{1,0:T(8,128)(2,1)}, bf16[832,768]{1,0:T(8,128)(2,1)}, f32[16,83...) custom-call(f32[832,768]{1,0:T(8,128)} %get-tuple-element.82.refs_0_, ...), custom_call_target="tpu_custom_call" | custom-call | flops 20000000000 | bytes 33265664 | tf_op jit(solution)/shard_map/block_forward/pallas_call | solution.py:259
  212.3 1.4 copy-done
  213.7 31.9 %dispatch.3.refs_0_ = bf16[960,768]{1,0:T(8,128)(2,1)S(1)} custom-call(bf16[960,768]{1,0:T(8,128)(2,1)S(1)} %copy-done), custom_call_target="tpu_custom_call" | custom-call | flops 35000000512 | bytes 1000000 | tf_op jit(solution)/shard_map/dispatch/pallas_call | solution.py:675
  245.5 1.1 copy-done.3
  246.6 113.6 %experts_both.1 = (bf16[960,768]{1,0:T(8,128)(2,1)}, bf16[960,768]{1,0:T(8,128)(2,1)}, bf16[8,2304,256]{2,1,0:T(8,128)(2,1)}, f32[832,768]{1,0:T(8,128)}, f32[32...) custom-call(bf16[960,768]{1,0:T(8,128)(2,1)} %copy-done.3, ...), custom_call_target="tpu_custom_call" | custom-call | flops 67179089920 | bytes 9437184 | tf_op jit(solution)/shard_map/experts_both/pallas_call | solution.py:856
  360.3 57.5 %block_backward.2 = (f32[832,768]{1,0:T(8,128)}, bf16[768,3200]{1,0:T(8,128)(2,1)}, bf16[960,768]{1,0:T(8,128)(2,1)}, bf16[960,768]{1,0:T(8,128)(2,1)}) custom-call(bf16[832,768]{1,0:T(8,128)(2,1)} %refs_0_.3, f32[832,768]{1,0:T(8,128)} %get-tuple-element.100.refs_1_, bf16[960,768]{1,0:T(8,128)(2,1)} %get-tuple-element.101.refs_2_, ...), custom_call_target="tpu_custom_call" | custom-call | flops 40000000000 | bytes 35318784 | tf_op jit(solution)/shard_map/block_backward/pallas_call | solution.py:259
  417.8 16.4 %reduce-scatter.5.cloned.1.call-done = bf16[1,2304,256]{2,1,0:T(8,128)(2,1)} async-done(((bf16[8,2304,256]{2,1,0:T(8,128)(2,1)}), bf16[1,2304,256]{2,1,0:T(8,128)(2,1)}) %reduce-scatter.5.cloned.1.call-update) | async-done | bytes 1179664 | tf_op jit(solution)/shard_map/reduce_scatter | solution.py:1065
  434.3 78.3 %experts_backward.1 = (bf16[960,768]{1,0:T(8,128)(2,1)}, bf16[8,2304,256]{2,1,0:T(8,128)(2,1)}, f32[832,768]{1,0:T(8,128)}, f32[32,768]{1,0:T(8,128)}, f32[16,16]{1,0:T(8,128)}, /*index=5*/f32[16,832]{1,0:T(8,128)}) custom-call(bf16[960,768]{1,0:T(8,128)(2,1)} %copy-done.2, bf16[8,2304,256]{2,1,0:T(8,128)(2,1)} %bitcast.154, ...), custom_call_target="tpu_custom_call" | custom-call | flops 58119393280 | bytes 9437184 | tf_op jit(solution)/shard_map/experts_backward/pallas_call | solution.py:856
  512.7 53.7 %block_backward.3 = (f32[832,768]{1,0:T(8,128)}, bf16[768,3200]{1,0:T(8,128)(2,1)}) custom-call(f32[832,768]{1,0:T(8,128)} %get-tuple-element.109.refs_5_.refs_0_, f32[832,768]{1,0:T(8,128)} %get-tuple-element.123.refs_1_, bf16[960,768]{1,0:T(8,128)(2,1)} %get-tuple-element.124.refs_2_, f32[832,4]{1,0:T(8,128)} %get-tuple-element.231.refs_4_.refs_3_, ...), custom_call_target="tpu_custom_call" | custom-call | flops 40000000000 | bytes 32130048 | tf_op jit(solution)/shard_map/block_backward/pallas_call | solution.py:259
  566.4 22.0 %reduce-scatter.9.cloned.1.call-done = bf16[1,2304,256]{2,1,0:T(8,128)(2,1)} async-done(((bf16[8,2304,256]{2,1,0:T(8,128)(2,1)}), bf16[1,2304,256]{2,1,0:T(8,128)(2,1)}) %reduce-scatter.9.cloned.1.call-update) | async-done | bytes 1179664 | tf_op jit(solution)/shard_map/reduce_scatter | solution.py:1065
  588.6 58.7 %reduce-scatter.11.cloned.1.call-done = bf16[96,3200]{1,0:T(8,128)(2,1)} async-done(((bf16[768,3200]{1,0:T(8,128)(2,1)}), bf16[96,3200]{1,0:T(8,128)(2,1)}) %reduce-scatter.11.cloned.1.call-update) | async-done | bytes 614416 | tf_op jit(solution)/shard_map/reduce_scatter | solution.py:1081
  647.3 2.2 pad_maximum_fusion
  650.2 41.2 %psum.15 = f32[2,16,16]{2,1,0:T(8,128)S(1)} all-reduce(f32[2,16,16]{2,1,0:T(8,128)S(1)} %pad_maximum_fusion.4), channel_id=1, replica_groups=mesh['expert'=4,'shard'=8] {'expert','shard'}, use_global_device_ids=true, to_apply=%region_7.8 | all-reduce | flops 512 | bytes 4096 | tf_op jit(solution)/shard_map/psum | solution.py:1085
  692.0 3.9 expert_outputs.1
  695.9 13.1 %all-reduce.12.cloned.1.call-done = bf16[2,96,3200]{2,1,0:T(8,128)(2,1)} async-done(((bf16[2,96,3200]{2,1,0:T(8,128)(2,1)}), bf16[2,96,3200]{2,1,0:T(8,128)(2,1)}) %all-reduce.12.cloned.1.call-update) | async-done | bytes 1228816 | tf_op jit(solution)/shard_map/psum | solution.py:1083
  709.0 2.4 slice_bitcast_fusion
  711.4 2.8 dense_outputs.1
  714.2 1.6 copy.193
  715.8 1.6 copy.192
  717.4 1.0 copy.219
  (100 shorter events, 7.0 us)
Async XLA Ops:
  7.2 7.5 %copy-start.7 = (bf16[2,1,96,2048]{3,2,1,0:T(8,128)(2,1)S(1)}, bf16[2,1,96,2048]{3,2,1,0:T(8,128)(2,1)}, u32[]{:S(2)}) copy-start(bf16[2,1,96,2048]{3,2,1,0:T(8,128)(2,1)} %param.25) | copy-start | bytes 2359300
  7.2 50.0 %all-gather.7.cloned.1.call-start = ((), (), s32[]{:S(2)}) async-start(), calls=%async_computation.4 | async-start | bytes 5529600 | tf_op jit(solution)/shard_map/all_gather | solution.py:968
  11.6 3.3 copy-start.8
  13.8 0.8 copy-start.6
  14.6 109.5 %all-gather.11.cloned.1.call-start = ((), (), s32[]{:S(2)}) async-start(), calls=%async_computation.11 | async-start | bytes 10616832 | tf_op jit(solution)/shard_map/all_gather | solution.py:970
  14.7 1.1 copy-start.9
  17.4 158.0 %all-gather.9.cloned.1.call-start = ((), (), s32[]{:S(2)}) async-start(), calls=%async_computation.5 | async-start | bytes 5529600 | tf_op jit(solution)/shard_map/all_gather | solution.py:968
  17.7 0.8 copy-start.5
  18.5 228.1 %all-gather.13.cloned.1.call-start = ((), (), s32[]{:S(2)}) async-start(), calls=%async_computation.12 | async-start | bytes 10616832 | tf_op jit(solution)/shard_map/all_gather | solution.py:970
  19.1 1.4 copy-start.13
  19.1 1.4 copy-start.14
  19.1 4.0 copy-start.11
  19.3 5.9 copy-start.17
  19.3 6.0 copy-start.19
  20.4 413.8 %reduce-scatter.5.cloned.1.call-start = ((), (), s32[]{:S(2)}) async-start(), calls=%async_computation.6 | async-start | bytes 10616832 | tf_op jit(solution)/shard_map/reduce_scatter | solution.py:1065
  25.0 2.8 copy-start.18
  88.3 1.8 copy-start.1
  123.0 1.1 copy-start.2
  212.3 1.4 copy-start
  245.5 1.1 copy-start.3
  360.2 152.5 %reduce-scatter.7.cloned.1.call-start = ((), (), s32[]{:S(2)}) async-start(), calls=%async_computation.7 | async-start | bytes 5529600 | tf_op jit(solution)/shard_map/reduce_scatter | solution.py:1081
  434.3 154.2 %reduce-scatter.9.cloned.1.call-start = ((), (), s32[]{:S(2)}) async-start(), calls=%async_computation.8 | async-start | bytes 10616832 | tf_op jit(solution)/shard_map/reduce_scatter | solution.py:1065
  512.7 134.6 %reduce-scatter.11.cloned.1.call-start = ((), (), s32[]{:S(2)}) async-start(), calls=%async_computation.9 | async-start | bytes 5529600 | tf_op jit(solution)/shard_map/reduce_scatter | solution.py:1081
  588.5 58.8 %copy-start.10 = (bf16[96,3200]{1,0:T(8,128)(2,1)S(1)}, bf16[96,3200]{1,0:T(8,128)(2,1)}, u32[]{:S(2)}) copy-start(bf16[96,3200]{1,0:T(8,128)(2,1)} %reduce-scatter.7.cloned.1.call-done) | copy-start | bytes 1843204
  588.5 61.0 %copy-start.12 = (f32[16,832]{1,0:T(8,128)S(1)}, f32[16,832]{1,0:T(8,128)}, u32[]{:S(2)}) copy-start(f32[16,832]{1,0:T(8,128)} %get-tuple-element.131) | copy-start | bytes 159748
  588.5 61.7 %copy-start.15 = (f32[16,16]{1,0:T(8,128)S(1)}, f32[16,16]{1,0:T(8,128)}, u32[]{:S(2)}) copy-start(f32[16,16]{1,0:T(8,128)} %get-tuple-element.143) | copy-start | bytes 3076
  588.5 61.6 %copy-start.16 = (f32[16,16]{1,0:T(8,128)S(1)}, f32[16,16]{1,0:T(8,128)}, u32[]{:S(2)}) copy-start(f32[16,16]{1,0:T(8,128)} %get-tuple-element.142) | copy-start | bytes 3076
  588.5 120.5 %all-reduce.12.cloned.1.call-start = ((), (), s32[]{:S(2)}) async-start(), calls=%async_computation.10 | async-start | bytes 2457600 | tf_op jit(solution)/shard_map/psum | solution.py:1083
  695.9 21.5 %copy-start.4 = (bf16[832,768]{1,0:T(8,128)(2,1)S(1)}, bf16[832,768]{1,0:T(8,128)(2,1)}, u32[]{:S(2)}) copy-start(bf16[832,768]{1,0:T(8,128)(2,1)} %get-tuple-element.275) | copy-start | bytes 3833860
Sparse Core Ops, SparseCore 0:
  14.7 42.4 all-gather.6
  59.7 58.8 all-gather.10
  121.0 39.7 all-gather.8
  162.5 58.8 all-gather.12
  360.4 73.8 reduce-scatter.4
  437.6 54.8 reduce-scatter.6
  512.8 75.6 reduce-scatter.8
  592.4 54.8 reduce-scatter.10
  650.3 58.6 all-reduce.11

commit v5 on v4

--- a/solution.py
+++ b/solution.py
@@ -820,6 +820,109 @@
         copy.wait()
 
 
+SPLIT = 13 * 128
+
+
+def cube_kernel(part, g_ref, out_ref, got_c, sums, got_a, got_b, half_a, half_b, end_a, end_b, send, recv):
+    me = lax.axis_index("shard")
+    core, x, y = lax.rem(me, 2), lax.rem(me // 2, 2), me // 4
+    near, over_x, over_y = (
+        me + 1 - 2 * core,
+        me + 2 - 4 * x,
+        me + 4 - 8 * y,
+    )
+    barrier = pltpu.get_barrier_semaphore()
+    for other in (near, over_x, over_y):
+        pl.semaphore_signal(barrier, inc=1, device_id={"shard": other}, device_id_type=MESH)
+    pl.semaphore_wait(barrier, 3)
+    cols_a, cols_b = slice(0, SPLIT), slice(SPLIT, W_ALL)
+
+    def rows(shard):
+        return pl.ds(pl.multiple_of(shard * part, 16), part)
+
+    def copy(n, src, dst, to):
+        made = pltpu.make_async_remote_copy(
+            src_ref=src,
+            dst_ref=dst,
+            send_sem=send.at[n],
+            recv_sem=recv.at[n],
+            device_id={"shard": to},
+            device_id_type=MESH,
+        )
+        made.start()
+        return made
+
+    chips = [2 * (1 - y) + 1 - x, 2 * y + 1 - x, 2 * (1 - y) + x, 2 * y + x]
+    first = [
+        copy(n, g_ref.at[rows(2 * chip + 1 - core)], got_c.at[chip], near)
+        for n, chip in enumerate(chips)
+    ]
+
+    def merge(n):
+        chip = chips[n]
+        first[n].wait_recv()
+        own = g_ref[rows(2 * chip + core), :].astype(f32)
+        sums[chip] = (own + got_c[chip].astype(f32)).astype(bf16)
+
+    def total(chip, cols, got):
+        return sums[chip, :, cols].astype(f32) + got[...].astype(f32)
+
+    merge(0)
+    a0 = copy(4, sums.at[chips[0], :, cols_a], got_a.at[1 - y], over_x)
+    b0 = copy(5, sums.at[chips[0], :, cols_b], got_b.at[1 - x], over_y)
+    merge(1)
+    a1 = copy(6, sums.at[chips[1], :, cols_a], got_a.at[y], over_x)
+    merge(2)
+    b1 = copy(7, sums.at[chips[2], :, cols_b], got_b.at[x], over_y)
+    merge(3)
+    a0.wait_recv()
+    half_a[...] = total(chips[2], cols_a, got_a.at[1 - y]).astype(bf16)
+    a2 = copy(8, half_a, end_a, over_y)
+    b0.wait_recv()
+    half_b[...] = total(chips[1], cols_b, got_b.at[1 - x]).astype(bf16)
+    b2 = copy(9, half_b, end_b, over_x)
+    a1.wait_recv()
+    keep_a = total(chips[3], cols_a, got_a.at[y])
+    a2.wait_recv()
+    out_ref[:, cols_a] = (keep_a + end_a[...].astype(f32)).astype(bf16)
+    b1.wait_recv()
+    keep_b = total(chips[3], cols_b, got_b.at[x])
+    b2.wait_recv()
+    out_ref[:, cols_b] = (keep_b + end_b[...].astype(f32)).astype(bf16)
+    for made in first + [a0, b0, a1, b1, a2, b2]:
+        made.wait_send()
+
+
+def scatter_sum(grads, part):
+    if lax.axis_size("shard") != 8:
+        return lax.psum_scatter(grads, "shard", scatter_dimension=0, tiled=True)
+    vmem = pl.BlockSpec(memory_space=pltpu.VMEM)
+    rest = W_ALL - SPLIT
+    return pl.pallas_call(
+        functools.partial(cube_kernel, part),
+        out_shape=shape((part, W_ALL), bf16),
+        in_specs=[vmem],
+        out_specs=vmem,
+        scratch_shapes=[
+            pltpu.VMEM((4, part, W_ALL), bf16),
+            pltpu.VMEM((4, part, W_ALL), bf16),
+            pltpu.VMEM((2, part, SPLIT), bf16),
+            pltpu.VMEM((2, part, rest), bf16),
+            pltpu.VMEM((part, SPLIT), bf16),
+            pltpu.VMEM((part, rest), bf16),
+            pltpu.VMEM((part, SPLIT), bf16),
+            pltpu.VMEM((part, rest), bf16),
+            pltpu.SemaphoreType.DMA((10,)),
+            pltpu.SemaphoreType.DMA((10,)),
+        ],
+        compiler_params=pltpu.CompilerParams(
+            vmem_limit_bytes=32 << 20, collective_id=4, has_side_effects=True
+        ),
+        cost_estimate=pl.CostEstimate(flops=35 * 10**9, bytes_accessed=10**7, transcendentals=0),
+        name="scatter_sum",
+    )(grads)
+
+
 EXCHANGE_IDS = {"forward": 0, "both": 1, "backward": 2}
 
 
@@ -863,7 +966,9 @@
             vmem_limit_bytes=62 << 20, collective_id=EXCHANGE_IDS[mode], has_side_effects=True
         ),
         cost_estimate=pl.CostEstimate(
-            flops=work + 40 * 10**9, bytes_accessed=6 * D * ff, transcendentals=0
+            flops=10**9 if mode == "backward" else work + 40 * 10**9,
+            bytes_accessed=6 * D * ff,
+            transcendentals=0,
         ),
         name="experts_" + mode,
     )(*args)
@@ -1061,7 +1166,7 @@
             hidden_out = keep["gating"][4]
         d_experts, gn2 = lax.optimization_barrier((keep["dw"], gn2))
         if not last:
-            gn2, dense_grads[l + 1] = lax.optimization_barrier((gn2, dense_grads[l + 1]))
+            gn2, expert_grads[l + 1] = lax.optimization_barrier((gn2, expert_grads[l + 1]))
         expert_grads[l] = lax.psum_scatter(d_experts, "shard", scatter_dimension=0, tiled=False)
         args = [
             gx, gn2, keep["gin"], slot_col[l], keep["middle"], keep["att"], dense[l], keep["qkv"],
@@ -1071,14 +1176,14 @@
             args += [slot_row[l - 1], saved[l - 1]["gpack"]]
         outs = backward_call(l == 0, experts, slots, args)
         gx, d_dense = outs[:2]
-        d_dense, expert_grads[l] = lax.optimization_barrier((d_dense, expert_grads[l]))
         if l > 0:
-            saved[l - 1]["gxs"] = outs[2]
-            gy, d_dense = lax.optimization_barrier((outs[3], d_dense))
-            saved[l - 1]["gy"] = gy
+            saved[l - 1]["gxs"], saved[l - 1]["gy"] = outs[2:4]
         if l == 0:
             mix_grads[0], d_dense = lax.optimization_barrier((mix_grads[0], d_dense))
-        dense_grads[l] = lax.psum_scatter(d_dense, "shard", scatter_dimension=0, tiled=True)
+        if l == 0:
+            dense_grads[l] = scatter_sum(d_dense, part)
+        else:
+            dense_grads[l] = lax.psum_scatter(d_dense, "shard", scatter_dimension=0, tiled=True)
 
     both_dense = lax.psum(jnp.stack(dense_grads), "expert")
     dense_grads = [both_dense[l] for l in range(LAYERS)]

time: 729 us -> 667 us (0.915)
  waiting for transfers between devices: 134 us -> 41.6 us
  Pallas kernels: 492 us -> 518 us
    reduce_scatter x2 -> x1, waiting for transfers between devices: 58.7 us -> 0.02 us  [on_device(): lax.psum_scatter(d_dense, 'shard', scatter_dimension=0, tiled=True)]
    reduce_scatter x2, waiting for transfers between devices: 38.5 us -> 0.02 us  [on_device(): lax.psum_scatter(d_experts, 'shard', scatter_dimension=0, tiled=False)]
    pallas_call x0 -> x1, Pallas kernels: none -> 35 us  [scatter_sum(): pl.pallas_call(functools.partial(cube_kernel, part), out_shape=shape((par...]
    pallas_call x3, Pallas kernels: 243 us -> 235 us  [exchange_call(): pl.pallas_call(functools.partial(exchange_kernel, mode, pack, ex), out_sh...]
  transfers between devices with their start and end apart: 9 -> 8, of which waited for: 5 -> 2; matrix products, arithmetic and copies ran while one was open for 3% -> 3% of each run, Pallas kernels for 52% -> 61%
where the time goes in v5:
time: 667 us; the launch traced here: 662 us
  Pallas kernels  518 us (78%)
  blocking collectives  42.7 us (6%)
  waiting for transfers between devices  41.6 us (6%)
  local copies, waits for them, and re-layouts  35.1 us (5%)
  between operations  14.9 us (2%)
  other arithmetic  8.94 us (1%)
    pallas_call x3, Pallas kernels, exchange_call(): pl.pallas_call(functools.partial(exchange_kernel, mode, pack, ex), out_sh...  235 us
    pallas_call x6, Pallas kernels, whole_call(): pl.pallas_call(body, out_shape=outs, in_specs=[pl.BlockSpec(memory_space=...  183 us
    pallas_call x2, Pallas kernels, dispatch_call(): pl.pallas_call(functools.partial(dispatch_kernel, ex), out_shape=shape((e...  64.7 us
    psum x1, blocking collectives, on_device(): mixing_total = lax.psum(jnp.stack(mix_grads), ('expert', 'shard'))  42.7 us
    pallas_call x1, Pallas kernels, scatter_sum(): pl.pallas_call(functools.partial(cube_kernel, part), out_shape=shape((par...  35 us
    all_gather x2, waiting for transfers between devices, on_device(): dense.append(lax.all_gather(packed, 'shard', axis=0, tiled=True))  23.4 us
    unnamed x54, local copies, waits for them, and re-layouts  19.4 us
    psum x1, waiting for transfers between devices, on_device(): both_dense = lax.psum(jnp.stack(dense_grads), 'expert')  18.1 us
  transfers between devices with their start and end apart: 8, of which 2 were waited for; matrix products, arithmetic and copies ran while one was open for 3% of the time, Pallas kernels for 61%

profile of v5, /device:TPU:0, one launch (start us, length us, event | category | flops | bytes accessed | tf_op | source)
XLA Modules:
  0.0 662.5 jit_solution(14545374705087494701)
XLA Ops:
  7.2 0.8 slice_bitcast_fusion.13
  8.0 0.7 slice_bitcast_fusion.9
  8.7 0.7 slice_bitcast_fusion.11
  9.6 1.0 bitcast_dynamic-update-slice_fusion.3
  10.6 1.0 bitcast_dynamic-update-slice_fusion.2
  11.7 1.1 bitcast_dynamic-update-slice_fusion.1
  12.7 1.0 bitcast_dynamic-update-slice_fusion
  13.8 0.8 copy-done.7
  15.2 0.7 copy-done.10
  16.3 1.1 pad_maximum_fusion.1
  17.7 0.8 copy-done.6
  19.3 1.1 pad_maximum_fusion.2
  21.2 0.7 copy.183.refs_9_
  22.4 0.7 copy.174.refs_4_
  23.1 0.6 pad.40.refs_3_.refs_14_
  23.7 0.6 pad.47.refs_10_.refs_8_
  25.3 0.6 broadcast_select_fusion
  25.9 0.8 copy.175.refs_6_.refs_13_.refs_9_
  27.1 0.7 pad.48.clone.refs_11_.refs_6_
  27.9 0.6 and_select_fusion
  28.5 1.0 fusion.45
  29.5 4.3 fusion.7
  33.8 23.4 %all-gather.7.cloned.1.call-done.refs_1_.refs_6_ = bf16[768,3200]{1,0:T(8,128)(2,1)} async-done(((bf16[96,3200]{1,0:T(8,128)(2,1)}), bf16[768,3200]{1,0:T(8,128)(2,1)}) %all-gather.7.cloned.1.call-update) | async-done | bytes 4915216 | tf_op jit(solution)/shard_map/all_gather | solution.py:1073
  57.2 29.7 %block_forward.2 = (bf16[832,768]{1,0:T(8,128)(2,1)}, bf16[832,2304]{1,0:T(8,128)(2,1)}, bf16[832,768]{1,0:T(8,128)(2,1)}, f32[16,832]{1,0:T(8,128)}, f32[832,76...) custom-call(bf16[832,768]{1,0:T(8,128)(2,1)} %refs_9_.1, ...), custom_call_target="tpu_custom_call" | custom-call | flops 20000000000 | bytes 21816320 | tf_op jit(solution)/shard_map/block_forward/pallas_call | solution.py:259
  86.9 1.4 slice.142.refs_8_.refs_11_
  88.3 1.8 copy-done.2
  90.2 32.9 %dispatch.2.refs_0_ = bf16[960,768]{1,0:T(8,128)(2,1)S(1)} custom-call(bf16[960,768]{1,0:T(8,128)(2,1)S(1)} %copy-done.2), custom_call_target="tpu_custom_call" | custom-call | flops 35000000512 | bytes 1000000 | tf_op jit(solution)/shard_map/dispatch/pallas_call | solution.py:675
  123.0 1.1 copy-done
  124.1 51.2 %experts_forward.1 = (bf16[960,768]{1,0:T(8,128)(2,1)}, bf16[960,2048]{1,0:T(8,128)(2,1)}, bf16[960,2048]{1,0:T(8,128)(2,1)}) custom-call(bf16[960,768]{1,0:T(8,128)(2,1)} %copy-done, bf16[8,2304,256]{2,1,0:T(8,128)(2,1)} %bitcast.130), custom_call_target="tpu_custom_call" | custom-call | flops 49059696640 | bytes 9437184 | tf_op jit(solution)/shard_map/experts_forward/pallas_call | solution.py:959
  175.4 36.9 %block_forward.3 = (f32[832,768]{1,0:T(8,128)}, bf16[832,768]{1,0:T(8,128)(2,1)}, bf16[832,2304]{1,0:T(8,128)(2,1)}, bf16[832,768]{1,0:T(8,128)(2,1)}, f32[16,83...) custom-call(f32[832,768]{1,0:T(8,128)} %get-tuple-element.76.refs_0_, ...), custom_call_target="tpu_custom_call" | custom-call | flops 20000000000 | bytes 33265664 | tf_op jit(solution)/shard_map/block_forward/pallas_call | solution.py:259
  212.3 1.4 copy-done.1
  213.7 31.9 %dispatch.3.refs_0_ = bf16[960,768]{1,0:T(8,128)(2,1)S(1)} custom-call(bf16[960,768]{1,0:T(8,128)(2,1)S(1)} %copy-done.1), custom_call_target="tpu_custom_call" | custom-call | flops 35000000512 | bytes 1000000 | tf_op jit(solution)/shard_map/dispatch/pallas_call | solution.py:675
  245.6 1.1 copy-done.4
  246.7 113.7 %experts_both.1 = (bf16[960,768]{1,0:T(8,128)(2,1)}, bf16[960,768]{1,0:T(8,128)(2,1)}, bf16[8,2304,256]{2,1,0:T(8,128)(2,1)}, f32[832,768]{1,0:T(8,128)}, f32[32...) custom-call(bf16[960,768]{1,0:T(8,128)(2,1)} %copy-done.4, ...), custom_call_target="tpu_custom_call" | custom-call | flops 67179089920 | bytes 9437184 | tf_op jit(solution)/shard_map/experts_both/pallas_call | solution.py:959
  360.4 57.5 %block_backward.2 = (f32[832,768]{1,0:T(8,128)}, bf16[768,3200]{1,0:T(8,128)(2,1)}, bf16[960,768]{1,0:T(8,128)(2,1)}, bf16[960,768]{1,0:T(8,128)(2,1)}) custom-call(bf16[832,768]{1,0:T(8,128)(2,1)} %refs_0_.3, f32[832,768]{1,0:T(8,128)} %get-tuple-element.94.refs_1_, bf16[960,768]{1,0:T(8,128)(2,1)} %get-tuple-element.95.refs_2_, ...), custom_call_target="tpu_custom_call" | custom-call | flops 40000000000 | bytes 35318784 | tf_op jit(solution)/shard_map/block_backward/pallas_call | solution.py:259
  418.0 70.3 %experts_backward.1 = (bf16[960,768]{1,0:T(8,128)(2,1)}, bf16[8,2304,256]{2,1,0:T(8,128)(2,1)}, f32[832,768]{1,0:T(8,128)}, f32[32,768]{1,0:T(8,128)}, f32[16,16]{1,0:T(8,128)}, /*index=5*/f32[16,832]{1,0:T(8,128)}) custom-call(bf16[960,768]{1,0:T(8,128)(2,1)} %copy-done, bf16[8,2304,256]{2,1,0:T(8,128)(2,1)} %bitcast.131, ...), custom_call_target="tpu_custom_call" | custom-call | flops 1000000000 | bytes 9437184 | tf_op jit(solution)/shard_map/experts_backward/pallas_call | solution.py:959
  488.4 51.7 %block_backward.3 = (f32[832,768]{1,0:T(8,128)}, bf16[768,3200]{1,0:T(8,128)(2,1)}) custom-call(f32[832,768]{1,0:T(8,128)} %get-tuple-element.103.refs_5_.refs_0_, f32[832,768]{1,0:T(8,128)} %get-tuple-element.113.refs_1_, bf16[960,768]{1,0:T(8,128)(2,1)} %get-tuple-element.114.refs_2_, f32[832,4]{1,0:T(8,128)} %get-tuple-element.219.refs_4_.refs_3_, ...), custom_call_target="tpu_custom_call" | custom-call | flops 40000000000 | bytes 32130048 | tf_op jit(solution)/shard_map/block_backward/pallas_call | solution.py:259
  540.1 2.5 copy-done.3
  542.6 35.0 %scatter_sum.1 = bf16[96,3200]{1,0:T(8,128)(2,1)S(1)} custom-call(bf16[768,3200]{1,0:T(8,128)(2,1)S(1)} %copy-done.3), custom_call_target="tpu_custom_call" | custom-call | flops 35000000512 | bytes 10000000 | tf_op jit(solution)/shard_map/scatter_sum/pallas_call | solution.py:901
  577.7 2.2 pad_maximum_fusion
  580.6 42.7 %psum.15 = f32[2,16,16]{2,1,0:T(8,128)S(1)} all-reduce(f32[2,16,16]{2,1,0:T(8,128)S(1)} %pad_maximum_fusion.4), channel_id=1, replica_groups=mesh['expert'=4,'shard'=8] {'expert','shard'}, use_global_device_ids=true, to_apply=%region_5.6 | all-reduce | flops 512 | bytes 4096 | tf_op jit(solution)/shard_map/psum | solution.py:1190
  623.9 4.0 expert_outputs.1
  627.9 18.1 %all-reduce.12.cloned.1.call-done = bf16[2,96,3200]{2,1,0:T(8,128)(2,1)} async-done(((bf16[2,96,3200]{2,1,0:T(8,128)(2,1)}), bf16[2,96,3200]{2,1,0:T(8,128)(2,1)}) %all-reduce.12.cloned.1.call-update) | async-done | bytes 1228816 | tf_op jit(solution)/shard_map/psum | solution.py:1188
  646.0 2.4 slice_bitcast_fusion
  648.3 2.8 dense_outputs.1
  651.2 1.6 copy.193
  652.8 1.6 copy.192
  654.4 1.0 copy.219
  (98 shorter events, 6.3 us)
Async XLA Ops:
  7.2 7.5 %copy-start.8 = (bf16[2,1,96,2048]{3,2,1,0:T(8,128)(2,1)S(1)}, bf16[2,1,96,2048]{3,2,1,0:T(8,128)(2,1)}, u32[]{:S(2)}) copy-start(bf16[2,1,96,2048]{3,2,1,0:T(8,128)(2,1)} %param.25) | copy-start | bytes 2359300
  7.2 50.0 %all-gather.7.cloned.1.call-start = ((), (), s32[]{:S(2)}) async-start(), calls=%async_computation.3 | async-start | bytes 5529600 | tf_op jit(solution)/shard_map/all_gather | solution.py:1073
  11.6 3.3 copy-start.9
  13.8 0.8 copy-start.7
  14.6 109.5 %all-gather.11.cloned.1.call-start = ((), (), s32[]{:S(2)}) async-start(), calls=%async_computation.9 | async-start | bytes 10616832 | tf_op jit(solution)/shard_map/all_gather | solution.py:1075
  14.7 1.1 copy-start.10
  17.4 158.0 %all-gather.9.cloned.1.call-start = ((), (), s32[]{:S(2)}) async-start(), calls=%async_computation.4 | async-start | bytes 5529600 | tf_op jit(solution)/shard_map/all_gather | solution.py:1073
  17.7 0.8 copy-start.6
  18.5 228.1 %all-gather.13.cloned.1.call-start = ((), (), s32[]{:S(2)}) async-start(), calls=%async_computation.10 | async-start | bytes 10616832 | tf_op jit(solution)/shard_map/all_gather | solution.py:1075
  19.1 1.4 copy-start.13
  19.1 1.5 copy-start.14
  19.1 4.0 copy-start.11
  19.3 6.0 copy-start.17
  19.3 6.0 copy-start.19
  20.4 468.0 %reduce-scatter.4.cloned.1.call-start = ((), (), s32[]{:S(2)}) async-start(), calls=%async_computation.5 | async-start | bytes 10616832 | tf_op jit(solution)/shard_map/reduce_scatter | solution.py:1170
  25.0 2.8 copy-start.18
  88.3 1.8 copy-start.2
  123.0 1.1 copy-start
  212.3 1.4 copy-start.1
  245.6 1.1 copy-start.4
  360.4 217.3 %reduce-scatter.6.cloned.1.call-start = ((), (), s32[]{:S(2)}) async-start(), calls=%async_computation.6 | async-start | bytes 5529600 | tf_op jit(solution)/shard_map/reduce_scatter | solution.py:1186
  418.0 206.0 %reduce-scatter.8.cloned.1.call-start = ((), (), s32[]{:S(2)}) async-start(), calls=%async_computation.8 | async-start | bytes 10616832 | tf_op jit(solution)/shard_map/reduce_scatter | solution.py:1170
  488.3 157.6 %all-reduce.12.cloned.1.call-start = ((), (), s32[]{:S(2)}) async-start(), calls=%async_computation.7 | async-start | bytes 2457600 | tf_op jit(solution)/shard_map/psum | solution.py:1188
  540.1 2.5 copy-start.3
  577.6 2.3 copy-start.12
  577.7 2.9 copy-start.15
  577.7 2.9 copy-start.16
  627.9 26.5 %copy-start.5 = (bf16[832,768]{1,0:T(8,128)(2,1)S(1)}, bf16[832,768]{1,0:T(8,128)(2,1)}, u32[]{:S(2)}) copy-start(bf16[832,768]{1,0:T(8,128)(2,1)} %get-tuple-element.263) | copy-start | bytes 3833860
Sparse Core Ops, SparseCore 0:
  14.7 42.4 all-gather.6
  59.7 58.8 all-gather.10
  121.0 39.7 all-gather.8
  162.5 58.8 all-gather.12
  360.5 73.8 reduce-scatter.3
  437.8 54.8 reduce-scatter.5
  496.6 87.4 reduce-scatter.7
  587.1 58.7 all-reduce.11

commit v6 on v5

--- a/solution.py
+++ b/solution.py
@@ -28,7 +28,7 @@
 masked_fill = -1e30
 f32 = jnp.float32
 bf16 = jnp.bfloat16
-BLOCKS = 4
+BLOCKS = 2
 VMEM = 56 << 20
 
 
@@ -93,14 +93,18 @@
     return total
 
 
-def send_grads(slot_row, gx, gpack, gxs_ref, gy_ref, experts, slots):
+def all_one_hot(slot_row, experts, slots):
+    return jnp.concatenate([one_hot(slot_row, e, slots) for e in range(experts)], axis=0)
+
+
+def send_grads(hot, gx, gpack, gxs_ref, gy_ref, experts, slots):
+    got = dot(hot, gx)
+    gates = dot(hot, gpack)
+    gxs_ref[...] = got.astype(bf16)
     for e in range(experts):
-        hot = one_hot(slot_row, e, slots)
         rows = slice(e * slots, (e + 1) * slots)
-        got = dot(hot, gx)
-        gates = dot(hot, gpack)
-        gxs_ref[rows, :] = got.astype(bf16)
-        gy_ref[rows, :] = (got * (gates[:, e : e + 1] + gates[:, 64 + e : 65 + e])).astype(bf16)
+        gate = gates[rows, e : e + 1] + gates[rows, 64 + e : 65 + e]
+        gy_ref[rows, :] = (got[rows, :] * gate).astype(bf16)
 
 
 def row_blocks(tokens):
@@ -113,7 +117,7 @@
     return list(zip(edges[:-1], edges[1:]))
 
 
-def forward_kernel(first, last, experts, slots, *refs):
+def forward_kernel(first, last, experts, slots, traffic, *refs):
     refs = list(refs)
     if first:
         x_in = refs.pop(0)
@@ -156,6 +160,11 @@
         return carry
 
     lax.fori_loop(0, BLOCKS, project, 0)
+    if not first:
+        traffic.flush(x_out)
+    traffic.flush(n1_ref)
+    traffic.flush(qkv_ref)
+    traffic.need(bias_ref)
     lane = lax.broadcasted_iota(jnp.int32, (1, 128), 1)
     low_f = jnp.where(lane < HD, 1.0, 0.0)
     low = low_f.astype(bf16)
@@ -189,6 +198,7 @@
         return carry
 
     lax.fori_loop(0, H // 2, pair, 0)
+    traffic.flush(att_ref)
     lse_ref[...] = lse_cols[...].T[0:16, :]
 
     def finish(i, carry):
@@ -203,6 +213,8 @@
         return carry
 
     lax.fori_loop(0, BLOCKS, finish, 0)
+    traffic.flush(mid_ref)
+    traffic.flush(n2_ref)
     n2 = n2_ref[...]
     scores = dot_nt(small[0:32, :].astype(bf16), n2)
     logits = scores[0:16, :]
@@ -239,29 +251,87 @@
     upper, lower = split_bf16(jnp.where(lane < 16, gcol, 0.0))
     gpack = upper + pltpu.roll(lower.astype(f32), 64, 1).astype(bf16)
     gpack_ref[...] = gpack
-    slot_row = slotr_ref[...]
-    for e in range(experts):
-        hot = one_hot(slot_row, e, slots)
-        rows = slice(e * slots, (e + 1) * slots)
-        send_ref[rows, :] = dot(hot, n2).astype(bf16)
+    hot = all_one_hot(slotr_ref[...], experts, slots)
+    send_ref[...] = dot(hot, n2).astype(bf16)
     if last:
-        send_grads(slot_row, cot_ref[...], gpack, gxs_ref, gy_ref, experts, slots)
+        traffic.need(cot_ref)
+        send_grads(hot, cot_ref[...], gpack, gxs_ref, gy_ref, experts, slots)
 
 
 def shape(dims, dtype=f32):
     return jax.ShapeDtypeStruct(tuple(dims), dtype)
 
 
-def whole_call(body, name, outs, scratch, args, flops):
+class Traffic:
+    def __init__(self):
+        self.fetches, self.sinks, self.flushes = {}, {}, []
+
+    def fetch(self, src, buffer, sem):
+        copy = pltpu.make_async_copy(src, buffer, sem)
+        copy.start()
+        self.fetches[id(buffer)] = copy
+
+    def need(self, *buffers):
+        for buffer in buffers:
+            copy = self.fetches.pop(id(buffer), None)
+            if copy is not None:
+                copy.wait()
+
+    def sink(self, buffer, dst, sems):
+        self.sinks[id(buffer)] = [dst, sems, 0]
+
+    def flush(self, buffer, part=None):
+        entry = self.sinks.get(id(buffer))
+        if entry is None:
+            return
+        dst, sems, used = entry
+        entry[2] += 1
+        src, dst = (buffer, dst) if part is None else (buffer.at[part], dst.at[part])
+        copy = pltpu.make_async_copy(src, dst, sems.at[used])
+        copy.start()
+        self.flushes.append(copy)
+
+    def finish(self):
+        for copy in self.flushes:
+            copy.wait()
+
+
+FLUSHES = 3
+
+
+def whole_call(body, name, outs, scratch, args, flops, late=(), early=()):
     moved = sum(a.size * a.dtype.itemsize for a in args) + sum(
         o.size * o.dtype.itemsize for o in outs
     )
+    late, early = sorted(late), sorted(early)
+
+    def kernel(*refs):
+        ins, rest = list(refs[: len(args)]), refs[len(args) :]
+        results, rest = list(rest[: len(outs)]), rest[len(outs) :]
+        own, rest = rest[: len(scratch)], rest[len(scratch) :]
+        traffic = Traffic()
+        fetch_sems, flush_sems = rest[len(late) + len(early) :]
+        for n, at in enumerate(late):
+            traffic.fetch(ins[at], rest[n], fetch_sems.at[n])
+            ins[at] = rest[n]
+        for n, at in enumerate(early):
+            buffer = rest[len(late) + n]
+            traffic.sink(buffer, results[at], flush_sems.at[n])
+            results[at] = buffer
+        body(traffic, *ins, *results, *own)
+        traffic.finish()
+
+    near, far = pl.BlockSpec(memory_space=pltpu.VMEM), pl.BlockSpec(memory_space=pl.ANY)
+    buffers = [pltpu.VMEM(args[at].shape, args[at].dtype) for at in late]
+    buffers += [pltpu.VMEM(outs[at].shape, outs[at].dtype) for at in early]
+    buffers.append(pltpu.SemaphoreType.DMA((max(len(late), 1),)))
+    buffers.append(pltpu.SemaphoreType.DMA((max(len(early), 1), FLUSHES)))
     return pl.pallas_call(
-        body,
+        kernel,
         out_shape=outs,
-        in_specs=[pl.BlockSpec(memory_space=pltpu.VMEM)] * len(args),
-        out_specs=[pl.BlockSpec(memory_space=pltpu.VMEM)] * len(outs),
-        scratch_shapes=scratch,
+        in_specs=[far if n in late else near for n in range(len(args))],
+        out_specs=[far if n in early else near for n in range(len(outs))],
+        scratch_shapes=list(scratch) + buffers,
         compiler_params=pltpu.CompilerParams(vmem_limit_bytes=VMEM),
         cost_estimate=pl.CostEstimate(flops=flops, bytes_accessed=moved, transcendentals=0),
         name=name,
@@ -290,7 +360,10 @@
     padded = -(-tokens // 128) * 128
     scratch = [pltpu.VMEM((tokens, 128), f32), pltpu.VMEM((128, padded), f32)]
     body = functools.partial(forward_kernel, first, last, experts, slots)
-    return whole_call(body, "block_forward", outs, scratch, args, 20 * 10**9)
+    inputs, results = (1, 0) if first else (6, 1)
+    late = [inputs + 1] + ([inputs + 6] if last else [])
+    early = ([] if first else [0]) + [results + n for n in (0, 1, 2, 4, 5)]
+    return whole_call(body, "block_forward", outs, scratch, args, 20 * 10**9, late, early)
 
 
 def gating_kernel(last, experts, slots, *refs):
@@ -395,7 +468,7 @@
     return outs
 
 
-def backward_kernel(first, experts, slots, *refs):
+def backward_kernel(first, experts, slots, traffic, *refs):
     refs = list(refs)
     gx_ref, gn2p_ref, gn2e_ref, slotc_ref, mid_ref, att_ref, w_ref, qkv_ref, n1_ref, x_ref = [
         refs.pop(0) for _ in range(10)
@@ -431,6 +504,7 @@
         return total + jnp.sum(gn2 * middle * r, axis=0, keepdims=True)
 
     ggain1 = lax.fori_loop(0, BLOCKS, enter, jnp.zeros((1, D), f32))
+    traffic.need(att_ref)
     lane = lax.broadcasted_iota(jnp.int32, (1, 128), 1)
     low_f = jnp.where(lane < HD, 1.0, 0.0)
     low = low_f.astype(bf16)
@@ -443,6 +517,8 @@
         return carry
 
     lax.fori_loop(0, D // 128, out_grad, 0)
+    traffic.flush(dw_ref, (slice(None), slice(W_OUT, W_SMALL)))
+    traffic.need(qkv_ref, biast_ref, lse_ref)
     spans = causal_spans(tokens)
 
     def pair(p, carry):
@@ -494,6 +570,7 @@
 
     turn[...] = jnp.zeros_like(turn)
     lax.fori_loop(0, H // 2, pair, 0)
+    traffic.need(n1_ref)
 
     def in_grad(p, carry):
         here = pl.ds(pl.multiple_of(p * 128, 128), 128)
@@ -501,6 +578,8 @@
         return carry
 
     lax.fori_loop(0, D // 128, in_grad, 0)
+    traffic.flush(dw_ref, (slice(None), slice(0, W_OUT)))
+    traffic.need(x_ref)
 
     def leave(i, total):
         rows = block(i)
@@ -519,8 +598,11 @@
         [gsm_ref[0:24, :], ggain0, ggain1, gsm_ref[26:32, :], jnp.zeros((96, D), f32)], axis=0
     )
     dw_ref[:, W_SMALL:] = rows.T.astype(bf16)
+    traffic.flush(dw_ref, (slice(None), slice(W_SMALL, W_ALL)))
+    traffic.flush(gout_ref)
     if not first:
-        send_grads(slotr_ref[...], gatt[...], gpack_ref[...], gxs_ref, gy_ref, experts, slots)
+        hot = all_one_hot(slotr_ref[...], experts, slots)
+        send_grads(hot, gatt[...], gpack_ref[...], gxs_ref, gy_ref, experts, slots)
 
 
 def backward_call(first, experts, slots, args):
@@ -537,7 +619,9 @@
         pltpu.VMEM((padded, 128), f32),
     ]
     body = functools.partial(backward_kernel, first, experts, slots)
-    return whole_call(body, "block_backward", outs, scratch, args, 40 * 10**9)
+    return whole_call(
+        body, "block_backward", outs, scratch, args, 40 * 10**9, (5, 7, 8, 9, 10, 11), (0, 1)
+    )
 
 
 class Packing:
@@ -691,34 +775,42 @@
     forward, backward = mode in ("forward", "both"), mode in ("backward", "both")
     recv_n = refs.pop(0)
     w_hbm = refs.pop(0)
-    gating = []
     if backward:
         send_g = refs.pop(0)
         if mode == "backward":
             gate_hbm, up_hbm = refs.pop(0), refs.pop(0)
-        gating = [refs.pop(0) for _ in range(12)]
+        gating_far = [refs.pop(0) for _ in range(12)]
     if forward:
         back_y = refs.pop(0)
     if mode == "forward":
-        gates, ups = refs.pop(0), refs.pop(0)
+        gates_far, ups_far, gates, ups = [refs.pop(0) for _ in range(4)]
     else:
-        back_g, dw = refs.pop(0), refs.pop(0)
+        back_g, dw_far = refs.pop(0), refs.pop(0)
         gating_outs = [refs.pop(0) for _ in range(5 if mode == "both" else 4)]
     if forward:
         out_y, acc_y = refs.pop(0), refs.pop(0)
     if backward:
         recv_g, out_g, hids, gates, ups, rows_t, acc_g = [refs.pop(0) for _ in range(7)]
-        w = dw
-    else:
-        w = refs.pop(0)
+        gating = [refs.pop(0) for _ in range(12)]
+    w = refs.pop(0)
     sends, recvs, backs, gots, local = refs
+    traffic = Traffic()
+    if mode == "forward":
+        traffic.sink(gates, gates_far, local.at[4:7])
+        traffic.sink(ups, ups_far, local.at[7:10])
 
     loads = [pltpu.make_async_copy(w_hbm, w, local.at[0])]
     if mode == "backward":
         loads.append(pltpu.make_async_copy(gate_hbm, gates, local.at[1]))
         loads.append(pltpu.make_async_copy(up_hbm, ups, local.at[2]))
+    if mode == "backward":
+        for n, (far, near) in enumerate(zip(gating_far, gating)):
+            traffic.fetch(far, near, local.at[4 + n])
     for copy in loads:
         copy.start()
+    if mode == "both":
+        for n, (far, near) in enumerate(zip(gating_far, gating)):
+            traffic.fetch(far, near, local.at[4 + n])
     greet(ex.experts)
 
     def work(start, size):
@@ -757,6 +849,10 @@
             return carry
 
         lax.fori_loop(0, pack.chunks, chunk, 0)
+        if mode == "forward":
+            here = pl.ds(start, size)
+            traffic.flush(gates, here)
+            traffic.flush(ups, here)
         if forward:
             out_y[rows, :] = acc_y[part, :].astype(bf16)
         if backward:
@@ -775,6 +871,7 @@
             copy.start()
         recv_g[0 : ex.slots, :] = send_g[own_slots(ex), :]
         if mode == "backward":
+            traffic.need(*gating)
             gating_kernel(False, ex.experts, ex.slots, *gating, *gating_outs)
     for copy in loads:
         copy.wait()
@@ -801,6 +898,7 @@
     if backward:
         back_g[own_slots(ex), :] = out_g[0 : ex.slots, :]
         rows_t[...] = recv_n[...].T
+        dw = w
         if pack.padded != pack.part:
             dw[...] = jnp.zeros_like(dw)
 
@@ -812,12 +910,18 @@
             return carry
 
         lax.fori_loop(0, pack.chunks, weights, 0)
+        leaving = pltpu.make_async_copy(dw, dw_far, local.at[3])
+        leaving.start()
     for copy in ys:
         copy.wait()
     if mode == "both":
+        traffic.need(*gating)
         gating_kernel(True, ex.experts, ex.slots, *gating[:2], back_y, *gating[2:], *gating_outs)
     for copy in gs:
         copy.wait()
+    if backward:
+        leaving.wait()
+    traffic.finish()
 
 
 SPLIT = 13 * 128
@@ -944,23 +1048,30 @@
     else:
         in_specs[3] = in_specs[4] = far
         outs = [flat, shape(packed, bf16)] + gating_outputs(False)
+    out_specs = [vmem] * len(outs)
+    if mode == "forward":
+        out_specs[1] = out_specs[2] = far
+        scratch += [pltpu.VMEM((rows, ff), bf16)] * 2
+    else:
+        in_specs[-12:] = [far] * 12
+        out_specs[2 if mode == "both" else 1] = far
     if forward:
         scratch += [pltpu.VMEM((rows, D), bf16), pltpu.VMEM((most, D), f32)]
     if backward:
         scratch += [pltpu.VMEM((rows, D), bf16)] * 2
         scratch += [pltpu.VMEM((rows, ff), bf16)] * 3
         scratch += [pltpu.VMEM((D, rows), bf16), pltpu.VMEM((most, D), f32)]
-    else:
-        scratch.append(pltpu.VMEM(packed, bf16))
+        scratch += [pltpu.VMEM(a.shape, a.dtype) for a in args[-12:]]
+    scratch.append(pltpu.VMEM(packed, bf16))
     scratch += [pltpu.SemaphoreType.DMA((2, ex.experts - 1))] * 2
     scratch += [pltpu.SemaphoreType.DMA((2, 2, ex.experts - 1))] * 2
-    scratch.append(pltpu.SemaphoreType.DMA((3,)))
+    scratch.append(pltpu.SemaphoreType.DMA((16,)))
     work = 6 * rows * D * ff * (1 if mode == "forward" else 2 if mode == "backward" else 3)
     return pl.pallas_call(
         functools.partial(exchange_kernel, mode, pack, ex),
         out_shape=outs,
         in_specs=in_specs,
-        out_specs=[vmem] * len(outs),
+        out_specs=out_specs,
         scratch_shapes=scratch,
         compiler_params=pltpu.CompilerParams(
             vmem_limit_bytes=62 << 20, collective_id=EXCHANGE_IDS[mode], has_side_effects=True
@@ -974,7 +1085,7 @@
     )(*args)
 
 
-def expert_outputs_kernel(pack, first_ref, second_ref, gate_ref, up_ref, down_ref):
+def expert_outputs_kernel(pack, traffic, first_ref, second_ref, gate_ref, up_ref, down_ref):
     for l, ref in enumerate((first_ref, second_ref)):
         for n, out in enumerate((gate_ref, up_ref)):
             for j in range(pack.chunks):
@@ -993,7 +1104,7 @@
 
 
 def dense_outputs_kernel(
-    part, labels, first_ref, second_ref, proj_ref, out_ref, gain_ref, router_ref, vec_ref, const_ref,
+    part, labels, traffic, first_ref, second_ref, proj_ref, out_ref, gain_ref, router_ref, vec_ref, const_ref,
     turn,
 ):
     for l, ref in enumerate((first_ref, second_ref)):

time: 667 us -> 664 us (level)
  Pallas kernels: 518 us -> 499 us
  waiting for transfers between devices: 41.6 us -> 59.8 us
    pallas_call x6, Pallas kernels: 183 us -> 163 us  [whole_call(): pl.pallas_call(kernel, out_shape=outs, in_specs=[far if n in late else ne...]
    psum x1, waiting for transfers between devices: 18.1 us -> 36.3 us  [on_device(): both_dense = lax.psum(jnp.stack(dense_grads), 'expert')]
    pallas_call x1, Pallas kernels: 35 us -> 42.7 us  [scatter_sum(): pl.pallas_call(functools.partial(cube_kernel, part), out_shape=shape((par...]
    pallas_call x3, Pallas kernels: 235 us -> 228 us  [exchange_call(): pl.pallas_call(functools.partial(exchange_kernel, mode, pack, ex), out_sh...]
  transfers between devices with their start and end apart: 8 -> 8, of which waited for: 2 -> 2; matrix products, arithmetic and copies ran while one was open for 3% -> 3% of each run, Pallas kernels for 61% -> 59%
where the time goes in v6:
time: 664 us; the launch traced here: 659 us
  Pallas kernels  499 us (75%)
  waiting for transfers between devices  59.8 us (9%)
  blocking collectives  39.8 us (6%)
  local copies, waits for them, and re-layouts  34.6 us (5%)
  between operations  15 us (2%)
  other arithmetic  8.94 us (1%)
    pallas_call x3, Pallas kernels, exchange_call(): pl.pallas_call(functools.partial(exchange_kernel, mode, pack, ex), out_sh...  228 us
    pallas_call x6, Pallas kernels, whole_call(): pl.pallas_call(kernel, out_shape=outs, in_specs=[far if n in late else ne...  163 us
    pallas_call x2, Pallas kernels, dispatch_call(): pl.pallas_call(functools.partial(dispatch_kernel, ex), out_shape=shape((e...  65.3 us
    pallas_call x1, Pallas kernels, scatter_sum(): pl.pallas_call(functools.partial(cube_kernel, part), out_shape=shape((par...  42.7 us
    psum x1, blocking collectives, on_device(): mixing_total = lax.psum(jnp.stack(mix_grads), ('expert', 'shard'))  39.8 us
    psum x1, waiting for transfers between devices, on_device(): both_dense = lax.psum(jnp.stack(dense_grads), 'expert')  36.3 us
    all_gather x2, waiting for transfers between devices, on_device(): dense.append(lax.all_gather(packed, 'shard', axis=0, tiled=True))  23.4 us
    unnamed x54, local copies, waits for them, and re-layouts  18.9 us
  transfers between devices with their start and end apart: 8, of which 2 were waited for; matrix products, arithmetic and copies ran while one was open for 3% of the time, Pallas kernels for 59%

profile of v6, /device:TPU:0, one launch (start us, length us, event | category | flops | bytes accessed | tf_op | source)
XLA Modules:
  0.0 659.4 jit_solution(15720199014744355142)
XLA Ops:
  7.2 0.8 slice_bitcast_fusion.13
  8.0 0.7 slice_bitcast_fusion.9
  8.7 0.7 slice_bitcast_fusion.11
  9.6 1.0 bitcast_dynamic-update-slice_fusion.3
  10.6 1.0 bitcast_dynamic-update-slice_fusion.2
  11.7 1.1 bitcast_dynamic-update-slice_fusion.1
  12.7 1.0 bitcast_dynamic-update-slice_fusion
  13.8 0.8 copy-done.7
  15.2 0.7 copy-done.10
  16.3 1.1 pad_maximum_fusion.1
  17.7 0.8 copy-done.6
  19.3 1.1 pad_maximum_fusion.2
  21.2 0.7 copy.183.refs_9_
  22.4 0.7 copy.174.refs_4_
  23.1 0.6 pad.40.refs_3_.refs_14_
  23.7 0.6 pad.47.refs_10_.refs_8_
  25.3 0.6 broadcast_select_fusion
  25.9 0.8 copy.175.refs_6_.refs_13_.refs_9_
  27.1 0.7 pad.48.clone.refs_11_.refs_6_
  27.9 0.6 and_select_fusion
  28.5 1.0 fusion.45
  29.5 4.3 fusion.7
  33.8 23.4 %all-gather.7.cloned.1.call-done.refs_1_.refs_6_ = bf16[768,3200]{1,0:T(8,128)(2,1)} async-done(((bf16[96,3200]{1,0:T(8,128)(2,1)}), bf16[768,3200]{1,0:T(8,128)(2,1)}) %all-gather.7.cloned.1.call-update) | async-done | bytes 4915216 | tf_op jit(solution)/shard_map/all_gather | solution.py:1184
  57.2 27.3 %block_forward.2 = (bf16[832,768]{1,0:T(8,128)(2,1)}, bf16[832,2304]{1,0:T(8,128)(2,1)}, bf16[832,768]{1,0:T(8,128)(2,1)}, f32[16,832]{1,0:T(8,128)}, f32[832,76...) custom-call(bf16[832,768]{1,0:T(8,128)(2,1)} %refs_9_.1, ...), custom_call_target="tpu_custom_call" | custom-call | flops 20000000000 | bytes 21816320 | tf_op jit(solution)/shard_map/block_forward/pallas_call | solution.py:329
  84.6 1.4 slice.142.refs_8_.refs_11_
  86.0 1.4 copy-done.2
  87.4 32.9 %dispatch.2.refs_0_ = bf16[960,768]{1,0:T(8,128)(2,1)S(1)} custom-call(bf16[960,768]{1,0:T(8,128)(2,1)S(1)} %copy-done.2), custom_call_target="tpu_custom_call" | custom-call | flops 35000000512 | bytes 1000000 | tf_op jit(solution)/shard_map/dispatch/pallas_call | solution.py:759
  120.3 1.1 copy-done
  121.4 48.8 %experts_forward.1 = (bf16[960,768]{1,0:T(8,128)(2,1)}, bf16[960,2048]{1,0:T(8,128)(2,1)}, bf16[960,2048]{1,0:T(8,128)(2,1)}) custom-call(bf16[960,768]{1,0:T(8,128)(2,1)} %copy-done, bf16[8,2304,256]{2,1,0:T(8,128)(2,1)} %bitcast.130), custom_call_target="tpu_custom_call" | custom-call | flops 49059696640 | bytes 9437184 | tf_op jit(solution)/shard_map/experts_forward/pallas_call | solution.py:1070
  170.3 35.7 %block_forward.3 = (f32[832,768]{1,0:T(8,128)}, bf16[832,768]{1,0:T(8,128)(2,1)}, bf16[832,2304]{1,0:T(8,128)(2,1)}, bf16[832,768]{1,0:T(8,128)(2,1)}, f32[16,83...) custom-call(f32[832,768]{1,0:T(8,128)} %get-tuple-element.76.refs_0_, ...), custom_call_target="tpu_custom_call" | custom-call | flops 20000000000 | bytes 33265664 | tf_op jit(solution)/shard_map/block_forward/pallas_call | solution.py:329
  206.0 1.4 copy-done.1
  207.4 32.4 %dispatch.3.refs_0_ = bf16[960,768]{1,0:T(8,128)(2,1)S(1)} custom-call(bf16[960,768]{1,0:T(8,128)(2,1)S(1)} %copy-done.1), custom_call_target="tpu_custom_call" | custom-call | flops 35000000512 | bytes 1000000 | tf_op jit(solution)/shard_map/dispatch/pallas_call | solution.py:759
  239.8 1.1 copy-done.4
  240.9 108.6 %experts_both.1 = (bf16[960,768]{1,0:T(8,128)(2,1)}, bf16[960,768]{1,0:T(8,128)(2,1)}, bf16[8,2304,256]{2,1,0:T(8,128)(2,1)}, f32[832,768]{1,0:T(8,128)}, f32[32...) custom-call(bf16[960,768]{1,0:T(8,128)(2,1)} %copy-done.4, ...), custom_call_target="tpu_custom_call" | custom-call | flops 67179089920 | bytes 9437184 | tf_op jit(solution)/shard_map/experts_both/pallas_call | solution.py:1070
  349.6 48.5 %block_backward.2 = (f32[832,768]{1,0:T(8,128)}, bf16[768,3200]{1,0:T(8,128)(2,1)}, bf16[960,768]{1,0:T(8,128)(2,1)}, bf16[960,768]{1,0:T(8,128)(2,1)}) custom-call(bf16[832,768]{1,0:T(8,128)(2,1)} %refs_0_.3, f32[832,768]{1,0:T(8,128)} %get-tuple-element.94.refs_1_, bf16[960,768]{1,0:T(8,128)(2,1)} %get-tuple-element.95.refs_2_, ...), custom_call_target="tpu_custom_call" | custom-call | flops 40000000000 | bytes 35318784 | tf_op jit(solution)/shard_map/block_backward/pallas_call | solution.py:329
  398.4 70.5 %experts_backward.1 = (bf16[960,768]{1,0:T(8,128)(2,1)}, bf16[8,2304,256]{2,1,0:T(8,128)(2,1)}, f32[832,768]{1,0:T(8,128)}, f32[32,768]{1,0:T(8,128)}, f32[16,16]{1,0:T(8,128)}, /*index=5*/f32[16,832]{1,0:T(8,128)}) custom-call(bf16[960,768]{1,0:T(8,128)(2,1)} %copy-done, bf16[8,2304,256]{2,1,0:T(8,128)(2,1)} %bitcast.131, ...), custom_call_target="tpu_custom_call" | custom-call | flops 1000000000 | bytes 9437184 | tf_op jit(solution)/shard_map/experts_backward/pallas_call | solution.py:1070
  469.3 44.7 %block_backward.3 = (f32[832,768]{1,0:T(8,128)}, bf16[768,3200]{1,0:T(8,128)(2,1)}) custom-call(f32[832,768]{1,0:T(8,128)} %get-tuple-element.103.refs_5_.refs_0_, f32[832,768]{1,0:T(8,128)} %get-tuple-element.113.refs_1_, bf16[960,768]{1,0:T(8,128)(2,1)} %get-tuple-element.114.refs_2_, f32[832,4]{1,0:T(8,128)} %get-tuple-element.219.refs_4_.refs_3_, ...), custom_call_target="tpu_custom_call" | custom-call | flops 40000000000 | bytes 32130048 | tf_op jit(solution)/shard_map/block_backward/pallas_call | solution.py:329
  514.0 2.4 copy-done.3
  516.4 42.7 %scatter_sum.1 = bf16[96,3200]{1,0:T(8,128)(2,1)S(1)} custom-call(bf16[768,3200]{1,0:T(8,128)(2,1)S(1)} %copy-done.3), custom_call_target="tpu_custom_call" | custom-call | flops 35000000512 | bytes 10000000 | tf_op jit(solution)/shard_map/scatter_sum/pallas_call | solution.py:1005
  559.2 2.2 pad_maximum_fusion
  562.1 39.8 %psum.15 = f32[2,16,16]{2,1,0:T(8,128)S(1)} all-reduce(f32[2,16,16]{2,1,0:T(8,128)S(1)} %pad_maximum_fusion.4), channel_id=1, replica_groups=mesh['expert'=4,'shard'=8] {'expert','shard'}, use_global_device_ids=true, to_apply=%region_5.6 | all-reduce | flops 512 | bytes 4096 | tf_op jit(solution)/shard_map/psum | solution.py:1301
  602.5 4.0 expert_outputs.1
  606.5 36.3 %all-reduce.12.cloned.1.call-done = bf16[2,96,3200]{2,1,0:T(8,128)(2,1)} async-done(((bf16[2,96,3200]{2,1,0:T(8,128)(2,1)}), bf16[2,96,3200]{2,1,0:T(8,128)(2,1)}) %all-reduce.12.cloned.1.call-update) | async-done | bytes 1228816 | tf_op jit(solution)/shard_map/psum | solution.py:1299
  642.8 2.4 slice_bitcast_fusion
  645.1 2.9 dense_outputs.1
  648.0 1.6 copy.193
  649.6 1.6 copy.192
  651.2 1.0 copy.219
  (98 shorter events, 6.8 us)
Async XLA Ops:
  7.2 7.5 %copy-start.8 = (bf16[2,1,96,2048]{3,2,1,0:T(8,128)(2,1)S(1)}, bf16[2,1,96,2048]{3,2,1,0:T(8,128)(2,1)}, u32[]{:S(2)}) copy-start(bf16[2,1,96,2048]{3,2,1,0:T(8,128)(2,1)} %param.25) | copy-start | bytes 2359300
  7.2 50.0 %all-gather.7.cloned.1.call-start = ((), (), s32[]{:S(2)}) async-start(), calls=%async_computation.3 | async-start | bytes 5529600 | tf_op jit(solution)/shard_map/all_gather | solution.py:1184
  11.6 3.3 copy-start.9
  13.8 0.8 copy-start.7
  14.6 106.8 %all-gather.11.cloned.1.call-start = ((), (), s32[]{:S(2)}) async-start(), calls=%async_computation.9 | async-start | bytes 10616832 | tf_op jit(solution)/shard_map/all_gather | solution.py:1186
  14.7 1.1 copy-start.10
  17.4 152.9 %all-gather.9.cloned.1.call-start = ((), (), s32[]{:S(2)}) async-start(), calls=%async_computation.4 | async-start | bytes 5529600 | tf_op jit(solution)/shard_map/all_gather | solution.py:1184
  17.7 0.8 copy-start.6
  18.5 222.4 %all-gather.13.cloned.1.call-start = ((), (), s32[]{:S(2)}) async-start(), calls=%async_computation.10 | async-start | bytes 10616832 | tf_op jit(solution)/shard_map/all_gather | solution.py:1186
  19.1 1.4 copy-start.13
  19.1 1.5 copy-start.14
  19.1 4.0 copy-start.11
  19.3 6.0 copy-start.17
  19.3 6.0 copy-start.19
  20.4 448.8 %reduce-scatter.4.cloned.1.call-start = ((), (), s32[]{:S(2)}) async-start(), calls=%async_computation.5 | async-start | bytes 10616832 | tf_op jit(solution)/shard_map/reduce_scatter | solution.py:1281
  25.0 2.8 copy-start.18
  86.0 1.4 copy-start.2
  120.3 1.1 copy-start
  206.0 1.4 copy-start.1
  239.8 1.1 copy-start.4
  349.5 209.7 %reduce-scatter.6.cloned.1.call-start = ((), (), s32[]{:S(2)}) async-start(), calls=%async_computation.6 | async-start | bytes 5529600 | tf_op jit(solution)/shard_map/reduce_scatter | solution.py:1297
  398.1 204.4 %reduce-scatter.8.cloned.1.call-start = ((), (), s32[]{:S(2)}) async-start(), calls=%async_computation.8 | async-start | bytes 10616832 | tf_op jit(solution)/shard_map/reduce_scatter | solution.py:1281
  468.9 173.8 %all-reduce.12.cloned.1.call-start = ((), (), s32[]{:S(2)}) async-start(), calls=%async_computation.7 | async-start | bytes 2457600 | tf_op jit(solution)/shard_map/psum | solution.py:1299
  514.0 2.4 copy-start.3
  559.1 2.3 copy-start.12
  559.2 2.9 copy-start.15
  559.2 2.9 copy-start.16
  606.5 44.7 %copy-start.5 = (bf16[832,768]{1,0:T(8,128)(2,1)S(1)}, bf16[832,768]{1,0:T(8,128)(2,1)}, u32[]{:S(2)}) copy-start(bf16[832,768]{1,0:T(8,128)(2,1)} %get-tuple-element.263) | copy-start | bytes 3833860
Sparse Core Ops, SparseCore 0:
  14.7 42.4 all-gather.6
  59.7 58.8 all-gather.10
  121.0 39.7 all-gather.8
  162.5 58.8 all-gather.12
  349.6 73.9 reduce-scatter.3
  427.0 54.8 reduce-scatter.5
  485.8 96.1 reduce-scatter.7
  585.1 57.6 all-reduce.11

commit v7 on v6

--- a/solution.py
+++ b/solution.py
@@ -927,40 +927,112 @@
 SPLIT = 13 * 128
 
 
-def cube_kernel(part, g_ref, out_ref, got_c, sums, got_a, got_b, half_a, half_b, end_a, end_b, send, recv):
+def cube_kernel(part, labels, g_ref, upper_ref, mix_ref, *refs):
+    outs, refs = refs[:7], refs[7:]
+    got_c, sums, got_a, got_b, half_a, half_b, end_a, end_b = refs[:8]
+    mine, quarters, ready, mix_held, mix_got, turn, send, recv, z_send, z_recv, mix_send, mix_recv = refs[8:]
+    mix_out = outs[6]
     me = lax.axis_index("shard")
+    z = lax.axis_index("expert")
+    owners = quarters.shape[1]
     core, x, y = lax.rem(me, 2), lax.rem(me // 2, 2), me // 4
-    near, over_x, over_y = (
-        me + 1 - 2 * core,
-        me + 2 - 4 * x,
-        me + 4 - 8 * y,
-    )
+    near, over_x, over_y = me + 1 - 2 * core, me + 2 - 4 * x, me + 4 - 8 * y
     barrier = pltpu.get_barrier_semaphore()
     for other in (near, over_x, over_y):
         pl.semaphore_signal(barrier, inc=1, device_id={"shard": other}, device_id_type=MESH)
-    pl.semaphore_wait(barrier, 3)
+    for d in range(1, owners):
+        pl.semaphore_signal(
+            barrier, inc=1, device_id={"expert": lax.rem(z + d, owners)}, device_id_type=MESH
+        )
+    pl.semaphore_wait(barrier, 3 + owners - 1)
     cols_a, cols_b = slice(0, SPLIT), slice(SPLIT, W_ALL)
 
     def rows(shard):
         return pl.ds(pl.multiple_of(shard * part, 16), part)
 
-    def copy(n, src, dst, to):
+    def remote(src, dst, send_sem, recv_sem, to):
         made = pltpu.make_async_remote_copy(
             src_ref=src,
             dst_ref=dst,
-            send_sem=send.at[n],
-            recv_sem=recv.at[n],
-            device_id={"shard": to},
+            send_sem=send_sem,
+            recv_sem=recv_sem,
+            device_id=to,
             device_id_type=MESH,
         )
         made.start()
         return made
+
+    def copy(n, src, dst, to):
+        return remote(src, dst, send.at[n], recv.at[n], {"shard": to})
+
+    def quarter(owner):
+        return (
+            pl.ds(pl.multiple_of((owner // 2) * (part // 2), 16), part // 2),
+            pl.ds(pl.multiple_of(lax.rem(owner, 2) * SPLIT, 128), SPLIT),
+        )
+
+    def spread(l):
+        made = []
+        for d in range(1, owners):
+            to = lax.rem(z + d, owners)
+            made.append(
+                remote(
+                    mine.at[(l, *quarter(to))],
+                    quarters.at[l, z],
+                    z_send.at[l, 0, d - 1],
+                    z_recv.at[l, 0, d - 1],
+                    {"expert": to},
+                )
+            )
+        quarters[l, z] = mine[(l, *quarter(z))]
+        return made
+
+    def gather(l, made):
+        for one in made:
+            one.wait_recv()
+        total = quarters[l, 0].astype(f32)
+        for owner in range(1, owners):
+            total = total + quarters[l, owner].astype(f32)
+        ready[(l, *quarter(z))] = total.astype(bf16)
+        here = (l, *quarter(z))
+        return [
+            remote(
+                ready.at[here],
+                ready.at[here],
+                z_send.at[l, 1, d - 1],
+                z_recv.at[l, 1, d - 1],
+                {"expert": lax.rem(z + d, owners)},
+            )
+            for d in range(1, owners)
+        ]
+
+    pairs = [{"shard": near}, {"shard": over_x}, {"shard": over_y}]
+    pairs += [{"expert": z + 1 - 2 * lax.rem(z, 2)}, {"expert": z + 2 - 4 * (z // 2)}]
+    mix_held[0] = mix_ref[...]
+
+    def mix_start(n):
+        return remote(mix_held.at[n], mix_got.at[n], mix_send.at[n], mix_recv.at[n], pairs[n])
+
+    def mix_end(n, made):
+        made.wait_recv()
+        total = mix_held[n] + mix_got[n]
+        if n + 1 < len(pairs):
+            mix_held[n + 1] = total
+        else:
+            for l in range(LAYERS):
+                mix_out[l] = total[l * 16 : l * 16 + labels, 0:labels]
 
     chips = [2 * (1 - y) + 1 - x, 2 * y + 1 - x, 2 * (1 - y) + x, 2 * y + x]
     first = [
         copy(n, g_ref.at[rows(2 * chip + 1 - core)], got_c.at[chip], near)
         for n, chip in enumerate(chips)
     ]
+    mix = [mix_start(0)]
+    mine[0, :, W_ALL:] = jnp.zeros((part, 2 * SPLIT - W_ALL), bf16)
+    mine[1, :, W_ALL:] = jnp.zeros((part, 2 * SPLIT - W_ALL), bf16)
+    mine[1, :, 0:W_ALL] = upper_ref[...]
+    upper = spread(1)
+    turn[...] = jnp.zeros_like(turn)
 
     def merge(n):
         chip = chips[n]
@@ -979,34 +1051,53 @@
     merge(2)
     b1 = copy(7, sums.at[chips[2], :, cols_b], got_b.at[x], over_y)
     merge(3)
+    mix_end(0, mix[0])
+    mix.append(mix_start(1))
     a0.wait_recv()
     half_a[...] = total(chips[2], cols_a, got_a.at[1 - y]).astype(bf16)
     a2 = copy(8, half_a, end_a, over_y)
     b0.wait_recv()
     half_b[...] = total(chips[1], cols_b, got_b.at[1 - x]).astype(bf16)
     b2 = copy(9, half_b, end_b, over_x)
+    mix_end(1, mix[1])
+    mix.append(mix_start(2))
+    last_upper = gather(1, upper)
     a1.wait_recv()
     keep_a = total(chips[3], cols_a, got_a.at[y])
     a2.wait_recv()
-    out_ref[:, cols_a] = (keep_a + end_a[...].astype(f32)).astype(bf16)
+    mine[0, :, cols_a] = (keep_a + end_a[...].astype(f32)).astype(bf16)
     b1.wait_recv()
     keep_b = total(chips[3], cols_b, got_b.at[x])
     b2.wait_recv()
-    out_ref[:, cols_b] = (keep_b + end_b[...].astype(f32)).astype(bf16)
-    for made in first + [a0, b0, a1, b1, a2, b2]:
+    mine[0, :, cols_b] = (keep_b + end_b[...].astype(f32)).astype(bf16)
+    lower = spread(0)
+    mix_end(2, mix[2])
+    mix.append(mix_start(3))
+    for made in last_upper:
+        made.wait_recv()
+    write_dense(part, labels, 1, ready.at[1], outs[:6], turn)
+    mix_end(3, mix[3])
+    mix.append(mix_start(4))
+    last_lower = gather(0, lower)
+    mix_end(4, mix[4])
+    for made in last_lower:
+        made.wait_recv()
+    write_dense(part, labels, 0, ready.at[0], outs[:6], turn)
+    for made in first + [a0, b0, a1, b1, a2, b2] + mix + upper + lower + last_upper + last_lower:
         made.wait_send()
 
 
-def scatter_sum(grads, part):
-    if lax.axis_size("shard") != 8:
-        return lax.psum_scatter(grads, "shard", scatter_dimension=0, tiled=True)
+def finish_call(part, labels, grads, upper, mix):
     vmem = pl.BlockSpec(memory_space=pltpu.VMEM)
     rest = W_ALL - SPLIT
+    owners = lax.axis_size("expert")
+    outs = dense_shapes(part, labels) + [shape((LAYERS, labels, labels))]
+    dma = pltpu.SemaphoreType.DMA
     return pl.pallas_call(
-        functools.partial(cube_kernel, part),
-        out_shape=shape((part, W_ALL), bf16),
-        in_specs=[vmem],
-        out_specs=vmem,
+        functools.partial(cube_kernel, part, labels),
+        out_shape=outs,
+        in_specs=[vmem] * 3,
+        out_specs=[vmem] * len(outs),
         scratch_shapes=[
             pltpu.VMEM((4, part, W_ALL), bf16),
             pltpu.VMEM((4, part, W_ALL), bf16),
@@ -1016,15 +1107,25 @@
             pltpu.VMEM((part, rest), bf16),
             pltpu.VMEM((part, SPLIT), bf16),
             pltpu.VMEM((part, rest), bf16),
-            pltpu.SemaphoreType.DMA((10,)),
-            pltpu.SemaphoreType.DMA((10,)),
+            pltpu.VMEM((2, part, 2 * SPLIT), bf16),
+            pltpu.VMEM((2, owners, part // 2, SPLIT), bf16),
+            pltpu.VMEM((2, part, 2 * SPLIT), bf16),
+            pltpu.VMEM((5, 32, 128), f32),
+            pltpu.VMEM((5, 32, 128), f32),
+            pltpu.VMEM((128, 128), f32),
+            dma((10,)),
+            dma((10,)),
+            dma((2, 2, owners - 1)),
+            dma((2, 2, owners - 1)),
+            dma((5,)),
+            dma((5,)),
         ],
         compiler_params=pltpu.CompilerParams(
-            vmem_limit_bytes=32 << 20, collective_id=4, has_side_effects=True
+            vmem_limit_bytes=40 << 20, collective_id=4, has_side_effects=True
         ),
-        cost_estimate=pl.CostEstimate(flops=35 * 10**9, bytes_accessed=10**7, transcendentals=0),
-        name="scatter_sum",
-    )(grads)
+        cost_estimate=pl.CostEstimate(flops=70 * 10**9, bytes_accessed=10**7, transcendentals=0),
+        name="dense_sums",
+    )(grads, upper, mix)
 
 
 EXCHANGE_IDS = {"forward": 0, "both": 1, "backward": 2}
@@ -1103,26 +1204,30 @@
     return whole_call(body, "expert_outputs", outs, [], grads, 10**6)
 
 
-def dense_outputs_kernel(
-    part, labels, traffic, first_ref, second_ref, proj_ref, out_ref, gain_ref, router_ref, vec_ref, const_ref,
-    turn,
-):
+def write_dense(part, labels, l, ref, outs, turn):
+    proj_ref, out_ref, gain_ref, router_ref, vec_ref, const_ref = outs
+    for c in range(3):
+        proj_ref[l, c] = ref[:, c * D : (c + 1) * D].astype(f32)
+    out_ref[l] = ref[:, W_OUT:W_SMALL].astype(f32)
+    small = ref[:, W_SMALL:W_ALL].astype(f32)
+    router_ref[l] = small[:, 0:labels]
+    for c in range(2):
+        const_ref[l, c] = small[:, S_CONST + 2 * c : S_CONST + 2 * c + 2]
+    turn[0:part, :] = small
+    rows = turn[...].T
+    gain_ref[l] = rows[S_GAIN : S_GAIN + 2, 0:part]
+    vec_ref[l] = rows[S_VEC : S_VEC + 2, 0:part]
+
+
+def dense_outputs_kernel(part, labels, traffic, first_ref, second_ref, *refs):
+    outs, turn = refs[:6], refs[6]
+    turn[...] = jnp.zeros_like(turn)
     for l, ref in enumerate((first_ref, second_ref)):
-        for c in range(3):
-            proj_ref[l, c] = ref[:, c * D : (c + 1) * D].astype(f32)
-        out_ref[l] = ref[:, W_OUT:W_SMALL].astype(f32)
-        small = ref[:, W_SMALL:].astype(f32)
-        router_ref[l] = small[:, 0:labels]
-        for c in range(2):
-            const_ref[l, c] = small[:, S_CONST + 2 * c : S_CONST + 2 * c + 2]
-        turn[0:part, :] = small
-        rows = turn[...].T
-        gain_ref[l] = rows[S_GAIN : S_GAIN + 2, 0:part]
-        vec_ref[l] = rows[S_VEC : S_VEC + 2, 0:part]
-
-
-def dense_outputs(part, labels, grads):
-    outs = [
+        write_dense(part, labels, l, ref, outs, turn)
+
+
+def dense_shapes(part, labels):
+    return [
         shape((LAYERS, 3, part, D)),
         shape((LAYERS, part, D)),
         shape((LAYERS, 2, part)),
@@ -1130,7 +1235,11 @@
         shape((LAYERS, 2, part)),
         shape((LAYERS, 2, part, 2)),
     ]
+
+
+def dense_outputs(part, labels, grads):
     body = functools.partial(dense_outputs_kernel, part, labels)
+    outs = dense_shapes(part, labels)
     return whole_call(body, "dense_outputs", outs, [pltpu.VMEM((128, 128), f32)], grads, 10**6)
 
 
@@ -1289,20 +1398,21 @@
         gx, d_dense = outs[:2]
         if l > 0:
             saved[l - 1]["gxs"], saved[l - 1]["gy"] = outs[2:4]
-        if l == 0:
-            mix_grads[0], d_dense = lax.optimization_barrier((mix_grads[0], d_dense))
-        if l == 0:
-            dense_grads[l] = scatter_sum(d_dense, part)
-        else:
+        if l > 0:
             dense_grads[l] = lax.psum_scatter(d_dense, "shard", scatter_dimension=0, tiled=True)
 
-    both_dense = lax.psum(jnp.stack(dense_grads), "expert")
-    dense_grads = [both_dense[l] for l in range(LAYERS)]
-    mixing_total = lax.psum(jnp.stack(mix_grads), ("expert", "shard"))
+    if pack.shards == 8 and experts == 4:
+        mix = jnp.pad(jnp.concatenate(mix_grads), [(0, 0), (0, 112)])
+        dense_outs = finish_call(part, total_experts, d_dense, dense_grads[1], mix)
+        mixing_grad = dense_outs[6]
+    else:
+        dense_grads[0] = lax.psum_scatter(d_dense, "shard", scatter_dimension=0, tiled=True)
+        both_dense = lax.psum(jnp.stack(dense_grads), "expert")
+        mixing_grad = lax.psum(jnp.stack(mix_grads), ("expert", "shard"))
+        mixing_grad = mixing_grad[:, 0:total_experts, 0:total_experts]
+        dense_outs = dense_outputs(part, total_experts, [both_dense[l] for l in range(LAYERS)])
+    project_grad, output_grad, gain_grad, router_grad, vector_grad, const_grad = dense_outs[:6]
     gate_grad, up_grad, down_grad = expert_outputs(pack, expert_grads)
-    project_grad, output_grad, gain_grad, router_grad, vector_grad, const_grad = dense_outputs(
-        part, total_experts, dense_grads
-    )
     return (
         hidden_out,
         gx,
@@ -1311,7 +1421,7 @@
         output_grad,
         gain_grad,
         router_grad,
-        mixing_total[:, 0:total_experts, 0:total_experts],
+        mixing_grad,
         vector_grad,
         const_grad,
         gate_grad[:, None],

time: 664 us -> 620 us (0.934)
  blocking collectives: 39.8 us -> 0 us
  waiting for transfers between devices: 59.8 us -> 23.5 us
  Pallas kernels: 499 us -> 531 us
    psum x1 -> x0, blocking collectives: 39.8 us -> none  [on_device(): mixing_total = lax.psum(jnp.stack(mix_grads), ('expert', 'shard'))]
    psum x1 -> x0, waiting for transfers between devices: 36.3 us -> none  [on_device(): both_dense = lax.psum(jnp.stack(dense_grads), 'expert')]
    pallas_call x1, Pallas kernels: 42.7 us -> 76.9 us  [finish_call(): pl.pallas_call(functools.partial(cube_kernel, part, labels), out_shape=ou...]
    unnamed x54 -> x61, local copies, waits for them, and re-layouts: 18.9 us -> 22.7 us
    pallas_call x6 -> x5, Pallas kernels: 163 us -> 161 us  [whole_call(): pl.pallas_call(kernel, out_shape=outs, in_specs=[far if n in late else ne...]
  transfers between devices with their start and end apart: 8 -> 7, of which waited for: 2 -> 1; matrix products, arithmetic and copies ran while one was open for 3% -> 3% of each run, Pallas kernels for 59% -> 68%
where the time goes in v7:
time: 620 us; the launch traced here: 613 us
  Pallas kernels  531 us (86%)
  local copies, waits for them, and re-layouts  35.4 us (6%)
  waiting for transfers between devices  23.5 us (4%)
  between operations  15 us (2%)
  other arithmetic  6.73 us (1%)
    pallas_call x3, Pallas kernels, exchange_call(): pl.pallas_call(functools.partial(exchange_kernel, mode, pack, ex), out_sh...  228 us
    pallas_call x5, Pallas kernels, whole_call(): pl.pallas_call(kernel, out_shape=outs, in_specs=[far if n in late else ne...  161 us
    pallas_call x1, Pallas kernels, finish_call(): pl.pallas_call(functools.partial(cube_kernel, part, labels), out_shape=ou...  76.9 us
    pallas_call x2, Pallas kernels, dispatch_call(): pl.pallas_call(functools.partial(dispatch_kernel, ex), out_shape=shape((e...  65.3 us
    all_gather x2, waiting for transfers between devices, on_device(): dense.append(lax.all_gather(packed, 'shard', axis=0, tiled=True))  23.4 us
    unnamed x61, local copies, waits for them, and re-layouts  22.7 us
  transfers between devices with their start and end apart: 7, of which 1 were waited for; matrix products, arithmetic and copies ran while one was open for 3% of the time, Pallas kernels for 68%

profile of v7, /device:TPU:0, one launch (start us, length us, event | category | flops | bytes accessed | tf_op | source)
XLA Modules:
  0.0 612.9 jit_solution(5093285320216861853)
XLA Ops:
  7.2 0.8 slice_bitcast_fusion.11
  8.0 0.7 slice_bitcast_fusion.7
  8.7 0.7 slice_bitcast_fusion.9
  9.6 1.0 bitcast_dynamic-update-slice_fusion.3
  10.6 1.0 bitcast_dynamic-update-slice_fusion.2
  11.7 1.1 bitcast_dynamic-update-slice_fusion.1
  12.7 1.0 bitcast_dynamic-update-slice_fusion
  13.8 0.8 copy-done.8
  15.2 0.7 copy-done.11
  16.3 1.1 pad_maximum_fusion
  17.7 0.8 copy-done.7
  19.3 1.1 pad_maximum_fusion.1
  21.2 0.7 copy.183.refs_9_
  22.4 0.7 copy.174.refs_4_
  23.1 0.6 pad.44.refs_3_.refs_14_
  23.7 0.6 pad.51.refs_10_.refs_8_
  24.4 0.6 pad.46.refs_5_.refs_11_
  25.3 0.6 broadcast_select_fusion
  25.9 0.8 copy.175.refs_6_.refs_13_.refs_9_
  27.1 0.7 pad.52.clone.refs_11_.refs_6_
  27.9 0.6 and_select_fusion
  28.5 1.0 fusion.45
  29.5 4.3 fusion.7
  33.8 23.4 %all-gather.7.cloned.1.call-done.refs_1_.refs_6_ = bf16[768,3200]{1,0:T(8,128)(2,1)} async-done(((bf16[96,3200]{1,0:T(8,128)(2,1)}), bf16[768,3200]{1,0:T(8,128)(2,1)}) %all-gather.7.cloned.1.call-update) | async-done | bytes 4915216 | tf_op jit(solution)/shard_map/all_gather | solution.py:1293
  57.2 27.4 %block_forward.2 = (bf16[832,768]{1,0:T(8,128)(2,1)}, bf16[832,2304]{1,0:T(8,128)(2,1)}, bf16[832,768]{1,0:T(8,128)(2,1)}, f32[16,832]{1,0:T(8,128)}, f32[832,76...) custom-call(bf16[832,768]{1,0:T(8,128)(2,1)} %refs_9_.1, ...), custom_call_target="tpu_custom_call" | custom-call | flops 20000000000 | bytes 21816320 | tf_op jit(solution)/shard_map/block_forward/pallas_call | solution.py:329
  84.6 1.5 slice.133.refs_8_.refs_11_
  86.0 1.4 copy-done.3
  87.4 32.9 %dispatch.2.refs_0_ = bf16[960,768]{1,0:T(8,128)(2,1)S(1)} custom-call(bf16[960,768]{1,0:T(8,128)(2,1)S(1)} %copy-done.3), custom_call_target="tpu_custom_call" | custom-call | flops 35000000512 | bytes 1000000 | tf_op jit(solution)/shard_map/dispatch/pallas_call | solution.py:759
  120.3 1.1 copy-done
  121.4 48.8 %experts_forward.1 = (bf16[960,768]{1,0:T(8,128)(2,1)}, bf16[960,2048]{1,0:T(8,128)(2,1)}, bf16[960,2048]{1,0:T(8,128)(2,1)}) custom-call(bf16[960,768]{1,0:T(8,128)(2,1)} %copy-done, bf16[8,2304,256]{2,1,0:T(8,128)(2,1)} %bitcast.121), custom_call_target="tpu_custom_call" | custom-call | flops 49059696640 | bytes 9437184 | tf_op jit(solution)/shard_map/experts_forward/pallas_call | solution.py:1171
  170.2 35.7 %block_forward.3 = (f32[832,768]{1,0:T(8,128)}, bf16[832,768]{1,0:T(8,128)(2,1)}, bf16[832,2304]{1,0:T(8,128)(2,1)}, bf16[832,768]{1,0:T(8,128)(2,1)}, f32[16,83...) custom-call(f32[832,768]{1,0:T(8,128)} %get-tuple-element.75.refs_0_, ...), custom_call_target="tpu_custom_call" | custom-call | flops 20000000000 | bytes 33265664 | tf_op jit(solution)/shard_map/block_forward/pallas_call | solution.py:329
  206.0 1.4 copy-done.2
  207.4 32.4 %dispatch.3.refs_0_ = bf16[960,768]{1,0:T(8,128)(2,1)S(1)} custom-call(bf16[960,768]{1,0:T(8,128)(2,1)S(1)} %copy-done.2), custom_call_target="tpu_custom_call" | custom-call | flops 35000000512 | bytes 1000000 | tf_op jit(solution)/shard_map/dispatch/pallas_call | solution.py:759
  239.8 1.1 copy-done.5
  240.9 108.5 %experts_both.1 = (bf16[960,768]{1,0:T(8,128)(2,1)}, bf16[960,768]{1,0:T(8,128)(2,1)}, bf16[8,2304,256]{2,1,0:T(8,128)(2,1)}, f32[832,768]{1,0:T(8,128)}, f32[32...) custom-call(bf16[960,768]{1,0:T(8,128)(2,1)} %copy-done.5, ...), custom_call_target="tpu_custom_call" | custom-call | flops 67179089920 | bytes 9437184 | tf_op jit(solution)/shard_map/experts_both/pallas_call | solution.py:1171
  349.5 48.5 %block_backward.2 = (f32[832,768]{1,0:T(8,128)}, bf16[768,3200]{1,0:T(8,128)(2,1)}, bf16[960,768]{1,0:T(8,128)(2,1)}, bf16[960,768]{1,0:T(8,128)(2,1)}) custom-call(bf16[832,768]{1,0:T(8,128)(2,1)} %refs_0_.3, f32[832,768]{1,0:T(8,128)} %get-tuple-element.93.refs_1_, bf16[960,768]{1,0:T(8,128)(2,1)} %get-tuple-element.94.refs_2_, ...), custom_call_target="tpu_custom_call" | custom-call | flops 40000000000 | bytes 35318784 | tf_op jit(solution)/shard_map/block_backward/pallas_call | solution.py:329
  398.1 70.5 %experts_backward.1 = (bf16[960,768]{1,0:T(8,128)(2,1)}, bf16[8,2304,256]{2,1,0:T(8,128)(2,1)}, f32[832,768]{1,0:T(8,128)}, f32[32,768]{1,0:T(8,128)}, f32[16,16]{1,0:T(8,128)}, /*index=5*/f32[16,832]{1,0:T(8,128)}) custom-call(bf16[960,768]{1,0:T(8,128)(2,1)} %copy-done, bf16[8,2304,256]{2,1,0:T(8,128)(2,1)} %bitcast.122, ...), custom_call_target="tpu_custom_call" | custom-call | flops 1000000000 | bytes 9437184 | tf_op jit(solution)/shard_map/experts_backward/pallas_call | solution.py:1171
  468.7 0.6 copy-done.16
  470.1 45.0 %block_backward.3 = (f32[832,768]{1,0:T(8,128)}, bf16[768,3200]{1,0:T(8,128)(2,1)}) custom-call(f32[832,768]{1,0:T(8,128)} %get-tuple-element.102.refs_5_.refs_0_, f32[832,768]{1,0:T(8,128)} %get-tuple-element.112.refs_1_, bf16[960,768]{1,0:T(8,128)(2,1)} %get-tuple-element.113.refs_2_, f32[832,4]{1,0:T(8,128)} %get-tuple-element.215.refs_4_.refs_3_, ...), custom_call_target="tpu_custom_call" | custom-call | flops 40000000000 | bytes 32130048 | tf_op jit(solution)/shard_map/block_backward/pallas_call | solution.py:329
  515.1 1.1 copy-done.1
  516.2 2.4 copy-done.4
  518.6 76.9 %dense_sums.1 = (f32[2,3,96,768]{3,2,1,0:T(8,128)S(1)}, f32[2,96,768]{2,1,0:T(8,128)S(1)}, f32[2,2,96]{2,1,0:T(2,128)S(1)}, f32[2,96,8]{2,1,0:T(8,128)S(1)}, f32...) custom-call(bf16[768,3200]{1,0:T(8,128)(2,1)S(1)} %copy-done.4, ...), custom_call_target="tpu_custom_call" | custom-call | flops 70000001024 | bytes 10000000 | tf_op jit(solution)/shard_map/dense_sums/pallas_call | solution.py:1096
  595.5 0.7 copy.193
  596.2 0.7 copy.192
  596.9 4.0 expert_outputs.1
  601.0 1.0 copy.223
  602.0 1.2 copy.224
  603.2 0.8 copy.225
  (97 shorter events, 6.9 us)
Async XLA Ops:
  7.2 7.5 %copy-start.9 = (bf16[2,1,96,2048]{3,2,1,0:T(8,128)(2,1)S(1)}, bf16[2,1,96,2048]{3,2,1,0:T(8,128)(2,1)}, u32[]{:S(2)}) copy-start(bf16[2,1,96,2048]{3,2,1,0:T(8,128)(2,1)} %param.25) | copy-start | bytes 2359300
  7.2 50.0 %all-gather.7.cloned.1.call-start = ((), (), s32[]{:S(2)}) async-start(), calls=%async_computation.3 | async-start | bytes 5529600 | tf_op jit(solution)/shard_map/all_gather | solution.py:1293
  11.6 3.3 copy-start.10
  13.8 0.8 copy-start.8
  14.6 106.8 %all-gather.11.cloned.1.call-start = ((), (), s32[]{:S(2)}) async-start(), calls=%async_computation.8 | async-start | bytes 10616832 | tf_op jit(solution)/shard_map/all_gather | solution.py:1295
  14.7 1.1 copy-start.11
  17.4 152.8 %all-gather.9.cloned.1.call-start = ((), (), s32[]{:S(2)}) async-start(), calls=%async_computation.4 | async-start | bytes 5529600 | tf_op jit(solution)/shard_map/all_gather | solution.py:1293
  17.7 0.8 copy-start.7
  18.5 222.4 %all-gather.13.cloned.1.call-start = ((), (), s32[]{:S(2)}) async-start(), calls=%async_computation.9 | async-start | bytes 10616832 | tf_op jit(solution)/shard_map/all_gather | solution.py:1295
  19.1 1.4 copy-start.14
  19.1 1.5 copy-start.15
  19.1 4.0 copy-start.12
  19.3 6.0 copy-start.18
  19.3 6.0 copy-start.20
  20.4 449.7 %reduce-scatter.4.cloned.1.call-start = ((), (), s32[]{:S(2)}) async-start(), calls=%async_computation.5 | async-start | bytes 10616832 | tf_op jit(solution)/shard_map/reduce_scatter | solution.py:1390
  25.0 2.8 copy-start.19
  86.0 1.4 copy-start.3
  120.3 1.1 copy-start
  206.0 1.4 copy-start.2
  239.8 1.1 copy-start.5
  349.4 165.7 %reduce-scatter.6.cloned.1.call-start = ((), (), s32[]{:S(2)}) async-start(), calls=%async_computation.6 | async-start | bytes 5529600 | tf_op jit(solution)/shard_map/reduce_scatter | solution.py:1402
  398.0 198.8 %reduce-scatter.8.cloned.1.call-start = ((), (), s32[]{:S(2)}) async-start(), calls=%async_computation.7 | async-start | bytes 10616832 | tf_op jit(solution)/shard_map/reduce_scatter | solution.py:1390
  468.6 0.7 copy-start.16
  468.6 0.7 copy-start.17
  468.7 0.8 copy-start.13
  515.1 1.1 copy-start.1
  516.2 2.4 copy-start.4
  596.9 4.1 copy-start.6
Sparse Core Ops, SparseCore 0:
  14.7 42.4 all-gather.6
  59.7 58.8 all-gather.10
  121.0 39.7 all-gather.8
  162.5 58.8 all-gather.12
  349.6 73.9 reduce-scatter.3
  426.9 54.8 reduce-scatter.5
  485.7 90.2 reduce-scatter.7

commit v8 on v7

--- a/solution.py
+++ b/solution.py
@@ -113,7 +113,7 @@
 
 
 def causal_spans(tokens):
-    edges = [0, 384, 640, tokens]
+    edges = [0, 256, 512, tokens]
     return list(zip(edges[:-1], edges[1:]))
 
 
@@ -177,14 +177,20 @@
         va = v * low + high
         vb = v * high + low
         here = pl.ds(pl.multiple_of(p * 128, 128), 128)
-        for start, stop in causal_spans(tokens):
+        spans = causal_spans(tokens)
+        scores = []
+        for start, stop in spans:
             q = qkv_ref[start:stop, here] * bf16(HD**-0.5)
-            outs = []
-            for mask, value in ((low, va), (high, vb)):
-                s = dot_nt(q * mask, k[:stop]) + bias_ref[start:stop, :stop]
-                peak = jnp.max(s, axis=1, keepdims=True)
-                expo = jnp.exp(s - peak).astype(bf16)
-                outs.append((dot(expo, value[:stop]), peak))
+            scores.append(
+                [dot_nt(q * mask, k[:stop]) + bias_ref[start:stop, :stop] for mask in (low, high)]
+            )
+        for (start, stop), pairs in zip(spans, scores):
+            peaks = [jnp.max(one, axis=1, keepdims=True) for one in pairs]
+            expos = [jnp.exp(one - peak).astype(bf16) for one, peak in zip(pairs, peaks)]
+            outs = [
+                (dot(expo, value[:stop]), peak)
+                for expo, value, peak in zip(expos, (va, vb), peaks)
+            ]
             (oa, ma), (ob, mb) = outs
             numer = jnp.where(lane < HD, oa, ob)
             denom = pltpu.roll(jnp.where(lane < HD, ob, oa), HD, 1)
@@ -533,30 +539,36 @@
         inner = turn[...].T[:, 0:tokens]
         turn[0:tokens, :] = k.astype(f32)
         kt = turn[...].T[:, 0:tokens].astype(bf16)
-        gq_t = []
         gk = [0.0] * len(spans)
         gv = [0.0] * len(spans)
-        for h, mask in ((0, low), (1, high)):
-            qh = q * mask
-            gh = g * mask
-            dsum = jnp.sum(inner[h * HD : (h + 1) * HD, :], axis=0, keepdims=True)
-            lse = lse_ref[pl.ds(2 * p + h, 1), :]
-            gq_h = []
-            for n, (start, stop) in enumerate(spans):
-                st = dot_nt(k[start:stop], qh[start:]) + biast_ref[start:stop, start:]
-                pt = jnp.exp(st - lse[:, start:])
-                gpt = dot_nt(v[start:stop], gh[start:])
-                gst = (pt * (gpt - dsum[:, start:])).astype(bf16)
-                gv[n] = gv[n] + dot(pt.astype(bf16), gh[start:])
-                gk[n] = gk[n] + dot(gst, qh[start:])
-                part = dot(kt[h * HD : (h + 1) * HD, start:stop], gst)
-                gq_h.append(part)
+        masks = (low, high)
+        qs = [q * mask for mask in masks]
+        gs = [g * mask for mask in masks]
+        dsums = [
+            jnp.sum(inner[h * HD : (h + 1) * HD, :], axis=0, keepdims=True) for h in range(2)
+        ]
+        lses = [lse_ref[pl.ds(2 * p + h, 1), :] for h in range(2)]
+        parts = [[], []]
+        for n, (start, stop) in enumerate(spans):
+            st = [
+                dot_nt(k[start:stop], qs[h][start:]) + biast_ref[start:stop, start:]
+                for h in range(2)
+            ]
+            gpt = [dot_nt(v[start:stop], gs[h][start:]) for h in range(2)]
+            pt = [jnp.exp(st[h] - lses[h][:, start:]) for h in range(2)]
+            gst = [(pt[h] * (gpt[h] - dsums[h][:, start:])).astype(bf16) for h in range(2)]
+            for h in range(2):
+                gv[n] = gv[n] + dot(pt[h].astype(bf16), gs[h][start:])
+                gk[n] = gk[n] + dot(gst[h], qs[h][start:])
+                parts[h].append(dot(kt[h * HD : (h + 1) * HD, start:stop], gst[h]))
+        gq_t = []
+        for h in range(2):
             cols = []
             for n, (start, stop) in enumerate(spans):
                 piece = 0.0
                 for m in range(n + 1):
                     origin = spans[m][0]
-                    piece = piece + gq_h[m][:, start - origin : stop - origin]
+                    piece = piece + parts[h][m][:, start - origin : stop - origin]
                 cols.append(piece)
             gq_t.append(jnp.concatenate(cols, axis=1))
         turn_t = jnp.concatenate(gq_t, axis=0) * scale
@@ -673,13 +685,19 @@
 class Exchange:
     def __init__(self, experts, slots):
         self.experts, self.slots = experts, slots
-        first = -(-slots // 32) * 16
-        self.waves = ((0, first), (first, slots - first))
+        half = -(-slots // 32) * 16
+        quarter = -(-half // 32) * 16
+        edges = (0, quarter, half, slots)
+        self.waves = tuple((low, high - low) for low, high in zip(edges[:-1], edges[1:]))
         self.ranges = [(0, slots)]
         for _, size in self.waves:
             start = self.ranges[-1][0] + self.ranges[-1][1]
             self.ranges.append((start, (experts - 1) * size))
         self.total = experts * slots
+
+    def span(self, group):
+        start = self.ranges[1 + group[0]][0]
+        return start, sum(self.ranges[1 + wave][1] for wave in group)
 
     def held(self, wave, d):
         size = self.waves[wave][1]
@@ -743,27 +761,31 @@
     return pl.ds(pl.multiple_of(me * ex.slots, 16), ex.slots)
 
 
-def dispatch_kernel(ex, send, recv, sends, recvs):
+def dispatch_kernel(ex, send, recv, sends, recvs, local):
+    own = pltpu.make_async_copy(send.at[own_slots(ex)], recv.at[pl.ds(0, ex.slots)], local)
+    own.start()
     greet(ex.experts)
-    copies = out_copies(ex, 0, send, recv, sends, recvs)
-    copies += out_copies(ex, 1, send, recv, sends, recvs)
+    copies = []
+    for wave in range(len(ex.waves)):
+        copies += out_copies(ex, wave, send, recv, sends, recvs)
     for copy in copies:
         copy.start()
-    recv[0 : ex.slots, :] = send[own_slots(ex), :]
     for copy in copies:
         copy.wait()
+    own.wait()
 
 
 def dispatch_call(ex, rows):
-    vmem = pl.BlockSpec(memory_space=pltpu.VMEM)
+    far = pl.BlockSpec(memory_space=pl.ANY)
     return pl.pallas_call(
         functools.partial(dispatch_kernel, ex),
         out_shape=shape((ex.total, D), bf16),
-        in_specs=[vmem],
-        out_specs=vmem,
-        scratch_shapes=[pltpu.SemaphoreType.DMA((2, ex.experts - 1))] * 2,
+        in_specs=[far],
+        out_specs=far,
+        scratch_shapes=[pltpu.SemaphoreType.DMA((len(ex.waves), ex.experts - 1))] * 2
+        + [pltpu.SemaphoreType.DMA],
         compiler_params=pltpu.CompilerParams(
-            vmem_limit_bytes=8 << 20, collective_id=3, has_side_effects=True
+            vmem_limit_bytes=60 << 20, collective_id=3, has_side_effects=True
         ),
         cost_estimate=pl.CostEstimate(flops=35 * 10**9, bytes_accessed=10**6, transcendentals=0),
         name="dispatch",
@@ -796,8 +818,8 @@
     sends, recvs, backs, gots, local = refs
     traffic = Traffic()
     if mode == "forward":
-        traffic.sink(gates, gates_far, local.at[4:7])
-        traffic.sink(ups, ups_far, local.at[7:10])
+        traffic.sink(gates, gates_far, local.at[4:8])
+        traffic.sink(ups, ups_far, local.at[8:12])
 
     loads = [pltpu.make_async_copy(w_hbm, w, local.at[0])]
     if mode == "backward":
@@ -858,16 +880,27 @@
         if backward:
             out_g[rows, :] = acc_g[part, :].astype(bf16)
 
-    def send_back(wave):
-        ys = back_copies(ex, wave, 0, out_y, back_y, backs, gots) if forward else []
-        gs = back_copies(ex, wave, 1, out_g, back_g, backs, gots) if backward else []
-        for copy in ys + gs:
-            copy.start()
-        return ys, gs
-
+    def send_back(group):
+        for wave in group:
+            if forward:
+                ys.extend(back_copies(ex, wave, 0, out_y, back_y, backs, gots))
+                for copy in ys[1 - ex.experts :]:
+                    copy.start()
+        for wave in group:
+            if backward:
+                gs.extend(back_copies(ex, wave, 1, out_g, back_g, backs, gots))
+                for copy in gs[1 - ex.experts :]:
+                    copy.start()
+
+    ys, gs = [], []
+    groups = ((0,), (1,), (2,)) if mode == "forward" else ((0, 1), (2,))
     if backward:
-        waves = [out_copies(ex, n, send_g, recv_g, sends, recvs) for n in range(2)]
-        for copy in waves[0]:
+        arrivals = []
+        for group in groups:
+            arrivals.append([])
+            for wave in group:
+                arrivals[-1] += out_copies(ex, wave, send_g, recv_g, sends, recvs)
+        for copy in arrivals[0]:
             copy.start()
         recv_g[0 : ex.slots, :] = send_g[own_slots(ex), :]
         if mode == "backward":
@@ -877,20 +910,18 @@
         copy.wait()
     if backward:
         work(*ex.ranges[0])
-        for copy in waves[0]:
+        for copy in arrivals[0]:
             copy.wait_send()
-        for copy in waves[1]:
+        for copy in arrivals[1]:
             copy.start()
-        for copy in waves[0]:
+        for copy in arrivals[0]:
             copy.wait_recv()
-    work(*ex.ranges[1])
-    ys, gs = send_back(0)
-    if backward:
-        for copy in waves[1]:
-            copy.wait()
-    work(*ex.ranges[2])
-    more = send_back(1)
-    ys, gs = ys + more[0], gs + more[1]
+    for n, group in enumerate(groups):
+        if backward and n > 0:
+            for copy in arrivals[n]:
+                copy.wait()
+        work(*ex.span(group))
+        send_back(group)
     if mode == "forward":
         work(*ex.ranges[0])
     if forward:
@@ -927,16 +958,25 @@
 SPLIT = 13 * 128
 
 
-def cube_kernel(part, labels, g_ref, upper_ref, mix_ref, *refs):
-    outs, refs = refs[:7], refs[7:]
-    got_c, sums, got_a, got_b, half_a, half_b, end_a, end_b = refs[:8]
-    mine, quarters, ready, mix_held, mix_got, turn, send, recv, z_send, z_recv, mix_send, mix_recv = refs[8:]
-    mix_out = outs[6]
+def cube_kernel(part, labels, g_ref, upper_ref, mix_ref, ready, mix_out, own, *refs):
+    got_c, sums, got_a, got_b, half_a, half_b, end_a, end_b, mine, quarters, mix_held, mix_got = refs[:12]
+    send, recv, z_send, z_recv, mix_send, mix_recv, own_sem = refs[12:]
     me = lax.axis_index("shard")
     z = lax.axis_index("expert")
     owners = quarters.shape[1]
     core, x, y = lax.rem(me, 2), lax.rem(me // 2, 2), me // 4
     near, over_x, over_y = me + 1 - 2 * core, me + 2 - 4 * x, me + 4 - 8 * y
+    chips = [2 * (1 - y) + 1 - x, 2 * y + 1 - x, 2 * (1 - y) + x, 2 * y + x]
+
+    def rows(shard):
+        return pl.ds(pl.multiple_of(shard * part, 16), part)
+
+    loads = [
+        pltpu.make_async_copy(g_ref.at[rows(2 * chip + core)], own.at[n], own_sem.at[n])
+        for n, chip in enumerate(chips)
+    ]
+    for load in loads:
+        load.start()
     barrier = pltpu.get_barrier_semaphore()
     for other in (near, over_x, over_y):
         pl.semaphore_signal(barrier, inc=1, device_id={"shard": other}, device_id_type=MESH)
@@ -946,9 +986,6 @@
         )
     pl.semaphore_wait(barrier, 3 + owners - 1)
     cols_a, cols_b = slice(0, SPLIT), slice(SPLIT, W_ALL)
-
-    def rows(shard):
-        return pl.ds(pl.multiple_of(shard * part, 16), part)
 
     def remote(src, dst, send_sem, recv_sem, to):
         made = pltpu.make_async_remote_copy(
@@ -1022,7 +1059,6 @@
             for l in range(LAYERS):
                 mix_out[l] = total[l * 16 : l * 16 + labels, 0:labels]
 
-    chips = [2 * (1 - y) + 1 - x, 2 * y + 1 - x, 2 * (1 - y) + x, 2 * y + x]
     first = [
         copy(n, g_ref.at[rows(2 * chip + 1 - core)], got_c.at[chip], near)
         for n, chip in enumerate(chips)
@@ -1032,13 +1068,12 @@
     mine[1, :, W_ALL:] = jnp.zeros((part, 2 * SPLIT - W_ALL), bf16)
     mine[1, :, 0:W_ALL] = upper_ref[...]
     upper = spread(1)
-    turn[...] = jnp.zeros_like(turn)
 
     def merge(n):
         chip = chips[n]
+        loads[n].wait()
         first[n].wait_recv()
-        own = g_ref[rows(2 * chip + core), :].astype(f32)
-        sums[chip] = (own + got_c[chip].astype(f32)).astype(bf16)
+        sums[chip] = (own[n].astype(f32) + got_c[chip].astype(f32)).astype(bf16)
 
     def total(chip, cols, got):
         return sums[chip, :, cols].astype(f32) + got[...].astype(f32)
@@ -1075,14 +1110,12 @@
     mix.append(mix_start(3))
     for made in last_upper:
         made.wait_recv()
-    write_dense(part, labels, 1, ready.at[1], outs[:6], turn)
     mix_end(3, mix[3])
     mix.append(mix_start(4))
     last_lower = gather(0, lower)
     mix_end(4, mix[4])
     for made in last_lower:
         made.wait_recv()
-    write_dense(part, labels, 0, ready.at[0], outs[:6], turn)
     for made in first + [a0, b0, a1, b1, a2, b2] + mix + upper + lower + last_upper + last_lower:
         made.wait_send()
 
@@ -1091,14 +1124,15 @@
     vmem = pl.BlockSpec(memory_space=pltpu.VMEM)
     rest = W_ALL - SPLIT
     owners = lax.axis_size("expert")
-    outs = dense_shapes(part, labels) + [shape((LAYERS, labels, labels))]
+    outs = [shape((2, part, 2 * SPLIT), bf16), shape((LAYERS, labels, labels))]
     dma = pltpu.SemaphoreType.DMA
     return pl.pallas_call(
         functools.partial(cube_kernel, part, labels),
         out_shape=outs,
-        in_specs=[vmem] * 3,
+        in_specs=[pl.BlockSpec(memory_space=pl.ANY), vmem, vmem],
         out_specs=[vmem] * len(outs),
         scratch_shapes=[
+            pltpu.VMEM((4, part, W_ALL), bf16),
             pltpu.VMEM((4, part, W_ALL), bf16),
             pltpu.VMEM((4, part, W_ALL), bf16),
             pltpu.VMEM((2, part, SPLIT), bf16),
@@ -1109,19 +1143,18 @@
             pltpu.VMEM((part, rest), bf16),
             pltpu.VMEM((2, part, 2 * SPLIT), bf16),
             pltpu.VMEM((2, owners, part // 2, SPLIT), bf16),
-            pltpu.VMEM((2, part, 2 * SPLIT), bf16),
             pltpu.VMEM((5, 32, 128), f32),
             pltpu.VMEM((5, 32, 128), f32),
-            pltpu.VMEM((128, 128), f32),
             dma((10,)),
             dma((10,)),
             dma((2, 2, owners - 1)),
             dma((2, 2, owners - 1)),
             dma((5,)),
             dma((5,)),
+            dma((4,)),
         ],
         compiler_params=pltpu.CompilerParams(
-            vmem_limit_bytes=40 << 20, collective_id=4, has_side_effects=True
+            vmem_limit_bytes=60 << 20, collective_id=4, has_side_effects=True
         ),
         cost_estimate=pl.CostEstimate(flops=70 * 10**9, bytes_accessed=10**7, transcendentals=0),
         name="dense_sums",
@@ -1136,7 +1169,7 @@
     forward, backward = mode in ("forward", "both"), mode in ("backward", "both")
     flat, wide = shape((rows, D), bf16), shape((rows, ff), bf16)
     packed = (pack.shards, pack.rows, 256)
-    most = max(size for _, size in ex.ranges)
+    most = max(ex.slots, ex.span((0, 1))[1], ex.span((2,))[1])
     vmem = pl.BlockSpec(memory_space=pltpu.VMEM)
     far = pl.BlockSpec(memory_space=pl.ANY)
     in_specs = [vmem] * len(args)
@@ -1164,8 +1197,9 @@
         scratch += [pltpu.VMEM((D, rows), bf16), pltpu.VMEM((most, D), f32)]
         scratch += [pltpu.VMEM(a.shape, a.dtype) for a in args[-12:]]
     scratch.append(pltpu.VMEM(packed, bf16))
-    scratch += [pltpu.SemaphoreType.DMA((2, ex.experts - 1))] * 2
-    scratch += [pltpu.SemaphoreType.DMA((2, 2, ex.experts - 1))] * 2
+    count = len(ex.waves)
+    scratch += [pltpu.SemaphoreType.DMA((count, ex.experts - 1))] * 2
+    scratch += [pltpu.SemaphoreType.DMA((2, count, ex.experts - 1))] * 2
     scratch.append(pltpu.SemaphoreType.DMA((16,)))
     work = 6 * rows * D * ff * (1 if mode == "forward" else 2 if mode == "backward" else 3)
     return pl.pallas_call(
@@ -1186,8 +1220,26 @@
     )(*args)
 
 
-def expert_outputs_kernel(pack, traffic, first_ref, second_ref, gate_ref, up_ref, down_ref):
-    for l, ref in enumerate((first_ref, second_ref)):
+def write_dense(part, labels, l, ref, outs, turn):
+    proj_ref, out_ref, gain_ref, router_ref, vec_ref, const_ref = outs
+    for c in range(3):
+        proj_ref[l, c] = ref[:, c * D : (c + 1) * D].astype(f32)
+    out_ref[l] = ref[:, W_OUT:W_SMALL].astype(f32)
+    small = ref[:, W_SMALL:W_ALL].astype(f32)
+    turn[0:part, :] = small
+    rows = turn[...].T
+    router_ref[l] = rows[0:labels, 0:part]
+    for c in range(2):
+        const_ref[l, c] = rows[S_CONST + 2 * c : S_CONST + 2 * c + 2, 0:part]
+    gain_ref[l] = rows[S_GAIN : S_GAIN + 2, 0:part]
+    vec_ref[l] = rows[S_VEC : S_VEC + 2, 0:part]
+
+
+def outputs_kernel(pack, labels, traffic, low_ref, high_ref, dense_ref, hidden_ref, *refs):
+    gate_ref, up_ref, down_ref = refs[:3]
+    outs, hidden_out, turn = refs[3:9], refs[9], refs[10]
+    turn[...] = jnp.zeros_like(turn)
+    for l, ref in enumerate((low_ref, high_ref)):
         for n, out in enumerate((gate_ref, up_ref)):
             for j in range(pack.chunks):
                 at = (n * pack.chunks + j) * pack.padded
@@ -1195,35 +1247,14 @@
         for c in range(D // 256):
             at = pack.down + c * pack.own
             down_ref[l, :, c * 256 : (c + 1) * 256] = ref[at : at + pack.own, :].astype(f32)
-
-
-def expert_outputs(pack, grads):
-    wide = shape((LAYERS, pack.part, pack.ff))
-    outs = [wide, wide, shape((LAYERS, pack.own, D))]
-    body = functools.partial(expert_outputs_kernel, pack)
-    return whole_call(body, "expert_outputs", outs, [], grads, 10**6)
-
-
-def write_dense(part, labels, l, ref, outs, turn):
-    proj_ref, out_ref, gain_ref, router_ref, vec_ref, const_ref = outs
-    for c in range(3):
-        proj_ref[l, c] = ref[:, c * D : (c + 1) * D].astype(f32)
-    out_ref[l] = ref[:, W_OUT:W_SMALL].astype(f32)
-    small = ref[:, W_SMALL:W_ALL].astype(f32)
-    router_ref[l] = small[:, 0:labels]
-    for c in range(2):
-        const_ref[l, c] = small[:, S_CONST + 2 * c : S_CONST + 2 * c + 2]
-    turn[0:part, :] = small
-    rows = turn[...].T
-    gain_ref[l] = rows[S_GAIN : S_GAIN + 2, 0:part]
-    vec_ref[l] = rows[S_VEC : S_VEC + 2, 0:part]
-
-
-def dense_outputs_kernel(part, labels, traffic, first_ref, second_ref, *refs):
-    outs, turn = refs[:6], refs[6]
-    turn[...] = jnp.zeros_like(turn)
-    for l, ref in enumerate((first_ref, second_ref)):
-        write_dense(part, labels, l, ref, outs, turn)
+        for out in (gate_ref, up_ref, down_ref):
+            traffic.flush(out, l)
+        write_dense(pack.part, labels, l, dense_ref.at[l], outs, turn)
+        for out in outs[:2]:
+            traffic.flush(out, l)
+    traffic.need(hidden_ref)
+    hidden_out[...] = hidden_ref[...]
+    traffic.flush(hidden_out)
 
 
 def dense_shapes(part, labels):
@@ -1231,16 +1262,19 @@
         shape((LAYERS, 3, part, D)),
         shape((LAYERS, part, D)),
         shape((LAYERS, 2, part)),
-        shape((LAYERS, part, labels)),
+        shape((LAYERS, labels, part)),
         shape((LAYERS, 2, part)),
-        shape((LAYERS, 2, part, 2)),
+        shape((LAYERS, 2, 2, part)),
     ]
 
 
-def dense_outputs(part, labels, grads):
-    body = functools.partial(dense_outputs_kernel, part, labels)
-    outs = dense_shapes(part, labels)
-    return whole_call(body, "dense_outputs", outs, [pltpu.VMEM((128, 128), f32)], grads, 10**6)
+def outputs_call(pack, labels, grads, dense, hidden):
+    wide = shape((LAYERS, pack.part, pack.ff))
+    outs = [wide, wide, shape((LAYERS, pack.own, D))] + dense_shapes(pack.part, labels)
+    outs.append(shape(hidden.shape, hidden.dtype))
+    body = functools.partial(outputs_kernel, pack, labels)
+    turn = [pltpu.VMEM((128, 128), f32)]
+    return whole_call(body, "outputs", outs, turn, grads + [dense, hidden], 10**6, (3,), (0, 1, 2, 3, 4, 9))
 
 
 def on_device(
@@ -1301,13 +1335,16 @@
     chosen_rows = [jnp.pad(hits[l].T, [(0, 16 - total_experts), (0, 0)]) for l in range(LAYERS)]
     loaded = jnp.concatenate([hits[l, :, :experts] for l in range(LAYERS)], axis=1)
     loaded_half = loaded.astype(bf16)
-    rank_col = dot(earlier, loaded_half)
     rank_row = lax.dot_general(
         loaded_half, earlier, (((0,), (1,)), ((), ())), preferred_element_type=f32
     )
-    slot_col_all = jnp.where((loaded > 0) & (rank_col < capacity), rank_col, -1.0)
     slot_row_all = jnp.where((loaded.T > 0) & (rank_row < capacity), rank_row, -1.0)
-    slot_col = [slot_col_all[:, l * experts : (l + 1) * experts] for l in range(LAYERS)]
+    slot_col = []
+    for l in range(LAYERS):
+        rank_col = dot(earlier, hits[l, :, :experts].astype(bf16))
+        slot_col.append(
+            jnp.where((hits[l, :, :experts] > 0) & (rank_col < capacity), rank_col, -1.0)
+        )
     slot_row = [
         jnp.pad(
             slot_row_all[l * experts : (l + 1) * experts],
@@ -1403,16 +1440,15 @@
 
     if pack.shards == 8 and experts == 4:
         mix = jnp.pad(jnp.concatenate(mix_grads), [(0, 0), (0, 112)])
-        dense_outs = finish_call(part, total_experts, d_dense, dense_grads[1], mix)
-        mixing_grad = dense_outs[6]
+        dense_sums, mixing_grad = finish_call(part, total_experts, d_dense, dense_grads[1], mix)
     else:
         dense_grads[0] = lax.psum_scatter(d_dense, "shard", scatter_dimension=0, tiled=True)
-        both_dense = lax.psum(jnp.stack(dense_grads), "expert")
+        dense_sums = lax.psum(jnp.stack(dense_grads), "expert")
         mixing_grad = lax.psum(jnp.stack(mix_grads), ("expert", "shard"))
         mixing_grad = mixing_grad[:, 0:total_experts, 0:total_experts]
-        dense_outs = dense_outputs(part, total_experts, [both_dense[l] for l in range(LAYERS)])
-    project_grad, output_grad, gain_grad, router_grad, vector_grad, const_grad = dense_outs[:6]
-    gate_grad, up_grad, down_grad = expert_outputs(pack, expert_grads)
+    made = outputs_call(pack, total_experts, expert_grads, dense_sums, hidden_out)
+    gate_grad, up_grad, down_grad, project_grad, output_grad = made[:5]
+    gain_grad, router_grad, vector_grad, const_grad, hidden_out = made[5:]
     return (
         hidden_out,
         gx,
@@ -1420,10 +1456,10 @@
         project_grad,
         output_grad,
         gain_grad,
-        router_grad,
+        router_grad.transpose(0, 2, 1),
         mixing_grad,
         vector_grad,
-        const_grad,
+        const_grad.transpose(0, 1, 3, 2),
         gate_grad[:, None],
         up_grad[:, None],
         down_grad[:, None],

time: 620 us -> 595 us (0.960)
  local copies, waits for them, and re-layouts: 35.4 us -> 19.7 us
  Pallas kernels: 531 us -> 517 us
    unnamed x61 -> x43, local copies, waits for them, and re-layouts: 22.7 us -> 8.81 us
    pallas_call x5, Pallas kernels: 161 us -> 149 us  [whole_call(): pl.pallas_call(kernel, out_shape=outs, in_specs=[far if n in late else ne...]
  transfers between devices with their start and end apart: 7 -> 7, of which waited for: 1 -> 2; matrix products, arithmetic and copies ran while one was open for 3% -> 4% of each run, Pallas kernels for 68% -> 68%
where the time goes in v8:
time: 595 us; the launch traced here: 590 us
  Pallas kernels  517 us (87%)
  waiting for transfers between devices  26.7 us (4%)
  local copies, waits for them, and re-layouts  19.7 us (3%)
  between operations  14.9 us (3%)
  other arithmetic  7.32 us (1%)
    pallas_call x3, Pallas kernels, exchange_call(): pl.pallas_call(functools.partial(exchange_kernel, mode, pack, ex), out_sh...  223 us
    pallas_call x5, Pallas kernels, whole_call(): pl.pallas_call(kernel, out_shape=outs, in_specs=[far if n in late else ne...  149 us
    pallas_call x1, Pallas kernels, finish_call(): pl.pallas_call(functools.partial(cube_kernel, part, labels), out_shape=ou...  79.1 us
    pallas_call x2, Pallas kernels, dispatch_call(): pl.pallas_call(functools.partial(dispatch_kernel, ex), out_shape=shape((e...  66.1 us
    all_gather x2, waiting for transfers between devices, on_device(): dense.append(lax.all_gather(packed, 'shard', axis=0, tiled=True))  22.3 us
  transfers between devices with their start and end apart: 7, of which 2 were waited for; matrix products, arithmetic and copies ran while one was open for 4% of the time, Pallas kernels for 68%

profile of v8, /device:TPU:0, one launch (start us, length us, event | category | flops | bytes accessed | tf_op | source)
XLA Modules:
  0.0 589.8 jit_solution(14374466138687704824)
XLA Ops:
  7.2 0.8 slice_bitcast_fusion.9
  8.0 0.7 slice_bitcast_fusion.5
  8.7 0.7 slice_bitcast_fusion.7
  9.6 1.0 bitcast_dynamic-update-slice_fusion.3
  10.6 1.0 bitcast_dynamic-update-slice_fusion.2
  11.7 1.1 bitcast_dynamic-update-slice_fusion.1
  12.7 1.0 bitcast_dynamic-update-slice_fusion
  13.8 0.8 copy-done.1
  15.2 0.7 copy-done.4
  15.9 0.2 copy.195
  16.1 0.2 copy.177
  16.3 1.1 pad_maximum_fusion
  17.7 0.8 copy-done
  18.9 0.2 copy.196
  19.1 0.2 copy.185
  19.3 1.1 pad_maximum_fusion.1
  20.6 0.6 fusion.58
  21.2 0.7 copy.181.refs_9_
  21.8 0.6 fusion.57
  22.4 0.7 copy.173.refs_4_
  23.1 0.6 pad.44.refs_3_.refs_14_
  23.7 0.6 pad.51.refs_10_.refs_8_
  24.4 0.6 pad.46.refs_5_.refs_11_
  25.0 0.2 copy.193
  25.3 0.2 copy.194
  25.8 1.3 broadcast_select_fusion
  27.1 0.6 pad.52.refs_11_.refs_6_
  27.8 1.4 and_select_fusion.1.refs_4_.refs_3_
  29.2 1.4 and_select_fusion.refs_14_.refs_3_
  30.6 4.3 fusion.9
  34.9 22.3 %all-gather.7.cloned.1.call-done.refs_1_.refs_6_ = bf16[768,3200]{1,0:T(8,128)(2,1)} async-done(((bf16[96,3200]{1,0:T(8,128)(2,1)}), bf16[768,3200]{1,0:T(8,128)(2,1)}) %all-gather.7.cloned.1.call-update) | async-done | bytes 4915216 | tf_op jit(solution)/shard_map/all_gather | solution.py:1327
  57.2 22.4 %block_forward.2 = (bf16[832,768]{1,0:T(8,128)(2,1)}, bf16[832,2304]{1,0:T(8,128)(2,1)}, bf16[832,768]{1,0:T(8,128)(2,1)}, f32[16,832]{1,0:T(8,128)}, f32[832,76...) custom-call(bf16[832,768]{1,0:T(8,128)(2,1)} %refs_9_.1, ...), custom_call_target="tpu_custom_call" | custom-call | flops 20000000000 | bytes 21816320 | tf_op jit(solution)/shard_map/block_forward/pallas_call | solution.py:335
  79.6 1.4 slice.130.refs_8_.refs_11_
  81.1 33.2 %dispatch.2.refs_0_ = bf16[960,768]{1,0:T(8,128)(2,1)} custom-call(bf16[960,768]{1,0:T(8,128)(2,1)} %get-tuple-element.77.send), custom_call_target="tpu_custom_call" | custom-call | flops 35000000512 | bytes 1000000 | tf_op jit(solution)/shard_map/dispatch/pallas_call | solution.py:780
  114.3 4.3 all-gather.11.cloned.1.call-done
  118.5 46.0 %experts_forward.1 = (bf16[960,768]{1,0:T(8,128)(2,1)}, bf16[960,2048]{1,0:T(8,128)(2,1)}, bf16[960,2048]{1,0:T(8,128)(2,1)}) custom-call(bf16[960,768]{1,0:T(8,128)(2,1)} %dispatch.2.refs_0_, bf16[8,2304,256]{2,1,0:T(8,128)(2,1)} %bitcast.129), custom_call_target="tpu_custom_call" | custom-call | flops 49059696640 | bytes 9437184 | tf_op jit(solution)/shard_map/experts_forward/pallas_call | solution.py:1205
  164.6 30.5 %block_forward.3 = (f32[832,768]{1,0:T(8,128)}, bf16[832,768]{1,0:T(8,128)(2,1)}, bf16[832,2304]{1,0:T(8,128)(2,1)}, bf16[832,768]{1,0:T(8,128)(2,1)}, f32[16,83...) custom-call(f32[832,768]{1,0:T(8,128)} %get-tuple-element.78.refs_0_, ...), custom_call_target="tpu_custom_call" | custom-call | flops 20000000000 | bytes 33265664 | tf_op jit(solution)/shard_map/block_forward/pallas_call | solution.py:335
  195.1 32.9 %dispatch.3.refs_0_ = bf16[960,768]{1,0:T(8,128)(2,1)} custom-call(bf16[960,768]{1,0:T(8,128)(2,1)} %get-tuple-element.84.send), custom_call_target="tpu_custom_call" | custom-call | flops 35000000512 | bytes 1000000 | tf_op jit(solution)/shard_map/dispatch/pallas_call | solution.py:780
  228.0 108.4 %experts_both.1 = (bf16[960,768]{1,0:T(8,128)(2,1)}, bf16[960,768]{1,0:T(8,128)(2,1)}, bf16[8,2304,256]{2,1,0:T(8,128)(2,1)}, f32[832,768]{1,0:T(8,128)}, f32[32...) custom-call(bf16[960,768]{1,0:T(8,128)(2,1)} %dispatch.3.refs_0_, ...), custom_call_target="tpu_custom_call" | custom-call | flops 67179089920 | bytes 9437184 | tf_op jit(solution)/shard_map/experts_both/pallas_call | solution.py:1205
  336.5 46.6 %block_backward.2 = (f32[832,768]{1,0:T(8,128)}, bf16[768,3200]{1,0:T(8,128)(2,1)}, bf16[960,768]{1,0:T(8,128)(2,1)}, bf16[960,768]{1,0:T(8,128)(2,1)}) custom-call(bf16[832,768]{1,0:T(8,128)(2,1)} %refs_0_.3, f32[832,768]{1,0:T(8,128)} %get-tuple-element.94.refs_1_, bf16[960,768]{1,0:T(8,128)(2,1)} %get-tuple-element.95.refs_2_, ...), custom_call_target="tpu_custom_call" | custom-call | flops 40000000000 | bytes 35318784 | tf_op jit(solution)/shard_map/block_backward/pallas_call | solution.py:335
  383.1 68.6 %experts_backward.1 = (bf16[960,768]{1,0:T(8,128)(2,1)}, bf16[8,2304,256]{2,1,0:T(8,128)(2,1)}, f32[832,768]{1,0:T(8,128)}, f32[32,768]{1,0:T(8,128)}, f32[16,16]{1,0:T(8,128)}, /*index=5*/f32[16,832]{1,0:T(8,128)}) custom-call(bf16[960,768]{1,0:T(8,128)(2,1)} %dispatch.2.refs_0_, bf16[8,2304,256]{2,1,0:T(8,128)(2,1)} %bitcast.130, ...), custom_call_target="tpu_custom_call" | custom-call | flops 1000000000 | bytes 9437184 | tf_op jit(solution)/shard_map/experts_backward/pallas_call | solution.py:1205
  451.8 0.6 copy-done.10
  452.5 0.6 select_maximum_fusion.mix_ref
  453.1 0.6 slice_bitcast_fusion.2
  453.7 42.9 %block_backward.3 = (f32[832,768]{1,0:T(8,128)}, bf16[768,3200]{1,0:T(8,128)(2,1)}) custom-call(f32[832,768]{1,0:T(8,128)} %get-tuple-element.106.refs_5_.refs_0_, f32[832,768]{1,0:T(8,128)} %get-tuple-element.115.refs_1_, bf16[960,768]{1,0:T(8,128)(2,1)} %get-tuple-element.116.refs_2_, f32[832,4]{1,0:T(8,128)} %and_select_fusion.1.refs_4_.refs_3_, ...), custom_call_target="tpu_custom_call" | custom-call | flops 40000000000 | bytes 32130048 | tf_op jit(solution)/shard_map/block_backward/pallas_call | solution.py:335
  496.6 79.1 %dense_sums.1 = (bf16[2,96,3328]{2,1,0:T(8,128)(2,1)}, f32[2,8,8]{2,1,0:T(8,128)}) custom-call(bf16[768,3200]{1,0:T(8,128)(2,1)} %get-tuple-element.122.g_ref, bf16[96,3200]{1,0:T(8,128)(2,1)} %reduce-scatter.8.cloned.1.call-done.upper_ref, f32[32,128]{1,0:T(8,128)} %select_maximum_fusion.mix_ref), custom_call_target="tpu_custom_call" | custom-call | flops 70000001024 | bytes 10000000 | tf_op jit(solution)/shard_map/dense_sums/pallas_call | solution.py:1129
  575.7 6.3 %outputs.1 = (f32[2,96,2048]{2,1,0:T(8,128)}, f32[2,96,2048]{2,1,0:T(8,128)}, f32[2,256,768]{2,1,0:T(8,128)}, f32[2,3,96,768]{3,2,1,0:T(8,128)}, f32[2,96,768]{2...) custom-call(bf16[2304,256]{1,0:T(8,128)(2,1)} %bitcast.150, ...), custom_call_target="tpu_custom_call" | custom-call | flops 1000000 | bytes 13283328 | tf_op jit(solution)/shard_map/outputs/pallas_call | solution.py:335
  582.1 0.6 copy.210
  (77 shorter events, 2.3 us)
Async XLA Ops:
  7.2 7.5 %copy-start.2 = (bf16[2,1,96,2048]{3,2,1,0:T(8,128)(2,1)S(1)}, bf16[2,1,96,2048]{3,2,1,0:T(8,128)(2,1)}, u32[]{:S(2)}) copy-start(bf16[2,1,96,2048]{3,2,1,0:T(8,128)(2,1)} %param.25) | copy-start | bytes 2359300
  7.2 50.0 %all-gather.7.cloned.1.call-start = ((), (), s32[]{:S(2)}) async-start(), calls=%async_computation.3 | async-start | bytes 5529600 | tf_op jit(solution)/shard_map/all_gather | solution.py:1327
  11.6 3.3 copy-start.3
  13.8 0.8 copy-start.1
  14.6 103.9 %all-gather.11.cloned.1.call-start = ((), (), s32[]{:S(2)}) async-start(), calls=%async_computation.8 | async-start | bytes 10616832 | tf_op jit(solution)/shard_map/all_gather | solution.py:1329
  14.7 1.1 copy-start.4
  17.4 147.2 %all-gather.9.cloned.1.call-start = ((), (), s32[]{:S(2)}) async-start(), calls=%async_computation.4 | async-start | bytes 5529600 | tf_op jit(solution)/shard_map/all_gather | solution.py:1327
  17.7 0.8 copy-start
  18.5 209.5 %all-gather.13.cloned.1.call-start = ((), (), s32[]{:S(2)}) async-start(), calls=%async_computation.9 | async-start | bytes 10616832 | tf_op jit(solution)/shard_map/all_gather | solution.py:1329
  19.1 1.4 copy-start.7
  19.1 1.5 copy-start.8
  19.1 4.0 copy-start.5
  20.4 5.3 copy-start.12
  20.4 5.4 copy-start.14
  20.4 7.3 %copy-start.13 = (s32[1,8]{1,0:T(1,128)S(1)}, s32[1,8]{1,0:T(1,128)}, u32[]{:S(2)}) copy-start(s32[1,8]{1,0:T(1,128)} %param.30) | copy-start | bytes 100
  20.4 433.3 %reduce-scatter.6.cloned.1.call-start = ((), (), s32[]{:S(2)}) async-start(), calls=%async_computation.6 | async-start | bytes 10616832 | tf_op jit(solution)/shard_map/reduce_scatter | solution.py:1427
  336.4 160.2 %reduce-scatter.8.cloned.1.call-start = ((), (), s32[]{:S(2)}) async-start(), calls=%async_computation.7 | async-start | bytes 5529600 | tf_op jit(solution)/shard_map/reduce_scatter | solution.py:1439
  383.1 192.6 %reduce-scatter.4.cloned.1.call-start = ((), (), s32[]{:S(2)}) async-start(), calls=%async_computation.5 | async-start | bytes 10616832 | tf_op jit(solution)/shard_map/reduce_scatter | solution.py:1427
  451.8 0.7 copy-start.10
  451.8 0.7 copy-start.11
  451.8 1.3 copy-start.6
  575.7 6.4 %copy-start.9 = (f32[2,8,8]{2,1,0:T(8,128)S(1)}, f32[2,8,8]{2,1,0:T(8,128)}, u32[]{:S(2)}) copy-start(f32[2,8,8]{2,1,0:T(8,128)} %get-tuple-element.268) | copy-start | bytes 1540
Sparse Core Ops, SparseCore 0:
  14.7 42.4 all-gather.6
  59.7 58.8 all-gather.10
  121.0 39.7 all-gather.8
  162.5 58.8 all-gather.12
  336.5 74.3 reduce-scatter.5
  414.3 54.8 reduce-scatter.7
  473.1 96.7 reduce-scatter.3

commit v9 on v8

--- a/solution.py
+++ b/solution.py
@@ -100,7 +100,8 @@
 def send_grads(hot, gx, gpack, gxs_ref, gy_ref, experts, slots):
     got = dot(hot, gx)
     gates = dot(hot, gpack)
-    gxs_ref[...] = got.astype(bf16)
+    if gxs_ref is not None:
+        gxs_ref[...] = got.astype(bf16)
     for e in range(experts):
         rows = slice(e * slots, (e + 1) * slots)
         gate = gates[rows, e : e + 1] + gates[rows, 64 + e : 65 + e]
@@ -134,7 +135,7 @@
     small_out = refs.pop(0)
     small_out[...] = w_ref[:, W_SMALL:]
     if last:
-        gxs_ref, gy_ref = refs.pop(0), refs.pop(0)
+        gy_ref = refs.pop(0)
     lse_cols, turn = refs
     tokens = n1_ref.shape[0]
     size, block = row_blocks(tokens)
@@ -261,7 +262,7 @@
     send_ref[...] = dot(hot, n2).astype(bf16)
     if last:
         traffic.need(cot_ref)
-        send_grads(hot, cot_ref[...], gpack, gxs_ref, gy_ref, experts, slots)
+        send_grads(hot, cot_ref[...], gpack, None, gy_ref, experts, slots)
 
 
 def shape(dims, dtype=f32):
@@ -305,7 +306,7 @@
 FLUSHES = 3
 
 
-def whole_call(body, name, outs, scratch, args, flops, late=(), early=()):
+def whole_call(body, name, outs, scratch, args, flops, late=(), early=(), raw=(), collective=None):
     moved = sum(a.size * a.dtype.itemsize for a in args) + sum(
         o.size * o.dtype.itemsize for o in outs
     )
@@ -335,10 +336,14 @@
     return pl.pallas_call(
         kernel,
         out_shape=outs,
-        in_specs=[far if n in late else near for n in range(len(args))],
+        in_specs=[far if n in late or n in raw else near for n in range(len(args))],
         out_specs=[far if n in early else near for n in range(len(outs))],
         scratch_shapes=list(scratch) + buffers,
-        compiler_params=pltpu.CompilerParams(vmem_limit_bytes=VMEM),
+        compiler_params=pltpu.CompilerParams(
+            vmem_limit_bytes=VMEM,
+            collective_id=collective,
+            has_side_effects=collective is not None,
+        ),
         cost_estimate=pl.CostEstimate(flops=flops, bytes_accessed=moved, transcendentals=0),
         name=name,
     )(*args)
@@ -362,7 +367,7 @@
         shape((D, 128), bf16),
     ]
     if last:
-        outs += [shape((sent, D), bf16), shape((sent, D), bf16)]
+        outs += [shape((sent, D), bf16)]
     padded = -(-tokens // 128) * 128
     scratch = [pltpu.VMEM((tokens, 128), f32), pltpu.VMEM((128, padded), f32)]
     body = functools.partial(forward_kernel, first, last, experts, slots)
@@ -372,33 +377,42 @@
     return whole_call(body, "block_forward", outs, scratch, args, 20 * 10**9, late, early)
 
 
+def row_dots(a, b):
+    ones = jnp.ones((16, D), bf16)
+    upper, lower = split_bf16(a.astype(f32) * b.astype(f32))
+    return (dot_nt(ones, upper) + dot_nt(ones, lower))[0:8, :]
+
+
 def gating_kernel(last, experts, slots, *refs):
     refs = list(refs)
-    gx_ref, n2_ref, y_ref, gxs_ref, slotr_ref, info_ref, chosen_ref, gcol_ref, small_ref = [
-        refs.pop(0) for _ in range(9)
+    gx_ref, n2_ref = refs.pop(0), refs.pop(0)
+    if last:
+        dots_ref = refs.pop(0)
+    else:
+        y_ref, gxs_ref = refs.pop(0), refs.pop(0)
+    slotr_ref, info_ref, chosen_ref, gcol_ref, small_ref, z_ref, mix_ref = [
+        refs.pop(0) for _ in range(7)
     ]
-    z_ref, mix_ref = refs.pop(0), refs.pop(0)
-    if last:
-        mid_ref, slotc_ref = refs.pop(0), refs.pop(0)
-    else:
+    if not last:
         gz_ref = refs.pop(0)
-    gn2_ref, gsm_ref, gmix_ref, gprev_ref = [refs.pop(0) for _ in range(4)]
-    if last:
-        out_ref = refs.pop(0)
+    gn2_ref, gsm_ref, gmix_ref, gprev_ref = refs
     tokens = n2_ref.shape[0]
     size, block = row_blocks(tokens)
     small = small_ref[...].astype(f32).T
     small_half = small[0:32, :].astype(bf16)
-    vectors = small[S_VEC : S_VEC + 2, :]
     slot_row = slotr_ref[...]
     ones = jnp.ones((16, D), bf16)
     row = lax.broadcasted_iota(jnp.int32, (16, slots), 0)
     scattered = jnp.zeros((16, tokens), f32)
     for e in range(experts):
-        rows = slice(e * slots, (e + 1) * slots)
-        inner = y_ref[rows, :].astype(f32) * gxs_ref[rows, :].astype(f32)
-        upper, lower = split_bf16(inner)
-        sums = dot_nt(ones, upper) + dot_nt(ones, lower)
+        if last:
+            half = Exchange(experts, slots).half
+            sums = jnp.concatenate(
+                [dots_ref[0, e, 0:1, 0:half], dots_ref[1, e, 0:1, 0 : slots - half]], axis=1
+            )
+        else:
+            rows = slice(e * slots, (e + 1) * slots)
+            sums = row_dots(y_ref[rows, :], gxs_ref[rows, :])[0:1, :]
         upper, lower = split_bf16(sums)
         lhs = jnp.where(row == e, upper.astype(f32), 0.0) + jnp.where(
             row == 8 + e, lower.astype(f32), 0.0
@@ -415,7 +429,9 @@
     gates = prob * chosen
     trow = lax.broadcasted_iota(jnp.int32, (16, tokens), 0)
     gp = jnp.concatenate([scattered[0:8, :] + scattered[8:16, :], jnp.zeros((8, tokens), f32)], 0)
-    gp = jnp.where(trow == experts + 1, gx_n2, jnp.where(trow < experts, gp, 0.0))
+    weighted = gp if last else prob * gp
+    weighted = jnp.where(trow < experts, weighted, 0.0) * chosen
+    gp = jnp.where(trow == experts + 1, gx_n2, 0.0)
     crow = lax.broadcasted_iota(jnp.int32, (8, tokens), 0)
     glog = jnp.zeros((8, tokens), f32)
     coefs = jnp.zeros((8, tokens), f32)
@@ -428,8 +444,8 @@
         gl = share * (gx_n2 - gx_v) * a0 * a1
         glog = jnp.where(crow == 2 * c, gl, jnp.where(crow == 2 * c + 1, -gl, glog))
         coefs = jnp.where(crow == c, share * a1, coefs)
-    gp = gp * chosen
-    gz = prob * (gp - jnp.sum(prob * gp, axis=0, keepdims=True))
+    weighted = weighted + prob * gp * chosen
+    gz = weighted - prob * jnp.sum(weighted, axis=0, keepdims=True)
     if not last:
         gz = gz + gz_ref[...]
     z = z_ref[...]
@@ -457,21 +473,14 @@
     def add(i, carry):
         rows = block(i)
         gn2_ref[rows, :] = gn2_ref[rows, :] + gcol_ref[rows, 16:17] * gx_ref[rows, :].astype(f32)
-        if last:
-            out_ref[rows, :] = combine_rows(
-                rows, mid_ref, n2_ref, y_ref, gcol_ref, slotc_ref, vectors, experts, slots
-            ).astype(bf16)
         return carry
 
     lax.fori_loop(0, BLOCKS, add, 0)
 
 
-def gating_outputs(last):
+def gating_outputs():
     tokens = TREE
-    outs = [shape((tokens, D)), shape((32, D)), shape((16, 16)), shape((16, tokens))]
-    if last:
-        outs += [shape((tokens, D), bf16)]
-    return outs
+    return [shape((tokens, D)), shape((32, D)), shape((16, 16)), shape((16, tokens))]
 
 
 def backward_kernel(first, experts, slots, traffic, *refs):
@@ -482,10 +491,24 @@
     biast_ref, lse_ref, gsm_ref = [refs.pop(0) for _ in range(3)]
     if not first:
         slotr_ref, gpack_ref = refs.pop(0), refs.pop(0)
+        y_held, n2_ref, gcol_ref = refs.pop(0), refs.pop(0), refs.pop(0)
     gout_ref, dw_ref = refs.pop(0), refs.pop(0)
     if not first:
-        gxs_ref, gy_ref = refs.pop(0), refs.pop(0)
-    gatt, go, gqkv, turn = refs
+        gxs_ref, gy_ref, hidden_out = refs.pop(0), refs.pop(0), refs.pop(0)
+    gatt, go, gqkv, turn = refs[:4]
+    if not first:
+        y_home, y_sends, y_recvs, y_local = refs[4:]
+        ex = Exchange(experts, slots)
+        own = pltpu.make_async_copy(
+            y_held.at[pl.ds(0, slots)], y_home.at[own_slots(ex)], y_local
+        )
+        own.start()
+        greet(experts)
+        returning = []
+        for wave in range(len(ex.waves)):
+            returning += back_copies(ex, wave, 0, y_held, y_home, y_sends, y_recvs)
+        for copy in returning:
+            copy.start()
     tokens = n1_ref.shape[0]
     size, block = row_blocks(tokens)
     small = w_ref[:, W_SMALL:].astype(f32).T
@@ -615,6 +638,20 @@
     if not first:
         hot = all_one_hot(slotr_ref[...], experts, slots)
         send_grads(hot, gatt[...], gpack_ref[...], gxs_ref, gy_ref, experts, slots)
+        own.wait()
+        for copy in returning:
+            copy.wait()
+        traffic.need(n2_ref, gcol_ref)
+        vectors = small[S_VEC : S_VEC + 2, :]
+
+        def home(i, carry):
+            rows = block(i)
+            hidden_out[rows, :] = combine_rows(
+                rows, mid_ref, n2_ref, y_home, gcol_ref, slotc_ref, vectors, experts, slots
+            ).astype(bf16)
+            return carry
+
+        lax.fori_loop(0, BLOCKS, home, 0)
 
 
 def backward_call(first, experts, slots, args):
@@ -622,7 +659,7 @@
     sent = experts * slots
     outs = [shape((tokens, D)), shape((D, W_ALL), bf16)]
     if not first:
-        outs += [shape((sent, D), bf16), shape((sent, D), bf16)]
+        outs += [shape((sent, D), bf16)] * 2 + [shape((tokens, D), bf16)]
     padded = -(-tokens // 128) * 128
     scratch = [
         pltpu.VMEM((tokens, D), bf16),
@@ -631,8 +668,16 @@
         pltpu.VMEM((padded, 128), f32),
     ]
     body = functools.partial(backward_kernel, first, experts, slots)
+    late = (5, 7, 8, 9, 10, 11)
+    if first:
+        return whole_call(body, "block_backward", outs, scratch, args, 40 * 10**9, late, (0, 1))
+    count = len(Exchange(experts, slots).waves)
+    scratch.append(pltpu.VMEM((sent, D), bf16))
+    scratch += [pltpu.SemaphoreType.DMA((1, count, experts - 1))] * 2
+    scratch.append(pltpu.SemaphoreType.DMA)
+    late += (16, 17)
     return whole_call(
-        body, "block_backward", outs, scratch, args, 40 * 10**9, (5, 7, 8, 9, 10, 11), (0, 1)
+        body, "block_backward", outs, scratch, args, 40 * 10**9, late, (0, 1), (15,), 5
     )
 
 
@@ -687,6 +732,7 @@
         self.experts, self.slots = experts, slots
         half = -(-slots // 32) * 16
         quarter = -(-half // 32) * 16
+        self.half = half
         edges = (0, quarter, half, slots)
         self.waves = tuple((low, high - low) for low, high in zip(edges[:-1], edges[1:]))
         self.ranges = [(0, slots)]
@@ -801,19 +847,26 @@
         send_g = refs.pop(0)
         if mode == "backward":
             gate_hbm, up_hbm = refs.pop(0), refs.pop(0)
-        gating_far = [refs.pop(0) for _ in range(12)]
-    if forward:
+        inputs = 9 if mode == "both" else 12
+        gating_far = [refs.pop(0) for _ in range(inputs)]
+    if mode == "forward":
         back_y = refs.pop(0)
+    if mode == "both":
+        out_y = refs.pop(0)
     if mode == "forward":
         gates_far, ups_far, gates, ups = [refs.pop(0) for _ in range(4)]
     else:
         back_g, dw_far = refs.pop(0), refs.pop(0)
-        gating_outs = [refs.pop(0) for _ in range(5 if mode == "both" else 4)]
+        gating_outs = [refs.pop(0) for _ in range(4)]
+    if mode == "forward":
+        out_y = refs.pop(0)
     if forward:
-        out_y, acc_y = refs.pop(0), refs.pop(0)
+        acc_y = refs.pop(0)
     if backward:
         recv_g, out_g, hids, gates, ups, rows_t, acc_g = [refs.pop(0) for _ in range(7)]
-        gating = [refs.pop(0) for _ in range(12)]
+        gating = [refs.pop(0) for _ in range(inputs)]
+    if mode == "both":
+        dots_out, dots, dots_send, dots_recv = [refs.pop(0) for _ in range(4)]
     w = refs.pop(0)
     sends, recvs, backs, gots, local = refs
     traffic = Traffic()
@@ -880,9 +933,31 @@
         if backward:
             out_g[rows, :] = acc_g[part, :].astype(bf16)
 
+    def send_dots(n, group):
+        me = lax.axis_index("expert")
+        for d in range(1, ex.experts):
+            pieces = []
+            for wave in group:
+                here = ex.held(wave, d)
+                pieces.append(row_dots(out_y[here, :], recv_g[here, :]))
+            size = sum(ex.waves[wave][1] for wave in group)
+            if size < 128:
+                pieces.append(jnp.zeros((8, 128 - size), f32))
+            dots_out[n, d - 1] = jnp.concatenate(pieces, axis=1)
+            copy = pltpu.make_async_remote_copy(
+                src_ref=dots_out.at[n, d - 1],
+                dst_ref=dots.at[n, me],
+                send_sem=dots_send.at[n, d - 1],
+                recv_sem=dots_recv.at[n, d - 1],
+                device_id={"expert": lax.rem(me + ex.experts - d, ex.experts)},
+                device_id_type=MESH,
+            )
+            copy.start()
+            dot_copies.append(copy)
+
     def send_back(group):
         for wave in group:
-            if forward:
+            if mode == "forward":
                 ys.extend(back_copies(ex, wave, 0, out_y, back_y, backs, gots))
                 for copy in ys[1 - ex.experts :]:
                     copy.start()
@@ -892,7 +967,7 @@
                 for copy in gs[1 - ex.experts :]:
                     copy.start()
 
-    ys, gs = [], []
+    ys, gs, dot_copies = [], [], []
     groups = ((0,), (1,), (2,)) if mode == "forward" else ((0, 1), (2,))
     if backward:
         arrivals = []
@@ -910,6 +985,11 @@
         copy.wait()
     if backward:
         work(*ex.ranges[0])
+        if mode == "both":
+            own_dots = row_dots(out_y[0 : ex.slots, :], recv_g[0 : ex.slots, :])
+            me = lax.axis_index("expert")
+            dots[0, me, :, 0 : ex.half] = own_dots[:, 0 : ex.half]
+            dots[1, me, :, 0 : ex.slots - ex.half] = own_dots[:, ex.half :]
         for copy in arrivals[0]:
             copy.wait_send()
         for copy in arrivals[1]:
@@ -921,10 +1001,11 @@
             for copy in arrivals[n]:
                 copy.wait()
         work(*ex.span(group))
+        if mode == "both":
+            send_dots(n, group)
         send_back(group)
     if mode == "forward":
         work(*ex.ranges[0])
-    if forward:
         back_y[own_slots(ex), :] = out_y[0 : ex.slots, :]
     if backward:
         back_g[own_slots(ex), :] = out_g[0 : ex.slots, :]
@@ -943,11 +1024,11 @@
         lax.fori_loop(0, pack.chunks, weights, 0)
         leaving = pltpu.make_async_copy(dw, dw_far, local.at[3])
         leaving.start()
-    for copy in ys:
+    for copy in ys + dot_copies:
         copy.wait()
     if mode == "both":
         traffic.need(*gating)
-        gating_kernel(True, ex.experts, ex.slots, *gating[:2], back_y, *gating[2:], *gating_outs)
+        gating_kernel(True, ex.experts, ex.slots, *gating[:2], dots, *gating[2:], *gating_outs)
     for copy in gs:
         copy.wait()
     if backward:
@@ -1178,24 +1259,31 @@
     if mode == "forward":
         outs = [flat, wide, wide]
     elif mode == "both":
-        outs = [flat, flat, shape(packed, bf16)] + gating_outputs(True)
+        outs = [flat, flat, shape(packed, bf16)] + gating_outputs()
     else:
         in_specs[3] = in_specs[4] = far
-        outs = [flat, shape(packed, bf16)] + gating_outputs(False)
+        outs = [flat, shape(packed, bf16)] + gating_outputs()
     out_specs = [vmem] * len(outs)
     if mode == "forward":
         out_specs[1] = out_specs[2] = far
         scratch += [pltpu.VMEM((rows, ff), bf16)] * 2
     else:
-        in_specs[-12:] = [far] * 12
+        inputs = 9 if mode == "both" else 12
+        in_specs[-inputs:] = [far] * inputs
         out_specs[2 if mode == "both" else 1] = far
+    if mode == "forward":
+        scratch.append(pltpu.VMEM((rows, D), bf16))
     if forward:
-        scratch += [pltpu.VMEM((rows, D), bf16), pltpu.VMEM((most, D), f32)]
+        scratch.append(pltpu.VMEM((most, D), f32))
     if backward:
         scratch += [pltpu.VMEM((rows, D), bf16)] * 2
         scratch += [pltpu.VMEM((rows, ff), bf16)] * 3
         scratch += [pltpu.VMEM((D, rows), bf16), pltpu.VMEM((most, D), f32)]
-        scratch += [pltpu.VMEM(a.shape, a.dtype) for a in args[-12:]]
+        scratch += [pltpu.VMEM(a.shape, a.dtype) for a in args[-inputs:]]
+    if mode == "both":
+        scratch.append(pltpu.VMEM((2, ex.experts - 1, 8, 128), f32))
+        scratch.append(pltpu.VMEM((2, ex.experts, 8, 128), f32))
+        scratch += [pltpu.SemaphoreType.DMA((2, ex.experts - 1))] * 2
     scratch.append(pltpu.VMEM(packed, bf16))
     count = len(ex.waves)
     scratch += [pltpu.SemaphoreType.DMA((count, ex.experts - 1))] * 2
@@ -1382,19 +1470,18 @@
         keep["received"] = dispatch_call(ex, send)
         if last:
             gating = [
-                cotangent, n2, outs[11], slot_row[l], info, chosen_rows[l], gcol, small, z_rows,
-                mixes[l], middle, slot_col[l],
+                cotangent, n2, slot_row[l], info, chosen_rows[l], gcol, small, z_rows, mixes[l],
             ]
             done = exchange_call(
-                "both", pack, ex, [keep["received"], experts_w[l], outs[12]] + gating
+                "both", pack, ex, [keep["received"], experts_w[l], outs[11]] + gating
             )
-            keep["y"], keep["gin"], keep["dw"] = done[:3]
+            y_held, keep["gin"], keep["dw"] = done[:3]
             keep["gating"] = done[3:]
         else:
             keep["y"], keep["gate"], keep["up"] = exchange_call(
                 "forward", pack, ex, [keep["received"], experts_w[l]]
             )
-        front = [middle, n2, keep["y"], gcol, slot_col[l], small]
+            front = [middle, n2, keep["y"], gcol, slot_col[l], small]
         z_rows = info[0:16]
         saved.append(keep)
 
@@ -1419,8 +1506,6 @@
             keep["gin"], keep["dw"] = done[:2]
             keep["gating"] = done[2:]
         gn2, gsm, mix_grads[l], gz = keep["gating"][:4]
-        if last:
-            hidden_out = keep["gating"][4]
         d_experts, gn2 = lax.optimization_barrier((keep["dw"], gn2))
         if not last:
             gn2, expert_grads[l + 1] = lax.optimization_barrier((gn2, expert_grads[l + 1]))
@@ -1430,11 +1515,11 @@
             keep["n1"], keep["x"], bias_t, keep["lse"], gsm,
         ]
         if l > 0:
-            args += [slot_row[l - 1], saved[l - 1]["gpack"]]
+            args += [slot_row[l - 1], saved[l - 1]["gpack"], y_held, keep["n2"], keep["gcol"]]
         outs = backward_call(l == 0, experts, slots, args)
         gx, d_dense = outs[:2]
         if l > 0:
-            saved[l - 1]["gxs"], saved[l - 1]["gy"] = outs[2:4]
+            saved[l - 1]["gxs"], saved[l - 1]["gy"], hidden_out = outs[2:5]
         if l > 0:
             dense_grads[l] = lax.psum_scatter(d_dense, "shard", scatter_dimension=0, tiled=True)
 

time: 595 us -> 577 us (0.970)
  Pallas kernels: 517 us -> 495 us
    pallas_call x3, Pallas kernels: 223 us -> 190 us  [exchange_call(): pl.pallas_call(functools.partial(exchange_kernel, mode, pack, ex), out_sh...]
    pallas_call x5, Pallas kernels: 149 us -> 156 us  [whole_call(): pl.pallas_call(kernel, out_shape=outs, in_specs=[far if n in late or n in...]
  transfers between devices with their start and end apart: 7 -> 7, of which waited for: 2 -> 2; matrix products, arithmetic and copies ran while one was open for 4% -> 4% of each run, Pallas kernels for 68% -> 72%
where the time goes in v9:
time: 577 us; the launch traced here: 571 us
  Pallas kernels  495 us (86%)
  waiting for transfers between devices  28 us (5%)
  local copies, waits for them, and re-layouts  20.6 us (4%)
  between operations  15.1 us (3%)
  other arithmetic  7.41 us (1%)
    pallas_call x3, Pallas kernels, exchange_call(): pl.pallas_call(functools.partial(exchange_kernel, mode, pack, ex), out_sh...  190 us
    pallas_call x5, Pallas kernels, whole_call(): pl.pallas_call(kernel, out_shape=outs, in_specs=[far if n in late or n in...  156 us
    pallas_call x1, Pallas kernels, finish_call(): pl.pallas_call(functools.partial(cube_kernel, part, labels), out_shape=ou...  83 us
    pallas_call x2, Pallas kernels, dispatch_call(): pl.pallas_call(functools.partial(dispatch_kernel, ex), out_shape=shape((e...  66 us
    all_gather x2, waiting for transfers between devices, on_device(): dense.append(lax.all_gather(packed, 'shard', axis=0, tiled=True))  23.6 us
  transfers between devices with their start and end apart: 7, of which 2 were waited for; matrix products, arithmetic and copies ran while one was open for 4% of the time, Pallas kernels for 72%

profile of v9, /device:TPU:0, one launch (start us, length us, event | category | flops | bytes accessed | tf_op | source)
XLA Modules:
  0.0 570.7 jit_solution(8976239823778231924)
XLA Ops:
  7.2 0.8 slice_bitcast_fusion.9
  8.0 0.7 slice_bitcast_fusion.5
  8.7 0.7 slice_bitcast_fusion.7
  9.6 1.0 bitcast_dynamic-update-slice_fusion.3
  10.6 1.0 bitcast_dynamic-update-slice_fusion.2
  11.7 1.1 bitcast_dynamic-update-slice_fusion.1
  12.7 1.0 bitcast_dynamic-update-slice_fusion
  13.8 0.8 copy-done.3
  15.2 0.7 copy-done.6
  16.1 0.2 copy.177
  16.3 1.1 pad_maximum_fusion
  17.7 0.8 copy-done.2
  19.1 0.2 copy.185
  19.3 1.2 pad_maximum_fusion.1
  20.6 0.6 fusion.58
  21.2 0.7 copy.181.refs_9_
  21.9 0.6 fusion.57
  22.5 0.7 copy.173.refs_4_
  23.2 0.6 pad.44.refs_3_.refs_14_
  23.8 0.6 pad.51.refs_10_.refs_7_
  24.4 0.6 pad.46.refs_5_.refs_11_
  25.0 0.2 copy.193
  25.4 0.2 copy.194
  25.9 1.3 broadcast_select_fusion
  27.2 0.6 pad.52.refs_11_.refs_5_
  27.9 1.4 and_select_fusion.1.refs_4_.refs_3_
  29.3 4.3 fusion.9
  33.6 23.6 %all-gather.7.cloned.1.call-done.refs_1_.refs_6_ = bf16[768,3200]{1,0:T(8,128)(2,1)} async-done(((bf16[96,3200]{1,0:T(8,128)(2,1)}), bf16[768,3200]{1,0:T(8,128)(2,1)}) %all-gather.7.cloned.1.call-update) | async-done | bytes 4915216 | tf_op jit(solution)/shard_map/all_gather | solution.py:1415
  57.2 22.4 %block_forward.2 = (bf16[832,768]{1,0:T(8,128)(2,1)}, bf16[832,2304]{1,0:T(8,128)(2,1)}, bf16[832,768]{1,0:T(8,128)(2,1)}, f32[16,832]{1,0:T(8,128)}, f32[832,76...) custom-call(bf16[832,768]{1,0:T(8,128)(2,1)} %refs_9_.1, ...), custom_call_target="tpu_custom_call" | custom-call | flops 20000000000 | bytes 21816320 | tf_op jit(solution)/shard_map/block_forward/pallas_call | solution.py:336
  79.7 1.4 slice.130.refs_8_.refs_10_
  81.1 33.2 %dispatch.2.refs_0_ = bf16[960,768]{1,0:T(8,128)(2,1)} custom-call(bf16[960,768]{1,0:T(8,128)(2,1)} %get-tuple-element.77.send), custom_call_target="tpu_custom_call" | custom-call | flops 35000000512 | bytes 1000000 | tf_op jit(solution)/shard_map/dispatch/pallas_call | solution.py:826
  114.3 4.2 all-gather.11.cloned.1.call-done
  118.5 46.0 %experts_forward.1 = (bf16[960,768]{1,0:T(8,128)(2,1)}, bf16[960,2048]{1,0:T(8,128)(2,1)}, bf16[960,2048]{1,0:T(8,128)(2,1)}) custom-call(bf16[960,768]{1,0:T(8,128)(2,1)} %dispatch.2.refs_0_, bf16[8,2304,256]{2,1,0:T(8,128)(2,1)} %bitcast.129), custom_call_target="tpu_custom_call" | custom-call | flops 49059696640 | bytes 9437184 | tf_op jit(solution)/shard_map/experts_forward/pallas_call | solution.py:1293
  164.6 30.1 %block_forward.3 = (f32[832,768]{1,0:T(8,128)}, bf16[832,768]{1,0:T(8,128)(2,1)}, bf16[832,2304]{1,0:T(8,128)(2,1)}, bf16[832,768]{1,0:T(8,128)(2,1)}, f32[16,83...) custom-call(f32[832,768]{1,0:T(8,128)} %get-tuple-element.78.refs_0_, ...), custom_call_target="tpu_custom_call" | custom-call | flops 20000000000 | bytes 31791104 | tf_op jit(solution)/shard_map/block_forward/pallas_call | solution.py:336
  194.7 32.8 %dispatch.3.refs_0_ = bf16[960,768]{1,0:T(8,128)(2,1)} custom-call(bf16[960,768]{1,0:T(8,128)(2,1)} %get-tuple-element.84.send), custom_call_target="tpu_custom_call" | custom-call | flops 35000000512 | bytes 1000000 | tf_op jit(solution)/shard_map/dispatch/pallas_call | solution.py:826
  227.6 77.7 %experts_both.1 = (bf16[960,768]{1,0:T(8,128)(2,1)}, bf16[960,768]{1,0:T(8,128)(2,1)}, bf16[8,2304,256]{2,1,0:T(8,128)(2,1)}, f32[832,768]{1,0:T(8,128)}, f32[32...) custom-call(bf16[960,768]{1,0:T(8,128)(2,1)} %dispatch.3.refs_0_, bf16[8,2304,256]{2,1,0:T(8,128)(2,1)} %bitcast.153, ...), custom_call_target="tpu_custom_call" | custom-call | flops 67179089920 | bytes 9437184 | tf_op jit(solution)/shard_map/experts_both/pallas_call | solution.py:1293
  305.4 0.9 copy-done.1
  306.3 1.4 and_select_fusion.refs_3_
  307.7 53.8 %block_backward.2 = (f32[832,768]{1,0:T(8,128)}, bf16[768,3200]{1,0:T(8,128)(2,1)}, bf16[960,768]{1,0:T(8,128)(2,1)}, bf16[960,768]{1,0:T(8,128)(2,1)}, bf16[832,768]{1,0:T(8,128)(2,1)}) custom-call(bf16[832,768]{1,0:T(8,128)(2,1)} %refs_0_.3, f32[832,768]{1,0:T(8,128)} %get-tuple-element.92.refs_1_, bf16[960,768]{1,0:T(8,128)(2,1)} %get-tuple-element.93.refs_2_, ...), custom_call_target="tpu_custom_call" | custom-call | flops 40000000000 | bytes 39775232 | tf_op jit(solution)/shard_map/block_backward/pallas_call | solution.py:336
  361.5 0.3 reduce-scatter.4.cloned.1.call-start
  361.8 66.4 %experts_backward.1 = (bf16[960,768]{1,0:T(8,128)(2,1)}, bf16[8,2304,256]{2,1,0:T(8,128)(2,1)}, f32[832,768]{1,0:T(8,128)}, f32[32,768]{1,0:T(8,128)}, f32[16,16]{1,0:T(8,128)}, /*index=5*/f32[16,832]{1,0:T(8,128)}) custom-call(bf16[960,768]{1,0:T(8,128)(2,1)} %dispatch.2.refs_0_, bf16[8,2304,256]{2,1,0:T(8,128)(2,1)} %bitcast.130, ...), custom_call_target="tpu_custom_call" | custom-call | flops 1000000000 | bytes 9437184 | tf_op jit(solution)/shard_map/experts_backward/pallas_call | solution.py:1293
  428.2 0.6 copy-done.12
  428.9 0.6 select_maximum_fusion.mix_ref
  429.5 0.6 slice_bitcast_fusion.2
  430.1 43.3 %block_backward.3 = (f32[832,768]{1,0:T(8,128)}, bf16[768,3200]{1,0:T(8,128)(2,1)}) custom-call(f32[832,768]{1,0:T(8,128)} %get-tuple-element.106.refs_5_.refs_0_, f32[832,768]{1,0:T(8,128)} %get-tuple-element.115.refs_1_, bf16[960,768]{1,0:T(8,128)(2,1)} %get-tuple-element.116.refs_2_, f32[832,4]{1,0:T(8,128)} %and_select_fusion.1.refs_4_.refs_3_, ...), custom_call_target="tpu_custom_call" | custom-call | flops 40000000000 | bytes 32130048 | tf_op jit(solution)/shard_map/block_backward/pallas_call | solution.py:336
  473.4 83.0 %dense_sums.1 = (bf16[2,96,3328]{2,1,0:T(8,128)(2,1)}, f32[2,8,8]{2,1,0:T(8,128)}) custom-call(bf16[768,3200]{1,0:T(8,128)(2,1)} %get-tuple-element.122.g_ref, bf16[96,3200]{1,0:T(8,128)(2,1)} %reduce-scatter.8.cloned.1.call-done.upper_ref, f32[32,128]{1,0:T(8,128)} %select_maximum_fusion.mix_ref), custom_call_target="tpu_custom_call" | custom-call | flops 70000001024 | bytes 10000000 | tf_op jit(solution)/shard_map/dense_sums/pallas_call | solution.py:1210
  556.5 6.3 %outputs.1 = (f32[2,96,2048]{2,1,0:T(8,128)}, f32[2,96,2048]{2,1,0:T(8,128)}, f32[2,256,768]{2,1,0:T(8,128)}, f32[2,3,96,768]{3,2,1,0:T(8,128)}, f32[2,96,768]{2...) custom-call(bf16[2304,256]{1,0:T(8,128)(2,1)} %bitcast.150, ...), custom_call_target="tpu_custom_call" | custom-call | flops 1000000 | bytes 13283328 | tf_op jit(solution)/shard_map/outputs/pallas_call | solution.py:336
  562.8 0.6 copy.210
  (85 shorter events, 2.6 us)
Async XLA Ops:
  7.2 7.5 %copy-start.4 = (bf16[2,1,96,2048]{3,2,1,0:T(8,128)(2,1)S(1)}, bf16[2,1,96,2048]{3,2,1,0:T(8,128)(2,1)}, u32[]{:S(2)}) copy-start(bf16[2,1,96,2048]{3,2,1,0:T(8,128)(2,1)} %param.25) | copy-start | bytes 2359300
  7.2 50.0 %all-gather.7.cloned.1.call-start = ((), (), s32[]{:S(2)}) async-start(), calls=%async_computation.3 | async-start | bytes 5529600 | tf_op jit(solution)/shard_map/all_gather | solution.py:1415
  11.6 3.3 copy-start.5
  13.8 0.8 copy-start.3
  14.6 103.9 %all-gather.11.cloned.1.call-start = ((), (), s32[]{:S(2)}) async-start(), calls=%async_computation.8 | async-start | bytes 10616832 | tf_op jit(solution)/shard_map/all_gather | solution.py:1417
  14.7 1.1 copy-start.6
  17.4 147.2 %all-gather.9.cloned.1.call-start = ((), (), s32[]{:S(2)}) async-start(), calls=%async_computation.4 | async-start | bytes 5529600 | tf_op jit(solution)/shard_map/all_gather | solution.py:1415
  17.7 0.8 copy-start.2
  18.5 209.0 %all-gather.13.cloned.1.call-start = ((), (), s32[]{:S(2)}) async-start(), calls=%async_computation.9 | async-start | bytes 10616832 | tf_op jit(solution)/shard_map/all_gather | solution.py:1417
  19.1 1.5 copy-start.10
  19.1 4.0 copy-start.9
  19.1 4.0 copy-start.7
  20.5 5.3 copy-start.16
  20.5 5.4 copy-start.18
  20.5 7.3 %copy-start.17 = (s32[1,8]{1,0:T(1,128)S(1)}, s32[1,8]{1,0:T(1,128)}, u32[]{:S(2)}) copy-start(s32[1,8]{1,0:T(1,128)} %param.30) | copy-start | bytes 100
  20.5 409.6 %reduce-scatter.6.cloned.1.call-start = ((), (), s32[]{:S(2)}) async-start(), calls=%async_computation.6 | async-start | bytes 10616832 | tf_op jit(solution)/shard_map/reduce_scatter | solution.py:1512
  25.6 8.0 %copy-start = (f32[1,832,4]{2,1,0:T(8,128)}, f32[1,832,4]{2,1,0:T(8,128)S(1)}, u32[]{:S(2)}) copy-start(f32[1,832,4]{2,1,0:T(8,128)S(1)} %copy.194) | copy-start | bytes 39940
  25.9 7.8 %copy-start.14 = (s32[832]{0:T(1024)}, s32[832]{0:T(1024)S(1)}, u32[]{:S(2)}) copy-start(s32[832]{0:T(1024)S(1)} %reduce) | copy-start | bytes 9988
  305.3 1.0 copy-start.1
  305.3 1.0 copy-start.15
  305.4 168.1 %reduce-scatter.8.cloned.1.call-start = ((), (), s32[]{:S(2)}) async-start(), calls=%async_computation.7 | async-start | bytes 5529600 | tf_op jit(solution)/shard_map/reduce_scatter | solution.py:1524
  361.5 194.9 %reduce-scatter.4.cloned.1.call-start = ((), (), s32[]{:S(2)}) async-start(), calls=%async_computation.5 | async-start | bytes 10616832 | tf_op jit(solution)/shard_map/reduce_scatter | solution.py:1512
  428.2 0.7 copy-start.12
  428.2 0.7 copy-start.13
  428.2 1.3 copy-start.8
  556.5 6.4 %copy-start.11 = (f32[2,8,8]{2,1,0:T(8,128)S(1)}, f32[2,8,8]{2,1,0:T(8,128)}, u32[]{:S(2)}) copy-start(f32[2,8,8]{2,1,0:T(8,128)} %get-tuple-element.268) | copy-start | bytes 1540
Sparse Core Ops, SparseCore 0:
  14.7 42.4 all-gather.6
  59.7 58.8 all-gather.10
  121.0 39.7 all-gather.8
  162.5 58.8 all-gather.12
  305.5 78.6 reduce-scatter.5
  387.6 54.8 reduce-scatter.7
  446.4 91.6 reduce-scatter.3

commit v10 on v9

--- a/solution.py
+++ b/solution.py
@@ -132,7 +132,7 @@
     n1_ref, qkv_ref, att_ref, lse_ref, mid_ref, n2_ref, info_ref, gcol_ref, gpack_ref, send_ref = [
         refs.pop(0) for _ in range(10)
     ]
-    small_out = refs.pop(0)
+    small_out, z_out = refs.pop(0), refs.pop(0)
     small_out[...] = w_ref[:, W_SMALL:]
     if last:
         gy_ref = refs.pop(0)
@@ -236,6 +236,7 @@
     prob = expo / jnp.sum(expo, axis=0, keepdims=True)
     gates = prob * chosen_ref[...]
     info_ref[0:16, :] = logits
+    z_out[...] = logits
     info_ref[16:32, :] = prob
     turn[...] = jnp.zeros_like(turn)
     turn[0:16, 0:tokens] = gates
@@ -365,6 +366,7 @@
         shape((tokens, 128), bf16),
         shape((sent, D), bf16),
         shape((D, 128), bf16),
+        shape((16, tokens)),
     ]
     if last:
         outs += [shape((sent, D), bf16)]
@@ -1037,6 +1039,7 @@
 
 
 SPLIT = 13 * 128
+QUARTER = 7 * 128
 
 
 def cube_kernel(part, labels, g_ref, upper_ref, mix_ref, ready, mix_out, own, *refs):
@@ -1083,42 +1086,45 @@
     def copy(n, src, dst, to):
         return remote(src, dst, send.at[n], recv.at[n], {"shard": to})
 
-    def quarter(owner):
-        return (
-            pl.ds(pl.multiple_of((owner // 2) * (part // 2), 16), part // 2),
-            pl.ds(pl.multiple_of(lax.rem(owner, 2) * SPLIT, 128), SPLIT),
-        )
-
-    def spread(l):
+    half = part // 2
+    jobs = ((1, 0, part), (0, 0, half), (0, half, half))
+
+    def quarter(job, owner):
+        l, start, size = jobs[job]
+        return l, pl.ds(start, size), pl.ds(pl.multiple_of(owner * QUARTER, 128), QUARTER)
+
+    def spread(job):
         made = []
+        held = pl.ds(0, jobs[job][2])
         for d in range(1, owners):
             to = lax.rem(z + d, owners)
             made.append(
                 remote(
-                    mine.at[(l, *quarter(to))],
-                    quarters.at[l, z],
-                    z_send.at[l, 0, d - 1],
-                    z_recv.at[l, 0, d - 1],
+                    mine.at[quarter(job, to)],
+                    quarters.at[job, z, held],
+                    z_send.at[job, 0, d - 1],
+                    z_recv.at[job, 0, d - 1],
                     {"expert": to},
                 )
             )
-        quarters[l, z] = mine[(l, *quarter(z))]
+        quarters[job, z, held] = mine[quarter(job, z)]
         return made
 
-    def gather(l, made):
+    def gather(job, made):
         for one in made:
             one.wait_recv()
-        total = quarters[l, 0].astype(f32)
+        held = pl.ds(0, jobs[job][2])
+        total = quarters[job, 0, held].astype(f32)
         for owner in range(1, owners):
-            total = total + quarters[l, owner].astype(f32)
-        ready[(l, *quarter(z))] = total.astype(bf16)
-        here = (l, *quarter(z))
+            total = total + quarters[job, owner, held].astype(f32)
+        here = quarter(job, z)
+        ready[here] = total.astype(bf16)
         return [
             remote(
                 ready.at[here],
                 ready.at[here],
-                z_send.at[l, 1, d - 1],
-                z_recv.at[l, 1, d - 1],
+                z_send.at[job, 1, d - 1],
+                z_recv.at[job, 1, d - 1],
                 {"expert": lax.rem(z + d, owners)},
             )
             for d in range(1, owners)
@@ -1140,64 +1146,95 @@
             for l in range(LAYERS):
                 mix_out[l] = total[l * 16 : l * 16 + labels, 0:labels]
 
-    first = [
-        copy(n, g_ref.at[rows(2 * chip + 1 - core)], got_c.at[chip], near)
-        for n, chip in enumerate(chips)
-    ]
+    def begin(h):
+        shift = h * half
+        return [
+            copy(
+                10 * h + n,
+                g_ref.at[pl.ds(pl.multiple_of((2 * chip + 1 - core) * part + shift, 16), half)],
+                got_c.at[chip, pl.ds(shift, half)],
+                near,
+            )
+            for n, chip in enumerate(chips)
+        ]
+
+    def cross(h, first):
+        hs = pl.ds(h * half, half)
+
+        def merge(n):
+            if h == 0:
+                loads[n].wait()
+            first[n].wait_recv()
+            chip = chips[n]
+            value = own[n, hs, :].astype(f32) + got_c[chip, hs, :].astype(f32)
+            sums[chip, hs, :] = value.astype(bf16)
+
+        merge(0)
+        a0 = copy(10 * h + 4, sums.at[chips[0], hs, cols_a], got_a.at[1 - y, hs], over_x)
+        b0 = copy(10 * h + 5, sums.at[chips[0], hs, cols_b], got_b.at[1 - x, hs], over_y)
+        merge(1)
+        a1 = copy(10 * h + 6, sums.at[chips[1], hs, cols_a], got_a.at[y, hs], over_x)
+        merge(2)
+        b1 = copy(10 * h + 7, sums.at[chips[2], hs, cols_b], got_b.at[x, hs], over_y)
+        merge(3)
+        return a0, b0, a1, b1
+
+    def turn_over(h, crossed):
+        hs = pl.ds(h * half, half)
+        a0, b0 = crossed[:2]
+        a0.wait_recv()
+        value = sums[chips[2], hs, cols_a].astype(f32) + got_a[1 - y, hs, :].astype(f32)
+        half_a[hs, :] = value.astype(bf16)
+        a2 = copy(10 * h + 8, half_a.at[hs], end_a.at[hs], over_y)
+        b0.wait_recv()
+        value = sums[chips[1], hs, cols_b].astype(f32) + got_b[1 - x, hs, :].astype(f32)
+        half_b[hs, :] = value.astype(bf16)
+        b2 = copy(10 * h + 9, half_b.at[hs], end_b.at[hs], over_x)
+        return a2, b2
+
+    def end(h, crossed, turned):
+        hs = pl.ds(h * half, half)
+        parts = (
+            (cols_a, crossed[2], turned[0], got_a.at[y], end_a),
+            (cols_b, crossed[3], turned[1], got_b.at[x], end_b),
+        )
+        for cols, one, two, got, last in parts:
+            one.wait_recv()
+            value = sums[chips[3], hs, cols].astype(f32) + got[hs, :].astype(f32)
+            two.wait_recv()
+            mine[0, hs, cols] = (value + last[hs, :].astype(f32)).astype(bf16)
+        return spread(1 + h)
+
+    first = [begin(0), begin(1)]
     mix = [mix_start(0)]
-    mine[0, :, W_ALL:] = jnp.zeros((part, 2 * SPLIT - W_ALL), bf16)
-    mine[1, :, W_ALL:] = jnp.zeros((part, 2 * SPLIT - W_ALL), bf16)
+    for l in range(2):
+        mine[l, :, W_ALL:] = jnp.zeros((part, 4 * QUARTER - W_ALL), bf16)
     mine[1, :, 0:W_ALL] = upper_ref[...]
-    upper = spread(1)
-
-    def merge(n):
-        chip = chips[n]
-        loads[n].wait()
-        first[n].wait_recv()
-        sums[chip] = (own[n].astype(f32) + got_c[chip].astype(f32)).astype(bf16)
-
-    def total(chip, cols, got):
-        return sums[chip, :, cols].astype(f32) + got[...].astype(f32)
-
-    merge(0)
-    a0 = copy(4, sums.at[chips[0], :, cols_a], got_a.at[1 - y], over_x)
-    b0 = copy(5, sums.at[chips[0], :, cols_b], got_b.at[1 - x], over_y)
-    merge(1)
-    a1 = copy(6, sums.at[chips[1], :, cols_a], got_a.at[y], over_x)
-    merge(2)
-    b1 = copy(7, sums.at[chips[2], :, cols_b], got_b.at[x], over_y)
-    merge(3)
+    upper = spread(0)
+    crossed = [cross(0, first[0])]
     mix_end(0, mix[0])
     mix.append(mix_start(1))
-    a0.wait_recv()
-    half_a[...] = total(chips[2], cols_a, got_a.at[1 - y]).astype(bf16)
-    a2 = copy(8, half_a, end_a, over_y)
-    b0.wait_recv()
-    half_b[...] = total(chips[1], cols_b, got_b.at[1 - x]).astype(bf16)
-    b2 = copy(9, half_b, end_b, over_x)
+    crossed.append(cross(1, first[1]))
+    turned = [turn_over(0, crossed[0])]
     mix_end(1, mix[1])
     mix.append(mix_start(2))
-    last_upper = gather(1, upper)
-    a1.wait_recv()
-    keep_a = total(chips[3], cols_a, got_a.at[y])
-    a2.wait_recv()
-    mine[0, :, cols_a] = (keep_a + end_a[...].astype(f32)).astype(bf16)
-    b1.wait_recv()
-    keep_b = total(chips[3], cols_b, got_b.at[x])
-    b2.wait_recv()
-    mine[0, :, cols_b] = (keep_b + end_b[...].astype(f32)).astype(bf16)
-    lower = spread(0)
+    upper_back = gather(0, upper)
+    turned.append(turn_over(1, crossed[1]))
+    lower = [end(0, crossed[0], turned[0])]
     mix_end(2, mix[2])
     mix.append(mix_start(3))
-    for made in last_upper:
-        made.wait_recv()
+    lower.append(end(1, crossed[1], turned[1]))
+    lower_back = gather(1, lower[0])
     mix_end(3, mix[3])
     mix.append(mix_start(4))
-    last_lower = gather(0, lower)
+    lower_back += gather(2, lower[1])
     mix_end(4, mix[4])
-    for made in last_lower:
+    for made in upper_back + lower_back:
         made.wait_recv()
-    for made in first + [a0, b0, a1, b1, a2, b2] + mix + upper + lower + last_upper + last_lower:
+    started = mix + upper + upper_back + lower_back
+    for h in range(2):
+        started += first[h] + list(crossed[h]) + list(turned[h]) + lower[h]
+    for made in started:
         made.wait_send()
 
 
@@ -1205,7 +1242,7 @@
     vmem = pl.BlockSpec(memory_space=pltpu.VMEM)
     rest = W_ALL - SPLIT
     owners = lax.axis_size("expert")
-    outs = [shape((2, part, 2 * SPLIT), bf16), shape((LAYERS, labels, labels))]
+    outs = [shape((2, part, 4 * QUARTER), bf16), shape((LAYERS, labels, labels))]
     dma = pltpu.SemaphoreType.DMA
     return pl.pallas_call(
         functools.partial(cube_kernel, part, labels),
@@ -1222,14 +1259,14 @@
             pltpu.VMEM((part, rest), bf16),
             pltpu.VMEM((part, SPLIT), bf16),
             pltpu.VMEM((part, rest), bf16),
-            pltpu.VMEM((2, part, 2 * SPLIT), bf16),
-            pltpu.VMEM((2, owners, part // 2, SPLIT), bf16),
+            pltpu.VMEM((2, part, 4 * QUARTER), bf16),
+            pltpu.VMEM((3, owners, part, QUARTER), bf16),
             pltpu.VMEM((5, 32, 128), f32),
             pltpu.VMEM((5, 32, 128), f32),
-            dma((10,)),
-            dma((10,)),
-            dma((2, 2, owners - 1)),
-            dma((2, 2, owners - 1)),
+            dma((20,)),
+            dma((20,)),
+            dma((3, 2, owners - 1)),
+            dma((3, 2, owners - 1)),
             dma((5,)),
             dma((5,)),
             dma((4,)),
@@ -1365,6 +1402,19 @@
     return whole_call(body, "outputs", outs, turn, grads + [dense, hidden], 10**6, (3,), (0, 1, 2, 3, 4, 9))
 
 
+def pack_kernel(traffic, proj_ref, out_ref, small_ref, *packed):
+    for l, ref in enumerate(packed):
+        for c in range(3):
+            ref[:, c * D : (c + 1) * D] = proj_ref[l, c]
+        ref[:, W_OUT:W_SMALL] = out_ref[l]
+        ref[:, W_SMALL:] = small_ref[l]
+
+
+def pack_call(project, output, small):
+    outs = [shape((project.shape[2], W_ALL), bf16)] * LAYERS
+    return whole_call(pack_kernel, "pack", outs, [], [project, output, small], 10**6)
+
+
 def on_device(
     hidden_in,
     prior_logits,
@@ -1396,23 +1446,20 @@
     dense = []
     experts_w = []
     pack = Packing(lax.axis_size("shard"), part, gate_weight.shape[3])
+    small = jnp.concatenate(
+        [
+            pad_cols(router_weight, S_CONST),
+            const_weight[:, 0],
+            const_weight[:, 1],
+            jnp.zeros((LAYERS, part, S_GAIN - S_CONST - 4), bf16),
+            norm_gain.transpose(0, 2, 1),
+            const_vector.transpose(0, 2, 1),
+        ],
+        axis=2,
+    )
+    packed = pack_call(project_weight, output_weight, pad_cols(small, 128))
     for l in range(LAYERS):
-        small = jnp.concatenate(
-            [
-                pad_cols(router_weight[l], S_CONST),
-                const_weight[l, 0],
-                const_weight[l, 1],
-                jnp.zeros((part, S_GAIN - S_CONST - 4), bf16),
-                norm_gain[l].T,
-                const_vector[l].T,
-            ],
-            axis=1,
-        )
-        packed = jnp.concatenate(
-            [project_weight[l, c] for c in range(3)] + [output_weight[l], pad_cols(small, 128)],
-            axis=1,
-        )
-        dense.append(lax.all_gather(packed, "shard", axis=0, tiled=True))
+        dense.append(lax.all_gather(packed[l], "shard", axis=0, tiled=True))
         mine = pack.pack(gate_weight[l, 0], up_weight[l, 0], down_weight[l, 0])
         experts_w.append(lax.all_gather(mine, "shard", axis=0, tiled=False))
 
@@ -1450,6 +1497,8 @@
     ]
     z_rows = jnp.pad(prior_logits.T, [(0, 16 - total_experts), (0, 0)])
 
+    plan = (bias, bias_t, slot_col, slot_row, chosen_rows, mixes, z_rows)
+    bias, bias_t, slot_col, slot_row, chosen_rows, mixes, z_rows = lax.optimization_barrier(plan)
     ex = Exchange(experts, slots)
     saved = []
     front = [hidden_in]
@@ -1462,7 +1511,7 @@
         outs = list(forward_call(l == 0, last, experts, slots, args))
         if l > 0:
             x_now = outs.pop(0)
-        n1, qkv, att, lse, middle, n2, info, gcol, gpack, send, small = outs[:11]
+        n1, qkv, att, lse, middle, n2, info, gcol, gpack, send, small, z_next = outs[:12]
         keep = dict(
             x=x_now, n1=n1, qkv=qkv, att=att, lse=lse, middle=middle, n2=n2, info=info,
             gcol=gcol, gpack=gpack, z=z_rows, small=small,
@@ -1473,7 +1522,7 @@
                 cotangent, n2, slot_row[l], info, chosen_rows[l], gcol, small, z_rows, mixes[l],
             ]
             done = exchange_call(
-                "both", pack, ex, [keep["received"], experts_w[l], outs[11]] + gating
+                "both", pack, ex, [keep["received"], experts_w[l], outs[12]] + gating
             )
             y_held, keep["gin"], keep["dw"] = done[:3]
             keep["gating"] = done[3:]
@@ -1482,7 +1531,7 @@
                 "forward", pack, ex, [keep["received"], experts_w[l]]
             )
             front = [middle, n2, keep["y"], gcol, slot_col[l], small]
-        z_rows = info[0:16]
+        z_rows = z_next
         saved.append(keep)
 
     gx = cotangent

time: 577 us -> 568 us (0.984)
  local copies, waits for them, and re-layouts: 20.6 us -> 12.4 us
    pallas_call x1, Pallas kernels: 83 us -> 75.5 us  [finish_call(): pl.pallas_call(functools.partial(cube_kernel, part, labels), out_shape=ou...]
    pallas_call x5 -> x6, Pallas kernels: 156 us -> 158 us  [whole_call(): pl.pallas_call(kernel, out_shape=outs, in_specs=[far if n in late or n in...]
  transfers between devices with their start and end apart: 7 -> 7, of which waited for: 2 -> 2; matrix products, arithmetic and copies ran while one was open for 4% -> 3% of each run, Pallas kernels for 72% -> 72%
where the time goes in v10:
time: 568 us; the launch traced here: 564 us
  Pallas kernels  494 us (87%)
  waiting for transfers between devices  30.1 us (5%)
  between operations  15 us (3%)
  local copies, waits for them, and re-layouts  12.4 us (2%)
  other arithmetic  7.37 us (1%)
    pallas_call x3, Pallas kernels, exchange_call(): pl.pallas_call(functools.partial(exchange_kernel, mode, pack, ex), out_sh...  195 us
    pallas_call x6, Pallas kernels, whole_call(): pl.pallas_call(kernel, out_shape=outs, in_specs=[far if n in late or n in...  158 us
    pallas_call x1, Pallas kernels, finish_call(): pl.pallas_call(functools.partial(cube_kernel, part, labels), out_shape=ou...  75.5 us
    pallas_call x2, Pallas kernels, dispatch_call(): pl.pallas_call(functools.partial(dispatch_kernel, ex), out_shape=shape((e...  66 us
    all_gather x2, waiting for transfers between devices, on_device(): dense.append(lax.all_gather(packed[l], 'shard', axis=0, tiled=True))  23.7 us
  transfers between devices with their start and end apart: 7, of which 2 were waited for; matrix products, arithmetic and copies ran while one was open for 3% of the time, Pallas kernels for 72%

profile of v10, /device:TPU:0, one launch (start us, length us, event | category | flops | bytes accessed | tf_op | source)
XLA Modules:
  0.0 563.8 jit_solution(1893394083612381220)
XLA Ops:
  7.2 0.8 fusion.57
  8.0 0.7 copy.157
  8.7 0.7 constant_dynamic-update-slice_fusion.1
  9.4 0.7 constant_dynamic-update-slice_fusion
  10.1 0.1 copy.162
  10.3 0.6 pad.37.refs_2_
  10.9 2.4 pack.1
  13.9 0.7 copy-done.2
  14.7 0.2 copy.190
  14.9 0.2 copy.175
  15.0 1.1 pad_maximum_fusion
  16.2 0.7 all-gather.9.cloned.1.call-update
  17.3 0.2 copy.191
  17.5 0.2 copy.180
  17.7 1.1 pad_maximum_fusion.1
  19.0 0.6 pad.41.refs_10_.refs_7_
  19.6 0.6 pad.40.refs_5_.refs_11_
  20.3 0.6 pad.44.refs_3_.refs_14_
  20.9 0.2 copy.189
  21.1 0.2 copy.170
  21.3 0.2 copy.188
  21.5 0.2 copy.169
  21.7 1.3 broadcast_select_fusion
  23.0 0.6 pad.39.refs_11_.refs_5_
  23.6 0.1 select_reduce_fusion
  23.7 1.4 and_select_fusion.1.refs_4_.refs_3_
  25.2 1.4 and_select_fusion.refs_3_
  26.6 4.4 fusion.9
  30.9 0.7 copy.176.refs_9_
  31.6 0.7 copy.171.refs_4_
  32.3 23.7 %all-gather.7.cloned.1.call-done.refs_1_.refs_6_ = bf16[768,3200]{1,0:T(8,128)(2,1)} async-done(((bf16[96,3200]{1,0:T(8,128)(2,1)}), bf16[768,3200]{1,0:T(8,128)(2,1)}) %all-gather.7.cloned.1.call-update) | async-done | bytes 4915216 | tf_op jit(solution)/shard_map/all_gather | solution.py:1462
  56.0 22.5 %block_forward.2 = (bf16[832,768]{1,0:T(8,128)(2,1)}, bf16[832,2304]{1,0:T(8,128)(2,1)}, bf16[832,768]{1,0:T(8,128)(2,1)}, f32[16,832]{1,0:T(8,128)}, f32[832,76...) custom-call(bf16[832,768]{1,0:T(8,128)(2,1)} %refs_9_.1, ...), custom_call_target="tpu_custom_call" | custom-call | flops 20000000000 | bytes 21869568 | tf_op jit(solution)/shard_map/block_forward/pallas_call | solution.py:337
  78.5 33.2 %dispatch.2.refs_0_ = bf16[960,768]{1,0:T(8,128)(2,1)} custom-call(bf16[960,768]{1,0:T(8,128)(2,1)} %get-tuple-element.97.send), custom_call_target="tpu_custom_call" | custom-call | flops 35000000512 | bytes 1000000 | tf_op jit(solution)/shard_map/dispatch/pallas_call | solution.py:828
  111.7 5.6 all-gather.11.cloned.1.call-done
  117.3 46.0 %experts_forward.1 = (bf16[960,768]{1,0:T(8,128)(2,1)}, bf16[960,2048]{1,0:T(8,128)(2,1)}, bf16[960,2048]{1,0:T(8,128)(2,1)}) custom-call(bf16[960,768]{1,0:T(8,128)(2,1)} %dispatch.2.refs_0_, bf16[8,2304,256]{2,1,0:T(8,128)(2,1)} %bitcast.95), custom_call_target="tpu_custom_call" | custom-call | flops 49059696640 | bytes 9437184 | tf_op jit(solution)/shard_map/experts_forward/pallas_call | solution.py:1330
  163.3 30.2 %block_forward.3 = (f32[832,768]{1,0:T(8,128)}, bf16[832,768]{1,0:T(8,128)(2,1)}, bf16[832,2304]{1,0:T(8,128)(2,1)}, bf16[832,768]{1,0:T(8,128)(2,1)}, f32[16,83...) custom-call(f32[832,768]{1,0:T(8,128)} %get-tuple-element.98.refs_0_, ...), custom_call_target="tpu_custom_call" | custom-call | flops 20000000000 | bytes 31844352 | tf_op jit(solution)/shard_map/block_forward/pallas_call | solution.py:337
  193.5 32.8 %dispatch.3.refs_0_ = bf16[960,768]{1,0:T(8,128)(2,1)} custom-call(bf16[960,768]{1,0:T(8,128)(2,1)} %get-tuple-element.109.send), custom_call_target="tpu_custom_call" | custom-call | flops 35000000512 | bytes 1000000 | tf_op jit(solution)/shard_map/dispatch/pallas_call | solution.py:828
  226.3 77.7 %experts_both.1 = (bf16[960,768]{1,0:T(8,128)(2,1)}, bf16[960,768]{1,0:T(8,128)(2,1)}, bf16[8,2304,256]{2,1,0:T(8,128)(2,1)}, f32[832,768]{1,0:T(8,128)}, f32[32...) custom-call(bf16[960,768]{1,0:T(8,128)(2,1)} %dispatch.3.refs_0_, bf16[8,2304,256]{2,1,0:T(8,128)(2,1)} %bitcast.121, ...), custom_call_target="tpu_custom_call" | custom-call | flops 67179089920 | bytes 9437184 | tf_op jit(solution)/shard_map/experts_both/pallas_call | solution.py:1330
  304.1 53.0 %block_backward.2 = (f32[832,768]{1,0:T(8,128)}, bf16[768,3200]{1,0:T(8,128)(2,1)}, bf16[960,768]{1,0:T(8,128)(2,1)}, bf16[960,768]{1,0:T(8,128)(2,1)}, bf16[832,768]{1,0:T(8,128)(2,1)}) custom-call(bf16[832,768]{1,0:T(8,128)(2,1)} %refs_0_.5, f32[832,768]{1,0:T(8,128)} %get-tuple-element.117.refs_1_, bf16[960,768]{1,0:T(8,128)(2,1)} %get-tuple-element.118.refs_2_, ...), custom_call_target="tpu_custom_call" | custom-call | flops 40000000000 | bytes 39775232 | tf_op jit(solution)/shard_map/block_backward/pallas_call | solution.py:337
  357.1 0.3 reduce-scatter.4.cloned.1.call-start
  357.4 71.5 %experts_backward.1 = (bf16[960,768]{1,0:T(8,128)(2,1)}, bf16[8,2304,256]{2,1,0:T(8,128)(2,1)}, f32[832,768]{1,0:T(8,128)}, f32[32,768]{1,0:T(8,128)}, f32[16,16]{1,0:T(8,128)}, /*index=5*/f32[16,832]{1,0:T(8,128)}) custom-call(bf16[960,768]{1,0:T(8,128)(2,1)} %dispatch.2.refs_0_, bf16[8,2304,256]{2,1,0:T(8,128)(2,1)} %bitcast.96, ...), custom_call_target="tpu_custom_call" | custom-call | flops 1000000000 | bytes 9437184 | tf_op jit(solution)/shard_map/experts_backward/pallas_call | solution.py:1330
  429.0 0.6 copy-done.10
  429.7 0.6 select_maximum_fusion.mix_ref
  430.3 0.6 slice_bitcast_fusion.2
  430.9 43.1 %block_backward.3 = (f32[832,768]{1,0:T(8,128)}, bf16[768,3200]{1,0:T(8,128)(2,1)}) custom-call(f32[832,768]{1,0:T(8,128)} %get-tuple-element.133.refs_5_.refs_0_, f32[832,768]{1,0:T(8,128)} %get-tuple-element.143.refs_1_, bf16[960,768]{1,0:T(8,128)(2,1)} %get-tuple-element.144.refs_2_, f32[832,4]{1,0:T(8,128)} %and_select_fusion.1.refs_4_.refs_3_, ...), custom_call_target="tpu_custom_call" | custom-call | flops 40000000000 | bytes 32130048 | tf_op jit(solution)/shard_map/block_backward/pallas_call | solution.py:337
  474.0 75.5 %dense_sums.1 = (bf16[2,96,3584]{2,1,0:T(8,128)(2,1)}, f32[2,8,8]{2,1,0:T(8,128)}) custom-call(bf16[768,3200]{1,0:T(8,128)(2,1)} %get-tuple-element.150.g_ref, bf16[96,3200]{1,0:T(8,128)(2,1)} %reduce-scatter.8.cloned.1.call-done.upper_ref, f32[32,128]{1,0:T(8,128)} %select_maximum_fusion.mix_ref), custom_call_target="tpu_custom_call" | custom-call | flops 70000001024 | bytes 10000000 | tf_op jit(solution)/shard_map/dense_sums/pallas_call | solution.py:1247
  549.5 6.4 %outputs.1 = (f32[2,96,2048]{2,1,0:T(8,128)}, f32[2,96,2048]{2,1,0:T(8,128)}, f32[2,256,768]{2,1,0:T(8,128)}, f32[2,3,96,768]{3,2,1,0:T(8,128)}, f32[2,96,768]{2...) custom-call(bf16[2304,256]{1,0:T(8,128)(2,1)} %bitcast.116, ...), custom_call_target="tpu_custom_call" | custom-call | flops 1000000 | bytes 13381632 | tf_op jit(solution)/shard_map/outputs/pallas_call | solution.py:337
  555.9 0.6 copy.210
  (71 shorter events, 1.5 us)
Async XLA Ops:
  7.2 6.2 %copy-start = (bf16[2,1,96,2048]{3,2,1,0:T(8,128)(2,1)S(1)}, bf16[2,1,96,2048]{3,2,1,0:T(8,128)(2,1)}, u32[]{:S(2)}) copy-start(bf16[2,1,96,2048]{3,2,1,0:T(8,128)(2,1)} %param.25) | copy-start | bytes 2359300
  7.2 48.8 %all-gather.7.cloned.1.call-start = ((), (), s32[]{:S(2)}) async-start(), calls=%async_computation.3 | async-start | bytes 5529600 | tf_op jit(solution)/shard_map/all_gather | solution.py:1462
  10.9 2.8 copy-start.1
  13.4 103.9 %all-gather.11.cloned.1.call-start = ((), (), s32[]{:S(2)}) async-start(), calls=%async_computation.8 | async-start | bytes 10616832 | tf_op jit(solution)/shard_map/all_gather | solution.py:1464
  13.5 1.1 copy-start.2
  16.1 147.2 %all-gather.9.cloned.1.call-start = ((), (), s32[]{:S(2)}) async-start(), calls=%async_computation.4 | async-start | bytes 5529600 | tf_op jit(solution)/shard_map/all_gather | solution.py:1462
  16.9 209.4 %all-gather.13.cloned.1.call-start = ((), (), s32[]{:S(2)}) async-start(), calls=%async_computation.9 | async-start | bytes 10616832 | tf_op jit(solution)/shard_map/all_gather | solution.py:1464
  17.4 1.4 copy-start.7
  17.4 1.5 copy-start.8
  17.5 2.8 copy-start.5
  17.6 4.0 copy-start.12
  17.7 4.0 copy-start.14
  18.8 4.8 copy-start.13
  18.8 412.0 %reduce-scatter.6.cloned.1.call-start = ((), (), s32[]{:S(2)}) async-start(), calls=%async_computation.6 | async-start | bytes 10616832 | tf_op jit(solution)/shard_map/reduce_scatter | solution.py:1561
  19.0 12.0 %copy-start.4 = (f32[16,16]{1,0:T(8,128)}, f32[16,16]{1,0:T(8,128)S(1)}, u32[]{:S(2)}) copy-start(f32[16,16]{1,0:T(8,128)S(1)} %pad.43.refs_11_) | copy-start | bytes 3076
  19.0 12.6 %copy-start.3 = (f32[16,16]{1,0:T(8,128)}, f32[16,16]{1,0:T(8,128)S(1)}, u32[]{:S(2)}) copy-start(f32[16,16]{1,0:T(8,128)S(1)} %pad.42.refs_15_) | copy-start | bytes 3076
  304.0 170.0 %reduce-scatter.8.cloned.1.call-start = ((), (), s32[]{:S(2)}) async-start(), calls=%async_computation.7 | async-start | bytes 5529600 | tf_op jit(solution)/shard_map/reduce_scatter | solution.py:1573
  357.1 192.4 %reduce-scatter.4.cloned.1.call-start = ((), (), s32[]{:S(2)}) async-start(), calls=%async_computation.5 | async-start | bytes 10616832 | tf_op jit(solution)/shard_map/reduce_scatter | solution.py:1561
  428.9 0.7 copy-start.10
  428.9 0.7 copy-start.11
  429.0 1.3 copy-start.6
  549.5 6.4 %copy-start.9 = (f32[2,8,8]{2,1,0:T(8,128)S(1)}, f32[2,8,8]{2,1,0:T(8,128)}, u32[]{:S(2)}) copy-start(f32[2,8,8]{2,1,0:T(8,128)} %get-tuple-element.274) | copy-start | bytes 1540
Sparse Core Ops, SparseCore 0:
  13.5 42.4 all-gather.6
  58.4 58.8 all-gather.10
  119.7 39.7 all-gather.8
  161.3 58.8 all-gather.12
  304.2 78.9 reduce-scatter.5
  386.5 54.8 reduce-scatter.7
  445.3 93.6 reduce-scatter.3

commit v11 on v10

--- a/solution.py
+++ b/solution.py
@@ -983,6 +983,8 @@
         if mode == "backward":
             traffic.need(*gating)
             gating_kernel(False, ex.experts, ex.slots, *gating, *gating_outs)
+            for copy in arrivals[1]:
+                copy.start()
     for copy in loads:
         copy.wait()
     if backward:
@@ -994,8 +996,9 @@
             dots[1, me, :, 0 : ex.slots - ex.half] = own_dots[:, ex.half :]
         for copy in arrivals[0]:
             copy.wait_send()
-        for copy in arrivals[1]:
-            copy.start()
+        if mode == "both":
+            for copy in arrivals[1]:
+                copy.start()
         for copy in arrivals[0]:
             copy.wait_recv()
     for n, group in enumerate(groups):

time: 568 us -> 568 us (level)
  no operation moved by 1% of the time
where the time goes in v11:
time: 568 us; the launch traced here: 562 us
  Pallas kernels  493 us (87%)
  waiting for transfers between devices  30.1 us (5%)
  between operations  15 us (3%)
  local copies, waits for them, and re-layouts  12.4 us (2%)
  other arithmetic  7.37 us (1%)
    pallas_call x3, Pallas kernels, exchange_call(): pl.pallas_call(functools.partial(exchange_kernel, mode, pack, ex), out_sh...  191 us
    pallas_call x6, Pallas kernels, whole_call(): pl.pallas_call(kernel, out_shape=outs, in_specs=[far if n in late or n in...  157 us
    pallas_call x1, Pallas kernels, finish_call(): pl.pallas_call(functools.partial(cube_kernel, part, labels), out_shape=ou...  78.5 us
    pallas_call x2, Pallas kernels, dispatch_call(): pl.pallas_call(functools.partial(dispatch_kernel, ex), out_shape=shape((e...  66 us
    all_gather x2, waiting for transfers between devices, on_device(): dense.append(lax.all_gather(packed[l], 'shard', axis=0, tiled=True))  23.7 us
  transfers between devices with their start and end apart: 7, of which 2 were waited for; matrix products, arithmetic and copies ran while one was open for 3% of the time, Pallas kernels for 72%

profile of v11, /device:TPU:0, one launch (start us, length us, event | category | flops | bytes accessed | tf_op | source)
XLA Modules:
  0.0 562.0 jit_solution(6815717398392149682)
XLA Ops:
  7.2 0.8 fusion.57
  8.0 0.7 copy.157
  8.7 0.7 constant_dynamic-update-slice_fusion.1
  9.4 0.7 constant_dynamic-update-slice_fusion
  10.1 0.1 copy.162
  10.3 0.6 pad.37.refs_2_
  10.9 2.4 pack.1
  13.9 0.7 copy-done.2
  14.7 0.2 copy.190
  14.9 0.2 copy.175
  15.0 1.1 pad_maximum_fusion
  16.2 0.7 all-gather.9.cloned.1.call-update
  17.3 0.2 copy.191
  17.5 0.2 copy.180
  17.7 1.1 pad_maximum_fusion.1
  19.0 0.6 pad.41.refs_10_.refs_7_
  19.6 0.6 pad.40.refs_5_.refs_11_
  20.3 0.6 pad.44.refs_3_.refs_14_
  20.9 0.2 copy.189
  21.1 0.2 copy.170
  21.3 0.2 copy.188
  21.5 0.2 copy.169
  21.7 1.3 broadcast_select_fusion
  23.0 0.6 pad.39.refs_11_.refs_5_
  23.6 0.1 select_reduce_fusion
  23.7 1.4 and_select_fusion.1.refs_4_.refs_3_
  25.2 1.4 and_select_fusion.refs_3_
  26.6 4.4 fusion.9
  30.9 0.7 copy.176.refs_9_
  31.6 0.7 copy.171.refs_4_
  32.3 23.7 %all-gather.7.cloned.1.call-done.refs_1_.refs_6_ = bf16[768,3200]{1,0:T(8,128)(2,1)} async-done(((bf16[96,3200]{1,0:T(8,128)(2,1)}), bf16[768,3200]{1,0:T(8,128)(2,1)}) %all-gather.7.cloned.1.call-update) | async-done | bytes 4915216 | tf_op jit(solution)/shard_map/all_gather | solution.py:1465
  56.0 22.5 %block_forward.2 = (bf16[832,768]{1,0:T(8,128)(2,1)}, bf16[832,2304]{1,0:T(8,128)(2,1)}, bf16[832,768]{1,0:T(8,128)(2,1)}, f32[16,832]{1,0:T(8,128)}, f32[832,76...) custom-call(bf16[832,768]{1,0:T(8,128)(2,1)} %refs_9_.1, ...), custom_call_target="tpu_custom_call" | custom-call | flops 20000000000 | bytes 21869568 | tf_op jit(solution)/shard_map/block_forward/pallas_call | solution.py:337
  78.5 33.2 %dispatch.2.refs_0_ = bf16[960,768]{1,0:T(8,128)(2,1)} custom-call(bf16[960,768]{1,0:T(8,128)(2,1)} %get-tuple-element.97.send), custom_call_target="tpu_custom_call" | custom-call | flops 35000000512 | bytes 1000000 | tf_op jit(solution)/shard_map/dispatch/pallas_call | solution.py:828
  111.7 5.6 all-gather.11.cloned.1.call-done
  117.3 46.0 %experts_forward.1 = (bf16[960,768]{1,0:T(8,128)(2,1)}, bf16[960,2048]{1,0:T(8,128)(2,1)}, bf16[960,2048]{1,0:T(8,128)(2,1)}) custom-call(bf16[960,768]{1,0:T(8,128)(2,1)} %dispatch.2.refs_0_, bf16[8,2304,256]{2,1,0:T(8,128)(2,1)} %bitcast.95), custom_call_target="tpu_custom_call" | custom-call | flops 49059696640 | bytes 9437184 | tf_op jit(solution)/shard_map/experts_forward/pallas_call | solution.py:1333
  163.3 30.2 %block_forward.3 = (f32[832,768]{1,0:T(8,128)}, bf16[832,768]{1,0:T(8,128)(2,1)}, bf16[832,2304]{1,0:T(8,128)(2,1)}, bf16[832,768]{1,0:T(8,128)(2,1)}, f32[16,83...) custom-call(f32[832,768]{1,0:T(8,128)} %get-tuple-element.98.refs_0_, ...), custom_call_target="tpu_custom_call" | custom-call | flops 20000000000 | bytes 31844352 | tf_op jit(solution)/shard_map/block_forward/pallas_call | solution.py:337
  193.5 32.8 %dispatch.3.refs_0_ = bf16[960,768]{1,0:T(8,128)(2,1)} custom-call(bf16[960,768]{1,0:T(8,128)(2,1)} %get-tuple-element.109.send), custom_call_target="tpu_custom_call" | custom-call | flops 35000000512 | bytes 1000000 | tf_op jit(solution)/shard_map/dispatch/pallas_call | solution.py:828
  226.3 77.7 %experts_both.1 = (bf16[960,768]{1,0:T(8,128)(2,1)}, bf16[960,768]{1,0:T(8,128)(2,1)}, bf16[8,2304,256]{2,1,0:T(8,128)(2,1)}, f32[832,768]{1,0:T(8,128)}, f32[32...) custom-call(bf16[960,768]{1,0:T(8,128)(2,1)} %dispatch.3.refs_0_, bf16[8,2304,256]{2,1,0:T(8,128)(2,1)} %bitcast.121, ...), custom_call_target="tpu_custom_call" | custom-call | flops 67179089920 | bytes 9437184 | tf_op jit(solution)/shard_map/experts_both/pallas_call | solution.py:1333
  304.1 53.0 %block_backward.2 = (f32[832,768]{1,0:T(8,128)}, bf16[768,3200]{1,0:T(8,128)(2,1)}, bf16[960,768]{1,0:T(8,128)(2,1)}, bf16[960,768]{1,0:T(8,128)(2,1)}, bf16[832,768]{1,0:T(8,128)(2,1)}) custom-call(bf16[832,768]{1,0:T(8,128)(2,1)} %refs_0_.5, f32[832,768]{1,0:T(8,128)} %get-tuple-element.117.refs_1_, bf16[960,768]{1,0:T(8,128)(2,1)} %get-tuple-element.118.refs_2_, ...), custom_call_target="tpu_custom_call" | custom-call | flops 40000000000 | bytes 39775232 | tf_op jit(solution)/shard_map/block_backward/pallas_call | solution.py:337
  357.1 0.3 reduce-scatter.4.cloned.1.call-start
  357.4 67.0 %experts_backward.1 = (bf16[960,768]{1,0:T(8,128)(2,1)}, bf16[8,2304,256]{2,1,0:T(8,128)(2,1)}, f32[832,768]{1,0:T(8,128)}, f32[32,768]{1,0:T(8,128)}, f32[16,16]{1,0:T(8,128)}, /*index=5*/f32[16,832]{1,0:T(8,128)}) custom-call(bf16[960,768]{1,0:T(8,128)(2,1)} %dispatch.2.refs_0_, bf16[8,2304,256]{2,1,0:T(8,128)(2,1)} %bitcast.96, ...), custom_call_target="tpu_custom_call" | custom-call | flops 1000000000 | bytes 9437184 | tf_op jit(solution)/shard_map/experts_backward/pallas_call | solution.py:1333
  424.5 0.6 copy-done.10
  425.1 0.6 select_maximum_fusion.mix_ref
  425.7 0.6 slice_bitcast_fusion.2
  426.3 42.9 %block_backward.3 = (f32[832,768]{1,0:T(8,128)}, bf16[768,3200]{1,0:T(8,128)(2,1)}) custom-call(f32[832,768]{1,0:T(8,128)} %get-tuple-element.133.refs_5_.refs_0_, f32[832,768]{1,0:T(8,128)} %get-tuple-element.143.refs_1_, bf16[960,768]{1,0:T(8,128)(2,1)} %get-tuple-element.144.refs_2_, f32[832,4]{1,0:T(8,128)} %and_select_fusion.1.refs_4_.refs_3_, ...), custom_call_target="tpu_custom_call" | custom-call | flops 40000000000 | bytes 32130048 | tf_op jit(solution)/shard_map/block_backward/pallas_call | solution.py:337
  469.2 78.5 %dense_sums.1 = (bf16[2,96,3584]{2,1,0:T(8,128)(2,1)}, f32[2,8,8]{2,1,0:T(8,128)}) custom-call(bf16[768,3200]{1,0:T(8,128)(2,1)} %get-tuple-element.150.g_ref, bf16[96,3200]{1,0:T(8,128)(2,1)} %reduce-scatter.8.cloned.1.call-done.upper_ref, f32[32,128]{1,0:T(8,128)} %select_maximum_fusion.mix_ref), custom_call_target="tpu_custom_call" | custom-call | flops 70000001024 | bytes 10000000 | tf_op jit(solution)/shard_map/dense_sums/pallas_call | solution.py:1250
  547.8 6.4 %outputs.1 = (f32[2,96,2048]{2,1,0:T(8,128)}, f32[2,96,2048]{2,1,0:T(8,128)}, f32[2,256,768]{2,1,0:T(8,128)}, f32[2,3,96,768]{3,2,1,0:T(8,128)}, f32[2,96,768]{2...) custom-call(bf16[2304,256]{1,0:T(8,128)(2,1)} %bitcast.116, ...), custom_call_target="tpu_custom_call" | custom-call | flops 1000000 | bytes 13381632 | tf_op jit(solution)/shard_map/outputs/pallas_call | solution.py:337
  554.1 0.6 copy.210
  (71 shorter events, 1.5 us)
Async XLA Ops:
  7.2 6.2 %copy-start = (bf16[2,1,96,2048]{3,2,1,0:T(8,128)(2,1)S(1)}, bf16[2,1,96,2048]{3,2,1,0:T(8,128)(2,1)}, u32[]{:S(2)}) copy-start(bf16[2,1,96,2048]{3,2,1,0:T(8,128)(2,1)} %param.25) | copy-start | bytes 2359300
  7.2 48.8 %all-gather.7.cloned.1.call-start = ((), (), s32[]{:S(2)}) async-start(), calls=%async_computation.3 | async-start | bytes 5529600 | tf_op jit(solution)/shard_map/all_gather | solution.py:1465
  10.9 2.8 copy-start.1
  13.4 103.9 %all-gather.11.cloned.1.call-start = ((), (), s32[]{:S(2)}) async-start(), calls=%async_computation.8 | async-start | bytes 10616832 | tf_op jit(solution)/shard_map/all_gather | solution.py:1467
  13.5 1.1 copy-start.2
  16.1 147.2 %all-gather.9.cloned.1.call-start = ((), (), s32[]{:S(2)}) async-start(), calls=%async_computation.4 | async-start | bytes 5529600 | tf_op jit(solution)/shard_map/all_gather | solution.py:1465
  16.9 209.4 %all-gather.13.cloned.1.call-start = ((), (), s32[]{:S(2)}) async-start(), calls=%async_computation.9 | async-start | bytes 10616832 | tf_op jit(solution)/shard_map/all_gather | solution.py:1467
  17.4 1.4 copy-start.7
  17.4 1.5 copy-start.8
  17.5 2.8 copy-start.5
  17.6 4.0 copy-start.12
  17.7 4.0 copy-start.14
  18.8 4.8 copy-start.13
  18.8 407.5 %reduce-scatter.6.cloned.1.call-start = ((), (), s32[]{:S(2)}) async-start(), calls=%async_computation.6 | async-start | bytes 10616832 | tf_op jit(solution)/shard_map/reduce_scatter | solution.py:1564
  19.0 12.0 %copy-start.4 = (f32[16,16]{1,0:T(8,128)}, f32[16,16]{1,0:T(8,128)S(1)}, u32[]{:S(2)}) copy-start(f32[16,16]{1,0:T(8,128)S(1)} %pad.43.refs_11_) | copy-start | bytes 3076
  19.0 12.6 %copy-start.3 = (f32[16,16]{1,0:T(8,128)}, f32[16,16]{1,0:T(8,128)S(1)}, u32[]{:S(2)}) copy-start(f32[16,16]{1,0:T(8,128)S(1)} %pad.42.refs_15_) | copy-start | bytes 3076
  304.0 165.2 %reduce-scatter.8.cloned.1.call-start = ((), (), s32[]{:S(2)}) async-start(), calls=%async_computation.7 | async-start | bytes 5529600 | tf_op jit(solution)/shard_map/reduce_scatter | solution.py:1576
  357.1 190.6 %reduce-scatter.4.cloned.1.call-start = ((), (), s32[]{:S(2)}) async-start(), calls=%async_computation.5 | async-start | bytes 10616832 | tf_op jit(solution)/shard_map/reduce_scatter | solution.py:1564
  424.4 0.7 copy-start.10
  424.4 0.7 copy-start.11
  424.4 1.3 copy-start.6
  547.7 6.4 %copy-start.9 = (f32[2,8,8]{2,1,0:T(8,128)S(1)}, f32[2,8,8]{2,1,0:T(8,128)}, u32[]{:S(2)}) copy-start(f32[2,8,8]{2,1,0:T(8,128)} %get-tuple-element.274) | copy-start | bytes 1540
Sparse Core Ops, SparseCore 0:
  13.5 42.4 all-gather.6
  58.4 58.8 all-gather.10
  119.7 39.7 all-gather.8
  161.3 58.8 all-gather.12
  304.2 78.9 reduce-scatter.5
  386.5 54.8 reduce-scatter.7
  445.3 94.4 reduce-scatter.3

commit v12 on v11

--- a/solution.py
+++ b/solution.py
@@ -385,7 +385,7 @@
     return (dot_nt(ones, upper) + dot_nt(ones, lower))[0:8, :]
 
 
-def gating_kernel(last, experts, slots, *refs):
+def gating_steps(last, experts, slots, *refs):
     refs = list(refs)
     gx_ref, n2_ref = refs.pop(0), refs.pop(0)
     if last:
@@ -402,8 +402,42 @@
     size, block = row_blocks(tokens)
     small = small_ref[...].astype(f32).T
     small_half = small[0:32, :].astype(bf16)
+    ones = jnp.ones((16, D), bf16)
+    gx = gx_ref[...].astype(f32)
+    gx_half = gx.astype(bf16)
+    n2 = n2_ref[...]
+    upper, lower = split_bf16(gx * n2.astype(f32))
+    gx_n2 = (dot_nt(ones, upper) + dot_nt(ones, lower))[0:1, :]
+    gx_small = dot_nt(small_half, gx_half)
+    prob = info_ref[16:32, :]
+    chosen = chosen_ref[...]
+    gates = prob * chosen
+    trow = lax.broadcasted_iota(jnp.int32, (16, tokens), 0)
+    gp = jnp.where(trow == experts + 1, gx_n2, 0.0)
+    crow = lax.broadcasted_iota(jnp.int32, (8, tokens), 0)
+    glog = jnp.zeros((8, tokens), f32)
+    coefs = jnp.zeros((8, tokens), f32)
+    for c in range(2):
+        a0 = info_ref[32 + 2 * c : 33 + 2 * c, :]
+        a1 = info_ref[33 + 2 * c : 34 + 2 * c, :]
+        gx_v = gx_small[S_VEC + c : S_VEC + c + 1, :]
+        share = gates[experts + 2 + c : experts + 3 + c, :]
+        gp = jnp.where(trow == experts + 2 + c, a0 * gx_n2 + a1 * gx_v, gp)
+        gl = share * (gx_n2 - gx_v) * a0 * a1
+        glog = jnp.where(crow == 2 * c, gl, jnp.where(crow == 2 * c + 1, -gl, glog))
+        coefs = jnp.where(crow == c, share * a1, coefs)
+    cu, cl = split_bf16(jnp.concatenate([coefs, jnp.zeros((8, tokens), f32)], axis=0))
+    gvec = dot(cu, gx_half) + dot(cl, gx_half)
+
+    def add(i, carry):
+        rows = block(i)
+        gn2_ref[rows, :] = gcol_ref[rows, 16:17] * gx_ref[rows, :].astype(f32)
+        return carry
+
+    lax.fori_loop(0, BLOCKS, add, 0)
+
+    yield
     slot_row = slotr_ref[...]
-    ones = jnp.ones((16, D), bf16)
     row = lax.broadcasted_iota(jnp.int32, (16, slots), 0)
     scattered = jnp.zeros((16, tokens), f32)
     for e in range(experts):
@@ -420,32 +454,9 @@
             row == 8 + e, lower.astype(f32), 0.0
         )
         scattered = scattered + dot(lhs.astype(bf16), one_hot(slot_row, e, slots))
-    gx = gx_ref[...].astype(f32)
-    gx_half = gx.astype(bf16)
-    n2 = n2_ref[...]
-    upper, lower = split_bf16(gx * n2.astype(f32))
-    gx_n2 = (dot_nt(ones, upper) + dot_nt(ones, lower))[0:1, :]
-    gx_small = dot_nt(small_half, gx_half)
-    prob = info_ref[16:32, :]
-    chosen = chosen_ref[...]
-    gates = prob * chosen
-    trow = lax.broadcasted_iota(jnp.int32, (16, tokens), 0)
-    gp = jnp.concatenate([scattered[0:8, :] + scattered[8:16, :], jnp.zeros((8, tokens), f32)], 0)
-    weighted = gp if last else prob * gp
+    dotted = jnp.concatenate([scattered[0:8, :] + scattered[8:16, :], jnp.zeros((8, tokens), f32)], 0)
+    weighted = dotted if last else prob * dotted
     weighted = jnp.where(trow < experts, weighted, 0.0) * chosen
-    gp = jnp.where(trow == experts + 1, gx_n2, 0.0)
-    crow = lax.broadcasted_iota(jnp.int32, (8, tokens), 0)
-    glog = jnp.zeros((8, tokens), f32)
-    coefs = jnp.zeros((8, tokens), f32)
-    for c in range(2):
-        a0 = info_ref[32 + 2 * c : 33 + 2 * c, :]
-        a1 = info_ref[33 + 2 * c : 34 + 2 * c, :]
-        gx_v = gx_small[S_VEC + c : S_VEC + c + 1, :]
-        share = gates[experts + 2 + c : experts + 3 + c, :]
-        gp = jnp.where(trow == experts + 2 + c, a0 * gx_n2 + a1 * gx_v, gp)
-        gl = share * (gx_n2 - gx_v) * a0 * a1
-        glog = jnp.where(crow == 2 * c, gl, jnp.where(crow == 2 * c + 1, -gl, glog))
-        coefs = jnp.where(crow == c, share * a1, coefs)
     weighted = weighted + prob * gp * chosen
     gz = weighted - prob * jnp.sum(weighted, axis=0, keepdims=True)
     if not last:
@@ -462,22 +473,18 @@
     allg = jnp.concatenate([gz, glog, jnp.zeros((8, tokens), f32)], axis=0)
     upper, lower = split_bf16(allg)
     gsm = dot(upper, n2) + dot(lower, n2)
-    cu, cl = split_bf16(jnp.concatenate([coefs, jnp.zeros((8, tokens), f32)], axis=0))
-    gvec = dot(cu, gx_half) + dot(cl, gx_half)
     gsm_ref[0:24, :] = gsm[0:24, :]
     gsm_ref[24:32, :] = jnp.concatenate(
         [jnp.zeros((2, D), f32), gvec[0:2, :], jnp.zeros((4, D), f32)], axis=0
     )
     both = jnp.concatenate([upper, lower], axis=0)
     twice = jnp.concatenate([small_half, small_half], axis=0)
-    gn2_ref[...] = dot_tn(both, twice)
-
-    def add(i, carry):
-        rows = block(i)
-        gn2_ref[rows, :] = gn2_ref[rows, :] + gcol_ref[rows, 16:17] * gx_ref[rows, :].astype(f32)
-        return carry
-
-    lax.fori_loop(0, BLOCKS, add, 0)
+    gn2_ref[...] = gn2_ref[...] + dot_tn(both, twice)
+
+
+def gating_kernel(*args):
+    for _ in gating_steps(*args):
+        pass
 
 
 def gating_outputs():
@@ -994,6 +1001,11 @@
             me = lax.axis_index("expert")
             dots[0, me, :, 0 : ex.half] = own_dots[:, 0 : ex.half]
             dots[1, me, :, 0 : ex.slots - ex.half] = own_dots[:, ex.half :]
+            traffic.need(*gating)
+            steps = gating_steps(
+                True, ex.experts, ex.slots, *gating[:2], dots, *gating[2:], *gating_outs
+            )
+            next(steps)
         for copy in arrivals[0]:
             copy.wait_send()
         if mode == "both":
@@ -1032,8 +1044,8 @@
     for copy in ys + dot_copies:
         copy.wait()
     if mode == "both":
-        traffic.need(*gating)
-        gating_kernel(True, ex.experts, ex.slots, *gating[:2], dots, *gating[2:], *gating_outs)
+        for _ in steps:
+            pass
     for copy in gs:
         copy.wait()
     if backward:

time: 568 us -> 566 us (level)
  transfers between devices with their start and end apart: 7 -> 7, of which waited for: 2 -> 2; matrix products, arithmetic and copies ran while one was open for 3% -> 3% of each run, Pallas kernels for 72% -> 73%
where the time goes in v12:
time: 566 us; the launch traced here: 561 us
  Pallas kernels  492 us (87%)
  waiting for transfers between devices  30.1 us (5%)
  between operations  15 us (3%)
  local copies, waits for them, and re-layouts  12.4 us (2%)
  other arithmetic  7.37 us (1%)
    pallas_call x3, Pallas kernels, exchange_call(): pl.pallas_call(functools.partial(exchange_kernel, mode, pack, ex), out_sh...  188 us
    pallas_call x6, Pallas kernels, whole_call(): pl.pallas_call(kernel, out_shape=outs, in_specs=[far if n in late or n in...  158 us
    pallas_call x1, Pallas kernels, finish_call(): pl.pallas_call(functools.partial(cube_kernel, part, labels), out_shape=ou...  78.7 us
    pallas_call x2, Pallas kernels, dispatch_call(): pl.pallas_call(functools.partial(dispatch_kernel, ex), out_shape=shape((e...  66 us
    all_gather x2, waiting for transfers between devices, on_device(): dense.append(lax.all_gather(packed[l], 'shard', axis=0, tiled=True))  23.7 us
  transfers between devices with their start and end apart: 7, of which 2 were waited for; matrix products, arithmetic and copies ran while one was open for 3% of the time, Pallas kernels for 73%

profile of v12, /device:TPU:0, one launch (start us, length us, event | category | flops | bytes accessed | tf_op | source)
XLA Modules:
  0.0 560.9 jit_solution(11896465397160684980)
XLA Ops:
  7.2 0.8 fusion.57
  8.0 0.7 copy.157
  8.7 0.7 constant_dynamic-update-slice_fusion.1
  9.4 0.7 constant_dynamic-update-slice_fusion
  10.1 0.1 copy.162
  10.3 0.6 pad.37.refs_2_
  10.9 2.4 pack.1
  13.8 0.1 copy.193
  13.9 0.7 copy-done.2
  14.7 0.2 copy.190
  14.9 0.2 copy.175
  15.0 1.1 pad_maximum_fusion
  16.2 0.7 all-gather.9.cloned.1.call-update
  17.3 0.2 copy.191
  17.5 0.2 copy.180
  17.7 1.1 pad_maximum_fusion.1
  19.0 0.6 pad.41.refs_10_.refs_7_
  19.6 0.6 pad.40.refs_5_.refs_11_
  20.3 0.6 pad.44.refs_3_.refs_14_
  20.9 0.2 copy.189
  21.1 0.2 copy.170
  21.3 0.2 copy.188
  21.5 0.2 copy.169
  21.7 1.3 broadcast_select_fusion
  23.0 0.6 pad.39.refs_11_.refs_5_
  23.6 0.1 select_reduce_fusion
  23.7 1.4 and_select_fusion.1.refs_4_.refs_3_
  25.2 1.4 and_select_fusion.refs_3_
  26.6 4.4 fusion.9
  30.9 0.7 copy.176.refs_9_
  31.6 0.7 copy.171.refs_4_
  32.3 23.7 %all-gather.7.cloned.1.call-done.refs_1_.refs_6_ = bf16[768,3200]{1,0:T(8,128)(2,1)} async-done(((bf16[96,3200]{1,0:T(8,128)(2,1)}), bf16[768,3200]{1,0:T(8,128)(2,1)}) %all-gather.7.cloned.1.call-update) | async-done | bytes 4915216 | tf_op jit(solution)/shard_map/all_gather | solution.py:1477
  56.0 22.5 %block_forward.2 = (bf16[832,768]{1,0:T(8,128)(2,1)}, bf16[832,2304]{1,0:T(8,128)(2,1)}, bf16[832,768]{1,0:T(8,128)(2,1)}, f32[16,832]{1,0:T(8,128)}, f32[832,76...) custom-call(bf16[832,768]{1,0:T(8,128)(2,1)} %refs_9_.1, ...), custom_call_target="tpu_custom_call" | custom-call | flops 20000000000 | bytes 21869568 | tf_op jit(solution)/shard_map/block_forward/pallas_call | solution.py:337
  78.5 33.2 %dispatch.2.refs_0_ = bf16[960,768]{1,0:T(8,128)(2,1)} custom-call(bf16[960,768]{1,0:T(8,128)(2,1)} %get-tuple-element.97.send), custom_call_target="tpu_custom_call" | custom-call | flops 35000000512 | bytes 1000000 | tf_op jit(solution)/shard_map/dispatch/pallas_call | solution.py:835
  111.7 5.6 all-gather.11.cloned.1.call-done
  117.3 46.0 %experts_forward.1 = (bf16[960,768]{1,0:T(8,128)(2,1)}, bf16[960,2048]{1,0:T(8,128)(2,1)}, bf16[960,2048]{1,0:T(8,128)(2,1)}) custom-call(bf16[960,768]{1,0:T(8,128)(2,1)} %dispatch.2.refs_0_, bf16[8,2304,256]{2,1,0:T(8,128)(2,1)} %bitcast.95), custom_call_target="tpu_custom_call" | custom-call | flops 49059696640 | bytes 9437184 | tf_op jit(solution)/shard_map/experts_forward/pallas_call | solution.py:1345
  163.3 30.2 %block_forward.3 = (f32[832,768]{1,0:T(8,128)}, bf16[832,768]{1,0:T(8,128)(2,1)}, bf16[832,2304]{1,0:T(8,128)(2,1)}, bf16[832,768]{1,0:T(8,128)(2,1)}, f32[16,83...) custom-call(f32[832,768]{1,0:T(8,128)} %get-tuple-element.98.refs_0_, ...), custom_call_target="tpu_custom_call" | custom-call | flops 20000000000 | bytes 31844352 | tf_op jit(solution)/shard_map/block_forward/pallas_call | solution.py:337
  193.5 32.8 %dispatch.3.refs_0_ = bf16[960,768]{1,0:T(8,128)(2,1)} custom-call(bf16[960,768]{1,0:T(8,128)(2,1)} %get-tuple-element.109.send), custom_call_target="tpu_custom_call" | custom-call | flops 35000000512 | bytes 1000000 | tf_op jit(solution)/shard_map/dispatch/pallas_call | solution.py:835
  226.3 76.1 %experts_both.1 = (bf16[960,768]{1,0:T(8,128)(2,1)}, bf16[960,768]{1,0:T(8,128)(2,1)}, bf16[8,2304,256]{2,1,0:T(8,128)(2,1)}, f32[832,768]{1,0:T(8,128)}, f32[32...) custom-call(bf16[960,768]{1,0:T(8,128)(2,1)} %dispatch.3.refs_0_, bf16[8,2304,256]{2,1,0:T(8,128)(2,1)} %bitcast.121, ...), custom_call_target="tpu_custom_call" | custom-call | flops 67179089920 | bytes 9437184 | tf_op jit(solution)/shard_map/experts_both/pallas_call | solution.py:1345
  302.5 54.1 %block_backward.2 = (f32[832,768]{1,0:T(8,128)}, bf16[768,3200]{1,0:T(8,128)(2,1)}, bf16[960,768]{1,0:T(8,128)(2,1)}, bf16[960,768]{1,0:T(8,128)(2,1)}, bf16[832,768]{1,0:T(8,128)(2,1)}) custom-call(bf16[832,768]{1,0:T(8,128)(2,1)} %refs_0_.5, f32[832,768]{1,0:T(8,128)} %get-tuple-element.117.refs_1_, bf16[960,768]{1,0:T(8,128)(2,1)} %get-tuple-element.118.refs_2_, ...), custom_call_target="tpu_custom_call" | custom-call | flops 40000000000 | bytes 39775232 | tf_op jit(solution)/shard_map/block_backward/pallas_call | solution.py:337
  356.6 66.4 %experts_backward.1 = (bf16[960,768]{1,0:T(8,128)(2,1)}, bf16[8,2304,256]{2,1,0:T(8,128)(2,1)}, f32[832,768]{1,0:T(8,128)}, f32[32,768]{1,0:T(8,128)}, f32[16,16]{1,0:T(8,128)}, /*index=5*/f32[16,832]{1,0:T(8,128)}) custom-call(bf16[960,768]{1,0:T(8,128)(2,1)} %dispatch.2.refs_0_, bf16[8,2304,256]{2,1,0:T(8,128)(2,1)} %bitcast.96, ...), custom_call_target="tpu_custom_call" | custom-call | flops 1000000000 | bytes 9437184 | tf_op jit(solution)/shard_map/experts_backward/pallas_call | solution.py:1345
  423.0 0.6 copy-done.10
  423.7 0.6 select_maximum_fusion.mix_ref
  424.3 0.6 slice_bitcast_fusion.2
  424.9 42.9 %block_backward.3 = (f32[832,768]{1,0:T(8,128)}, bf16[768,3200]{1,0:T(8,128)(2,1)}) custom-call(f32[832,768]{1,0:T(8,128)} %get-tuple-element.133.refs_5_.refs_0_, f32[832,768]{1,0:T(8,128)} %get-tuple-element.143.refs_1_, bf16[960,768]{1,0:T(8,128)(2,1)} %get-tuple-element.144.refs_2_, f32[832,4]{1,0:T(8,128)} %and_select_fusion.1.refs_4_.refs_3_, ...), custom_call_target="tpu_custom_call" | custom-call | flops 40000000000 | bytes 32130048 | tf_op jit(solution)/shard_map/block_backward/pallas_call | solution.py:337
  467.8 78.7 %dense_sums.1 = (bf16[2,96,3584]{2,1,0:T(8,128)(2,1)}, f32[2,8,8]{2,1,0:T(8,128)}) custom-call(bf16[768,3200]{1,0:T(8,128)(2,1)} %get-tuple-element.150.g_ref, bf16[96,3200]{1,0:T(8,128)(2,1)} %reduce-scatter.8.cloned.1.call-done.upper_ref, f32[32,128]{1,0:T(8,128)} %select_maximum_fusion.mix_ref), custom_call_target="tpu_custom_call" | custom-call | flops 70000001024 | bytes 10000000 | tf_op jit(solution)/shard_map/dense_sums/pallas_call | solution.py:1262
  546.6 6.4 %outputs.1 = (f32[2,96,2048]{2,1,0:T(8,128)}, f32[2,96,2048]{2,1,0:T(8,128)}, f32[2,256,768]{2,1,0:T(8,128)}, f32[2,3,96,768]{3,2,1,0:T(8,128)}, f32[2,96,768]{2...) custom-call(bf16[2304,256]{1,0:T(8,128)(2,1)} %bitcast.116, ...), custom_call_target="tpu_custom_call" | custom-call | flops 1000000 | bytes 13381632 | tf_op jit(solution)/shard_map/outputs/pallas_call | solution.py:337
  553.0 0.6 copy.210
  (71 shorter events, 1.4 us)
Async XLA Ops:
  7.2 6.2 %copy-start = (bf16[2,1,96,2048]{3,2,1,0:T(8,128)(2,1)S(1)}, bf16[2,1,96,2048]{3,2,1,0:T(8,128)(2,1)}, u32[]{:S(2)}) copy-start(bf16[2,1,96,2048]{3,2,1,0:T(8,128)(2,1)} %param.25) | copy-start | bytes 2359300
  7.2 48.8 %all-gather.7.cloned.1.call-start = ((), (), s32[]{:S(2)}) async-start(), calls=%async_computation.3 | async-start | bytes 5529600 | tf_op jit(solution)/shard_map/all_gather | solution.py:1477
  10.9 2.8 copy-start.1
  13.4 103.9 %all-gather.11.cloned.1.call-start = ((), (), s32[]{:S(2)}) async-start(), calls=%async_computation.8 | async-start | bytes 10616832 | tf_op jit(solution)/shard_map/all_gather | solution.py:1479
  13.5 1.1 copy-start.2
  16.1 147.2 %all-gather.9.cloned.1.call-start = ((), (), s32[]{:S(2)}) async-start(), calls=%async_computation.4 | async-start | bytes 5529600 | tf_op jit(solution)/shard_map/all_gather | solution.py:1477
  16.9 209.4 %all-gather.13.cloned.1.call-start = ((), (), s32[]{:S(2)}) async-start(), calls=%async_computation.9 | async-start | bytes 10616832 | tf_op jit(solution)/shard_map/all_gather | solution.py:1479
  17.4 1.4 copy-start.7
  17.4 1.5 copy-start.8
  17.5 2.8 copy-start.5
  17.6 4.0 copy-start.12
  17.7 4.0 copy-start.14
  18.8 4.8 copy-start.13
  18.8 406.1 %reduce-scatter.6.cloned.1.call-start = ((), (), s32[]{:S(2)}) async-start(), calls=%async_computation.6 | async-start | bytes 10616832 | tf_op jit(solution)/shard_map/reduce_scatter | solution.py:1576
  19.0 12.0 %copy-start.4 = (f32[16,16]{1,0:T(8,128)}, f32[16,16]{1,0:T(8,128)S(1)}, u32[]{:S(2)}) copy-start(f32[16,16]{1,0:T(8,128)S(1)} %pad.43.refs_11_) | copy-start | bytes 3076
  19.0 12.6 %copy-start.3 = (f32[16,16]{1,0:T(8,128)}, f32[16,16]{1,0:T(8,128)S(1)}, u32[]{:S(2)}) copy-start(f32[16,16]{1,0:T(8,128)S(1)} %pad.42.refs_15_) | copy-start | bytes 3076
  302.4 165.4 %reduce-scatter.8.cloned.1.call-start = ((), (), s32[]{:S(2)}) async-start(), calls=%async_computation.7 | async-start | bytes 5529600 | tf_op jit(solution)/shard_map/reduce_scatter | solution.py:1588
  356.6 190.0 %reduce-scatter.4.cloned.1.call-start = ((), (), s32[]{:S(2)}) async-start(), calls=%async_computation.5 | async-start | bytes 10616832 | tf_op jit(solution)/shard_map/reduce_scatter | solution.py:1576
  423.0 0.7 copy-start.10
  423.0 0.7 copy-start.11
  423.0 1.3 copy-start.6
  546.6 6.4 %copy-start.9 = (f32[2,8,8]{2,1,0:T(8,128)S(1)}, f32[2,8,8]{2,1,0:T(8,128)}, u32[]{:S(2)}) copy-start(f32[2,8,8]{2,1,0:T(8,128)} %get-tuple-element.274) | copy-start | bytes 1540
Sparse Core Ops, SparseCore 0:
  13.5 42.4 all-gather.6
  58.4 58.8 all-gather.10
  119.7 39.7 all-gather.8
  161.3 58.8 all-gather.12
  302.5 79.9 reduce-scatter.5
  385.9 54.8 reduce-scatter.7
  444.7 95.6 reduce-scatter.3
